TPU v7x, 32 devices: a whole 2x2x4 slice. The times are simulated.
32 devices in a mesh: dp: 8 (over y, x, core), fsdp: 4 (over z).
Axes of the slice: x: 2, y: 2, z: 4, core: 2. Of those that a mesh axis runs over, the one named last changes fastest.
Arguments:
- bytes_in: bfloat16 [24, 2048, 768], P('dp', 'fsdp'), may hold values from -6 to 6
- latents_in: bfloat16 [24, 256, 1280], P('dp', 'fsdp'), may hold values from -6 to 6
- cotangent: bfloat16 [24, 256, 1280], P('dp', 'fsdp'), may hold values from -6 to 6
- byte_segments: int32 [24, 2048], P('dp'), may hold values from 0 to 3, as said below
- latent_segments: int32 [24, 256], P('dp', 'fsdp'), may hold values from 0 to 3, as said below
- w_query: bfloat16 [1280, 1280], P(('dp', 'fsdp')), may hold values from -0.15625 to 0.15625
- w_key: bfloat16 [768, 1280], P(('dp', 'fsdp')), may hold values from -0.21875 to 0.21875
- w_value: bfloat16 [768, 1280], P(('dp', 'fsdp')), may hold values from -0.21875 to 0.21875
- w_out: bfloat16 [1280, 1280], P(('dp', 'fsdp')), may hold values from -2.5 to 2.5
- w_mlp_in: bfloat16 [1280, 1280], P(('dp', 'fsdp')), may hold values from -0.15625 to 0.15625
- w_mlp_out: bfloat16 [1280, 1280], P(('dp', 'fsdp')), may hold values from -0.15625 to 0.15625
- gain_latent: bfloat16 [1280], P(('dp', 'fsdp')), may hold values from 0.099609375 to 1.8984375
- gain_byte: bfloat16 [768], P(('dp', 'fsdp')), may hold values from 0.099609375 to 1.8984375
- gain_mlp: bfloat16 [1280], P(('dp', 'fsdp')), may hold values from 0.099609375 to 1.8984375
Outputs:
- new_latents: bfloat16 [24, 256, 1280], P('dp', 'fsdp')
- grad_latents: float32 [24, 256, 1280], P('dp', 'fsdp')
- grad_bytes: float32 [24, 2048, 768], P('dp', 'fsdp')
- grad_w_query: float32 [1280, 1280], P(('dp', 'fsdp'))
- grad_w_key: float32 [768, 1280], P(('dp', 'fsdp'))
- grad_w_value: float32 [768, 1280], P(('dp', 'fsdp'))
- grad_w_out: float32 [1280, 1280], P(('dp', 'fsdp'))
- grad_w_mlp_in: float32 [1280, 1280], P(('dp', 'fsdp'))
- grad_w_mlp_out: float32 [1280, 1280], P(('dp', 'fsdp'))
- grad_gain_latent: float32 [1280], P(('dp', 'fsdp'))
- grad_gain_byte: float32 [768], P(('dp', 'fsdp'))
- grad_gain_mlp: float32 [1280], P(('dp', 'fsdp'))
Inputs may be any that keep to these rules, and one draw needn't show every extreme that they name: `byte_segments`: in each row the bytes form 4 documents laid end to end: the ids never fall along a row, and every id 0 to 3 holds one or more bytes. `latent_segments`: in each row exactly 64 latents belong to each document.
All inputs are finite; a program needn't handle non-finite values.
Results may differ from a plain program's by a relative error of at most 0.014.
Values may be sent and summed in bfloat16 or wider, within the bound.
No kernel may reach another device: no remote copies, remote signals or barrier semaphores. Data moves between devices by JAX's collectives and lax.ppermute only.
A program may use at most 256 MiB of HBM per device.

v0:
```python
import math

import jax
import jax.numpy as jnp
from jax import lax
from jax.sharding import PartitionSpec as P

HEADS = 8
HEAD_DIM = 160
MB = 3
ROWS = 1
D_LAT = 1280


EPSILON = 1e-05
NEG_FILL = -1e30


def normalize(values, gain_vec):
    centered = values - jnp.mean(values, axis=-1, keepdims=True)
    return (
        centered
        * lax.rsqrt(jnp.mean(centered * centered, axis=-1, keepdims=True) + EPSILON)
        * gain_vec
    )


def product(formula, factor_one, factor_two):
    return jnp.einsum(formula, factor_one, factor_two, preferred_element_type=jnp.float32)


def precise(formula, factor_one, factor_two):
    return jnp.einsum(
        formula,
        factor_one.astype(jnp.float32),
        factor_two.astype(jnp.float32),
        precision=lax.Precision.HIGHEST,
    )


def local(
    bytes_in,
    latents_in,
    cotangent,
    byte_segments,
    latent_segments,
    w_query,
    w_key,
    w_value,
    w_out,
    w_mlp_in,
    w_mlp_out,
    gain_latent,
    gain_byte,
    gain_mlp,
):
    score_scale = 1.0 / math.sqrt(HEAD_DIM)
    byte_local = bytes_in.shape[1]
    latent_local = latents_in.shape[1]
    full_seq = byte_segments.shape[1]
    new_parts = []
    latent_parts = []
    byte_parts = []
    totals = None
    for micro_batch in range(MB):
        first_row = micro_batch * ROWS
        byte_block = bytes_in[first_row : first_row + ROWS].astype(jnp.float32)
        latent_block = latents_in[first_row : first_row + ROWS].astype(jnp.float32)
        cot_block = cotangent[first_row : first_row + ROWS]
        byte_ids = byte_segments[first_row : first_row + ROWS]
        latent_ids = latent_segments[first_row : first_row + ROWS]
        (
            query_mat,
            key_mat,
            value_mat,
            out_mat,
            inner_mat,
            outer_mat,
            latent_gain,
            byte_gain,
            mlp_gain,
        ) = (
            lax.all_gather(w_query, ("dp", "fsdp"), axis=0, tiled=True),
            lax.all_gather(w_key, ("dp", "fsdp"), axis=0, tiled=True),
            lax.all_gather(w_value, ("dp", "fsdp"), axis=0, tiled=True),
            lax.all_gather(w_out, ("dp", "fsdp"), axis=0, tiled=True),
            lax.all_gather(w_mlp_in, ("dp", "fsdp"), axis=0, tiled=True),
            lax.all_gather(w_mlp_out, ("dp", "fsdp"), axis=0, tiled=True),
            lax.all_gather(gain_latent, ("dp", "fsdp"), axis=0, tiled=True),
            lax.all_gather(gain_byte, ("dp", "fsdp"), axis=0, tiled=True),
            lax.all_gather(gain_mlp, ("dp", "fsdp"), axis=0, tiled=True),
        )
        latent_scale = latent_gain.astype(jnp.float32)
        byte_scale = byte_gain.astype(jnp.float32)
        mlp_scale = mlp_gain.astype(jnp.float32)
        latent_normed = normalize(latent_block, latent_scale).astype(jnp.bfloat16)
        byte_normed = normalize(byte_block, byte_scale).astype(jnp.bfloat16)
        queries = product("rld,de->rle", latent_normed, query_mat).astype(jnp.bfloat16)
        keys_here = product("rsd,de->sre", byte_normed, key_mat).astype(jnp.bfloat16)
        values_here = product("rsd,de->sre", byte_normed, value_mat).astype(jnp.bfloat16)
        keys_all, values_all = (
            lax.all_gather(keys_here, "fsdp", axis=0, tiled=True),
            lax.all_gather(values_here, "fsdp", axis=0, tiled=True),
        )
        head_query = queries.reshape(ROWS, latent_local, HEADS, HEAD_DIM)
        head_key = keys_all.reshape(full_seq, ROWS, HEADS, HEAD_DIM)
        head_value = values_all.reshape(full_seq, ROWS, HEADS, HEAD_DIM)
        allowed = (latent_ids[:, :, None] == byte_ids[:, None, :])[:, None]
        scores = product("rlhc,srhc->rhls", head_query, head_key) * score_scale
        masked = jnp.where(allowed, scores, NEG_FILL)
        row_max = jnp.max(masked, axis=-1, keepdims=True)
        exponent = jnp.exp(masked - row_max)
        row_total = jnp.sum(exponent, axis=-1, keepdims=True)
        attn_probs = exponent / row_total
        log_total = row_max + jnp.log(row_total)
        probs_low = attn_probs.astype(jnp.bfloat16)
        attended = (
            product("rhls,srhc->rlhc", probs_low, head_value)
            .reshape(ROWS, latent_local, D_LAT)
            .astype(jnp.bfloat16)
        )
        mixed_sum = latent_block + product("rle,ef->rlf", attended, out_mat)
        mlp_normed = normalize(mixed_sum, mlp_scale).astype(jnp.bfloat16)
        hidden = product("rle,ef->rlf", mlp_normed, inner_mat)
        activated = jax.nn.gelu(hidden).astype(jnp.bfloat16)
        new_parts.append(
            (mixed_sum + product("rle,ef->rlf", activated, outer_mat)).astype(jnp.bfloat16)
        )
        (
            query_mat,
            key_mat,
            value_mat,
            out_mat,
            inner_mat,
            outer_mat,
            latent_gain,
            byte_gain,
            mlp_gain,
        ) = (
            lax.all_gather(w_query, ("dp", "fsdp"), axis=0, tiled=True),
            lax.all_gather(w_key, ("dp", "fsdp"), axis=0, tiled=True),
            lax.all_gather(w_value, ("dp", "fsdp"), axis=0, tiled=True),
            lax.all_gather(w_out, ("dp", "fsdp"), axis=0, tiled=True),
            lax.all_gather(w_mlp_in, ("dp", "fsdp"), axis=0, tiled=True),
            lax.all_gather(w_mlp_out, ("dp", "fsdp"), axis=0, tiled=True),
            lax.all_gather(gain_latent, ("dp", "fsdp"), axis=0, tiled=True),
            lax.all_gather(gain_byte, ("dp", "fsdp"), axis=0, tiled=True),
            lax.all_gather(gain_mlp, ("dp", "fsdp"), axis=0, tiled=True),
        )
        latent_scale = latent_gain.astype(jnp.float32)
        byte_scale = byte_gain.astype(jnp.float32)
        mlp_scale = mlp_gain.astype(jnp.float32)
        grad_outer = product("rlf,rle->fe", activated, cot_block)
        grad_act = product("rle,fe->rlf", cot_block, outer_mat)
        _, gelu_pull = jax.vjp(jax.nn.gelu, hidden)
        grad_hidden = gelu_pull(grad_act)[0].astype(jnp.bfloat16)
        grad_inner = product("rle,rlf->ef", mlp_normed, grad_hidden)
        upstream = product("rlf,ef->rle", grad_hidden, inner_mat)
        _, mlp_pull = jax.vjp(normalize, mixed_sum, mlp_scale)
        grad_mix_part, grad_mlp_gain = mlp_pull(upstream)
        grad_mixed = cot_block.astype(jnp.float32) + grad_mix_part
        grad_branch = grad_mixed.astype(jnp.bfloat16)
        grad_outmat = product("rle,rlf->ef", attended, grad_branch)
        grad_attended = product("rlf,ef->rle", grad_branch, out_mat).astype(jnp.bfloat16)
        head_grad = grad_attended.reshape(ROWS, latent_local, HEADS, HEAD_DIM)
        scores_again = product("rlhc,srhc->rhls", head_query, head_key) * score_scale
        probs_again = jnp.exp(jnp.where(allowed, scores_again, NEG_FILL) - log_total)
        grad_probs = product("rlhc,srhc->rhls", head_grad, head_value)
        inner_sum = jnp.sum(probs_again * grad_probs, axis=-1, keepdims=True)
        grad_scores = (probs_again * (grad_probs - inner_sum)).astype(jnp.bfloat16)
        probs_low_again = probs_again.astype(jnp.bfloat16)
        grad_queries = (
            (product("rhls,srhc->rlhc", grad_scores, head_key) * score_scale)
            .reshape(ROWS, latent_local, D_LAT)
            .astype(jnp.bfloat16)
        )
        grad_keys_part = (product("rhls,rlhc->srhc", grad_scores, head_query) * score_scale).astype(
            jnp.bfloat16
        )
        grad_values_part = product("rhls,rlhc->srhc", probs_low_again, head_grad).astype(
            jnp.bfloat16
        )
        key_value_grad = lax.psum_scatter(
            jnp.concatenate(
                (
                    grad_keys_part.reshape(byte_local * lax.axis_size("fsdp"), ROWS, D_LAT),
                    grad_values_part.reshape(byte_local * lax.axis_size("fsdp"), ROWS, D_LAT),
                ),
                axis=2,
            )
            .astype(jnp.float32)
            .astype(jnp.bfloat16),
            "fsdp",
            scatter_dimension=0,
            tiled=True,
        ).astype(jnp.float32)
        grad_keys = key_value_grad[:, :, :D_LAT]
        grad_values = key_value_grad[:, :, D_LAT:]
        grad_keymat = precise("rsd,sre->de", byte_normed, grad_keys)
        grad_valuemat = precise("rsd,sre->de", byte_normed, grad_values)
        byte_grad_in = precise("sre,de->rsd", grad_keys, key_mat) + precise(
            "sre,de->rsd", grad_values, value_mat
        )
        _, byte_pull = jax.vjp(normalize, byte_block, byte_scale)
        grad_byte_block, grad_byte_gain = byte_pull(byte_grad_in)
        grad_querymat = product("rld,rle->de", latent_normed, grad_queries)
        latent_upstream = product("rle,de->rld", grad_queries, query_mat)
        _, latent_pull = jax.vjp(normalize, latent_block, latent_scale)
        grad_latent_part, grad_latent_gain = latent_pull(latent_upstream)
        latent_parts.append(grad_mixed + grad_latent_part)
        byte_parts.append(grad_byte_block)
        shares = (
            lax.psum_scatter(grad_querymat, ("dp", "fsdp"), scatter_dimension=0, tiled=True),
            lax.psum_scatter(grad_keymat, ("dp", "fsdp"), scatter_dimension=0, tiled=True),
            lax.psum_scatter(grad_valuemat, ("dp", "fsdp"), scatter_dimension=0, tiled=True),
            lax.psum_scatter(grad_outmat, ("dp", "fsdp"), scatter_dimension=0, tiled=True),
            lax.psum_scatter(grad_inner, ("dp", "fsdp"), scatter_dimension=0, tiled=True),
            lax.psum_scatter(grad_outer, ("dp", "fsdp"), scatter_dimension=0, tiled=True),
            lax.psum_scatter(grad_latent_gain, ("dp", "fsdp"), scatter_dimension=0, tiled=True),
            lax.psum_scatter(grad_byte_gain, ("dp", "fsdp"), scatter_dimension=0, tiled=True),
            lax.psum_scatter(grad_mlp_gain, ("dp", "fsdp"), scatter_dimension=0, tiled=True),
        )
        if totals is None:
            totals = shares
        else:
            totals = jax.tree.map(lambda total, extra: total + extra, totals, shares)
    return (
        jnp.concatenate(new_parts, axis=0),
        jnp.concatenate(latent_parts, axis=0),
        jnp.concatenate(byte_parts, axis=0),
        totals[0],
        totals[1],
        totals[2],
        totals[3],
        totals[4],
        totals[5],
        totals[6],
        totals[7],
        totals[8],
    )


def solution(mesh):
    in_specs = (
        P("dp", "fsdp", None),
        P("dp", "fsdp", None),
        P("dp", "fsdp", None),
        P("dp", None),
        P("dp", "fsdp"),
        P(("dp", "fsdp"), None),
        P(("dp", "fsdp"), None),
        P(("dp", "fsdp"), None),
        P(("dp", "fsdp"), None),
        P(("dp", "fsdp"), None),
        P(("dp", "fsdp"), None),
        P(("dp", "fsdp")),
        P(("dp", "fsdp")),
        P(("dp", "fsdp")),
    )
    out_specs = (
        P("dp", "fsdp", None),
        P("dp", "fsdp", None),
        P("dp", "fsdp", None),
        P(("dp", "fsdp"), None),
        P(("dp", "fsdp"), None),
        P(("dp", "fsdp"), None),
        P(("dp", "fsdp"), None),
        P(("dp", "fsdp"), None),
        P(("dp", "fsdp"), None),
        P(("dp", "fsdp")),
        P(("dp", "fsdp")),
        P(("dp", "fsdp")),
    )
    return jax.shard_map(local, mesh=mesh, in_specs=in_specs, out_specs=out_specs, check_vma=False)
```

profile of v0, /device:TPU:0, one launch (start us, length us, event | category | flops | bytes accessed | tf_op | source)
XLA Modules:
  0.0 2427.6 jit_solution(17851058516280447197)
XLA Ops:
  12.0 42.3 %all-reduce.7 = (bf16[768]{0:T(1024)(128)(2,1)S(1)}, bf16[1280]{0:T(1024)(128)(2,1)S(1)}, bf16[1280]{0:T(1024)(128)(2,1)S(1)}) all-reduce(bf16[768]{0:T(1024)(128)(2,1)S(1)} %dynamic-update-slice, bf16[1280]{0:T(1024)(128)(2,1)S(1)} %dynamic-update-slice.1, ...), channel_id=1, replica_groups=mesh['dp'=8,'fsdp'=4] {'dp','fsdp'}, use_global_device_ids=true, to_apply=%add | all-reduce | flops 3328 | bytes 13312
  57.3 12.4 all-gather.19.cloned.1.call-done
  69.8 3.9 fusion.9
  73.8 53.8 %all-gather.13.cloned.1.call-done = bf16[768,1280]{1,0:T(8,128)(2,1)} async-done(((bf16[24,1280]{1,0:T(8,128)(2,1)}), bf16[768,1280]{1,0:T(8,128)(2,1)}) %all-gather.13.cloned.1.call-update) | async-done | bytes 1966096 | tf_op jit(solution)/shard_map/all_gather | solution.py:85
  127.6 3.9 fusion.8
  132.2 3.9 fusion.11
  136.2 4.0 fusion.10
  141.6 4.0 fusion.7
  149.8 3.9 fusion.6
  153.9 34.7 %all-gather.17.cloned.1.call-done = bf16[1280,1280]{1,0:T(8,128)(2,1)} async-done(((bf16[40,1280]{1,0:T(8,128)(2,1)}), bf16[1280,1280]{1,0:T(8,128)(2,1)}) %all-gather.17.cloned.1.call-update) | async-done | bytes 3276816 | tf_op jit(solution)/shard_map/all_gather | solution.py:83
  196.2 90.8 %all-gather.31.cloned.1.call-done = bf16[2048,1,1280]{2,0,1:T(8,128)(2,1)} async-done(((bf16[512,1,1280]{2,0,1:T(8,128)(2,1)}), bf16[2048,1,1280]{2,0,1:T(8,128)(2,1)}) %all-gather.31.cloned.1.call-update) | async-done | bytes 5242896 | tf_op jit(solution)/shard_map/all_gather | solution.py:102
  287.1 8.1 copy.79
  295.1 4.4 fusion.236
  302.2 82.8 %all-gather.29.cloned.1.call-done = bf16[2048,1,1280]{2,0,1:T(8,128)(2,1)} async-done(((bf16[512,1,1280]{2,0,1:T(8,128)(2,1)}), bf16[2048,1,1280]{2,0,1:T(8,128)(2,1)}) %all-gather.29.cloned.1.call-update) | async-done | bytes 5242896 | tf_op jit(solution)/shard_map/all_gather | solution.py:103
  384.9 8.0 copy.78
  392.9 5.7 fusion.70
  399.1 46.3 %all-gather.23.cloned.1.call-done = bf16[1280,1280]{1,0:T(8,128)(2,1)} async-done(((bf16[40,1280]{1,0:T(8,128)(2,1)}), bf16[1280,1280]{1,0:T(8,128)(2,1)}) %all-gather.23.cloned.1.call-update) | async-done | bytes 3276816 | tf_op jit(solution)/shard_map/all_gather | solution.py:86
  450.1 94.4 %all-gather.35.cloned.1.call-done = bf16[2048,1,1280]{2,0,1:T(8,128)(2,1)} async-done(((bf16[512,1,1280]{2,0,1:T(8,128)(2,1)}), bf16[2048,1,1280]{2,0,1:T(8,128)(2,1)}) %all-gather.35.cloned.1.call-update) | async-done | bytes 5242896 | tf_op jit(solution)/shard_map/all_gather | solution.py:102
  544.5 8.0 copy.83
  552.5 4.4 fusion.234
  560.2 82.3 %all-gather.33.cloned.1.call-done = bf16[2048,1,1280]{2,0,1:T(8,128)(2,1)} async-done(((bf16[512,1,1280]{2,0,1:T(8,128)(2,1)}), bf16[2048,1,1280]{2,0,1:T(8,128)(2,1)}) %all-gather.33.cloned.1.call-update) | async-done | bytes 5242896 | tf_op jit(solution)/shard_map/all_gather | solution.py:103
  642.5 8.1 copy.82
  650.7 5.9 fusion.71
  663.1 40.0 %all-gather.25.cloned.1.call-done = bf16[1280,1280]{1,0:T(8,128)(2,1)} async-done(((bf16[40,1280]{1,0:T(8,128)(2,1)}), bf16[1280,1280]{1,0:T(8,128)(2,1)}) %all-gather.25.cloned.1.call-update) | async-done | bytes 3276816 | tf_op jit(solution)/shard_map/all_gather | solution.py:87
  703.1 3.6 fusion.209
  706.6 57.4 %all-gather.27.cloned.1.call-done = bf16[1280,1280]{1,0:T(8,128)(2,1)} async-done(((bf16[40,1280]{1,0:T(8,128)(2,1)}), bf16[1280,1280]{1,0:T(8,128)(2,1)}) %all-gather.27.cloned.1.call-update) | async-done | bytes 3276816 | tf_op jit(solution)/shard_map/all_gather | solution.py:88
  764.0 3.3 fusion.117
  785.6 5.6 multiply_reduce_fusion.1
  792.2 5.3 fusion.67
  800.9 6.0 multiply_reduce_fusion
  807.8 5.3 fusion.66
  819.9 3.5 fusion.128
  827.9 34.7 %all-gather.21.cloned.1.call-done = bf16[2048,1,1280]{2,0,1:T(8,128)(2,1)} async-done(((bf16[512,1,1280]{2,0,1:T(8,128)(2,1)}), bf16[2048,1,1280]{2,0,1:T(8,128)(2,1)}) %all-gather.21.cloned.1.call-update) | async-done | bytes 5242896 | tf_op jit(solution)/shard_map/all_gather | solution.py:102
  862.6 8.1 copy.75
  870.6 4.5 fusion.238
  879.0 81.4 %all-gather.15.cloned.1.call-done = bf16[2048,1,1280]{2,0,1:T(8,128)(2,1)} async-done(((bf16[512,1,1280]{2,0,1:T(8,128)(2,1)}), bf16[2048,1,1280]{2,0,1:T(8,128)(2,1)}) %all-gather.15.cloned.1.call-update) | async-done | bytes 5242896 | tf_op jit(solution)/shard_map/all_gather | solution.py:103
  960.5 8.1 copy.74
  968.6 5.6 fusion.69
  989.0 5.4 multiply_reduce_fusion.2
  998.6 12.7 pad_maximum_fusion
  1016.7 12.6 pad_maximum_fusion.1
  1034.7 13.0 pad_maximum_fusion.2
  1051.1 3.9 convolution_add_fusion.2
  1058.1 3.7 convolution_add_fusion.4
  1063.4 4.3 fusion.68
  1070.6 3.9 convolution_add_fusion.6
  1077.8 3.7 convolution_add_fusion
  1082.8 105.1 %reduce-scatter.10.cloned.1.call-done = bf16[512,1,2560]{0,2,1:T(8,128)(2,1)} async-done(((bf16[2048,1,2560]{0,2,1:T(8,128)(2,1)}), bf16[512,1,2560]{0,2,1:T(8,128)(2,1)}) %reduce-scatter.10.cloned.1.call-update) | async-done | bytes 2621456 | tf_op jit(solution)/shard_map/reduce_scatter | solution.py:183
  1187.9 4.8 fusion.74
  1192.6 176.5 %reduce-scatter.12.cloned.1.call-done = bf16[512,1,2560]{0,2,1:T(8,128)(2,1)} async-done(((bf16[2048,1,2560]{0,2,1:T(8,128)(2,1)}), bf16[512,1,2560]{0,2,1:T(8,128)(2,1)}) %reduce-scatter.12.cloned.1.call-update) | async-done | bytes 2621456 | tf_op jit(solution)/shard_map/reduce_scatter | solution.py:183
  1369.1 6.0 convolution_add_fusion.9
  1375.1 175.3 %reduce-scatter.14.cloned.1.call-done = bf16[512,1,2560]{0,2,1:T(8,128)(2,1)} async-done(((bf16[2048,1,2560]{0,2,1:T(8,128)(2,1)}), bf16[512,1,2560]{0,2,1:T(8,128)(2,1)}) %reduce-scatter.14.cloned.1.call-update) | async-done | bytes 2621456 | tf_op jit(solution)/shard_map/reduce_scatter | solution.py:183
  1550.4 6.0 convolution_add_fusion.8
  1570.8 3.5 convolution_add_fusion.10
  1574.4 3.3 fusion.76
  1585.0 3.7 fusion.49
  1588.7 42.8 %all-reduce.6 = (f32[1280]{0:T(1024)S(1)}, f32[768]{0:T(1024)S(1)}, f32[1280]{0:T(1024)S(1)}) all-reduce(f32[1280]{0:T(1024)S(1)} %add_add_fusion.16, f32[768]{0:T(1024)S(1)} %add_add_fusion.17, f32[1280]{0:T(1024)S(1)} %add_add_fusion.15), channel_id=29, replica_groups=mesh['dp'=8,'fsdp'=4] {'dp','fsdp'}, use_global_device_ids=true, to_apply=%region_67.68.clone | all-reduce | flops 3328 | bytes 26624
  1633.3 3.6 fusion.227
  1639.9 75.5 %reduce-scatter.24.cloned.1.call-done = f32[40,1280]{1,0:T(8,128)} async-done(((f32[1280,1280]{1,0:T(8,128)}), f32[40,1280]{1,0:T(8,128)}) %reduce-scatter.24.cloned.1.call-update) | async-done | bytes 204816 | tf_op jit(solution)/shard_map/reduce_scatter | solution.py:217
  1715.5 162.1 %reduce-scatter.22.cloned.1.call-done = f32[40,1280]{1,0:T(8,128)} async-done(((f32[1280,1280]{1,0:T(8,128)}), f32[40,1280]{1,0:T(8,128)}) %reduce-scatter.22.cloned.1.call-update) | async-done | bytes 204816 | tf_op jit(solution)/shard_map/reduce_scatter | solution.py:216
  1877.6 162.7 %reduce-scatter.16.cloned.1.call-done = f32[40,1280]{1,0:T(8,128)} async-done(((f32[1280,1280]{1,0:T(8,128)}), f32[40,1280]{1,0:T(8,128)}) %reduce-scatter.16.cloned.1.call-update) | async-done | bytes 204816 | tf_op jit(solution)/shard_map/reduce_scatter | solution.py:213
  2040.3 163.2 %reduce-scatter.26.cloned.1.call-done = f32[40,1280]{1,0:T(8,128)} async-done(((f32[1280,1280]{1,0:T(8,128)}), f32[40,1280]{1,0:T(8,128)}) %reduce-scatter.26.cloned.1.call-update) | async-done | bytes 204816 | tf_op jit(solution)/shard_map/reduce_scatter | solution.py:218
  2203.5 107.9 %reduce-scatter.20.cloned.1.call-done = f32[24,1280]{1,0:T(8,128)} async-done(((f32[768,1280]{1,0:T(8,128)}), f32[24,1280]{1,0:T(8,128)}) %reduce-scatter.20.cloned.1.call-update) | async-done | bytes 122896 | tf_op jit(solution)/shard_map/reduce_scatter | solution.py:215
  2311.4 108.9 %reduce-scatter.18.cloned.1.call-done = f32[24,1280]{1,0:T(8,128)} async-done(((f32[768,1280]{1,0:T(8,128)}), f32[24,1280]{1,0:T(8,128)}) %reduce-scatter.18.cloned.1.call-update) | async-done | bytes 122896 | tf_op jit(solution)/shard_map/reduce_scatter | solution.py:214
  (539 shorter events, 148.2 us)
Async XLA Ops:
  7.2 49.3 %copy-start.14 = (bf16[3,512,768]{2,1,0:T(8,128)(2,1)S(1)}, bf16[3,512,768]{2,1,0:T(8,128)(2,1)}, u32[]{:S(2)}) copy-start(bf16[3,512,768]{2,1,0:T(8,128)(2,1)} %param.14) | copy-start | bytes 7077892
  7.2 62.6 %all-gather.19.cloned.1.call-start = ((), (), s32[]{:S(2)}) async-start(), calls=%async_computation.12 | async-start | bytes 2027520 | tf_op jit(solution)/shard_map/all_gather | solution.py:84
  7.9 119.7 %all-gather.13.cloned.1.call-start = ((), (), s32[]{:S(2)}) async-start(), calls=%async_computation.9 | async-start | bytes 2027520 | tf_op jit(solution)/shard_map/all_gather | solution.py:85
  8.7 180.0 %all-gather.17.cloned.1.call-start = ((), (), s32[]{:S(2)}) async-start(), calls=%async_computation.11 | async-start | bytes 3379200 | tf_op jit(solution)/shard_map/all_gather | solution.py:83
  9.4 277.6 %all-gather.31.cloned.1.call-start = ((), (), s32[]{:S(2)}) async-start(), calls=%async_computation.18 | async-start | bytes 6553600 | tf_op jit(solution)/shard_map/all_gather | solution.py:102
  54.3 95.5 %copy-start.92 = (f32[768]{0:T(1024)}, f32[768]{0:T(1024)S(1)}, u32[]{:S(2)}) copy-start(f32[768]{0:T(1024)S(1)} %convert_element_type.443) | copy-start | bytes 9220
  56.4 93.4 %copy-start.121 = (f32[512]{0:T(512)}, f32[512]{0:T(512)S(1)}, u32[]{:S(2)}) copy-start(f32[512]{0:T(512)S(1)} %broadcast_multiply_fusion.2) | copy-start | bytes 6148
  56.4 71.2 %copy-start.101 = (f32[512]{0:T(512)}, f32[512]{0:T(512)S(1)}, u32[]{:S(2)}) copy-start(f32[512]{0:T(512)S(1)} %get-tuple-element.112) | copy-start | bytes 6148
  56.4 79.7 %copy-start.99 = (f32[512]{0:T(512)}, f32[512]{0:T(512)S(1)}, u32[]{:S(2)}) copy-start(f32[512]{0:T(512)S(1)} %get-tuple-element.111) | copy-start | bytes 6148
  57.3 16.4 copy-start.125
  57.3 74.9 %copy-start.127 = (f32[512]{0:T(512)}, f32[512]{0:T(512)S(1)}, u32[]{:S(2)}) copy-start(f32[512]{0:T(512)S(1)} %get-tuple-element.24) | copy-start | bytes 6148
  57.3 84.3 %copy-start.123 = (f32[512]{0:T(512)}, f32[512]{0:T(512)S(1)}, u32[]{:S(2)}) copy-start(f32[512]{0:T(512)S(1)} %get-tuple-element.22) | copy-start | bytes 6148
  57.3 70.3 %copy-start.109 = (f32[512]{0:T(512)}, f32[512]{0:T(512)S(1)}, u32[]{:S(2)}) copy-start(f32[512]{0:T(512)S(1)} %fusion.187) | copy-start | bytes 6148
  73.7 311.2 %all-gather.29.cloned.1.call-start = ((), (), s32[]{:S(2)}) async-start(), calls=%async_computation.17 | async-start | bytes 6553600 | tf_op jit(solution)/shard_map/all_gather | solution.py:103
  131.5 313.8 %all-gather.23.cloned.1.call-start = ((), (), s32[]{:S(2)}) async-start(), calls=%async_computation.14 | async-start | bytes 3379200 | tf_op jit(solution)/shard_map/all_gather | solution.py:86
  132.1 412.3 %all-gather.35.cloned.1.call-start = ((), (), s32[]{:S(2)}) async-start(), calls=%async_computation.20 | async-start | bytes 6553600 | tf_op jit(solution)/shard_map/all_gather | solution.py:102
  136.1 506.4 %all-gather.33.cloned.1.call-start = ((), (), s32[]{:S(2)}) async-start(), calls=%async_computation.19 | async-start | bytes 6553600 | tf_op jit(solution)/shard_map/all_gather | solution.py:103
  140.2 562.9 %all-gather.25.cloned.1.call-start = ((), (), s32[]{:S(2)}) async-start(), calls=%async_computation.15 | async-start | bytes 3379200 | tf_op jit(solution)/shard_map/all_gather | solution.py:87
  140.9 623.1 %all-gather.27.cloned.1.call-start = ((), (), s32[]{:S(2)}) async-start(), calls=%async_computation.16 | async-start | bytes 3379200 | tf_op jit(solution)/shard_map/all_gather | solution.py:88
  141.5 721.1 %all-gather.21.cloned.1.call-start = ((), (), s32[]{:S(2)}) async-start(), calls=%async_computation.13 | async-start | bytes 6553600 | tf_op jit(solution)/shard_map/all_gather | solution.py:102
  141.6 8.2 copy-start.142
  141.6 5.7 copy-start.158
  141.6 5.7 copy-start.129
  145.6 814.8 %all-gather.15.cloned.1.call-start = ((), (), s32[]{:S(2)}) async-start(), calls=%async_computation.10 | async-start | bytes 6553600 | tf_op jit(solution)/shard_map/all_gather | solution.py:103
  145.9 42.8 %copy-start.117 = (f32[64]{0:T(128)}, f32[64]{0:T(128)S(1)}, u32[]{:S(2)}) copy-start(f32[64]{0:T(128)S(1)} %get-tuple-element.114) | copy-start | bytes 772
  145.9 46.7 %copy-start.119 = (f32[64]{0:T(128)}, f32[64]{0:T(128)S(1)}, u32[]{:S(2)}) copy-start(f32[64]{0:T(128)S(1)} %get-tuple-element.113) | copy-start | bytes 772
  146.7 41.9 %copy-start.148 = (f32[64]{0:T(128)}, f32[64]{0:T(128)S(1)}, u32[]{:S(2)}) copy-start(f32[64]{0:T(128)S(1)} %fusion.191) | copy-start | bytes 772
  146.7 45.8 %copy-start.150 = (f32[64]{0:T(128)}, f32[64]{0:T(128)S(1)}, u32[]{:S(2)}) copy-start(f32[64]{0:T(128)S(1)} %fusion.193) | copy-start | bytes 772
  153.7 1034.1 %reduce-scatter.10.cloned.1.call-start = ((), (), s32[]{:S(2)}) async-start(), calls=%async_computation.21 | async-start | bytes 13107200 | tf_op jit(solution)/shard_map/reduce_scatter | solution.py:183
  196.2 98.9 %copy-start.48 = (bf16[64,8,160]{2,1,0:T(8,128)(2,1)S(1)}, bf16[64,8,160]{2,1,0:T(8,128)(2,1)}, u32[]{:S(2)}) copy-start(bf16[64,8,160]{2,1,0:T(8,128)(2,1)} %reshape.1293) | copy-start | bytes 491524
  196.2 98.9 %copy-start.85 = (pred[64,2048]{1,0:T(8,128)(4,1)S(1)}, pred[64,2048]{1,0:T(8,128)(4,1)}, u32[]{:S(2)}) copy-start(pred[64,2048]{1,0:T(8,128)(4,1)} %broadcast_compare_fusion.1) | copy-start | bytes 393220
  299.5 93.4 %copy-start.103 = (f32[8,64]{1,0:T(8,128)}, f32[8,64]{1,0:T(8,128)S(1)}, u32[]{:S(2)}) copy-start(f32[8,64]{1,0:T(8,128)S(1)} %get-tuple-element.92) | copy-start | bytes 6148
  302.2 90.8 %copy-start.132 = (f32[8,64]{1,0:T(8,128)}, f32[8,64]{1,0:T(8,128)S(1)}, u32[]{:S(2)}) copy-start(f32[8,64]{1,0:T(8,128)S(1)} %fusion.1) | copy-start | bytes 6148
  399.1 153.4 %copy-start.78 = (bf16[64,1280]{1,0:T(8,128)(2,1)}, bf16[64,1280]{1,0:T(8,128)(2,1)S(1)}, u32[]{:S(2)}) copy-start(bf16[64,1280]{1,0:T(8,128)(2,1)S(1)} %convert_element_type.482) | copy-start | bytes 491524
  450.1 102.4 %copy-start.84 = (pred[64,2048]{1,0:T(8,128)(4,1)S(1)}, pred[64,2048]{1,0:T(8,128)(4,1)}, u32[]{:S(2)}) copy-start(pred[64,2048]{1,0:T(8,128)(4,1)} %broadcast_compare_fusion) | copy-start | bytes 393220
  556.9 93.8 %copy-start.104 = (f32[8,64]{1,0:T(8,128)}, f32[8,64]{1,0:T(8,128)S(1)}, u32[]{:S(2)}) copy-start(f32[8,64]{1,0:T(8,128)S(1)} %get-tuple-element.88) | copy-start | bytes 6148
  650.7 8.6 copy-start.8
  785.6 5.6 copy-start.96
  785.6 5.6 copy-start.1
  800.9 6.0 copy-start.94
  800.9 6.0 copy-start.4
  1011.3 357.8 %reduce-scatter.12.cloned.1.call-start = ((), (), s32[]{:S(2)}) async-start(), calls=%async_computation.22 | async-start | bytes 13107200 | tf_op jit(solution)/shard_map/reduce_scatter | solution.py:183
  1029.3 521.1 %reduce-scatter.14.cloned.1.call-start = ((), (), s32[]{:S(2)}) async-start(), calls=%async_computation.23 | async-start | bytes 13107200 | tf_op jit(solution)/shard_map/reduce_scatter | solution.py:183
  1047.7 667.8 %reduce-scatter.24.cloned.1.call-start = ((), (), s32[]{:S(2)}) async-start(), calls=%async_computation.28 | async-start | bytes 6758400 | tf_op jit(solution)/shard_map/reduce_scatter | solution.py:217
  1055.0 822.6 %reduce-scatter.22.cloned.1.call-start = ((), (), s32[]{:S(2)}) async-start(), calls=%async_computation.27 | async-start | bytes 6758400 | tf_op jit(solution)/shard_map/reduce_scatter | solution.py:216
  1061.9 6.3 copy-start.22
  1061.9 6.3 copy-start.114
  1061.9 6.3 copy-start.116
  1061.9 978.4 %reduce-scatter.16.cloned.1.call-start = ((), (), s32[]{:S(2)}) async-start(), calls=%async_computation.24 | async-start | bytes 6758400 | tf_op jit(solution)/shard_map/reduce_scatter | solution.py:213
  1074.5 1129.0 %reduce-scatter.26.cloned.1.call-start = ((), (), s32[]{:S(2)}) async-start(), calls=%async_computation.29 | async-start | bytes 6758400 | tf_op jit(solution)/shard_map/reduce_scatter | solution.py:218
  1081.5 106.3 %copy-start.15 = (bf16[3,512,768]{2,1,0:T(8,128)(2,1)S(1)}, bf16[3,512,768]{2,1,0:T(8,128)(2,1)}, u32[]{:S(2)}) copy-start(bf16[3,512,768]{2,1,0:T(8,128)(2,1)} %param.14) | copy-start | bytes 7077892
  1081.5 106.3 %copy-start.93 = (f32[768]{0:T(1024)S(1)}, f32[768]{0:T(1024)}, u32[]{:S(2)}) copy-start(f32[768]{0:T(1024)} %copy-done.92) | copy-start | bytes 9220
  1081.5 106.3 %copy-start.122 = (f32[512]{0:T(512)S(1)}, f32[512]{0:T(512)}, u32[]{:S(2)}) copy-start(f32[512]{0:T(512)} %copy-done.121) | copy-start | bytes 6148
  1081.6 106.3 %copy-start.143 = (f32[512]{0:T(512)S(1)}, f32[512]{0:T(512)}, u32[]{:S(2)}) copy-start(f32[512]{0:T(512)} %copy-done.142) | copy-start | bytes 6148
  1081.6 1229.8 %reduce-scatter.20.cloned.1.call-start = ((), (), s32[]{:S(2)}) async-start(), calls=%async_computation.26 | async-start | bytes 4055040 | tf_op jit(solution)/shard_map/reduce_scatter | solution.py:215
  1082.2 474.6 %copy-start.167 = (f32[64]{0:T(128)}, f32[64]{0:T(128)S(1)}, u32[]{:S(2)}) copy-start(f32[64]{0:T(128)S(1)} %multiply_multiply_fusion.11) | copy-start | bytes 772
  1082.8 286.4 %copy-start.102 = (f32[512]{0:T(512)S(1)}, f32[512]{0:T(512)}, u32[]{:S(2)}) copy-start(f32[512]{0:T(512)} %copy-done.101) | copy-start | bytes 6148
  1082.8 286.4 %copy-start.110 = (f32[512]{0:T(512)S(1)}, f32[512]{0:T(512)}, u32[]{:S(2)}) copy-start(f32[512]{0:T(512)} %copy-done.109) | copy-start | bytes 6148
  1192.6 357.8 %copy-start.100 = (f32[512]{0:T(512)S(1)}, f32[512]{0:T(512)}, u32[]{:S(2)}) copy-start(f32[512]{0:T(512)} %copy-done.99) | copy-start | bytes 6148
  1192.6 357.8 %copy-start.112 = (f32[512]{0:T(512)S(1)}, f32[512]{0:T(512)}, u32[]{:S(2)}) copy-start(f32[512]{0:T(512)} %copy-done.111) | copy-start | bytes 6148
  1556.4 863.8 %reduce-scatter.18.cloned.1.call-start = ((), (), s32[]{:S(2)}) async-start(), calls=%async_computation.25 | async-start | bytes 4055040 | tf_op jit(solution)/shard_map/reduce_scatter | solution.py:214
  1584.9 48.3 %copy-start.128 = (f32[512]{0:T(512)S(1)}, f32[512]{0:T(512)}, u32[]{:S(2)}) copy-start(f32[512]{0:T(512)} %copy-done.127) | copy-start | bytes 6148
  1584.9 48.3 %copy-start.126 = (f32[512]{0:T(512)S(1)}, f32[512]{0:T(512)}, u32[]{:S(2)}) copy-start(f32[512]{0:T(512)} %copy-done.125) | copy-start | bytes 6148
  1584.9 48.3 %copy-start.124 = (f32[512]{0:T(512)S(1)}, f32[512]{0:T(512)}, u32[]{:S(2)}) copy-start(f32[512]{0:T(512)} %copy-done.123) | copy-start | bytes 6148
  (135 other events, 277.9 us)
Sparse Core Ops, SparseCore 0:
  10.8 58.8 all-gather.18
  72.6 54.9 all-gather.12
  130.4 58.1 all-gather.16
  190.1 96.9 all-gather.30
  288.5 96.4 all-gather.28
  387.6 57.6 all-gather.22
  447.5 96.9 all-gather.34
  546.0 96.4 all-gather.32
  645.3 57.6 all-gather.24
  705.8 58.2 all-gather.26
  765.6 96.9 all-gather.20
  864.0 96.4 all-gather.14
  1011.4 176.3 reduce-scatter.9
  1190.1 179.0 reduce-scatter.11
  1371.3 179.0 reduce-scatter.13
  1553.2 162.2 reduce-scatter.23
  1718.2 159.3 reduce-scatter.21
  1880.3 159.8 reduce-scatter.15
  2043.2 160.2 reduce-scatter.25
  2209.3 102.0 reduce-scatter.19
  2317.4 102.8 reduce-scatter.17
where the time goes:
time: 2440 us; the launch traced here: 2430 us
  waiting for transfers between devices  1950 us (80%)
  matrix products  201 us (8%)
  local copies, waits for them, and re-layouts  105 us (4%)
  blocking collectives  85.1 us (3%)
  other arithmetic  65 us (3%)
    reduce_scatter x3, waiting for transfers between devices, local(): lax.psum_scatter(jnp.concatenate((grad_keys_part.reshape(byte_local * lax...  457 us
    all_gather x3, waiting for transfers between devices, local(): lax.all_gather(values_here, 'fsdp', axis=0, tiled=True)  247 us
    all_gather x3, waiting for transfers between devices, local(): lax.all_gather(keys_here, 'fsdp', axis=0, tiled=True)  220 us
    dot_general x60, matrix products, product(): jnp.einsum(formula, factor_one, factor_two, preferred_element_type=jnp.fl...  166 us
    reduce_scatter x1, waiting for transfers between devices, local(): lax.psum_scatter(grad_outer, ('dp', 'fsdp'), scatter_dimension=0, tiled=T...  163 us
    reduce_scatter x1, waiting for transfers between devices, local(): lax.psum_scatter(grad_querymat, ('dp', 'fsdp'), scatter_dimension=0, tile...  163 us
    reduce_scatter x1, waiting for transfers between devices, local(): lax.psum_scatter(grad_outmat, ('dp', 'fsdp'), scatter_dimension=0, tiled=...  162 us
    reduce_scatter x1, waiting for transfers between devices, local(): lax.psum_scatter(grad_keymat, ('dp', 'fsdp'), scatter_dimension=0, tiled=...  109 us
  transfers between devices with their start and end apart: 21, of which 21 were waited for; matrix products, arithmetic and copies ran while one was open for 12% of the time, Pallas kernels for 0%

commit v1 on v0

v1 whole, which is shorter than its diff:
```python
import functools
import math

import jax
import jax.numpy as jnp
from jax import lax
from jax.experimental import pallas as pl
from jax.experimental.pallas import tpu as pltpu
from jax.sharding import PartitionSpec as P

HEADS = 8
HEAD_DIM = 160
EPSILON = 1e-05
NEG_FILL = -1e30
LANES = 128
WINDOW = 256
BF = jnp.bfloat16
F32 = jnp.float32
VMEM_LIMIT = 58 * 1024 * 1024


def head_window(head):
    start = head * HEAD_DIM // LANES * LANES
    return start, head * HEAD_DIM - start


def head_lanes(head):
    _, shift = head_window(head)
    lane = lax.broadcasted_iota(jnp.int32, (1, WINDOW), 1)
    return (lane >= shift) & (lane < shift + HEAD_DIM)


def dot(a, b, dims=((1,), (0,))):
    return lax.dot_general(a, b, (dims, ((), ())), preferred_element_type=F32)


def standardize(values):
    centered = values - jnp.mean(values, axis=-1, keepdims=True)
    scale = lax.rsqrt(jnp.mean(centered * centered, axis=-1, keepdims=True) + EPSILON)
    return centered * scale, scale


def norm_pull(upstream, gain, xhat, scale):
    scaled = upstream * gain
    return scale * (
        scaled
        - jnp.mean(scaled, axis=-1, keepdims=True)
        - xhat * jnp.mean(scaled * xhat, axis=-1, keepdims=True)
    )


def split_three(values):
    first = values.astype(BF).astype(F32)
    rest = values - first
    second = rest.astype(BF).astype(F32)
    return first, second, rest - second


def gelu(values):
    inner = math.sqrt(2 / math.pi) * (values + 0.044715 * values * values * values)
    return 0.5 * values * (1.0 + jnp.tanh(inner))


def gelu_slope(values):
    square = values * values
    tanh = jnp.tanh(math.sqrt(2 / math.pi) * (values + 0.044715 * square * values))
    slope = math.sqrt(2 / math.pi) * (1.0 + 3 * 0.044715 * square)
    return 0.5 * (1.0 + tanh) + 0.5 * values * (1.0 - tanh * tanh) * slope


def piece_copies(pieces, flat_refs, first, rows, target, me, sems, base):
    copies = []
    at = 0
    for distance, parts in pieces:
        owner = jnp.bitwise_xor(me, distance)
        for low, high in parts:
            ref = flat_refs[at]
            at += 1
            start, stop = max(low, first), min(high, first + rows)
            if start < stop:
                place = pl.multiple_of(owner * rows + (start - first), 16)
                copies.append(
                    pltpu.make_async_copy(
                        ref.at[pl.ds(start - low, stop - start), :],
                        target.at[pl.ds(place, stop - start), :],
                        sems.at[base + len(copies)],
                    )
                )
    return copies


def params(grid_rank):
    return pltpu.CompilerParams(
        dimension_semantics=("arbitrary",) * grid_rank, vmem_limit_bytes=VMEM_LIMIT
    )


def whole_spec():
    return pl.BlockSpec(memory_space=pltpu.VMEM)


def any_spec():
    return pl.BlockSpec(memory_space=pl.ANY)


def key_value_call(me, bytes_flat, gain, pieces, flat, key_rows, key_at, value_at, rows):
    tokens, width = bytes_flat.shape
    block = tokens // rows
    lat = flat[0].shape[1]
    count = len(flat)

    def kernel(me_ref, x_ref, gain_ref, *refs):
        piece_refs = refs[:count]
        normed_t_ref, key_ref, value_ref, wk, wv, sems = refs[count:]

        def copies():
            one = piece_copies(pieces, piece_refs, key_at, key_rows, wk, me_ref[0], sems, 0)
            two = piece_copies(
                pieces, piece_refs, value_at, key_rows, wv, me_ref[0], sems, len(one)
            )
            return one + two

        @pl.when(pl.program_id(0) == 0)
        def _():
            for copy in copies():
                copy.start()

        xhat, _ = standardize(x_ref[...].astype(F32))
        normed = (xhat * gain_ref[...]).astype(BF)
        normed_t_ref[...] = jnp.transpose(normed, (1, 0))

        @pl.when(pl.program_id(0) == 0)
        def _():
            for copy in copies():
                copy.wait()

        key_ref[...] = dot(normed, wk[...]).astype(BF)
        value_ref[...] = dot(normed, wv[...]).astype(BF)

    row_block = lambda i, m: (i, 0)
    return pl.pallas_call(
        kernel,
        grid_spec=pltpu.PrefetchScalarGridSpec(
            num_scalar_prefetch=1,
            grid=(rows,),
            in_specs=[
                pl.BlockSpec((block, width), row_block),
                pl.BlockSpec((1, width), lambda i, m: (0, 0)),
            ]
            + [any_spec()] * count,
            out_specs=[
                pl.BlockSpec((width, block), lambda i, m: (0, i)),
                pl.BlockSpec((block, lat), row_block),
                pl.BlockSpec((block, lat), row_block),
            ],
            scratch_shapes=[
                pltpu.VMEM((width, lat), BF),
                pltpu.VMEM((width, lat), BF),
                pltpu.SemaphoreType.DMA((4 * count,)),
            ],
        ),
        out_shape=[
            jax.ShapeDtypeStruct((width, tokens), BF),
            jax.ShapeDtypeStruct((tokens, lat), BF),
            jax.ShapeDtypeStruct((tokens, lat), BF),
        ],
        compiler_params=params(1),
        cost_estimate=pl.CostEstimate(
            flops=4 * tokens * width * lat,
            bytes_accessed=2 * (2 * tokens * width + 2 * tokens * lat + 2 * width * lat),
            transcendentals=0,
        ),
        name="keys_values",
    )(me, bytes_flat, gain, *flat)


def attend_call(
    me, latent_parts, gain, latent_ids, byte_ids, keys, values, pieces, flat, query_rows, query_at, rows
):
    groups = len(latent_parts)
    tokens, lat = keys.shape
    block = tokens // rows
    group = latent_ids.shape[1] // groups
    latents = groups * group
    count = len(flat)
    score_scale = 1.0 / math.sqrt(HEAD_DIM)

    def kernel(me_ref, *refs):
        part_refs = refs[:groups]
        gain_ref, lid_ref, bid_ref, key_ref, value_ref = refs[groups : groups + 5]
        piece_refs = refs[groups + 5 : groups + 5 + count]
        rest = refs[groups + 5 + count :]
        normed_t_ref, query_ref = rest[:2]
        out_refs = rest[2 : 2 + groups]
        wq, acc, sems = rest[2 + groups :]

        def copies():
            return piece_copies(pieces, piece_refs, query_at, query_rows, wq, me_ref[0], sems, 0)

        @pl.when(pl.program_id(0) == 0)
        def _():
            for copy in copies():
                copy.start()

        x = jnp.concatenate([ref[...].astype(F32) for ref in part_refs], axis=0)
        xhat, _ = standardize(x)
        normed = (xhat * gain_ref[...]).astype(BF)
        normed_t_ref[...] = jnp.transpose(normed, (1, 0))

        @pl.when(pl.program_id(0) == 0)
        def _():
            for copy in copies():
                copy.wait()

        query_ref[...] = dot(normed, wq[...]).astype(BF)
        allowed = lid_ref[0] == bid_ref[0]
        lane = lax.broadcasted_iota(jnp.int32, (latents, LANES), 1)
        stats = jnp.zeros((latents, LANES), F32)
        for head in range(HEADS):
            at, _ = head_window(head)
            mask = head_lanes(head)
            window = slice(at, at + WINDOW)
            query = jnp.where(mask, query_ref[:, window], jnp.zeros((), BF))
            scores = dot(query, key_ref[:, window], ((1,), (1,))) * score_scale
            scores = jnp.where(allowed, scores, NEG_FILL)
            top = jnp.max(scores, axis=-1, keepdims=True)
            exponent = jnp.exp(scores - top)
            total = jnp.sum(exponent, axis=-1, keepdims=True)
            found = dot(exponent.astype(BF), value_ref[:, window]) / total
            if head == 0:
                acc[:, window] = found
            else:
                acc[:, window] = jnp.where(mask, found, acc[:, window])
            log_total = jnp.where(top > -1e29, top + jnp.log(total), NEG_FILL)
            for index, term in enumerate(split_three(log_total)):
                stats = jnp.where(lane == index * HEADS + head, term, stats)
        for index, ref in enumerate(out_refs):
            chunk = slice(index * group, (index + 1) * group)
            ref[:, :lat] = acc[chunk, :].astype(BF)
            ref[:, lat:] = stats[chunk, :].astype(BF)

    row_block = lambda i, m: (i, 0)
    return pl.pallas_call(
        kernel,
        grid_spec=pltpu.PrefetchScalarGridSpec(
            num_scalar_prefetch=1,
            grid=(rows,),
            in_specs=[pl.BlockSpec((group, lat), row_block)] * groups
            + [
                pl.BlockSpec((1, lat), lambda i, m: (0, 0)),
                pl.BlockSpec((1, latents, 1), lambda i, m: (i, 0, 0)),
                pl.BlockSpec((1, 1, block), lambda i, m: (i, 0, 0)),
                pl.BlockSpec((block, lat), row_block),
                pl.BlockSpec((block, lat), row_block),
            ]
            + [any_spec()] * count,
            out_specs=[
                pl.BlockSpec((lat, latents), lambda i, m: (0, i)),
                pl.BlockSpec((latents, lat), row_block),
            ]
            + [pl.BlockSpec((group, lat + LANES), row_block)] * groups,
            scratch_shapes=[
                pltpu.VMEM((lat, lat), BF),
                pltpu.VMEM((latents, lat), F32),
                pltpu.SemaphoreType.DMA((2 * count,)),
            ],
        ),
        out_shape=[
            jax.ShapeDtypeStruct((lat, rows * latents), BF),
            jax.ShapeDtypeStruct((rows * latents, lat), BF),
        ]
        + [jax.ShapeDtypeStruct((rows * group, lat + LANES), BF)] * groups,
        compiler_params=params(1),
        cost_estimate=pl.CostEstimate(
            flops=2 * rows * latents * lat * lat
            + 4 * rows * HEADS * latents * block * WINDOW,
            bytes_accessed=2 * (4 * tokens * lat + lat * lat),
            transcendentals=rows * HEADS * latents * block,
        ),
        name="attend",
    )(me, *latent_parts, gain, latent_ids, byte_ids, keys, values, *flat)


def feed_call(me, parts, latents_flat, cot_flat, gain, pieces, flat, n):
    groups = len(parts)
    tokens, lat = latents_flat.shape
    count = len(flat)

    def kernel(me_ref, *refs):
        part_refs = refs[:groups]
        x_ref, cot_ref, gain_ref = refs[groups : groups + 3]
        piece_refs = refs[groups + 3 : groups + 3 + count]
        rest = refs[groups + 3 + count :]
        new_ref, mixed_grad_ref, message_ref, attended_t, branch, normed_t, inner, act_t = rest[:8]
        wo, w1, w2, sems = rest[8:]
        me = me_ref[0]
        loads = []
        base = 0
        for first, target in ((0, wo), (n, w1), (2 * n, w2)):
            found = piece_copies(pieces, piece_refs, first, n, target, me, sems, base)
            base += len(found)
            loads.append(found)
        for found in loads:
            for copy in found:
                copy.start()

        lane = lax.broadcasted_iota(jnp.int32, (LANES, lat), 0)
        column = lax.broadcasted_iota(jnp.int32, (LANES, lat), 1)
        spread = jnp.zeros((LANES, lat), jnp.bool_)
        for head in range(HEADS):
            inside = (column >= head * HEAD_DIM) & (column < (head + 1) * HEAD_DIM)
            own = (lane == head) | (lane == HEADS + head) | (lane == 2 * HEADS + head)
            spread = spread | (inside & own)
        spread = spread.astype(F32).astype(BF)
        logs = [dot(ref[:, lat:], spread) for ref in part_refs]
        top = functools.reduce(jnp.maximum, logs)
        shares = [jnp.exp(log - top) for log in logs]
        total = functools.reduce(jnp.add, shares)
        summed = functools.reduce(
            jnp.add, [s * ref[:, :lat].astype(F32) for s, ref in zip(shares, part_refs)]
        )
        attended = (summed / total).astype(BF)
        log_total = top + jnp.log(total)
        attended_t[...] = jnp.transpose(attended, (1, 0))

        for copy in loads[0]:
            copy.wait()
        mixed = x_ref[...].astype(F32) + dot(attended, wo[...])
        xhat, scale = standardize(mixed)
        gain = gain_ref[...]
        normed = (xhat * gain).astype(BF)
        normed_t[...] = jnp.transpose(normed, (1, 0))
        for copy in loads[1]:
            copy.wait()
        hidden = dot(normed, w1[...])
        activated = gelu(hidden).astype(BF)
        act_t[...] = jnp.transpose(activated, (1, 0))
        for copy in loads[2]:
            copy.wait()
        new_ref[...] = (mixed + dot(activated, w2[...])).astype(BF)
        cot = cot_ref[...]
        grad_hidden = (dot(cot, w2[...], ((1,), (1,))) * gelu_slope(hidden)).astype(BF)
        inner[...] = grad_hidden
        upstream = dot(grad_hidden, w1[...], ((1,), (1,)))
        grad_mixed = cot.astype(F32) + norm_pull(upstream, gain, xhat, scale)
        mixed_grad_ref[...] = grad_mixed
        grad_branch = grad_mixed.astype(BF)
        branch[...] = grad_branch
        grad_attended = dot(grad_branch, wo[...], ((1,), (1,))).astype(BF)
        message_ref[:, :lat] = grad_attended
        product = grad_attended.astype(F32) * attended.astype(F32)
        out_lane = lax.broadcasted_iota(jnp.int32, (tokens, LANES), 1)
        stats = jnp.zeros((tokens, LANES), F32)
        for head in range(HEADS):
            at, shift = head_window(head)
            mask = head_lanes(head)
            inner_sum = jnp.sum(
                jnp.where(mask, product[:, at : at + WINDOW], 0.0), axis=-1, keepdims=True
            )
            first_lane = at + shift
            log_column = log_total[:, first_lane : first_lane + 1]
            terms = split_three(log_column) + split_three(inner_sum)
            for index, term in enumerate(terms):
                stats = jnp.where(out_lane == index * HEADS + head, term, stats)
        message_ref[:, lat:] = stats.astype(BF)

    return pl.pallas_call(
        kernel,
        in_specs=[pl.BlockSpec(memory_space=pltpu.SMEM)]
        + [whole_spec()] * (groups + 3)
        + [any_spec()] * count,
        out_specs=[whole_spec()] * 8,
        out_shape=[
            jax.ShapeDtypeStruct((tokens, lat), BF),
            jax.ShapeDtypeStruct((tokens, lat), F32),
            jax.ShapeDtypeStruct((tokens, lat + LANES), BF),
            jax.ShapeDtypeStruct((lat, tokens), BF),
            jax.ShapeDtypeStruct((tokens, lat), BF),
            jax.ShapeDtypeStruct((lat, tokens), BF),
            jax.ShapeDtypeStruct((tokens, lat), BF),
            jax.ShapeDtypeStruct((lat, tokens), BF),
        ],
        scratch_shapes=[pltpu.VMEM((lat, lat), BF)] * 3
        + [pltpu.SemaphoreType.DMA((6 * count,))],
        compiler_params=params(0),
        cost_estimate=pl.CostEstimate(
            flops=12 * tokens * lat * lat,
            bytes_accessed=6 * lat * lat + 30 * tokens * lat,
            transcendentals=8 * tokens * lat,
        ),
        name="feed",
    )(me, *parts, latents_flat, cot_flat, gain, *flat)


def feed_grads_call(me, lefts, rights, n, far):
    lat, tokens = lefts[0].shape
    width = rights[0].shape[1]
    terms = len(lefts)

    def kernel(me_ref, *refs):
        left_refs, right_refs = refs[:terms], refs[terms : 2 * terms]
        outs = refs[2 * terms :]
        me = me_ref[0]
        for distance in range(far):
            place = pl.multiple_of(jnp.bitwise_xor(me, distance) * n, 16)
            for index in range(terms):
                chunk = left_refs[index][pl.ds(place, n), :]
                outs[distance][index * n : (index + 1) * n, :] = dot(
                    chunk, right_refs[index][...]
                ).astype(BF)

    return pl.pallas_call(
        kernel,
        in_specs=[pl.BlockSpec(memory_space=pltpu.SMEM)] + [whole_spec()] * (2 * terms),
        out_specs=[whole_spec()] * far,
        out_shape=[jax.ShapeDtypeStruct((terms * n, width), BF)] * far,
        compiler_params=params(0),
        cost_estimate=pl.CostEstimate(
            flops=2 * terms * tokens * lat * width,
            bytes_accessed=2 * terms * (lat * width + 2 * tokens * lat),
            transcendentals=0,
        ),
        name="feed_grads",
    )(me, *lefts, *rights)


def attend_back_call(
    me, parts, queries, keys, values, latent_ids, byte_ids, byte_t, latent_t, pieces, flat,
    key_rows, query_rows, query_at, rows, far,
):
    groups = len(parts)
    tokens, lat = keys.shape
    width = byte_t.shape[0]
    block = tokens // rows
    latents = queries.shape[0] // rows
    group = latents // groups
    count = len(flat)
    score_scale = 1.0 / math.sqrt(HEAD_DIM)
    chunk_rows = 2 * key_rows + query_rows

    def kernel(me_ref, *refs):
        part_refs = refs[:groups]
        query_ref, key_ref, value_ref, lid_ref, bid_ref, byte_t_ref, latent_t_ref = refs[
            groups : groups + 7
        ]
        piece_refs = refs[groups + 7 : groups + 7 + count]
        rest = refs[groups + 7 + count :]
        grad_key_ref, grad_value_ref = rest[:2]
        up_refs = rest[2 : 2 + groups]
        out_refs = rest[2 + groups : 2 + groups + far]
        wq, message, acc_q, acc_k, acc_v, all_q, all_k, all_v, sems = rest[2 + groups + far :]
        row = pl.program_id(0)
        me = me_ref[0]

        def copies():
            return piece_copies(pieces, piece_refs, query_at, query_rows, wq, me, sems, 0)

        @pl.when(row == 0)
        def _():
            for copy in copies():
                copy.start()

        for index, ref in enumerate(part_refs):
            message[index * group : (index + 1) * group, :] = ref[...]
        stats = jnp.transpose(message[:, lat:].astype(F32), (1, 0))
        allowed = bid_ref[0] == lid_ref[0]
        for head in range(HEADS):
            at, _ = head_window(head)
            mask = head_lanes(head)
            window = slice(at, at + WINDOW)
            take = lambda k: stats[k * HEADS + head : k * HEADS + head + 1, :]
            log_total = take(0) + take(1) + take(2)
            inner_sum = take(3) + take(4) + take(5)
            query = jnp.where(mask, query_ref[:, window], jnp.zeros((), BF))
            grad = jnp.where(mask, message[:, window], jnp.zeros((), BF))
            key = key_ref[:, window]
            scores = dot(key, query, ((1,), (1,))) * score_scale
            probs = jnp.exp(jnp.where(allowed, scores - log_total, NEG_FILL))
            grad_probs = dot(value_ref[:, window], grad, ((1,), (1,)))
            grad_scores = (probs * (grad_probs - inner_sum)).astype(BF)
            found_k = dot(grad_scores, query)
            found_v = dot(probs.astype(BF), grad)
            found_q = dot(grad_scores, key, ((0,), (0,)))
            if head == 0:
                acc_k[:, window] = found_k
                acc_v[:, window] = found_v
                acc_q[:, window] = found_q
            else:
                acc_k[:, window] = jnp.where(mask, found_k, acc_k[:, window])
                acc_v[:, window] = jnp.where(mask, found_v, acc_v[:, window])
                acc_q[:, window] = jnp.where(mask, found_q, acc_q[:, window])

        byte_place = pl.multiple_of(row * block, 16)
        latent_place = pl.multiple_of(row * latents, 16)
        grad_key = (acc_k[...] * score_scale).astype(BF)
        grad_value = acc_v[...].astype(BF)
        grad_query = (acc_q[...] * score_scale).astype(BF)
        grad_key_ref[...] = grad_key
        grad_value_ref[...] = grad_value
        all_k[pl.ds(byte_place, block), :] = grad_key
        all_v[pl.ds(byte_place, block), :] = grad_value
        all_q[pl.ds(latent_place, latents), :] = grad_query

        @pl.when(row == 0)
        def _():
            for copy in copies():
                copy.wait()

        upstream = dot(grad_query, wq[...], ((1,), (1,))).astype(BF)
        for index, ref in enumerate(up_refs):
            ref[...] = upstream[index * group : (index + 1) * group, :]

        @pl.when(row == rows - 1)
        def _():
            for distance in range(far):
                owner = jnp.bitwise_xor(me, distance)
                place = pl.multiple_of(owner * key_rows, 16)
                chunk = byte_t_ref[pl.ds(place, key_rows), :]
                out = out_refs[distance]
                out[:key_rows, :] = dot(chunk, all_k[...]).astype(BF)
                out[key_rows : 2 * key_rows, :] = dot(chunk, all_v[...]).astype(BF)
                place = pl.multiple_of(owner * query_rows, 16)
                chunk = latent_t_ref[pl.ds(place, query_rows), :]
                out[2 * key_rows :, :] = dot(chunk, all_q[...]).astype(BF)

    row_block = lambda i, m: (i, 0)
    once = pl.Buffered(buffer_count=1)
    return pl.pallas_call(
        kernel,
        grid_spec=pltpu.PrefetchScalarGridSpec(
            num_scalar_prefetch=1,
            grid=(rows,),
            in_specs=[pl.BlockSpec((group, lat + LANES), row_block)] * groups
            + [
                pl.BlockSpec((latents, lat), row_block),
                pl.BlockSpec((block, lat), row_block),
                pl.BlockSpec((block, lat), row_block),
                pl.BlockSpec((1, 1, latents), lambda i, m: (i, 0, 0)),
                pl.BlockSpec((1, block, 1), lambda i, m: (i, 0, 0)),
                pl.BlockSpec((width, tokens), lambda i, m: (0, 0), pipeline_mode=once),
                pl.BlockSpec((lat, rows * latents), lambda i, m: (0, 0), pipeline_mode=once),
            ]
            + [any_spec()] * count,
            out_specs=[pl.BlockSpec((block, lat), row_block)] * 2
            + [pl.BlockSpec((group, lat), row_block)] * groups
            + [
                pl.BlockSpec((chunk_rows, lat), lambda i, m: (0, 0), pipeline_mode=once)
            ]
            * far,
            scratch_shapes=[
                pltpu.VMEM((lat, lat), BF),
                pltpu.VMEM((latents, lat + LANES), BF),
                pltpu.VMEM((latents, lat), F32),
                pltpu.VMEM((block, lat), F32),
                pltpu.VMEM((block, lat), F32),
                pltpu.VMEM((rows * latents, lat), BF),
                pltpu.VMEM((tokens, lat), BF),
                pltpu.VMEM((tokens, lat), BF),
                pltpu.SemaphoreType.DMA((2 * count,)),
            ],
        ),
        out_shape=[jax.ShapeDtypeStruct((tokens, lat), BF)] * 2
        + [jax.ShapeDtypeStruct((rows * group, lat), BF)] * groups
        + [jax.ShapeDtypeStruct((chunk_rows, lat), BF)] * far,
        compiler_params=params(1),
        cost_estimate=pl.CostEstimate(
            flops=10 * rows * HEADS * latents * block * WINDOW
            + 4 * tokens * width * lat
            + 4 * rows * latents * lat * lat,
            bytes_accessed=2 * (8 * tokens * lat + 4 * lat * lat),
            transcendentals=rows * HEADS * latents * block,
        ),
        name="attend_back",
    )(me, *parts, queries, keys, values, latent_ids, byte_ids, byte_t, latent_t, *flat)


def byte_grad_call(me, bytes_flat, gain, grad_keys, grad_values, pieces, flat, key_rows, key_at, value_at, rows):
    tokens, width = bytes_flat.shape
    block = tokens // rows
    lat = grad_keys.shape[1]
    count = len(flat)

    def kernel(me_ref, x_ref, gain_ref, gk_ref, gv_ref, *refs):
        piece_refs = refs[:count]
        out_ref, wk, wv, sems = refs[count:]

        def copies():
            one = piece_copies(pieces, piece_refs, key_at, key_rows, wk, me_ref[0], sems, 0)
            two = piece_copies(
                pieces, piece_refs, value_at, key_rows, wv, me_ref[0], sems, len(one)
            )
            return one + two

        @pl.when(pl.program_id(0) == 0)
        def _():
            for copy in copies():
                copy.start()

        xhat, scale = standardize(x_ref[...].astype(F32))

        @pl.when(pl.program_id(0) == 0)
        def _():
            for copy in copies():
                copy.wait()

        upstream = dot(gk_ref[...], wk[...], ((1,), (1,))) + dot(
            gv_ref[...], wv[...], ((1,), (1,))
        )
        out_ref[...] = norm_pull(upstream, gain_ref[...], xhat, scale)

    row_block = lambda i, m: (i, 0)
    return pl.pallas_call(
        kernel,
        grid_spec=pltpu.PrefetchScalarGridSpec(
            num_scalar_prefetch=1,
            grid=(rows,),
            in_specs=[
                pl.BlockSpec((block, width), row_block),
                pl.BlockSpec((1, width), lambda i, m: (0, 0)),
                pl.BlockSpec((block, lat), row_block),
                pl.BlockSpec((block, lat), row_block),
            ]
            + [any_spec()] * count,
            out_specs=pl.BlockSpec((block, width), row_block),
            scratch_shapes=[
                pltpu.VMEM((width, lat), BF),
                pltpu.VMEM((width, lat), BF),
                pltpu.SemaphoreType.DMA((4 * count,)),
            ],
        ),
        out_shape=jax.ShapeDtypeStruct((tokens, width), F32),
        compiler_params=params(1),
        cost_estimate=pl.CostEstimate(
            flops=4 * tokens * width * lat,
            bytes_accessed=2 * (3 * tokens * width + 2 * tokens * lat + 2 * width * lat),
            transcendentals=0,
        ),
        name="byte_grad",
    )(me, bytes_flat, gain, grad_keys, grad_values, *flat)


def swap(value, axis, size, distance):
    return lax.ppermute(value, axis, [(i, i ^ distance) for i in range(size)])


def gather_shards(message, own, size):
    found = [message] + [swap(message, "fsdp", size, j) for j in range(1, size)]
    return [lax.select_n(jnp.bitwise_xor(own, k), *found) for k in range(size)]


def gather_blocks(block, n_dp, half):
    send = lambda value, distance: swap(value, "dp", n_dp, distance)
    rows = block.shape[0]
    full = [(0, rows)]
    chips = [(0, full, [block])]
    if n_dp == 8:
        one, two = send(block, 2), send(block, 4)
        chips.append((2, full, [one]))
        chips.append((4, full, [two]))
        low, high = send(one[:half], 4), send(two[half:], 2)
        chips.append((6, [(0, half), (half, rows)], [low, high]))
    else:
        for distance in range(2, n_dp, 2):
            chips.append((distance, full, [send(block, distance)]))
    pieces, flat = [], []
    for distance, parts, arrays in chips:
        pieces.append((distance, parts))
        flat.extend(arrays)
        pieces.append((distance + 1, parts))
        flat.extend(send(array, 1) for array in arrays)
    return pieces, flat


def add(*values):
    return functools.reduce(jnp.add, [v.astype(F32) for v in values]).astype(BF)


def scatter_blocks(parts, n_dp, half):
    send = lambda value, distance: swap(value, "dp", n_dp, distance)
    arrived = [send(parts[d + 1], 1) for d in range(0, n_dp, 2)]
    chips = [(parts[d], arrived[d // 2]) for d in range(0, n_dp, 2)]
    if n_dp == 8:
        low = send(add(*[v[:half] for v in chips[3]]), 2)
        high = send(add(*[v[half:] for v in chips[3]]), 4)
        one = jnp.concatenate(
            [add(*[v[:half] for v in chips[1]]), add(*[v[half:] for v in chips[1]], high)], axis=0
        )
        two = jnp.concatenate(
            [add(*[v[:half] for v in chips[2]], low), add(*[v[half:] for v in chips[2]])], axis=0
        )
        return add(*chips[0], send(one, 2), send(two, 4))
    return add(*chips[0], *[send(add(*chips[i]), 2 * i) for i in range(1, len(chips))])


def scatter_shards(block, own, size, rows_of):
    def message(distance):
        index = jnp.bitwise_xor(own, distance)
        found, at = [], 0
        for rows in rows_of:
            part = block[at : at + rows * size].reshape(size, rows, block.shape[1])
            found.append(lax.dynamic_index_in_dim(part, index, 0, keepdims=False))
            at += rows * size
        return found

    total = [part.astype(F32) for part in message(0)]
    for distance in range(1, size):
        arrived = swap(jnp.concatenate(message(distance), axis=0), "fsdp", size, distance)
        at = 0
        for index, rows in enumerate(rows_of):
            total[index] = total[index] + arrived[at : at + rows].astype(F32)
            at += rows
    return total


def up_to(value, step):
    return -(-value // step) * step


def pad_rows(value, rows):
    return jnp.pad(value, ((0, rows - value.shape[0]), (0, 0)))


def local(n_dp, n_f, bytes_in, latents_in, cotangent, byte_segments, latent_segments,
          w_query, w_key, w_value, w_out, w_mlp_in, w_mlp_out,
          gain_latent, gain_byte, gain_mlp):
    rows, byte_local, width = bytes_in.shape
    _, group, lat = latents_in.shape
    latents = group * n_f
    dp, own = lax.axis_index("dp"), lax.axis_index("fsdp")
    me = dp.astype(jnp.int32).reshape(1)
    bytes_flat = bytes_in.reshape(rows * byte_local, width)
    latents_flat = latents_in.reshape(rows * group, lat)
    cot_flat = cotangent.reshape(rows * group, lat)

    kr, qr = w_key.shape[0], w_query.shape[0]
    gains = jnp.concatenate([gain_latent, gain_byte, gain_mlp])
    gains = jnp.pad(gains, (0, lat - gains.shape[0]))[None, :]
    message = jnp.concatenate([w_key, w_value, w_query, gains], axis=0)
    message = pad_rows(message, up_to(2 * kr + qr + 1, 16))
    shards = gather_shards(message, own, n_f)
    block = jnp.concatenate(
        [s[:kr] for s in shards]
        + [s[kr : 2 * kr] for s in shards]
        + [s[2 * kr : 2 * kr + qr] for s in shards]
        + [s[2 * kr + qr : 2 * kr + qr + 1] for s in shards],
        axis=0,
    )
    key_rows, query_rows = n_f * kr, n_f * qr
    gain_at = 2 * key_rows + query_rows
    block = pad_rows(block, up_to(gain_at + n_f, 16))
    pieces, flat = gather_blocks(block, n_dp, 2 * key_rows)

    by_distance = [None] * n_dp
    index = 0
    for distance, parts in pieces:
        by_distance[distance] = flat[index + len(parts) - 1]
        index += len(parts)
    gain_rows = []
    for array in by_distance:
        end = array.shape[0] - (block.shape[0] - gain_at)
        gain_rows.append(array[end : end + n_f, : 2 * qr + kr])
    gain_rows = jnp.stack(gain_rows)
    gain_rows = jnp.take(gain_rows, jnp.bitwise_xor(jnp.arange(n_dp), dp), axis=0)
    gain_rows = gain_rows.astype(F32)
    latent_gain = gain_rows[:, :, :qr].reshape(1, lat)
    byte_gain = gain_rows[:, :, qr : qr + kr].reshape(1, width)
    mlp_gain = gain_rows[:, :, qr + kr :].reshape(1, lat)

    ids = latent_segments.reshape(1, rows * group).astype(BF)
    ids = jnp.pad(ids, ((0, 15), (0, lat - rows * group)))
    latent_message = jnp.concatenate([latents_flat, ids], axis=0)
    latent_parts = [latent_message] + [
        swap(latent_message, "fsdp", n_f, j) for j in range(1, n_f)
    ]
    latent_ids = jnp.stack(
        [p[rows * group, : rows * group].reshape(rows, group) for p in latent_parts], axis=1
    ).reshape(rows, latents)
    latent_ids = latent_ids.astype(F32)
    byte_ids = lax.dynamic_slice_in_dim(byte_segments, own * byte_local, byte_local, axis=1)
    byte_ids = byte_ids.astype(F32)

    message = jnp.concatenate([w_out, w_mlp_in, w_mlp_out], axis=0)
    shards = gather_shards(message, own, n_f)
    block_two = jnp.concatenate(
        [s[i * qr : (i + 1) * qr] for i in range(3) for s in shards], axis=0
    )
    half = up_to(3 * query_rows // 2, 16)
    pieces_two, flat_two = gather_blocks(block_two, n_dp, half)

    byte_t, keys, values = key_value_call(
        me, bytes_flat, byte_gain, pieces, flat, key_rows, 0, key_rows, rows
    )
    latent_t, queries, *found = attend_call(
        me, latent_parts, latent_gain, latent_ids[:, :, None], byte_ids[:, None, :],
        keys, values, pieces, flat, query_rows, 2 * key_rows, rows,
    )
    attended_parts = [found[0]] + [swap(found[j], "fsdp", n_f, j) for j in range(1, n_f)]
    new, grad_mixed, grad_message, attended_t, branch, normed_t, inner, act_t = feed_call(
        me, attended_parts, latents_flat, cot_flat, mlp_gain, pieces_two, flat_two, query_rows
    )
    grad_parts = [grad_message] + [swap(grad_message, "fsdp", n_f, j) for j in range(1, n_f)]
    feed_grads = feed_grads_call(
        me, (attended_t, normed_t, act_t), (branch, inner, cot_flat), query_rows, n_dp
    )
    grad_two = scatter_shards(scatter_blocks(feed_grads, n_dp, half), own, n_f, (qr, qr, qr))

    out = attend_back_call(
        me, grad_parts, queries, keys, values, latent_ids[:, None, :], byte_ids[:, :, None],
        byte_t, latent_t, pieces, flat, key_rows, query_rows, 2 * key_rows, rows, n_dp,
    )
    grad_keys, grad_values = out[:2]
    ups = out[2 : 2 + n_f]
    grad_one = scatter_shards(
        scatter_blocks(out[2 + n_f :], n_dp, 2 * key_rows), own, n_f, (kr, kr, qr)
    )
    up_parts = [ups[0]] + [swap(ups[j], "fsdp", n_f, j) for j in range(1, n_f)]
    grad_bytes = byte_grad_call(
        me, bytes_flat, byte_gain, grad_keys, grad_values, pieces, flat,
        key_rows, 0, key_rows, rows,
    )
    upstream = functools.reduce(jnp.add, [p.astype(F32) for p in up_parts])
    xhat, scale = standardize(latents_flat.astype(F32))
    grad_latents = grad_mixed + norm_pull(upstream, latent_gain, xhat, scale)

    def gain_grad(pairs, gain):
        total = sum(jnp.sum(w.astype(F32) * g, axis=1) for w, g in pairs)
        return total / gain.astype(F32)

    grad_key, grad_value, grad_query = grad_one
    grad_out, grad_inner, grad_outer = grad_two
    return (
        new.reshape(rows, group, lat),
        grad_latents.reshape(rows, group, lat),
        grad_bytes.reshape(rows, byte_local, width),
        grad_query,
        grad_key,
        grad_value,
        grad_out,
        grad_inner,
        grad_outer,
        gain_grad([(w_query, grad_query)], gain_latent),
        gain_grad([(w_key, grad_key), (w_value, grad_value)], gain_byte),
        gain_grad([(w_mlp_in, grad_inner)], gain_mlp),
    )


def solution(mesh):
    rows3 = P("dp", "fsdp", None)
    split2 = P(("dp", "fsdp"), None)
    split1 = P(("dp", "fsdp"))
    in_specs = (rows3,) * 3 + (P("dp", None), P("dp", "fsdp")) + (split2,) * 6 + (split1,) * 3
    out_specs = (rows3,) * 3 + (split2,) * 6 + (split1,) * 3
    body = functools.partial(local, mesh.shape["dp"], mesh.shape["fsdp"])
    return jax.shard_map(
        body, mesh=mesh, in_specs=in_specs, out_specs=out_specs, check_vma=False
    )
```

time: 2440 us -> 499 us (0.20)
  the two profiles are of different devices: /device:TPU:0 before, /device:TPU:12 now
where the time goes in v1:
time: 499 us; the launch traced here: 491 us
  waiting for transfers between devices  257 us (52%)
  Pallas kernels  112 us (22%)
  starting transfers between devices  56.7 us (11%)
  local copies, waits for them, and re-layouts  42 us (8%)
  other arithmetic  21.5 us (4%)
    ppermute x58, waiting for transfers between devices, swap(): return lax.ppermute(value, axis, [(i, i ^ distance) for i in range(size)])  257 us
    ppermute x58, starting transfers between devices, swap(): return lax.ppermute(value, axis, [(i, i ^ distance) for i in range(size)])  56.7 us
    pallas_call x1, Pallas kernels, attend_back_call(): pl.pallas_call(kernel, grid_spec=pltpu.PrefetchScalarGridSpec(num_scalar_...  49 us
    unnamed x105, local copies, waits for them, and re-layouts  22.3 us
    pallas_call x1, Pallas kernels, attend_call(): pl.pallas_call(kernel, grid_spec=pltpu.PrefetchScalarGridSpec(num_scalar_...  16.6 us
    pallas_call x1, Pallas kernels, byte_grad_call(): pl.pallas_call(kernel, grid_spec=pltpu.PrefetchScalarGridSpec(num_scalar_...  14.4 us
    pallas_call x1, Pallas kernels, key_value_call(): pl.pallas_call(kernel, grid_spec=pltpu.PrefetchScalarGridSpec(num_scalar_...  12.7 us
    pallas_call x1, Pallas kernels, feed_call(): pl.pallas_call(kernel, in_specs=[pl.BlockSpec(memory_space=pltpu.SMEM)] +...  12 us
  transfers between devices with their start and end apart: 58, of which 28 were waited for; matrix products, arithmetic and copies ran while one was open for 11% of the time, Pallas kernels for 20%

profile of v1, /device:TPU:12, one launch (start us, length us, event | category | flops | bytes accessed | tf_op | source)
XLA Modules:
  0.0 491.0 jit_solution(10555242089739135651)
XLA Ops:
  2.5 1.6 collective-permute-start.5
  4.1 2.5 collective-permute-start.3
  6.6 1.5 constant_dynamic-update-slice_fusion.10
  8.1 1.5 constant_dynamic-update-slice_fusion.9
  9.7 1.5 constant_dynamic-update-slice_fusion.8
  11.2 1.5 collective-permute-start.20
  12.7 1.7 collective-permute-start.19
  18.5 1.2 collective-permute-start.18
  19.7 1.5 collective-permute-start.2
  21.3 18.2 %collective-permute-done.4 = bf16[96,1280]{1,0:T(8,128)(2,1)S(1)} collective-permute-done((bf16[96,1280]{1,0:T(8,128)(2,1)S(1)}, bf16[96,1280]{1,0:T(8,128)(2,1)S(1)}, u32[]{:S(2)}, u32[]{:S(2)}) %collective-permute-start.4) | collective-permute-done | bytes 245792 | tf_op jit(solution)/shard_map/ppermute | solution.py:643
  39.5 3.4 collective-permute-start.1
  44.1 25.6 %collective-permute-done.20 = bf16[120,1280]{1,0:T(8,128)(2,1)} collective-permute-done((bf16[120,1280]{1,0:T(8,128)(2,1)}, bf16[120,1280]{1,0:T(8,128)(2,1)}, u32[]{:S(2)}, u32[]{:S(2)}) %collective-permute-start.20) | collective-permute-done | bytes 307232 | tf_op jit(solution)/shard_map/ppermute | solution.py:643
  69.7 5.9 %collective-permute-done.19 = bf16[120,1280]{1,0:T(8,128)(2,1)} collective-permute-done((bf16[120,1280]{1,0:T(8,128)(2,1)}, bf16[120,1280]{1,0:T(8,128)(2,1)}, u32[]{:S(2)}, u32[]{:S(2)}) %collective-permute-start.19) | collective-permute-done | bytes 307232 | tf_op jit(solution)/shard_map/ppermute | solution.py:643
  76.1 1.5 collective-permute-start.7
  77.6 1.4 select_select_fusion
  86.2 1.6 collective-permute-done.2.refs_3_
  88.4 8.9 %collective-permute-done.1.refs_2_ = bf16[208,1280]{1,0:T(8,128)(2,1)} collective-permute-done((bf16[208,1280]{1,0:T(8,128)(2,1)}, bf16[208,1280]{1,0:T(8,128)(2,1)}, u32[]{:S(2)}, u32[]{:S(2)}) %collective-permute-start.1) | collective-permute-done | bytes 532512 | tf_op jit(solution)/shard_map/ppermute | solution.py:643
  97.8 1.5 collective-permute-start.22
  108.6 1.3 constant_dynamic-update-slice_fusion.6
  110.4 15.1 %collective-permute-done.24.refs_11_ = bf16[480,1280]{1,0:T(8,128)(2,1)} collective-permute-done((bf16[480,1280]{1,0:T(8,128)(2,1)}, bf16[480,1280]{1,0:T(8,128)(2,1)}, u32[]{:S(2)}, u32[]{:S(2)}) %collective-permute-start.24) | collective-permute-done | bytes 1228832 | tf_op jit(solution)/shard_map/ppermute | solution.py:643
  125.5 2.0 slice.443
  128.1 1.5 collective-permute-start.13
  129.6 1.9 slice.442
  131.5 3.9 collective-permute-done.11.refs_7_.refs_16_.refs_18_
  135.4 1.5 collective-permute-start.27
  138.7 1.5 collective-permute-start.26
  140.8 1.2 constant_dynamic-update-slice_fusion.1
  143.6 1.4 gather_fusion
  147.4 12.7 %keys_values.1 = (bf16[768,1536]{1,0:T(8,128)(2,1)}, bf16[1536,1280]{1,0:T(8,128)(2,1)}, bf16[1536,1280]{1,0:T(8,128)(2,1)}) custom-call(s32[1]{0:T(128)} %bitcast.me_ref, bf16[1536,768]{1,0:T(8,128)(2,1)} %bitcast.114, f32[1,768]{1,0:T(1,128)} %reshape.209.gain_ref, bf16[368,1280]{1,0:T(8,128)(2,1)} %copy-done.2, ...), custom_call_target="tpu_custom_call" | custom-call | flops 6039797760 | bytes 16515072 | tf_op jit(solution)/shard_map/keys_values/pallas_call | solution.py:141
  160.1 16.6 %attend.1 = (bf16[1280,768]{1,0:T(8,128)(2,1)}, bf16[768,1280]{1,0:T(8,128)(2,1)}, bf16[192,1408]{1,0:T(8,128)(2,1)}, bf16[192,1408]{1,0:T(8,128)(2,1)}, bf16[19...) custom-call(s32[1]{0:T(128)} %bitcast.me_ref, bf16[208,1280]{1,0:T(8,128)(2,1)} %fusion.3.refs_0_, ...), custom_call_target="tpu_custom_call" | custom-call | flops 5737807872 | bytes 19005440 | tf_op jit(solution)/shard_map/attend/pallas_call | solution.py:243
  176.7 2.6 collective-permute-start.15
  180.3 22.6 %collective-permute-done.15.refs_1_ = bf16[192,1408]{1,0:T(8,128)(2,1)S(1)} collective-permute-done((bf16[192,1408]{1,0:T(8,128)(2,1)}, bf16[192,1408]{1,0:T(8,128)(2,1)S(1)}, u32[]{:S(2)}, u32[]{:S(2)}) %collective-permute-start.15) | collective-permute-done | bytes 540704 | tf_op jit(solution)/shard_map/ppermute | solution.py:643
  202.9 1.9 collective-permute-done.16.refs_2_
  207.1 24.3 %collective-permute-done.17.refs_3_ = bf16[192,1408]{1,0:T(8,128)(2,1)} collective-permute-done((bf16[192,1408]{1,0:T(8,128)(2,1)}, bf16[192,1408]{1,0:T(8,128)(2,1)}, u32[]{:S(2)}, u32[]{:S(2)}) %collective-permute-start.17) | collective-permute-done | bytes 540704 | tf_op jit(solution)/shard_map/ppermute | solution.py:643
  232.7 12.0 %feed.1 = (bf16[192,1280]{1,0:T(8,128)(2,1)}, f32[192,1280]{1,0:T(8,128)}, bf16[192,1408]{1,0:T(8,128)(2,1)}, bf16[1280,192]{1,0:T(8,128)(2,1)}, bf16[192,1280]{...) custom-call(s32[1]{0:T(128)} %bitcast.me_ref, ...), custom_call_target="tpu_custom_call" | custom-call | flops 3774873600 | bytes 17203200 | tf_op jit(solution)/shard_map/feed/pallas_call | solution.py:367
  245.4 2.9 collective-permute-start.30
  251.3 6.8 %feed_grads.1 = (bf16[480,1280]{1,0:T(8,128)(2,1)}, bf16[480,1280]{1,0:T(8,128)(2,1)}, bf16[480,1280]{1,0:T(8,128)(2,1)}, bf16[480,1280]{1,0:T(8,128)(2,1)}, bf1...) custom-call(s32[1]{0:T(128)} %bitcast.me_ref, ...), custom_call_target="tpu_custom_call" | custom-call | flops 1887436800 | bytes 12779520 | tf_op jit(solution)/shard_map/feed_grads/pallas_call | solution.py:412
  258.6 13.8 %collective-permute-done.32.refs_3_ = bf16[192,1408]{1,0:T(8,128)(2,1)S(1)} collective-permute-done((bf16[192,1408]{1,0:T(8,128)(2,1)}, bf16[192,1408]{1,0:T(8,128)(2,1)S(1)}, u32[]{:S(2)}, u32[]{:S(2)}) %collective-permute-start.32) | collective-permute-done | bytes 540704 | tf_op jit(solution)/shard_map/ppermute | solution.py:643
  272.4 11.3 %collective-permute-done.31.refs_2_ = bf16[192,1408]{1,0:T(8,128)(2,1)S(1)} collective-permute-done((bf16[192,1408]{1,0:T(8,128)(2,1)}, bf16[192,1408]{1,0:T(8,128)(2,1)S(1)}, u32[]{:S(2)}, u32[]{:S(2)}) %collective-permute-start.31) | collective-permute-done | bytes 540704 | tf_op jit(solution)/shard_map/ppermute | solution.py:643
  284.5 49.0 %attend_back.1 = (bf16[1536,1280]{1,0:T(8,128)(2,1)}, bf16[1536,1280]{1,0:T(8,128)(2,1)}, bf16[192,1280]{1,0:T(8,128)(2,1)}, bf16[192,1280]{1,0:T(8,128)(2,1)}, ...) custom-call(s32[1]{0:T(128)} %bitcast.me_ref, ...), custom_call_target="tpu_custom_call" | custom-call | flops 19126026240 | bytes 44564480 | tf_op jit(solution)/shard_map/attend_back/pallas_call | solution.py:528
  333.5 1.7 collective-permute-start.33
  335.3 1.7 collective-permute-start.34
  337.4 14.4 %byte_grad.1 = f32[1536,768]{1,0:T(8,128)} custom-call(s32[1]{0:T(128)} %bitcast.me_ref, bf16[1536,768]{1,0:T(8,128)(2,1)} %bitcast.115, f32[1,768]{1,0:T(1,128)} %reshape.209.gain_ref, bf16[1536,1280]{1,0:T(8,128)(2,1)} %get-tuple-element.67.gk_ref, bf16[1536,1280]{1,0:T(8,128)(2,1)} %get-tuple-element.68.gv_ref, bf16[368,1280]{1,0:T(8,128)(2,1)} %copy-done.2, ...), custom_call_target="tpu_custom_call" | custom-call | flops 6039797760 | bytes 18874368 | tf_op jit(solution)/shard_map/byte_grad/pallas_call | solution.py:612
  351.9 4.3 collective-permute-done.33
  356.2 13.7 %collective-permute-done.34 = bf16[192,1280]{1,0:T(8,128)(2,1)} collective-permute-done((bf16[192,1280]{1,0:T(8,128)(2,1)}, bf16[192,1280]{1,0:T(8,128)(2,1)}, u32[]{:S(2)}, u32[]{:S(2)}) %collective-permute-start.34) | collective-permute-done | bytes 491552 | tf_op jit(solution)/shard_map/ppermute | solution.py:643
  370.0 10.6 %collective-permute-done.35 = bf16[192,1280]{1,0:T(8,128)(2,1)} collective-permute-done((bf16[192,1280]{1,0:T(8,128)(2,1)}, bf16[192,1280]{1,0:T(8,128)(2,1)}, u32[]{:S(2)}, u32[]{:S(2)}) %collective-permute-start.35) | collective-permute-done | bytes 491552 | tf_op jit(solution)/shard_map/ppermute | solution.py:643
  380.5 1.9 fusion.30
  384.7 1.9 collective-permute-done.41
  388.3 1.8 collective-permute-start.39
  390.2 13.2 %collective-permute-done.50 = bf16[240,1280]{1,0:T(8,128)(2,1)S(1)} collective-permute-done((bf16[240,1280]{1,0:T(8,128)(2,1)S(1)}, bf16[240,1280]{1,0:T(8,128)(2,1)S(1)}, u32[]{:S(2)}, u32[]{:S(2)}) %collective-permute-start.50) | collective-permute-done | bytes 614432 | tf_op jit(solution)/shard_map/ppermute | solution.py:643
  404.9 6.5 %collective-permute-done.39 = bf16[160,1280]{1,0:T(8,128)(2,1)S(1)} collective-permute-done((bf16[160,1280]{1,0:T(8,128)(2,1)S(1)}, bf16[160,1280]{1,0:T(8,128)(2,1)S(1)}, u32[]{:S(2)}, u32[]{:S(2)}) %collective-permute-start.39) | collective-permute-done | bytes 409632 | tf_op jit(solution)/shard_map/ppermute | solution.py:643
  412.7 3.6 collective-permute-done.42
  420.0 1.8 collective-permute-start.54
  421.7 13.9 %collective-permute-done.40 = bf16[352,1280]{1,0:T(8,128)(2,1)S(1)} collective-permute-done((bf16[352,1280]{1,0:T(8,128)(2,1)S(1)}, bf16[352,1280]{1,0:T(8,128)(2,1)S(1)}, u32[]{:S(2)}, u32[]{:S(2)}) %collective-permute-start.40) | collective-permute-done | bytes 901152 | tf_op jit(solution)/shard_map/ppermute | solution.py:643
  435.7 3.9 collective-permute-done.43
  440.4 1.6 collective-permute-start.46
  442.1 7.1 %collective-permute-done.45 = bf16[88,1280]{1,0:T(8,128)(2,1)S(1)} collective-permute-done((bf16[88,1280]{1,0:T(8,128)(2,1)S(1)}, bf16[88,1280]{1,0:T(8,128)(2,1)S(1)}, u32[]{:S(2)}, u32[]{:S(2)}) %collective-permute-start.45) | collective-permute-done | bytes 225312 | tf_op jit(solution)/shard_map/ppermute | solution.py:643
  449.1 5.4 %collective-permute-start.44 = (bf16[88,1280]{1,0:T(8,128)(2,1)S(1)}, bf16[88,1280]{1,0:T(8,128)(2,1)S(1)}, u32[]{:S(2)}, u32[]{:S(2)}) collective-permute-start(bf16[88,1280]{1,0:T(8,128)(2,1)S(1)} %pad_maximum_fusion.7), channel_id=1, source_target_pairs={{0,1},{1,0},{2,3},{3,2},{4,5},{5,4},{6,7},{7,6},{8,9},{9,8},{10,11... | collective-permute-start | bytes 675848 | tf_op jit(solution)/shard_map/ppermute | solution.py:643
  454.5 1.3 multiply_add_fusion
  455.8 2.6 collective-permute-done.44
  462.1 2.7 collective-permute-start.57
  464.8 1.8 collective-permute-start.55
  467.7 15.1 %collective-permute-done.56 = bf16[120,1280]{1,0:T(8,128)(2,1)S(1)} collective-permute-done((bf16[120,1280]{1,0:T(8,128)(2,1)S(1)}, bf16[120,1280]{1,0:T(8,128)(2,1)S(1)}, u32[]{:S(2)}, u32[]{:S(2)}) %collective-permute-start.56) | collective-permute-done | bytes 307232 | tf_op jit(solution)/shard_map/ppermute | solution.py:643
  482.8 6.3 %collective-permute-done.57 = bf16[120,1280]{1,0:T(8,128)(2,1)S(1)} collective-permute-done((bf16[120,1280]{1,0:T(8,128)(2,1)S(1)}, bf16[120,1280]{1,0:T(8,128)(2,1)S(1)}, u32[]{:S(2)}, u32[]{:S(2)}) %collective-permute-start.57) | collective-permute-done | bytes 307232 | tf_op jit(solution)/shard_map/ppermute | solution.py:643
  (264 shorter events, 59.8 us)
Async XLA Ops:
  0.6 42.2 %copy-start.10 = (bf16[24,1280]{1,0:T(8,128)(2,1)S(1)}, bf16[24,1280]{1,0:T(8,128)(2,1)}, u32[]{:S(2)}) copy-start(bf16[24,1280]{1,0:T(8,128)(2,1)} %param.21) | copy-start | bytes 184324
  0.7 42.2 %copy-start.11 = (bf16[24,1280]{1,0:T(8,128)(2,1)S(1)}, bf16[24,1280]{1,0:T(8,128)(2,1)}, u32[]{:S(2)}) copy-start(bf16[24,1280]{1,0:T(8,128)(2,1)} %param.20) | copy-start | bytes 184324
  0.7 42.2 %copy-start.5 = (bf16[40,1280]{1,0:T(8,128)(2,1)S(1)}, bf16[40,1280]{1,0:T(8,128)(2,1)}, u32[]{:S(2)}) copy-start(bf16[40,1280]{1,0:T(8,128)(2,1)} %param.19) | copy-start | bytes 307204
  2.5 16.0 %collective-permute-start.5 = (bf16[96,1280]{1,0:T(8,128)(2,1)S(1)}, bf16[96,1280]{1,0:T(8,128)(2,1)S(1)}, u32[]{:S(2)}, u32[]{:S(2)}) collective-permute-start(bf16[96,1280]{1,0:T(8,128)(2,1)S(1)} %fusion.10), channel_id=1, source_target_pairs={{0,3},{1,2},{2,1},{3,0},{4,7},{5,6},{6,5},{7,4},{8,11},{9,10},{10,... | collective-permute-start | bytes 737288 | tf_op jit(solution)/shard_map/ppermute | solution.py:643
  4.1 15.6 %collective-permute-start.3 = (bf16[96,1280]{1,0:T(8,128)(2,1)S(1)}, bf16[96,1280]{1,0:T(8,128)(2,1)S(1)}, u32[]{:S(2)}, u32[]{:S(2)}) collective-permute-start(bf16[96,1280]{1,0:T(8,128)(2,1)S(1)} %fusion.10), channel_id=1, source_target_pairs={{0,1},{1,0},{2,3},{3,2},{4,5},{5,4},{6,7},{7,6},{8,9},{9,8},{10,11... | collective-permute-start | bytes 737288 | tf_op jit(solution)/shard_map/ppermute | solution.py:643
  6.6 32.9 %collective-permute-start.4 = (bf16[96,1280]{1,0:T(8,128)(2,1)S(1)}, bf16[96,1280]{1,0:T(8,128)(2,1)S(1)}, u32[]{:S(2)}, u32[]{:S(2)}) collective-permute-start(bf16[96,1280]{1,0:T(8,128)(2,1)S(1)} %fusion.10), channel_id=1, source_target_pairs={{0,2},{1,3},{2,0},{3,1},{4,6},{5,7},{6,4},{7,5},{8,10},{9,11},{10,... | collective-permute-start | bytes 737288 | tf_op jit(solution)/shard_map/ppermute | solution.py:643
  11.2 58.5 %collective-permute-start.20 = (bf16[120,1280]{1,0:T(8,128)(2,1)}, bf16[120,1280]{1,0:T(8,128)(2,1)}, u32[]{:S(2)}, u32[]{:S(2)}) collective-permute-start(bf16[120,1280]{1,0:T(8,128)(2,1)} %constant_dynamic-update-slice_fusion.8), channel_id=1, source_target_pairs={{0,3},{1,2},{2,1},{3,0},{4,7},{5,6},{6,5},{7,4},{8,11},{9,10},{10,... | collective-permute-start | bytes 921608 | tf_op jit(solution)/shard_map/ppermute | solution.py:643
  12.7 62.9 %collective-permute-start.19 = (bf16[120,1280]{1,0:T(8,128)(2,1)}, bf16[120,1280]{1,0:T(8,128)(2,1)}, u32[]{:S(2)}, u32[]{:S(2)}) collective-permute-start(bf16[120,1280]{1,0:T(8,128)(2,1)} %constant_dynamic-update-slice_fusion.8), channel_id=1, source_target_pairs={{0,2},{1,3},{2,0},{3,1},{4,6},{5,7},{6,4},{7,5},{8,10},{9,11},{10,... | collective-permute-start | bytes 921608 | tf_op jit(solution)/shard_map/ppermute | solution.py:643
  18.5 57.6 %collective-permute-start.18 = (bf16[120,1280]{1,0:T(8,128)(2,1)}, bf16[120,1280]{1,0:T(8,128)(2,1)}, u32[]{:S(2)}, u32[]{:S(2)}) collective-permute-start(bf16[120,1280]{1,0:T(8,128)(2,1)} %constant_dynamic-update-slice_fusion.8), channel_id=1, source_target_pairs={{0,1},{1,0},{2,3},{3,2},{4,5},{5,4},{6,7},{7,6},{8,9},{9,8},{10,11... | collective-permute-start | bytes 921608 | tf_op jit(solution)/shard_map/ppermute | solution.py:643
  19.7 68.0 %collective-permute-start.2 = (bf16[208,1280]{1,0:T(8,128)(2,1)}, bf16[208,1280]{1,0:T(8,128)(2,1)}, u32[]{:S(2)}, u32[]{:S(2)}) collective-permute-start(bf16[208,1280]{1,0:T(8,128)(2,1)} %fusion.3.refs_0_), channel_id=1, source_target_pairs={{0,3},{1,2},{2,1},{3,0},{4,7},{5,6},{6,5},{7,4},{8,11},{9,10},{10,... | collective-permute-start | bytes 1597448 | tf_op jit(solution)/shard_map/ppermute | solution.py:643
  39.5 57.8 %collective-permute-start.1 = (bf16[208,1280]{1,0:T(8,128)(2,1)}, bf16[208,1280]{1,0:T(8,128)(2,1)}, u32[]{:S(2)}, u32[]{:S(2)}) collective-permute-start(bf16[208,1280]{1,0:T(8,128)(2,1)} %fusion.3.refs_0_), channel_id=1, source_target_pairs={{0,2},{1,3},{2,0},{3,1},{4,6},{5,7},{6,4},{7,5},{8,10},{9,11},{10,... | collective-permute-start | bytes 1597448 | tf_op jit(solution)/shard_map/ppermute | solution.py:643
  44.1 43.7 %copy-start.2 = (bf16[368,1280]{1,0:T(8,128)(2,1)}, bf16[368,1280]{1,0:T(8,128)(2,1)S(1)}, u32[]{:S(2)}) copy-start(bf16[368,1280]{1,0:T(8,128)(2,1)S(1)} %pad.19.refs_0_.refs_9_.refs_11_) | copy-start | bytes 2826244
  69.7 28.1 %collective-permute-start = (bf16[208,1280]{1,0:T(8,128)(2,1)}, bf16[208,1280]{1,0:T(8,128)(2,1)S(1)}, u32[]{:S(2)}, u32[]{:S(2)}) collective-permute-start(bf16[208,1280]{1,0:T(8,128)(2,1)} %fusion.3.refs_0_), channel_id=1, source_target_pairs={{0,1},{1,0},{2,3},{3,2},{4,5},{5,4},{6,7},{7,6},{8,9},{9,8},{10,11... | collective-permute-start | bytes 1597448 | tf_op jit(solution)/shard_map/ppermute | solution.py:643
  75.6 29.5 %collective-permute-start.9 = (bf16[368,1280]{1,0:T(8,128)(2,1)S(1)}, bf16[368,1280]{1,0:T(8,128)(2,1)S(1)}, u32[]{:S(2)}, u32[]{:S(2)}) collective-permute-start(bf16[368,1280]{1,0:T(8,128)(2,1)S(1)} %pad.19.refs_0_.refs_9_.refs_11_), channel_id=1, source_target_pairs={{0,16},{4,20},{8,24},{12,28},{16,0},{20,4},{24,8},{28,12},{1,17},{... | collective-permute-start | bytes 2826248 | tf_op jit(solution)/shard_map/ppermute | solution.py:643
  76.1 24.3 %collective-permute-start.7 = (bf16[368,1280]{1,0:T(8,128)(2,1)S(1)}, bf16[368,1280]{1,0:T(8,128)(2,1)S(1)}, u32[]{:S(2)}, u32[]{:S(2)}) collective-permute-start(bf16[368,1280]{1,0:T(8,128)(2,1)S(1)} %pad.19.refs_0_.refs_9_.refs_11_), channel_id=1, source_target_pairs={{0,8},{4,12},{8,0},{12,4},{16,24},{20,28},{24,16},{28,20},{1,9},{5... | collective-permute-start | bytes 2826248 | tf_op jit(solution)/shard_map/ppermute | solution.py:643
  87.8 18.8 %collective-permute-start.6 = (bf16[368,1280]{1,0:T(8,128)(2,1)S(1)}, bf16[368,1280]{1,0:T(8,128)(2,1)}, u32[]{:S(2)}, u32[]{:S(2)}) collective-permute-start(bf16[368,1280]{1,0:T(8,128)(2,1)S(1)} %pad.19.refs_0_.refs_9_.refs_11_), channel_id=1, source_target_pairs={{0,4},{4,0},{8,12},{12,8},{16,20},{20,16},{24,28},{28,24},{1,5},{5... | collective-permute-start | bytes 2826248 | tf_op jit(solution)/shard_map/ppermute | solution.py:643
  97.3 28.2 %collective-permute-start.24 = (bf16[480,1280]{1,0:T(8,128)(2,1)}, bf16[480,1280]{1,0:T(8,128)(2,1)}, u32[]{:S(2)}, u32[]{:S(2)}) collective-permute-start(bf16[480,1280]{1,0:T(8,128)(2,1)} %slice_dynamic-update-slice_fusion.refs_7_), channel_id=1, source_target_pairs={{0,16},{4,20},{8,24},{12,28},{16,0},{20,4},{24,8},{28,12},{1,17},{... | collective-permute-start | bytes 3686408 | tf_op jit(solution)/shard_map/ppermute | solution.py:643
  97.8 30.3 %collective-permute-start.22 = (bf16[480,1280]{1,0:T(8,128)(2,1)}, bf16[480,1280]{1,0:T(8,128)(2,1)}, u32[]{:S(2)}, u32[]{:S(2)}) collective-permute-start(bf16[480,1280]{1,0:T(8,128)(2,1)} %slice_dynamic-update-slice_fusion.refs_7_), channel_id=1, source_target_pairs={{0,8},{4,12},{8,0},{12,4},{16,24},{20,28},{24,16},{28,20},{1,9},{5... | collective-permute-start | bytes 3686408 | tf_op jit(solution)/shard_map/ppermute | solution.py:643
  100.4 36.5 %collective-permute-start.8 = (bf16[368,1280]{1,0:T(8,128)(2,1)S(1)}, bf16[368,1280]{1,0:T(8,128)(2,1)}, u32[]{:S(2)}, u32[]{:S(2)}) collective-permute-start(bf16[368,1280]{1,0:T(8,128)(2,1)S(1)} %collective-permute-done.7.refs_2_.refs_11_.refs_13_), channel_id=1, source_target_pairs={{0,4},{4,0},{8,12},{12,8},{16,20},{20,16},{24,28},{28,24},{1,5},{5... | collective-permute-start | bytes 2826248 | tf_op jit(solution)/shard_map/ppermute | solution.py:643
  106.0 29.4 %collective-permute-start.11 = (bf16[176,1280]{1,0:T(8,128)(2,1)}, bf16[176,1280]{1,0:T(8,128)(2,1)}, u32[]{:S(2)}, u32[]{:S(2)}) collective-permute-start(bf16[176,1280]{1,0:T(8,128)(2,1)} %slice.420), channel_id=1, source_target_pairs={{0,8},{4,12},{8,0},{12,4},{16,24},{20,28},{24,16},{28,20},{1,9},{5... | collective-permute-start | bytes 1351688 | tf_op jit(solution)/shard_map/ppermute | solution.py:643
  106.5 32.2 %collective-permute-start.10 = (bf16[368,1280]{1,0:T(8,128)(2,1)S(1)}, bf16[368,1280]{1,0:T(8,128)(2,1)S(1)}, u32[]{:S(2)}, u32[]{:S(2)}) collective-permute-start(bf16[368,1280]{1,0:T(8,128)(2,1)S(1)} %collective-permute-done.9.refs_4_.refs_13_.refs_15_), channel_id=1, source_target_pairs={{0,4},{4,0},{8,12},{12,8},{16,20},{20,16},{24,28},{28,24},{1,5},{5... | collective-permute-start | bytes 2826248 | tf_op jit(solution)/shard_map/ppermute | solution.py:643
  110.4 34.6 %copy-start.30 = (pred[8]{0:T(512)(128)(4,1)S(1)}, pred[8]{0:T(512)(128)(4,1)}, u32[]{:S(2)}) copy-start(pred[8]{0:T(512)(128)(4,1)} %compare_and_fusion) | copy-start | bytes 28
  125.5 51.2 %collective-permute-start.21 = (bf16[480,1280]{1,0:T(8,128)(2,1)}, bf16[480,1280]{1,0:T(8,128)(2,1)}, u32[]{:S(2)}, u32[]{:S(2)}) collective-permute-start(bf16[480,1280]{1,0:T(8,128)(2,1)} %slice_dynamic-update-slice_fusion.refs_7_), channel_id=1, source_target_pairs={{0,4},{4,0},{8,12},{12,8},{16,20},{20,16},{24,28},{28,24},{1,5},{5... | collective-permute-start | bytes 3686408 | tf_op jit(solution)/shard_map/ppermute | solution.py:643
  128.1 13.9 %collective-permute-start.13 = (bf16[192,1280]{1,0:T(8,128)(2,1)S(1)}, bf16[192,1280]{1,0:T(8,128)(2,1)}, u32[]{:S(2)}, u32[]{:S(2)}) collective-permute-start(bf16[192,1280]{1,0:T(8,128)(2,1)S(1)} %slice.428), channel_id=1, source_target_pairs={{0,16},{4,20},{8,24},{12,28},{16,0},{20,4},{24,8},{28,12},{1,17},{... | collective-permute-start | bytes 1474568 | tf_op jit(solution)/shard_map/ppermute | solution.py:643
  135.4 44.0 %collective-permute-start.27 = (bf16[240,1280]{1,0:T(8,128)(2,1)}, bf16[240,1280]{1,0:T(8,128)(2,1)}, u32[]{:S(2)}, u32[]{:S(2)}) collective-permute-start(bf16[240,1280]{1,0:T(8,128)(2,1)} %slice.443), channel_id=1, source_target_pairs={{0,8},{4,12},{8,0},{12,4},{16,24},{20,28},{24,16},{28,20},{1,9},{5... | collective-permute-start | bytes 1843208 | tf_op jit(solution)/shard_map/ppermute | solution.py:643
  136.9 5.4 %collective-permute-start.12 = (bf16[176,1280]{1,0:T(8,128)(2,1)}, bf16[176,1280]{1,0:T(8,128)(2,1)S(1)}, u32[]{:S(2)}, u32[]{:S(2)}) collective-permute-start(bf16[176,1280]{1,0:T(8,128)(2,1)} %collective-permute-done.11.refs_7_.refs_16_.refs_18_), channel_id=1, source_target_pairs={{0,4},{4,0},{8,12},{12,8},{16,20},{20,16},{24,28},{28,24},{1,5},{5... | collective-permute-start | bytes 1351688 | tf_op jit(solution)/shard_map/ppermute | solution.py:643
  138.7 41.6 %collective-permute-start.26 = (bf16[240,1280]{1,0:T(8,128)(2,1)}, bf16[240,1280]{1,0:T(8,128)(2,1)}, u32[]{:S(2)}, u32[]{:S(2)}) collective-permute-start(bf16[240,1280]{1,0:T(8,128)(2,1)} %slice.442), channel_id=1, source_target_pairs={{0,16},{4,20},{8,24},{12,28},{16,0},{20,4},{24,8},{28,12},{1,17},{... | collective-permute-start | bytes 1843208 | tf_op jit(solution)/shard_map/ppermute | solution.py:643
  142.0 89.4 %collective-permute-start.25 = (bf16[480,1280]{1,0:T(8,128)(2,1)}, bf16[480,1280]{1,0:T(8,128)(2,1)}, u32[]{:S(2)}, u32[]{:S(2)}) collective-permute-start(bf16[480,1280]{1,0:T(8,128)(2,1)} %collective-permute-done.24.refs_11_), channel_id=1, source_target_pairs={{0,4},{4,0},{8,12},{12,8},{16,20},{20,16},{24,28},{28,24},{1,5},{5... | collective-permute-start | bytes 3686408 | tf_op jit(solution)/shard_map/ppermute | solution.py:643
  142.2 4.3 collective-permute-start.14
  146.6 84.9 %collective-permute-start.23 = (bf16[480,1280]{1,0:T(8,128)(2,1)}, bf16[480,1280]{1,0:T(8,128)(2,1)S(1)}, u32[]{:S(2)}, u32[]{:S(2)}) collective-permute-start(bf16[480,1280]{1,0:T(8,128)(2,1)} %collective-permute-done.22.refs_9_), channel_id=1, source_target_pairs={{0,4},{4,0},{8,12},{12,8},{16,20},{20,16},{24,28},{28,24},{1,5},{5... | collective-permute-start | bytes 3686408 | tf_op jit(solution)/shard_map/ppermute | solution.py:643
  176.7 26.1 %collective-permute-start.15 = (bf16[192,1408]{1,0:T(8,128)(2,1)}, bf16[192,1408]{1,0:T(8,128)(2,1)S(1)}, u32[]{:S(2)}, u32[]{:S(2)}) collective-permute-start(bf16[192,1408]{1,0:T(8,128)(2,1)} %get-tuple-element.54), channel_id=1, source_target_pairs={{0,1},{1,0},{2,3},{3,2},{4,5},{5,4},{6,7},{7,6},{8,9},{9,8},{10,11... | collective-permute-start | bytes 1622024 | tf_op jit(solution)/shard_map/ppermute | solution.py:643
  179.4 25.4 %collective-permute-start.16 = (bf16[192,1408]{1,0:T(8,128)(2,1)}, bf16[192,1408]{1,0:T(8,128)(2,1)S(1)}, u32[]{:S(2)}, u32[]{:S(2)}) collective-permute-start(bf16[192,1408]{1,0:T(8,128)(2,1)} %get-tuple-element.55), channel_id=1, source_target_pairs={{0,2},{1,3},{2,0},{3,1},{4,6},{5,7},{6,4},{7,5},{8,10},{9,11},{10,... | collective-permute-start | bytes 1622024 | tf_op jit(solution)/shard_map/ppermute | solution.py:643
  180.3 51.2 %collective-permute-start.29 = (bf16[240,1280]{1,0:T(8,128)(2,1)}, bf16[240,1280]{1,0:T(8,128)(2,1)S(1)}, u32[]{:S(2)}, u32[]{:S(2)}) collective-permute-start(bf16[240,1280]{1,0:T(8,128)(2,1)} %collective-permute-done.27.refs_14_), channel_id=1, source_target_pairs={{0,4},{4,0},{8,12},{12,8},{16,20},{20,16},{24,28},{28,24},{1,5},{5... | collective-permute-start | bytes 1843208 | tf_op jit(solution)/shard_map/ppermute | solution.py:643
  202.9 28.6 %collective-permute-start.28 = (bf16[240,1280]{1,0:T(8,128)(2,1)}, bf16[240,1280]{1,0:T(8,128)(2,1)}, u32[]{:S(2)}, u32[]{:S(2)}) collective-permute-start(bf16[240,1280]{1,0:T(8,128)(2,1)} %collective-permute-done.26.refs_13_), channel_id=1, source_target_pairs={{0,4},{4,0},{8,12},{12,8},{16,20},{20,16},{24,28},{28,24},{1,5},{5... | collective-permute-start | bytes 1843208 | tf_op jit(solution)/shard_map/ppermute | solution.py:643
  205.6 25.8 %collective-permute-start.17 = (bf16[192,1408]{1,0:T(8,128)(2,1)}, bf16[192,1408]{1,0:T(8,128)(2,1)}, u32[]{:S(2)}, u32[]{:S(2)}) collective-permute-start(bf16[192,1408]{1,0:T(8,128)(2,1)} %get-tuple-element.56), channel_id=1, source_target_pairs={{0,3},{1,2},{2,1},{3,0},{4,7},{5,6},{6,5},{7,4},{8,11},{9,10},{10,... | collective-permute-start | bytes 1622024 | tf_op jit(solution)/shard_map/ppermute | solution.py:643
  244.7 27.7 %collective-permute-start.32 = (bf16[192,1408]{1,0:T(8,128)(2,1)}, bf16[192,1408]{1,0:T(8,128)(2,1)S(1)}, u32[]{:S(2)}, u32[]{:S(2)}) collective-permute-start(bf16[192,1408]{1,0:T(8,128)(2,1)} %get-tuple-element.59.refs_0_), channel_id=1, source_target_pairs={{0,3},{1,2},{2,1},{3,0},{4,7},{5,6},{6,5},{7,4},{8,11},{9,10},{10,... | collective-permute-start | bytes 1622024 | tf_op jit(solution)/shard_map/ppermute | solution.py:643
  245.4 38.3 %collective-permute-start.31 = (bf16[192,1408]{1,0:T(8,128)(2,1)}, bf16[192,1408]{1,0:T(8,128)(2,1)S(1)}, u32[]{:S(2)}, u32[]{:S(2)}) collective-permute-start(bf16[192,1408]{1,0:T(8,128)(2,1)} %get-tuple-element.59.refs_0_), channel_id=1, source_target_pairs={{0,2},{1,3},{2,0},{3,1},{4,6},{5,7},{6,4},{7,5},{8,10},{9,11},{10,... | collective-permute-start | bytes 1622024 | tf_op jit(solution)/shard_map/ppermute | solution.py:643
  245.4 38.3 %collective-permute-start.30 = (bf16[192,1408]{1,0:T(8,128)(2,1)}, bf16[192,1408]{1,0:T(8,128)(2,1)}, u32[]{:S(2)}, u32[]{:S(2)}) collective-permute-start(bf16[192,1408]{1,0:T(8,128)(2,1)} %get-tuple-element.59.refs_0_), channel_id=1, source_target_pairs={{0,1},{1,0},{2,3},{3,2},{4,5},{5,4},{6,7},{7,6},{8,9},{9,8},{10,11... | collective-permute-start | bytes 1622024 | tf_op jit(solution)/shard_map/ppermute | solution.py:643
  258.1 130.2 %collective-permute-start.48 = (bf16[480,1280]{1,0:T(8,128)(2,1)}, bf16[480,1280]{1,0:T(8,128)(2,1)S(1)}, u32[]{:S(2)}, u32[]{:S(2)}) collective-permute-start(bf16[480,1280]{1,0:T(8,128)(2,1)} %get-tuple-element.85), channel_id=1, source_target_pairs={{0,4},{4,0},{8,12},{12,8},{16,20},{20,16},{24,28},{28,24},{1,5},{5... | collective-permute-start | bytes 3686408 | tf_op jit(solution)/shard_map/ppermute | solution.py:643
  258.1 124.3 %collective-permute-start.49 = (bf16[480,1280]{1,0:T(8,128)(2,1)}, bf16[480,1280]{1,0:T(8,128)(2,1)S(1)}, u32[]{:S(2)}, u32[]{:S(2)}) collective-permute-start(bf16[480,1280]{1,0:T(8,128)(2,1)} %get-tuple-element.87), channel_id=1, source_target_pairs={{0,4},{4,0},{8,12},{12,8},{16,20},{20,16},{24,28},{28,24},{1,5},{5... | collective-permute-start | bytes 3686408 | tf_op jit(solution)/shard_map/ppermute | solution.py:643
  333.5 22.7 %collective-permute-start.33 = (bf16[192,1280]{1,0:T(8,128)(2,1)}, bf16[192,1280]{1,0:T(8,128)(2,1)S(1)}, u32[]{:S(2)}, u32[]{:S(2)}) collective-permute-start(bf16[192,1280]{1,0:T(8,128)(2,1)} %get-tuple-element.64), channel_id=1, source_target_pairs={{0,1},{1,0},{2,3},{3,2},{4,5},{5,4},{6,7},{7,6},{8,9},{9,8},{10,11... | collective-permute-start | bytes 1474568 | tf_op jit(solution)/shard_map/ppermute | solution.py:643
  335.3 34.7 %collective-permute-start.34 = (bf16[192,1280]{1,0:T(8,128)(2,1)}, bf16[192,1280]{1,0:T(8,128)(2,1)}, u32[]{:S(2)}, u32[]{:S(2)}) collective-permute-start(bf16[192,1280]{1,0:T(8,128)(2,1)} %get-tuple-element.65), channel_id=1, source_target_pairs={{0,2},{1,3},{2,0},{3,1},{4,6},{5,7},{6,4},{7,5},{8,10},{9,11},{10,... | collective-permute-start | bytes 1474568 | tf_op jit(solution)/shard_map/ppermute | solution.py:643
  336.9 43.6 %collective-permute-start.35 = (bf16[192,1280]{1,0:T(8,128)(2,1)}, bf16[192,1280]{1,0:T(8,128)(2,1)}, u32[]{:S(2)}, u32[]{:S(2)}) collective-permute-start(bf16[192,1280]{1,0:T(8,128)(2,1)} %get-tuple-element.66), channel_id=1, source_target_pairs={{0,3},{1,2},{2,1},{3,0},{4,7},{5,6},{6,5},{7,4},{8,11},{9,10},{10,... | collective-permute-start | bytes 1474568 | tf_op jit(solution)/shard_map/ppermute | solution.py:643
  337.4 43.1 %copy-start.18 = (bf16[192,1280]{1,0:T(8,128)(2,1)S(1)}, bf16[192,1280]{1,0:T(8,128)(2,1)}, u32[]{:S(2)}) copy-start(bf16[192,1280]{1,0:T(8,128)(2,1)} %get-tuple-element.63) | copy-start | bytes 1474564
  356.2 60.9 %collective-permute-start.52 = (bf16[480,1280]{1,0:T(8,128)(2,1)}, bf16[480,1280]{1,0:T(8,128)(2,1)S(1)}, u32[]{:S(2)}, u32[]{:S(2)}) collective-permute-start(bf16[480,1280]{1,0:T(8,128)(2,1)} %get-tuple-element.89), channel_id=1, source_target_pairs={{0,4},{4,0},{8,12},{12,8},{16,20},{20,16},{24,28},{28,24},{1,5},{5... | collective-permute-start | bytes 3686408 | tf_op jit(solution)/shard_map/ppermute | solution.py:643
  370.0 50.0 %collective-permute-start.36 = (bf16[352,1280]{1,0:T(8,128)(2,1)}, bf16[352,1280]{1,0:T(8,128)(2,1)S(1)}, u32[]{:S(2)}, u32[]{:S(2)}) collective-permute-start(bf16[352,1280]{1,0:T(8,128)(2,1)} %get-tuple-element.70), channel_id=1, source_target_pairs={{0,4},{4,0},{8,12},{12,8},{16,20},{20,16},{24,28},{28,24},{1,5},{5... | collective-permute-start | bytes 2703368 | tf_op jit(solution)/shard_map/ppermute | solution.py:643
  380.5 2.8 collective-permute-start.38
  382.5 4.6 collective-permute-start.37
  384.2 2.4 collective-permute-start.41
  386.6 16.7 %collective-permute-start.50 = (bf16[240,1280]{1,0:T(8,128)(2,1)S(1)}, bf16[240,1280]{1,0:T(8,128)(2,1)S(1)}, u32[]{:S(2)}, u32[]{:S(2)}) collective-permute-start(bf16[240,1280]{1,0:T(8,128)(2,1)S(1)} %get-tuple-element.103), channel_id=1, source_target_pairs={{0,16},{4,20},{8,24},{12,28},{16,0},{20,4},{24,8},{28,12},{1,17},{... | collective-permute-start | bytes 1843208 | tf_op jit(solution)/shard_map/ppermute | solution.py:643
  387.0 31.2 %collective-permute-start.53 = (bf16[240,1280]{1,0:T(8,128)(2,1)S(1)}, bf16[240,1280]{1,0:T(8,128)(2,1)S(1)}, u32[]{:S(2)}, u32[]{:S(2)}) collective-permute-start(bf16[240,1280]{1,0:T(8,128)(2,1)S(1)} %get-tuple-element.104), channel_id=1, source_target_pairs={{0,8},{4,12},{8,0},{12,4},{16,24},{20,28},{24,16},{28,20},{1,9},{5... | collective-permute-start | bytes 1843208 | tf_op jit(solution)/shard_map/ppermute | solution.py:643
  388.3 23.0 %collective-permute-start.39 = (bf16[160,1280]{1,0:T(8,128)(2,1)S(1)}, bf16[160,1280]{1,0:T(8,128)(2,1)S(1)}, u32[]{:S(2)}, u32[]{:S(2)}) collective-permute-start(bf16[160,1280]{1,0:T(8,128)(2,1)S(1)} %add_convert_fusion.13), channel_id=1, source_target_pairs={{0,16},{4,20},{8,24},{12,28},{16,0},{20,4},{24,8},{28,12},{1,17},{... | collective-permute-start | bytes 1228808 | tf_op jit(solution)/shard_map/ppermute | solution.py:643
  403.3 13.0 %collective-permute-start.42 = (bf16[192,1280]{1,0:T(8,128)(2,1)S(1)}, bf16[192,1280]{1,0:T(8,128)(2,1)S(1)}, u32[]{:S(2)}, u32[]{:S(2)}) collective-permute-start(bf16[192,1280]{1,0:T(8,128)(2,1)S(1)} %add_convert_fusion.9), channel_id=1, source_target_pairs={{0,8},{4,12},{8,0},{12,4},{16,24},{20,28},{24,16},{28,20},{1,9},{5... | collective-permute-start | bytes 1474568 | tf_op jit(solution)/shard_map/ppermute | solution.py:643
  411.5 24.1 %collective-permute-start.40 = (bf16[352,1280]{1,0:T(8,128)(2,1)S(1)}, bf16[352,1280]{1,0:T(8,128)(2,1)S(1)}, u32[]{:S(2)}, u32[]{:S(2)}) collective-permute-start(bf16[352,1280]{1,0:T(8,128)(2,1)S(1)} %pad_maximum_fusion.2), channel_id=1, source_target_pairs={{0,8},{4,12},{8,0},{12,4},{16,24},{20,28},{24,16},{28,20},{1,9},{5... | collective-permute-start | bytes 2703368 | tf_op jit(solution)/shard_map/ppermute | solution.py:643
  416.6 23.0 %collective-permute-start.43 = (bf16[352,1280]{1,0:T(8,128)(2,1)S(1)}, bf16[352,1280]{1,0:T(8,128)(2,1)S(1)}, u32[]{:S(2)}, u32[]{:S(2)}) collective-permute-start(bf16[352,1280]{1,0:T(8,128)(2,1)S(1)} %pad_maximum_fusion.3), channel_id=1, source_target_pairs={{0,16},{4,20},{8,24},{12,28},{16,0},{20,4},{24,8},{28,12},{1,17},{... | collective-permute-start | bytes 2703368 | tf_op jit(solution)/shard_map/ppermute | solution.py:643
  418.3 42.0 %collective-permute-start.47 = (bf16[480,1280]{1,0:T(8,128)(2,1)S(1)}, bf16[480,1280]{1,0:T(8,128)(2,1)S(1)}, u32[]{:S(2)}, u32[]{:S(2)}) collective-permute-start(bf16[480,1280]{1,0:T(8,128)(2,1)S(1)} %copy-done.33), channel_id=1, source_target_pairs={{0,4},{4,0},{8,12},{12,8},{16,20},{20,16},{24,28},{28,24},{1,5},{5... | collective-permute-start | bytes 3686408 | tf_op jit(solution)/shard_map/ppermute | solution.py:643
  418.3 42.3 %collective-permute-start.51 = (bf16[480,1280]{1,0:T(8,128)(2,1)S(1)}, bf16[480,1280]{1,0:T(8,128)(2,1)S(1)}, u32[]{:S(2)}, u32[]{:S(2)}) collective-permute-start(bf16[480,1280]{1,0:T(8,128)(2,1)S(1)} %pad_maximum_fusion), channel_id=1, source_target_pairs={{0,8},{4,12},{8,0},{12,4},{16,24},{20,28},{24,16},{28,20},{1,9},{5... | collective-permute-start | bytes 3686408 | tf_op jit(solution)/shard_map/ppermute | solution.py:643
  420.0 41.2 %collective-permute-start.54 = (bf16[480,1280]{1,0:T(8,128)(2,1)S(1)}, bf16[480,1280]{1,0:T(8,128)(2,1)S(1)}, u32[]{:S(2)}, u32[]{:S(2)}) collective-permute-start(bf16[480,1280]{1,0:T(8,128)(2,1)S(1)} %pad_maximum_fusion.1), channel_id=1, source_target_pairs={{0,16},{4,20},{8,24},{12,28},{16,0},{20,4},{24,8},{28,12},{1,17},{... | collective-permute-start | bytes 3686408 | tf_op jit(solution)/shard_map/ppermute | solution.py:643
  440.3 8.8 %collective-permute-start.45 = (bf16[88,1280]{1,0:T(8,128)(2,1)S(1)}, bf16[88,1280]{1,0:T(8,128)(2,1)S(1)}, u32[]{:S(2)}, u32[]{:S(2)}) collective-permute-start(bf16[88,1280]{1,0:T(8,128)(2,1)S(1)} %pad_maximum_fusion.8), channel_id=1, source_target_pairs={{0,2},{1,3},{2,0},{3,1},{4,6},{5,7},{6,4},{7,5},{8,10},{9,11},{10,... | collective-permute-start | bytes 675848 | tf_op jit(solution)/shard_map/ppermute | solution.py:643
  440.4 15.4 %collective-permute-start.46 = (bf16[88,1280]{1,0:T(8,128)(2,1)S(1)}, bf16[88,1280]{1,0:T(8,128)(2,1)S(1)}, u32[]{:S(2)}, u32[]{:S(2)}) collective-permute-start(bf16[88,1280]{1,0:T(8,128)(2,1)S(1)} %pad_maximum_fusion.9), channel_id=1, source_target_pairs={{0,3},{1,2},{2,1},{3,0},{4,7},{5,6},{6,5},{7,4},{8,11},{9,10},{10,... | collective-permute-start | bytes 675848 | tf_op jit(solution)/shard_map/ppermute | solution.py:643
  449.1 9.4 %collective-permute-start.44 = (bf16[88,1280]{1,0:T(8,128)(2,1)S(1)}, bf16[88,1280]{1,0:T(8,128)(2,1)S(1)}, u32[]{:S(2)}, u32[]{:S(2)}) collective-permute-start(bf16[88,1280]{1,0:T(8,128)(2,1)S(1)} %pad_maximum_fusion.7), channel_id=1, source_target_pairs={{0,1},{1,0},{2,3},{3,2},{4,5},{5,4},{6,7},{7,6},{8,9},{9,8},{10,11... | collective-permute-start | bytes 675848 | tf_op jit(solution)/shard_map/ppermute | solution.py:643
  462.0 20.8 %collective-permute-start.56 = (bf16[120,1280]{1,0:T(8,128)(2,1)S(1)}, bf16[120,1280]{1,0:T(8,128)(2,1)S(1)}, u32[]{:S(2)}, u32[]{:S(2)}) collective-permute-start(bf16[120,1280]{1,0:T(8,128)(2,1)S(1)} %pad_maximum_fusion.5), channel_id=1, source_target_pairs={{0,2},{1,3},{2,0},{3,1},{4,6},{5,7},{6,4},{7,5},{8,10},{9,11},{10,... | collective-permute-start | bytes 921608 | tf_op jit(solution)/shard_map/ppermute | solution.py:643
  462.1 26.9 %collective-permute-start.57 = (bf16[120,1280]{1,0:T(8,128)(2,1)S(1)}, bf16[120,1280]{1,0:T(8,128)(2,1)S(1)}, u32[]{:S(2)}, u32[]{:S(2)}) collective-permute-start(bf16[120,1280]{1,0:T(8,128)(2,1)S(1)} %pad_maximum_fusion.6), channel_id=1, source_target_pairs={{0,3},{1,2},{2,1},{3,0},{4,7},{5,6},{6,5},{7,4},{8,11},{9,10},{10,... | collective-permute-start | bytes 921608 | tf_op jit(solution)/shard_map/ppermute | solution.py:643
  464.8 24.2 %collective-permute-start.55 = (bf16[120,1280]{1,0:T(8,128)(2,1)S(1)}, bf16[120,1280]{1,0:T(8,128)(2,1)S(1)}, u32[]{:S(2)}, u32[]{:S(2)}) collective-permute-start(bf16[120,1280]{1,0:T(8,128)(2,1)S(1)} %pad_maximum_fusion.4), channel_id=1, source_target_pairs={{0,1},{1,0},{2,3},{3,2},{4,5},{5,4},{6,7},{7,6},{8,9},{9,8},{10,11... | collective-permute-start | bytes 921608 | tf_op jit(solution)/shard_map/ppermute | solution.py:643
  (37 other events, 345.5 us)

commit v2 on v1

v2 whole, which is shorter than its diff:
```python
import functools
import math

import jax
import jax.numpy as jnp
from jax import lax
from jax.experimental import pallas as pl
from jax.experimental.pallas import tpu as pltpu
from jax.sharding import PartitionSpec as P

HEADS = 8
HEAD_DIM = 160
EPSILON = 1e-05
NEG_FILL = -1e30
LANES = 128
WINDOW = 256
BF = jnp.bfloat16
F32 = jnp.float32
GAIN_ROWS = 16
SMALL = pl.CostEstimate(flops=1, bytes_accessed=1, transcendentals=0)


def head_window(head):
    start = head * HEAD_DIM // LANES * LANES
    return start, head * HEAD_DIM - start


def head_lanes(head):
    _, shift = head_window(head)
    lane = lax.broadcasted_iota(jnp.int32, (1, WINDOW), 1)
    return (lane >= shift) & (lane < shift + HEAD_DIM)


def dot(a, b, dims=((1,), (0,))):
    return lax.dot_general(a, b, (dims, ((), ())), preferred_element_type=F32)


def standardize(values):
    centered = values - jnp.mean(values, axis=-1, keepdims=True)
    scale = lax.rsqrt(jnp.mean(centered * centered, axis=-1, keepdims=True) + EPSILON)
    return centered * scale, scale


def norm_pull(upstream, gain, xhat, scale):
    scaled = upstream * gain
    return scale * (
        scaled
        - jnp.mean(scaled, axis=-1, keepdims=True)
        - xhat * jnp.mean(scaled * xhat, axis=-1, keepdims=True)
    )


def split_three(values):
    first = values.astype(BF).astype(F32)
    rest = values - first
    second = rest.astype(BF).astype(F32)
    return first, second, rest - second


def gelu(values):
    inner = math.sqrt(2 / math.pi) * (values + 0.044715 * values * values * values)
    return 0.5 * values * (1.0 + jnp.tanh(inner))


def gelu_slope(values):
    square = values * values
    tanh = jnp.tanh(math.sqrt(2 / math.pi) * (values + 0.044715 * square * values))
    slope = math.sqrt(2 / math.pi) * (1.0 + 3 * 0.044715 * square)
    return 0.5 * (1.0 + tanh) + 0.5 * values * (1.0 - tanh * tanh) * slope


def piece_copies(pieces, flat_refs, first, rows, target, me, sems, base):
    copies = []
    lanes = target.shape[1]
    at = 0
    for distance, parts in pieces:
        owner = jnp.bitwise_xor(me, distance)
        for low, high in parts:
            ref = flat_refs[at]
            at += 1
            start, stop = max(low, first), min(high, first + rows)
            if start < stop:
                place = pl.multiple_of(owner * rows + (start - first), 16)
                copies.append(
                    pltpu.make_async_copy(
                        ref.at[pl.ds(start - low, stop - start), pl.ds(0, lanes)],
                        target.at[pl.ds(place, stop - start), :],
                        sems.at[base + len(copies)],
                    )
                )
    return copies


def group_values(refs, place):
    if len(refs) != 5:
        return [ref[...] for ref in refs]
    own = place[1]
    at_end = (own == 0) | (own == 3)
    values = [ref[...] for ref in refs[:3]]
    return values + [jnp.where(at_end, refs[4][...], refs[3][...])]


def gain_vector(held, size, lane_at, shards):
    per_shard = size // shards
    blocks = held.shape[0] // GAIN_ROWS
    per_block = shards // blocks
    lane = lax.broadcasted_iota(jnp.int32, (LANES, size), 0)
    column = lax.broadcasted_iota(jnp.int32, (LANES, size), 1)
    pick = (lane == lane_at + column % per_shard).astype(F32).astype(BF)
    spread = dot(held[...], pick)
    row = lax.broadcasted_iota(jnp.int32, spread.shape, 0)
    column = lax.broadcasted_iota(jnp.int32, spread.shape, 1) // per_shard
    owner = (row // GAIN_ROWS) * per_block + row % GAIN_ROWS
    right = (owner == column) & (row % GAIN_ROWS < per_block)
    return jnp.sum(jnp.where(right, spread, 0.0), axis=0, keepdims=True)


def params(grid_rank, mebibytes=60):
    return pltpu.CompilerParams(
        dimension_semantics=("arbitrary",) * grid_rank, vmem_limit_bytes=mebibytes << 20
    )


def whole_spec():
    return pl.BlockSpec(memory_space=pltpu.VMEM)


def any_spec():
    return pl.BlockSpec(memory_space=pltpu.HBM)


class Held:
    def __init__(self, pieces, flat, spans):
        self.pieces, self.flat, self.spans = pieces, flat, spans

    def crossed(self):
        at = 0
        for distance, parts in self.pieces:
            if distance == self.blocks - 2:
                return self.flat[at : at + len(parts)]
            at += len(parts)

    def copies(self, names, refs, targets, place, sems):
        found, base = [], 0
        for name, target in zip(names, targets):
            first, rows = self.spans[name]
            some = piece_copies(self.pieces, refs, first, rows, target, place[0], sems, base)
            base += len(some)
            found.append(some)
        return found


def run_all(groups, action):
    for group in groups:
        for copy in group:
            getattr(copy, action)()


def shape(dims, dtype=BF):
    return jax.ShapeDtypeStruct(dims, dtype)


def full_block(dims):
    return pl.BlockSpec(
        dims, lambda i, p: (0,) * len(dims), pipeline_mode=pl.Buffered(buffer_count=1)
    )


def scalar_spec():
    return pl.BlockSpec(memory_space=pltpu.SMEM)


def assemble_call(place, parts, segments, total, size):
    def kernel(place_ref, *refs):
        part_refs, out_ref, acc = refs[: len(parts)], refs[len(parts)], refs[len(parts) + 1]
        values = [v.astype(F32) for v in group_values(part_refs, place_ref)]
        end = max(at + size * rows for _, rows, at in segments)
        if end < total:
            first = end // 8 * 8
            acc[first:, :] = jnp.zeros((total - first, acc.shape[1]), F32)
        for index in range(size):
            want = jnp.bitwise_xor(place_ref[1], index)
            value = values[size - 1]
            for distance in range(size - 2, -1, -1):
                value = jnp.where(want == distance, values[distance], value)
            for first, rows, at in segments:
                acc[at + index * rows : at + (index + 1) * rows, :] = value[first : first + rows]
        out_ref[...] = acc[...].astype(BF)

    lat = parts[0].shape[1]
    return pl.pallas_call(
        kernel,
        in_specs=[scalar_spec()] + [whole_spec()] * len(parts),
        out_specs=whole_spec(),
        out_shape=shape((total, lat)),
        scratch_shapes=[pltpu.VMEM((total, lat), F32)],
        compiler_params=params(0, 24),
        cost_estimate=SMALL,
        name="assemble",
    )(place, *parts)


def key_value_call(place, bytes_flat, held, rows):
    tokens, width = bytes_flat.shape
    block = tokens // rows
    lat = held.flat[0].shape[1]
    count = len(held.flat)
    shards = place_shards(held)

    def kernel(place_ref, x_ref, *refs):
        piece_refs = refs[:count]
        normed_t_ref, key_ref, value_ref, wk, wv, gains, gain, sems = refs[count:]
        first = pl.program_id(0) == 0

        def loads():
            return held.copies(
                ("gains", "key", "value"), piece_refs, (gains, wk, wv), place_ref, sems
            )

        @pl.when(first)
        def _():
            run_all(loads(), "start")

        xhat, _ = standardize(x_ref[...].astype(F32))

        @pl.when(first)
        def _():
            run_all(loads(), "wait")
            gain[...] = gain_vector(gains, width, held.lanes["byte"], shards)

        normed = (xhat * gain[...]).astype(BF)
        key_ref[...] = dot(normed, wk[...]).astype(BF)
        value_ref[...] = dot(normed, wv[...]).astype(BF)
        normed_t_ref[...] = jnp.transpose(normed, (1, 0))

    row_block = lambda i, p: (i, 0)
    return pl.pallas_call(
        kernel,
        grid_spec=pltpu.PrefetchScalarGridSpec(
            num_scalar_prefetch=1,
            grid=(rows,),
            in_specs=[pl.BlockSpec((block, width), row_block)] + [any_spec()] * count,
            out_specs=[
                pl.BlockSpec((width, block), lambda i, p: (0, i)),
                pl.BlockSpec((block, lat), row_block),
                pl.BlockSpec((block, lat), row_block),
            ],
            scratch_shapes=[
                pltpu.VMEM((width, lat), BF),
                pltpu.VMEM((width, lat), BF),
                pltpu.VMEM((held.blocks * GAIN_ROWS, LANES), BF),
                pltpu.VMEM((1, width), F32),
                pltpu.SemaphoreType.DMA((6 * count,)),
            ],
        ),
        out_shape=[shape((width, tokens)), shape((tokens, lat)), shape((tokens, lat))],
        compiler_params=params(1),
        cost_estimate=SMALL,
        name="keys_values",
    )(place, bytes_flat, *held.flat)


def place_shards(held):
    return held.blocks * held.size


def attend_call(place, latent_parts, byte_ids, keys, values, held, groups, group, first, rows):
    parts = len(latent_parts)
    lat = keys.shape[1]
    block = byte_ids.shape[2]
    latents = groups * group
    count = len(held.flat)
    shards = place_shards(held)
    score_scale = 1.0 / math.sqrt(HEAD_DIM)

    def kernel(place_ref, *refs):
        part_refs = refs[:parts]
        bid_ref, key_ref, value_ref = refs[parts : parts + 3]
        piece_refs = refs[parts + 3 : parts + 3 + count]
        rest = refs[parts + 3 + count :]
        normed_t_ref, query_ref = rest[:2]
        out_refs = rest[2 : 2 + groups]
        wq, gains, gain, acc, sems = rest[2 + groups :]
        start = pl.program_id(0) == 0

        def loads():
            return held.copies(("gains", "query"), piece_refs, (gains, wq), place_ref, sems)

        @pl.when(start)
        def _():
            run_all(loads(), "start")

        message = jnp.concatenate(group_values(part_refs, place_ref), axis=0)
        ids = message[:, lat : lat + 1].astype(F32)
        xhat, _ = standardize(message[:, :lat].astype(F32))

        @pl.when(start)
        def _():
            run_all(loads(), "wait")
            gain[...] = gain_vector(gains, lat, held.lanes["latent"], shards)

        normed = (xhat * gain[...]).astype(BF)
        query_ref[...] = dot(normed, wq[...]).astype(BF)
        normed_t_ref[...] = jnp.transpose(normed, (1, 0))
        allowed = ids == bid_ref[0]
        lane = lax.broadcasted_iota(jnp.int32, (latents, LANES), 1)
        stats = jnp.zeros((latents, LANES), F32)
        for head in range(HEADS):
            at, _ = head_window(head)
            mask = head_lanes(head)
            window = slice(at, at + WINDOW)
            query = jnp.where(mask, query_ref[:, window], jnp.zeros((), BF))
            scores = dot(query, key_ref[:, window], ((1,), (1,))) * score_scale
            scores = jnp.where(allowed, scores, NEG_FILL)
            top = jnp.max(scores, axis=-1, keepdims=True)
            exponent = jnp.exp(scores - top)
            total = jnp.sum(exponent, axis=-1, keepdims=True)
            found = dot(exponent.astype(BF), value_ref[:, window]) / total
            if head == 0:
                acc[:, window] = found
            else:
                acc[:, window] = jnp.where(mask, found, acc[:, window])
            log_total = jnp.where(top > -1e29, top + jnp.log(total), NEG_FILL)
            for index, term in enumerate(split_three(log_total)):
                stats = jnp.where(lane == index * HEADS + head, term, stats)
        for index, ref in enumerate(out_refs):
            chunk = slice(index * group, (index + 1) * group)
            ref[:, :lat] = acc[chunk, :].astype(BF)
            ref[:, lat:] = stats[chunk, :].astype(BF)

    row_block = lambda i, p: (first + i, 0)
    own_block = lambda i, p: (i, 0)
    return pl.pallas_call(
        kernel,
        grid_spec=pltpu.PrefetchScalarGridSpec(
            num_scalar_prefetch=1,
            grid=(rows,),
            in_specs=[pl.BlockSpec((group, lat + LANES), row_block)] * parts
            + [
                pl.BlockSpec((1, 1, block), lambda i, p: (first + i, 0, 0)),
                pl.BlockSpec((block, lat), row_block),
                pl.BlockSpec((block, lat), row_block),
            ]
            + [any_spec()] * count,
            out_specs=[
                pl.BlockSpec((lat, latents), lambda i, p: (0, i)),
                pl.BlockSpec((latents, lat), own_block),
            ]
            + [pl.BlockSpec((group, lat + LANES), own_block)] * groups,
            scratch_shapes=[
                pltpu.VMEM((lat, lat), BF),
                pltpu.VMEM((held.blocks * GAIN_ROWS, LANES), BF),
                pltpu.VMEM((1, lat), F32),
                pltpu.VMEM((latents, lat), F32),
                pltpu.SemaphoreType.DMA((4 * count,)),
            ],
        ),
        out_shape=[shape((lat, rows * latents)), shape((rows * latents, lat))]
        + [shape((rows * group, lat + LANES))] * groups,
        compiler_params=params(1),
        cost_estimate=SMALL,
        name="attend",
    )(place, *latent_parts, byte_ids, keys, values, *held.flat)


def feed_call(place, parts, latent_message, cot_flat, held_gain, held, cuts):
    groups, pieces_of = len(parts), len(parts[0])
    tokens, lat = cot_flat.shape
    count, gain_count = len(held.flat), len(held_gain.flat)
    shards = place_shards(held_gain)

    def kernel(place_ref, *refs):
        refs = list(refs)
        take = lambda n: [refs.pop(0) for _ in range(n)]
        part_refs = [take(pieces_of) for _ in range(groups)]
        x_ref, cot_ref = take(2)
        gain_refs, piece_refs = take(gain_count), take(count)
        new_ref, mixed_grad_ref = take(2)
        message_refs = take(len(cuts))
        attended_t, branch, normed_t, inner, act_t = take(5)
        wo, w1, w2, gains, sems, gain_sems = refs
        gain_loads = held_gain.copies(("gains",), gain_refs, (gains,), place_ref, gain_sems)
        loads = held.copies(("out", "inner", "outer"), piece_refs, (wo, w1, w2), place_ref, sems)
        run_all(gain_loads, "start")
        run_all(loads, "start")

        lane = lax.broadcasted_iota(jnp.int32, (LANES, lat), 0)
        column = lax.broadcasted_iota(jnp.int32, (LANES, lat), 1)
        spread = jnp.zeros((LANES, lat), jnp.bool_)
        for head in range(HEADS):
            inside = (column >= head * HEAD_DIM) & (column < (head + 1) * HEAD_DIM)
            own = (lane == head) | (lane == HEADS + head) | (lane == 2 * HEADS + head)
            spread = spread | (inside & own)
        spread = spread.astype(F32).astype(BF)
        found = [jnp.concatenate([ref[...] for ref in some], axis=0) for some in part_refs]
        logs = [dot(value[:, lat:], spread) for value in found]
        top = functools.reduce(jnp.maximum, logs)
        shares = [jnp.exp(log - top) for log in logs]
        total = functools.reduce(jnp.add, shares)
        summed = functools.reduce(
            jnp.add, [s * value[:, :lat].astype(F32) for s, value in zip(shares, found)]
        )
        attended = (summed / total).astype(BF)
        log_total = top + jnp.log(total)
        attended_t[...] = jnp.transpose(attended, (1, 0))

        run_all(gain_loads, "wait")
        gain = gain_vector(gains, lat, held_gain.lanes["mlp"], shards)
        run_all(loads[:1], "wait")
        mixed = x_ref[:, :lat].astype(F32) + dot(attended, wo[...])
        xhat, scale = standardize(mixed)
        normed = (xhat * gain).astype(BF)
        normed_t[...] = jnp.transpose(normed, (1, 0))
        run_all(loads[1:2], "wait")
        hidden = dot(normed, w1[...])
        activated = gelu(hidden).astype(BF)
        act_t[...] = jnp.transpose(activated, (1, 0))
        run_all(loads[2:], "wait")
        new_ref[...] = (mixed + dot(activated, w2[...])).astype(BF)
        cot = cot_ref[...]
        grad_hidden = (dot(cot, w2[...], ((1,), (1,))) * gelu_slope(hidden)).astype(BF)
        inner[...] = grad_hidden
        upstream = dot(grad_hidden, w1[...], ((1,), (1,)))
        grad_mixed = cot.astype(F32) + norm_pull(upstream, gain, xhat, scale)
        mixed_grad_ref[...] = grad_mixed
        grad_branch = grad_mixed.astype(BF)
        branch[...] = grad_branch
        grad_attended = dot(grad_branch, wo[...], ((1,), (1,))).astype(BF)
        product = grad_attended.astype(F32) * attended.astype(F32)
        out_lane = lax.broadcasted_iota(jnp.int32, (tokens, LANES), 1)
        ids = x_ref[:, lat : lat + 1].astype(F32)
        stats = jnp.where(out_lane == 6 * HEADS, ids, 0.0)
        for head in range(HEADS):
            at, shift = head_window(head)
            mask = head_lanes(head)
            inner_sum = jnp.sum(
                jnp.where(mask, product[:, at : at + WINDOW], 0.0), axis=-1, keepdims=True
            )
            first_lane = at + shift
            log_column = log_total[:, first_lane : first_lane + 1]
            terms = split_three(log_column) + split_three(inner_sum)
            for index, term in enumerate(terms):
                stats = jnp.where(out_lane == index * HEADS + head, term, stats)
        stats = stats.astype(BF)
        for (first, some), ref in zip(cuts, message_refs):
            ref[:, :lat] = grad_attended[first : first + some]
            ref[:, lat:] = stats[first : first + some]

    flat_parts = [array for some in parts for array in some]
    return pl.pallas_call(
        kernel,
        in_specs=[scalar_spec()]
        + [whole_spec()] * (len(flat_parts) + 2)
        + [any_spec()] * (gain_count + count),
        out_specs=[whole_spec()] * (7 + len(cuts)),
        out_shape=[shape((tokens, lat)), shape((tokens, lat), F32)]
        + [shape((some, lat + LANES)) for _, some in cuts]
        + [
            shape((lat, tokens)),
            shape((tokens, lat)),
            shape((lat, tokens)),
            shape((tokens, lat)),
            shape((lat, tokens)),
        ],
        scratch_shapes=[pltpu.VMEM((lat, lat), BF)] * 3
        + [
            pltpu.VMEM((held_gain.blocks * GAIN_ROWS, LANES), BF),
            pltpu.SemaphoreType.DMA((6 * count,)),
            pltpu.SemaphoreType.DMA((2 * gain_count,)),
        ],
        compiler_params=params(0),
        cost_estimate=SMALL,
        name="feed",
    )(place, *flat_parts, latent_message, cot_flat, *held_gain.flat, *held.flat)


def feed_grads_call(place, lefts, rights, n, far):
    lat, tokens = lefts[0].shape
    width = rights[0].shape[1]
    terms = len(lefts)

    def kernel(place_ref, *refs):
        left_refs, right_refs = refs[:terms], refs[terms : 2 * terms]
        outs = refs[2 * terms :]
        for distance in range(far):
            at = pl.multiple_of(jnp.bitwise_xor(place_ref[0], distance) * n, 16)
            for index in range(terms):
                chunk = left_refs[index][pl.ds(at, n), :]
                outs[distance][index * n : (index + 1) * n, :] = dot(
                    chunk, right_refs[index][...]
                ).astype(BF)

    return pl.pallas_call(
        kernel,
        in_specs=[scalar_spec()] + [whole_spec()] * (2 * terms),
        out_specs=[whole_spec()] * far,
        out_shape=[shape((terms * n, width))] * far,
        compiler_params=params(0),
        cost_estimate=SMALL,
        name="feed_grads",
    )(place, *lefts, *rights)


def attend_back_call(
    place, parts, queries, keys, values, byte_ids, held, groups, group, first, rows
):
    count_parts = len(parts)
    lat = keys.shape[1]
    block = byte_ids.shape[1]
    latents = groups * group
    count = len(held.flat)
    score_scale = 1.0 / math.sqrt(HEAD_DIM)

    def kernel(place_ref, *refs):
        refs = list(refs)
        take = lambda n: [refs.pop(0) for _ in range(n)]
        part_refs = take(count_parts)
        query_ref, key_ref, value_ref, bid_ref = take(4)
        piece_refs = take(count)
        grad_key_ref, grad_value_ref, grad_query_ref = take(3)
        up_refs = take(groups)
        wq, acc_q, acc_k, acc_v, sems = refs
        row = pl.program_id(0)

        def loads():
            return held.copies(("query",), piece_refs, (wq,), place_ref, sems)

        @pl.when(row == 0)
        def _():
            run_all(loads(), "start")

        message = jnp.concatenate(group_values(part_refs, place_ref), axis=0)
        stats = jnp.transpose(message[:, lat:].astype(F32), (1, 0))
        allowed = bid_ref[0] == stats[6 * HEADS : 6 * HEADS + 1, :]
        for head in range(HEADS):
            at, _ = head_window(head)
            mask = head_lanes(head)
            window = slice(at, at + WINDOW)
            stat = lambda k: stats[k * HEADS + head : k * HEADS + head + 1, :]
            log_total = stat(0) + stat(1) + stat(2)
            inner_sum = stat(3) + stat(4) + stat(5)
            query = jnp.where(mask, query_ref[:, window], jnp.zeros((), BF))
            grad = jnp.where(mask, message[:, window], jnp.zeros((), BF))
            key = key_ref[:, window]
            scores = dot(key, query, ((1,), (1,))) * score_scale
            probs = jnp.exp(jnp.where(allowed, scores - log_total, NEG_FILL))
            grad_probs = dot(value_ref[:, window], grad, ((1,), (1,)))
            grad_scores = (probs * (grad_probs - inner_sum)).astype(BF)
            found_k = dot(grad_scores, query)
            found_v = dot(probs.astype(BF), grad)
            found_q = dot(grad_scores, key, ((0,), (0,)))
            if head == 0:
                acc_k[:, window] = found_k
                acc_v[:, window] = found_v
                acc_q[:, window] = found_q
            else:
                acc_k[:, window] = jnp.where(mask, found_k, acc_k[:, window])
                acc_v[:, window] = jnp.where(mask, found_v, acc_v[:, window])
                acc_q[:, window] = jnp.where(mask, found_q, acc_q[:, window])

        grad_query = (acc_q[...] * score_scale).astype(BF)
        grad_key_ref[...] = (acc_k[...] * score_scale).astype(BF)
        grad_value_ref[...] = acc_v[...].astype(BF)
        grad_query_ref[...] = grad_query

        @pl.when(row == 0)
        def _():
            run_all(loads(), "wait")

        upstream = dot(grad_query, wq[...], ((1,), (1,))).astype(BF)
        for index, ref in enumerate(up_refs):
            ref[...] = upstream[index * group : (index + 1) * group, :]

    row_block = lambda i, p: (first + i, 0)
    own_block = lambda i, p: (i, 0)
    return pl.pallas_call(
        kernel,
        grid_spec=pltpu.PrefetchScalarGridSpec(
            num_scalar_prefetch=1,
            grid=(rows,),
            in_specs=[pl.BlockSpec((group, lat + LANES), own_block)] * count_parts
            + [
                pl.BlockSpec((latents, lat), own_block),
                pl.BlockSpec((block, lat), row_block),
                pl.BlockSpec((block, lat), row_block),
                pl.BlockSpec((1, block, 1), lambda i, p: (first + i, 0, 0)),
            ]
            + [any_spec()] * count,
            out_specs=[
                pl.BlockSpec((block, lat), own_block),
                pl.BlockSpec((block, lat), own_block),
                pl.BlockSpec((latents, lat), own_block),
            ]
            + [pl.BlockSpec((group, lat), own_block)] * groups,
            scratch_shapes=[
                pltpu.VMEM((lat, lat), BF),
                pltpu.VMEM((latents, lat), F32),
                pltpu.VMEM((block, lat), F32),
                pltpu.VMEM((block, lat), F32),
                pltpu.SemaphoreType.DMA((2 * count,)),
            ],
        ),
        out_shape=[shape((rows * block, lat))] * 2
        + [shape((rows * latents, lat))]
        + [shape((rows * group, lat))] * groups,
        compiler_params=params(1),
        cost_estimate=SMALL,
        name="attend_back",
    )(place, *parts, queries, keys, values, byte_ids, *held.flat)


def weight_grads_call(place, lefts, rights, some_rows, far):
    lat = rights[0][0].shape[1]
    chunk = sum(some_rows)
    left_counts, counts = [len(parts) for parts in lefts], [len(parts) for parts in rights]

    def kernel(place_ref, *refs):
        refs = list(refs)
        take = lambda n: [refs.pop(0) for _ in range(n)]
        left_refs = [take(n) for n in left_counts]
        right_refs = [take(n) for n in counts]
        outs = take(far)
        at = 0
        for index, (left, held) in enumerate(zip((0, 0, 1), refs)):
            factors, column, found = left_refs[left], 0, 0.0
            for part, right in enumerate(right_refs[index]):
                some = right.shape[0]
                if len(factors) > 1:
                    factor = factors[part][...]
                else:
                    factor = factors[0][:, column : column + some]
                found = found + dot(factor, right[...])
                column += some
            held[...] = found.astype(BF)
            some = some_rows[index]
            for distance in range(far):
                owner = jnp.bitwise_xor(place_ref[0], distance)
                outs[distance][at : at + some, :] = held[
                    pl.ds(pl.multiple_of(owner * some, 16), some), :
                ]
            at += some

    tile = lambda i, p: (0, i)
    flat_lefts = [left for parts in lefts for left in parts]
    flat_rights = [right for parts in rights for right in parts]
    return pl.pallas_call(
        kernel,
        grid_spec=pltpu.PrefetchScalarGridSpec(
            num_scalar_prefetch=1,
            grid=(lat // WINDOW,),
            in_specs=[full_block(left.shape) for left in flat_lefts]
            + [pl.BlockSpec((right.shape[0], WINDOW), tile) for right in flat_rights],
            out_specs=[pl.BlockSpec((chunk, WINDOW), tile)] * far,
            scratch_shapes=[pltpu.VMEM((lefts[i][0].shape[0], WINDOW), BF) for i in (0, 0, 1)],
        ),
        out_shape=[shape((chunk, lat))] * far,
        compiler_params=params(1),
        cost_estimate=SMALL,
        name="weight_grads",
    )(place, *flat_lefts, *flat_rights)


def byte_grad_call(place, bytes_flat, grads, held, rows, cuts):
    tokens, width = bytes_flat.shape
    block = tokens // rows
    lat = grads[0][0].shape[1]
    count = len(held.flat)
    shards = place_shards(held)

    def kernel(place_ref, x_ref, *refs):
        grad_refs = refs[: 2 * len(cuts)]
        piece_refs = refs[2 * len(cuts) : 2 * len(cuts) + count]
        out_ref, wk, wv, gains, gain, sems = refs[2 * len(cuts) + count :]
        row = pl.program_id(0)

        def loads():
            return held.copies(
                ("gains", "key", "value"), piece_refs, (gains, wk, wv), place_ref, sems
            )

        @pl.when(row == 0)
        def _():
            run_all(loads(), "start")

        xhat, scale = standardize(x_ref[...].astype(F32))

        @pl.when(row == 0)
        def _():
            run_all(loads(), "wait")
            gain[...] = gain_vector(gains, width, held.lanes["byte"], shards)

        for index, (first, some) in enumerate(cuts):

            @pl.when((row >= first) & (row < first + some))
            def _():
                upstream = dot(grad_refs[2 * index][...], wk[...], ((1,), (1,))) + dot(
                    grad_refs[2 * index + 1][...], wv[...], ((1,), (1,))
                )
                out_ref[...] = norm_pull(upstream, gain[...], xhat, scale)

    row_block = lambda i, p: (i, 0)

    def cut_block(first, some):
        return lambda i, p: (jnp.clip(i - first, 0, some - 1), 0)

    return pl.pallas_call(
        kernel,
        grid_spec=pltpu.PrefetchScalarGridSpec(
            num_scalar_prefetch=1,
            grid=(rows,),
            in_specs=[pl.BlockSpec((block, width), row_block)]
            + [pl.BlockSpec((block, lat), cut_block(*cut)) for cut in cuts for _ in range(2)]
            + [any_spec()] * count,
            out_specs=pl.BlockSpec((block, width), row_block),
            scratch_shapes=[
                pltpu.VMEM((width, lat), BF),
                pltpu.VMEM((width, lat), BF),
                pltpu.VMEM((held.blocks * GAIN_ROWS, LANES), BF),
                pltpu.VMEM((1, width), F32),
                pltpu.SemaphoreType.DMA((6 * count,)),
            ],
        ),
        out_shape=shape((tokens, width), F32),
        compiler_params=params(1),
        cost_estimate=SMALL,
        name="byte_grad",
    )(place, bytes_flat, *[g for some in grads for g in some], *held.flat)


def latent_grad_call(place, latent_message, grad_mixed, ups, held):
    tokens, lat = grad_mixed.shape
    cuts, groups = len(ups), len(ups[0])
    count = len(held.flat)
    shards = place_shards(held)

    def kernel(place_ref, x_ref, mixed_ref, *refs):
        up_refs = [refs[i * groups : (i + 1) * groups] for i in range(cuts)]
        piece_refs = refs[cuts * groups : cuts * groups + count]
        out_ref, gains, sems = refs[cuts * groups + count :]
        loads = held.copies(("gains",), piece_refs, (gains,), place_ref, sems)
        run_all(loads, "start")
        xhat, scale = standardize(x_ref[:, :lat].astype(F32))
        upstream = jnp.concatenate(
            [
                functools.reduce(jnp.add, [ref[...].astype(F32) for ref in some])
                for some in up_refs
            ],
            axis=0,
        )
        run_all(loads, "wait")
        gain = gain_vector(gains, lat, held.lanes["latent"], shards)
        out_ref[...] = mixed_ref[...] + norm_pull(upstream, gain, xhat, scale)

    return pl.pallas_call(
        kernel,
        in_specs=[scalar_spec()]
        + [whole_spec()] * (2 + cuts * groups)
        + [any_spec()] * count,
        out_specs=whole_spec(),
        out_shape=shape((tokens, lat), F32),
        scratch_shapes=[
            pltpu.VMEM((held.blocks * GAIN_ROWS, LANES), BF),
            pltpu.SemaphoreType.DMA((2 * count,)),
        ],
        compiler_params=params(0, 24),
        cost_estimate=SMALL,
        name="latent_grad",
    )(place, latent_message, grad_mixed, *[u for some in ups for u in some], *held.flat)


def swap(value, axis, size, distance):
    return lax.ppermute(value, axis, [(i, i ^ distance) for i in range(size)])


def tie(value, *earlier):
    return lax.optimization_barrier((value, *earlier))[0]


def swap_all(parts, size):
    return [swap(parts[j], "fsdp", size, j) for j in range(1, size)]


def by_index(parts, own, size):
    if len(parts) == 5:
        parts = parts[:3] + [jnp.where((own == 0) | (own == 3), parts[4], parts[3])]
    return [lax.select_n(jnp.bitwise_xor(own, k), *parts) for k in range(size)]


def build_block(place, own, parts, sizes, size):
    segments, first, at = [], 0, 0
    for rows in sizes:
        segments.append((first, rows, at))
        first += rows
        at += rows * size
    total = up_to(at, 16)
    if all(first % 8 == 0 for first, _, _ in segments):
        return assemble_call(place, parts, segments, total, size)
    shards = by_index(parts, own, size)
    found = [s[first : first + rows] for first, rows, _ in segments for s in shards]
    return pad_rows(jnp.concatenate(found, axis=0), total)


def add(*values):
    return functools.reduce(jnp.add, [v.astype(F32) for v in values]).astype(BF)


def meet_call(first, high, second, low, half):
    rows, lat = first[0].shape

    def kernel(a, b, h, c, d, l, one, two):
        one[:half, :] = (a[:half, :].astype(F32) + b[:half, :].astype(F32)).astype(BF)
        one[half:, :] = (
            a[half:, :].astype(F32) + b[half:, :].astype(F32) + h[...].astype(F32)
        ).astype(BF)
        two[:half, :] = (
            c[:half, :].astype(F32) + d[:half, :].astype(F32) + l[...].astype(F32)
        ).astype(BF)
        two[half:, :] = (c[half:, :].astype(F32) + d[half:, :].astype(F32)).astype(BF)

    return pl.pallas_call(
        kernel,
        in_specs=[whole_spec()] * 6,
        out_specs=[whole_spec()] * 2,
        out_shape=[shape((rows, lat))] * 2,
        compiler_params=params(0, 24),
        cost_estimate=SMALL,
        name="meet",
    )(*first, high, *second, low)


def cut_call(place, terms, sizes, size):
    lat = terms[0].shape[1]
    rows = sum(sizes)

    def kernel(place_ref, *refs):
        term_refs, outs, acc = refs[: len(terms)], refs[len(terms) : -1], refs[-1]
        acc[...] = functools.reduce(jnp.add, [ref[...].astype(F32) for ref in term_refs])
        for distance, out in enumerate(outs):
            owner = jnp.bitwise_xor(place_ref[1], distance)
            found, at = [], 0
            for some in sizes:
                found.append(acc[pl.ds(pl.multiple_of(at + owner * some, 8), some), :])
                at += some * size
            out[...] = jnp.concatenate(found, axis=0).astype(out.dtype)

    return pl.pallas_call(
        kernel,
        in_specs=[scalar_spec()] + [whole_spec()] * len(terms),
        out_specs=[whole_spec()] * size,
        out_shape=[shape((rows, lat), F32)] + [shape((rows, lat))] * (size - 1),
        scratch_shapes=[pltpu.VMEM(terms[0].shape, F32)],
        compiler_params=params(0, 24),
        cost_estimate=SMALL,
        name="cut",
    )(place, *terms)


def cut_terms(place, own, terms, sizes, size):
    if all(some % 8 == 0 for some in sizes):
        return cut_call(place, terms, sizes, size)
    block = functools.reduce(jnp.add, [v.astype(F32) for v in terms])
    outs = []
    for distance in range(size):
        index = jnp.bitwise_xor(own, distance)
        found, at = [], 0
        for some in sizes:
            part = block[at : at + some * size].reshape(size, some, block.shape[1])
            found.append(lax.dynamic_index_in_dim(part, index, 0, keepdims=False))
            at += some * size
        value = jnp.concatenate(found, axis=0)
        outs.append(value if distance == 0 else value.astype(BF))
    return outs


def total(own, arrived):
    return functools.reduce(jnp.add, [v.astype(F32) for v in [own, *arrived]])


def split_rows(value, sizes):
    found, at = [], 0
    for some in sizes:
        found.append(value[at : at + some])
        at += some
    return found


def up_to(value, step):
    return -(-value // step) * step


def pad_rows(value, rows):
    return jnp.pad(value, ((0, rows - value.shape[0]), (0, 0)))


class Plan:
    def __init__(self, n_dp, n_f):
        self.n_dp, self.n_f = n_dp, n_f
        self.gate = ()

    def send(self, value, distance):
        return swap(tie(value, *self.gate), "dp", self.n_dp, distance)

    def pass_on(self, value, distance):
        return swap(tie(value, *self.gate), "fsdp", self.n_f, distance)

    def relay(self, own, two):
        middle = lax.ppermute(tie(own, *self.gate), "fsdp", [(1, 2), (2, 1)])
        return middle, lax.ppermute(tie(two, *self.gate), "fsdp", [(2, 3), (1, 0)])

    def spread(self, value):
        value = tie(value, *self.gate)
        middle = lax.ppermute(value, "fsdp", [(1, 2), (2, 1)])
        return middle, lax.ppermute(value, "fsdp", [(3, 2), (0, 1)])

    def tied(self, values):
        return [tie(values[0], *self.gate), *values[1:]]


def square_pieces(block, chips, half):
    rows = block.shape[0]
    full, halves = [(0, rows)], [(0, half), (half, rows)]
    pieces, flat = [], []
    for distance, parts, pairs in (
        (0, full, chips[:1]),
        (2, full, chips[1:2]),
        (4, full, chips[2:3]),
        (6, halves, chips[3:]),
    ):
        for core in range(2):
            pieces.append((distance + core, parts))
            flat.extend(pair[core] for pair in pairs)
    return pieces, flat


def local(n_dp, n_f, bytes_in, latents_in, cotangent, byte_segments, latent_segments,
          w_query, w_key, w_value, w_out, w_mlp_in, w_mlp_out,
          gain_latent, gain_byte, gain_mlp):
    rows, byte_local, width = bytes_in.shape
    _, group, lat = latents_in.shape
    dp, own = lax.axis_index("dp"), lax.axis_index("fsdp")
    place = jnp.stack([dp, own]).astype(jnp.int32)
    bytes_flat = bytes_in.reshape(rows * byte_local, width)
    latents_flat = latents_in.reshape(rows * group, lat)
    cot_flat = cotangent.reshape(rows * group, lat)
    kr, qr = w_key.shape[0], w_query.shape[0]
    key_rows, query_rows = n_f * kr, n_f * qr
    cuts = [(0, 1), (1, rows - 1)]
    cut_rows = [(first * group, some * group) for first, some in cuts]

    gains = jnp.concatenate([gain_latent, gain_byte, gain_mlp])
    gains = jnp.pad(gains, (0, lat - gains.shape[0]))[None, :]
    message_one = jnp.concatenate([w_key, w_value, w_query, gains], axis=0)
    message_one = pad_rows(message_one, up_to(2 * kr + qr + 1, 16))
    message_two = jnp.concatenate([w_out, w_mlp_in, w_mlp_out], axis=0)
    ids = latent_segments.reshape(rows * group, 1).astype(BF)
    ids = jnp.pad(ids, ((0, 0), (0, LANES - 1)))
    latent_message = jnp.concatenate([latents_flat, ids], axis=1)
    byte_ids = lax.dynamic_slice_in_dim(byte_segments, own * byte_local, byte_local, axis=1)
    byte_ids = byte_ids.astype(F32)
    byte_row, byte_column = byte_ids[:, None, :], byte_ids[:, :, None]
    sizes_one, sizes_two = (kr, kr, qr), (qr, qr, qr)
    half_one, half_two = 2 * key_rows, up_to(3 * query_rows // 2, 16)
    spans_one = {
        "key": (0, key_rows),
        "value": (key_rows, key_rows),
        "query": (2 * key_rows, query_rows),
        "gains": (2 * key_rows + query_rows, GAIN_ROWS),
    }
    spans_two = {name: (i * query_rows, query_rows) for i, name in enumerate(("out", "inner", "outer"))}

    def held_one(pieces, flat):
        held = Held(pieces, flat, spans_one)
        held.blocks, held.size = n_dp, n_f
        held.lanes = {"latent": 0, "byte": qr, "mlp": qr + kr}
        return held

    def key_value(one, bytes_flat):
        return key_value_call(place, bytes_flat, one, rows)

    def attend(index, one, parts, keys, values):
        found = attend_call(
            place, parts, byte_row, keys, values, one, n_f, group, *cuts[index]
        )
        return found[0], found[1], found[2:]

    def feed(one, two, attended):
        return feed_call(place, attended, latent_message, cot_flat, one, two, cut_rows)

    def feed_grads(lefts, rights):
        return feed_grads_call(place, lefts, rights, query_rows, n_dp)

    def attend_back(index, one, parts, saved):
        return attend_back_call(
            place, parts, *saved, byte_column, one, n_f, group, *cuts[index]
        )

    def weight_grads(lefts, first, last):
        return weight_grads_call(
            place, lefts, list(zip(first, last)), (key_rows, key_rows, query_rows), n_dp
        )

    def byte_grad(one, grads):
        return byte_grad_call(place, bytes_flat, grads, one, rows, cuts)

    run = square if (n_dp, n_f) == (8, 4) else plain
    new, grad_latents, grad_bytes, grad_one, grad_two = run(**locals())

    def gain_grad(pairs, gain):
        found = sum(jnp.sum(w.astype(F32) * g, axis=1) for w, g in pairs)
        return found / gain.astype(F32)

    grad_key, grad_value, grad_query = split_rows(grad_one, sizes_one)
    grad_out, grad_inner, grad_outer = split_rows(grad_two, sizes_two)
    return (
        new.reshape(rows, group, lat),
        grad_latents.reshape(rows, group, lat),
        grad_bytes.reshape(rows, byte_local, width),
        grad_query,
        grad_key,
        grad_value,
        grad_out,
        grad_inner,
        grad_outer,
        gain_grad([(w_query, grad_query)], gain_latent),
        gain_grad([(w_key, grad_key), (w_value, grad_value)], gain_byte),
        gain_grad([(w_mlp_in, grad_inner)], gain_mlp),
    )


def plain(*, n_dp, n_f, place, own, bytes_flat, message_one, message_two, latent_message,
          sizes_one, sizes_two, spans_two, cot_flat, held_one, key_value, attend, feed,
          feed_grads, attend_back, weight_grads, byte_grad, **_):
    def gather(message, sizes):
        parts = [message, *swap_all([message] * n_f, n_f)]
        block = build_block(place, own, parts, sizes, n_f)
        flat = [block] + [swap(block, "dp", n_dp, d) for d in range(1, n_dp)]
        return [(d, [(0, block.shape[0])]) for d in range(n_dp)], flat

    def scatter(parts, sizes):
        terms = [parts[0]] + [swap(parts[d], "dp", n_dp, d) for d in range(1, n_dp)]
        cut = cut_terms(place, own, terms, sizes, n_f)
        return total(cut[0], swap_all(cut, n_f))

    one = held_one(*gather(message_one, (*sizes_one, 1)))
    two = Held(*gather(message_two, sizes_two), spans_two)
    byte_t, keys, values = key_value(one, bytes_flat)
    latent_parts = [latent_message, *swap_all([latent_message] * n_f, n_f)]
    latent_t, queries, found = zip(*[attend(i, one, latent_parts, keys, values) for i in range(2)])
    attended = list(zip(*[[f[0], *swap_all(f, n_f)] for f in found]))
    new, grad_mixed, *messages, attended_t, branch, normed_t, inner, act_t = feed(
        one, two, attended
    )
    grad_two = scatter(feed_grads((attended_t, normed_t, act_t), (branch, inner, cot_flat)), sizes_two)
    parts = [[m, *swap_all([m] * n_f, n_f)] for m in messages]
    first, last = [attend_back(i, one, parts[i], (queries[i], keys, values)) for i in range(2)]
    grad_bytes = byte_grad(one, (first[:2], last[:2]))
    grad_one = scatter(weight_grads(((byte_t,), latent_t), first[:3], last[:3]), sizes_one)
    ups = [[ups[0], *swap_all(ups, n_f)] for ups in (first[3:], last[3:])]
    grad_latents = latent_grad_call(place, latent_message, grad_mixed, ups, one)
    return new, grad_latents, grad_bytes, grad_one, grad_two


def square(*, n_dp, n_f, place, own, bytes_flat, message_one, message_two, latent_message,
           sizes_one, sizes_two, spans_two, half_one, half_two, cot_flat, held_one, key_value,
           attend, feed, feed_grads, attend_back, weight_grads, byte_grad, **_):
    plan = Plan(n_dp, n_f)
    send, pass_on = plan.send, plan.pass_on

    near = [pass_on(message_one, 2), pass_on(message_one, 1)]
    plan.gate = near
    parts = [message_one, near[1], near[0], *plan.relay(message_one, near[0])]
    block = build_block(place, own, parts, (*sizes_one, 1), n_f)
    plan.gate = [block]
    x, y, other = send(block, 2), send(block, 4), send(block, 1)
    latent_two, latent_one = pass_on(latent_message, 2), pass_on(latent_message, 1)
    plan.gate = [x, y, other, latent_two, latent_one]
    low, high = send(x[:half_one], 4), send(y[half_one:], 2)
    latent_parts = [
        latent_message, latent_one, latent_two, *plan.relay(latent_message, latent_two)
    ]
    x_other = send(x, 1)
    y_other = send(tie(y, x_other), 1)
    plan.gate = [low, high, y_other, *latent_parts[3:]]
    low_other, high_other = send(low, 1), send(high, 1)
    pairs = [(block, other), (x, x_other), (y, y_other), (low, low_other), (high, high_other)]
    one = held_one(*square_pieces(block, pairs, half_one))
    two_two, two_one = pass_on(message_two, 2), pass_on(message_two, 1)
    plan.gate = [low_other, high_other]
    byte_t, keys, values = key_value(one, tie(bytes_flat, *plan.gate))
    plan.gate = [two_two, two_one, keys]
    parts = [message_two, two_one, two_two, *plan.relay(message_two, two_two)]
    latent_t_first, queries_first, found = attend(0, one, plan.tied(latent_parts), keys, values)
    plan.gate = [queries_first, *parts[3:]]
    block = build_block(place, own, plan.tied(parts), sizes_two, n_f)
    x, y = send(block, 2), send(block, 4)
    attended_first = [found[0], *[pass_on(found[j], j) for j in range(1, n_f)]]
    plan.gate = [block]
    latent_t_last, queries_last, found = attend(1, one, plan.tied(latent_parts), keys, values)
    plan.gate = attended_first[1:]
    attended_last = [found[0], *[pass_on(found[j], j) for j in range(1, n_f)]]
    plan.gate = [x, y, queries_last, *attended_first[1:]]
    low, high = send(x[:half_two], 4), send(y[half_two:], 2)
    plan.gate = [low, high, *attended_last[1:]]
    pairs = [(v, send(v, 1)) for v in (block, x, y, low, high)]
    two = Held(*square_pieces(block, pairs, half_two), spans_two)
    new, grad_mixed, first, last, attended_t, branch, normed_t, inner, act_t = feed(
        one, two, list(zip(attended_first, attended_last))
    )
    plan.gate = []
    near = [pass_on(first, 2), pass_on(first, 1)]
    grads = feed_grads((attended_t, normed_t, act_t), (branch, inner, cot_flat))
    plan.gate = near
    first_parts = [first, near[1], near[0], *plan.relay(first, near[0])]
    arrived = {d: send(grads[d + 1], 1) for d in (6, 4, 2)}
    plan.gate = [*arrived.values(), *first_parts[3:]]
    low = add(tie(grads[6][:half_two], *plan.gate), arrived[6][:half_two])
    high = add(tie(grads[6][half_two:], *plan.gate), arrived[6][half_two:])
    low, high = send(low, 2), send(high, 4)
    near = [pass_on(last, 2), pass_on(last, 1)]
    arrived[0] = send(grads[1], 1)
    back_first = attend_back(0, one, plan.tied(first_parts), (queries_first, keys, values))
    plan.gate = [low, high, arrived[0], *near, back_first[0]]
    last_parts = [last, near[1], near[0], *plan.relay(last, near[0])]
    x, y = meet_call(
        (grads[2], arrived[2]), tie(high, *plan.gate), (grads[4], arrived[4]), low, half_two
    )
    plan.gate = [x, y]
    terms_two = [grads[0], arrived[0], send(x, 2), send(y, 4)]
    plan.gate = [x, y, *last_parts[3:]]
    ups_first = back_first[3:]
    ups_first = [ups_first[0], *[pass_on(ups_first[j], j) for j in range(1, n_f)]]
    back_last = attend_back(1, one, plan.tied(last_parts), (queries_last, keys, values))
    plan.gate = [back_last[0], *ups_first[1:], *terms_two[2:]]
    cut_two = cut_terms(place, own, plan.tied(terms_two), sizes_two, n_f)
    ups = back_last[3:]
    plan.gate = [cut_two[0]]
    near = [pass_on(ups[1], 1), *plan.spread(ups[3])]
    arrived_two = [pass_on(cut_two[1], 1), pass_on(cut_two[3], 3)]
    grads = weight_grads(
        ((byte_t,), (latent_t_first, latent_t_last)),
        back_first[:3],
        [tie(back_last[0], *plan.gate), *back_last[1:3]],
    )
    plan.gate = [*near, grads[0]]
    arrived = {d: send(grads[d + 1], 1) for d in (6, 4, 2)}
    low = add(grads[6][:half_one], arrived[6][:half_one])
    high = add(grads[6][half_one:], arrived[6][half_one:])
    merged = add(tie(ups[2], *plan.gate), near[2])
    plan.gate = [low, high, merged, *arrived.values()]
    low, high = send(low, 2), send(high, 4)
    ups_last = [ups[0], *near[:2], pass_on(merged, 2)]
    plan.gate = [low, high, *arrived_two]
    x, y = meet_call(
        (grads[2], arrived[2]), tie(high, *plan.gate), (grads[4], arrived[4]), low, half_one
    )
    plan.gate = [x, y]
    arrived[0] = send(grads[1], 1)
    terms_one = [grads[0], arrived[0], send(x, 2), send(y, 4)]
    arrived_two.append(pass_on(cut_two[2], 2))
    grad_bytes = byte_grad(one, (plan.tied(back_first[:2]), back_last[:2]))
    plan.gate = [*terms_one[2:], grad_bytes, arrived_two[-1], ups_last[-1]]
    cut_one = cut_terms(place, own, plan.tied(terms_one), sizes_one, n_f)
    plan.gate = [cut_one[0]]
    grad_one = total(cut_one[0], [pass_on(cut_one[j], j) for j in range(1, n_f)])
    grad_two = total(cut_two[0], arrived_two)
    grad_latents = latent_grad_call(
        place, latent_message, tie(grad_mixed, *plan.gate), [ups_first, ups_last], one
    )
    return new, grad_latents, grad_bytes, grad_one, grad_two


def solution(mesh):
    rows3 = P("dp", "fsdp", None)
    split2 = P(("dp", "fsdp"), None)
    split1 = P(("dp", "fsdp"))
    in_specs = (rows3,) * 3 + (P("dp", None), P("dp", "fsdp")) + (split2,) * 6 + (split1,) * 3
    out_specs = (rows3,) * 3 + (split2,) * 6 + (split1,) * 3
    body = functools.partial(local, mesh.shape["dp"], mesh.shape["fsdp"])
    return jax.shard_map(
        body, mesh=mesh, in_specs=in_specs, out_specs=out_specs, check_vma=False
    )
```

time: 499 us -> 407 us (0.82)
  the two profiles are of different devices: /device:TPU:12 before, /device:TPU:0 now
where the time goes in v2:
time: 407 us; the launch traced here: 402 us
  waiting for transfers between devices  163 us (40%)
  Pallas kernels  131 us (32%)
  starting transfers between devices  74 us (18%)
  local copies, waits for them, and re-layouts  21.1 us (5%)
  other arithmetic  10.7 us (3%)
    ppermute x61, waiting for transfers between devices, swap(): return lax.ppermute(value, axis, [(i, i ^ distance) for i in range(size)])  136 us
    ppermute x61, starting transfers between devices, swap(): return lax.ppermute(value, axis, [(i, i ^ distance) for i in range(size)])  58.5 us
    ppermute x5, waiting for transfers between devices, relay(): lax.ppermute(tie(two, *self.gate), 'fsdp', [(2, 3), (1, 0)])  26.6 us
    pallas_call x2, Pallas kernels, attend_back_call(): pl.pallas_call(kernel, grid_spec=pltpu.PrefetchScalarGridSpec(num_scalar_...  24.2 us
    pallas_call x2, Pallas kernels, attend_call(): pl.pallas_call(kernel, grid_spec=pltpu.PrefetchScalarGridSpec(num_scalar_...  23.9 us
    unnamed x188, local copies, waits for them, and re-layouts  17 us
    pallas_call x1, Pallas kernels, byte_grad_call(): pl.pallas_call(kernel, grid_spec=pltpu.PrefetchScalarGridSpec(num_scalar_...  16.3 us
    pallas_call x1, Pallas kernels, weight_grads_call(): pl.pallas_call(kernel, grid_spec=pltpu.PrefetchScalarGridSpec(num_scalar_...  15.2 us
  transfers between devices with their start and end apart: 73, of which 29 were waited for; matrix products, arithmetic and copies ran while one was open for 3% of the time, Pallas kernels for 26%

profile of v2, /device:TPU:0, one launch (start us, length us, event | category | flops | bytes accessed | tf_op | source)
XLA Modules:
  0.0 401.8 jit_solution(2531499362704357740)
XLA Ops:
  2.4 4.1 %collective-permute-start.1 = (bf16[96,1280]{1,0:T(8,128)(2,1)S(1)}, bf16[96,1280]{1,0:T(8,128)(2,1)S(1)}, u32[]{:S(2)}, u32[]{:S(2)}) collective-permute-start(bf16[96,1280]{1,0:T(8,128)(2,1)S(1)} %fusion.8.refs_0_), channel_id=1, source_target_pairs={{0,2},{1,3},{2,0},{3,1},{4,6},{5,7},{6,4},{7,5},{8,10},{9,11},{10,... | collective-permute-start | bytes 737288 | tf_op jit(solution)/shard_map/ppermute | solution.py:772
  6.5 1.6 collective-permute-start
  8.1 9.7 %collective-permute-done.1.refs_2_ = bf16[96,1280]{1,0:T(8,128)(2,1)S(1)} collective-permute-done((bf16[96,1280]{1,0:T(8,128)(2,1)S(1)}, bf16[96,1280]{1,0:T(8,128)(2,1)S(1)}, u32[]{:S(2)}, u32[]{:S(2)}) %collective-permute-start.1) | collective-permute-done | bytes 245792 | tf_op jit(solution)/shard_map/ppermute | solution.py:772
  18.7 1.3 collective-permute-start.3
  20.1 7.9 %collective-permute-done.3.refs_4_ = bf16[96,1280]{1,0:T(8,128)(2,1)S(1)} collective-permute-done((bf16[96,1280]{1,0:T(8,128)(2,1)S(1)}, bf16[96,1280]{1,0:T(8,128)(2,1)S(1)}, u32[]{:S(2)}, u32[]{:S(2)}) %collective-permute-start.3) | collective-permute-done | bytes 245792 | tf_op jit(solution)/shard_map/ppermute | solution.py:908
  29.2 1.6 collective-permute-start.5
  30.8 1.5 collective-permute-start.4
  32.9 4.1 %collective-permute-start.7 = (bf16[192,1408]{1,0:T(8,128)(2,1)S(1)}, bf16[192,1408]{1,0:T(8,128)(2,1)S(1)}, u32[]{:S(2)}, u32[]{:S(2)}) collective-permute-start(bf16[192,1408]{1,0:T(8,128)(2,1)S(1)} %fusion.1.refs_0_.refs_8_.x_ref), channel_id=1, source_target_pairs={{0,2},{1,3},{2,0},{3,1},{4,6},{5,7},{6,4},{7,5},{8,10},{9,11},{10,... | collective-permute-start | bytes 1622024 | tf_op jit(solution)/shard_map/ppermute | solution.py:772
  37.0 21.1 %collective-permute-done.8.refs_1_ = bf16[192,1408]{1,0:T(8,128)(2,1)S(1)} collective-permute-done((bf16[192,1408]{1,0:T(8,128)(2,1)S(1)}, bf16[192,1408]{1,0:T(8,128)(2,1)S(1)}, u32[]{:S(2)}, u32[]{:S(2)}) %collective-permute-start.8) | collective-permute-done | bytes 540704 | tf_op jit(solution)/shard_map/ppermute | solution.py:772
  58.1 2.5 collective-permute-done.7.refs_2_
  60.8 2.5 collective-permute-done.11.refs_3_.refs_11_.refs_13_.refs_12_.refs_7_
  65.0 1.3 collective-permute-start.14
  68.9 10.5 %collective-permute-done.10.refs_7_.refs_15_.refs_17_.refs_16_.refs_11_ = bf16[176,1280]{1,0:T(8,128)(2,1)S(1)} collective-permute-done((bf16[176,1280]{1,0:T(8,128)(2,1)S(1)}, bf16[176,1280]{1,0:T(8,128)(2,1)S(1)}, u32[]{:S(2)}, u32[]{:S(2)}) %collective-permute-start.10) | collective-permute-done | bytes 450592 | tf_op jit(solution)/shard_map/ppermute | solution.py:772
  80.0 1.5 collective-permute-done.14.refs_4_
  83.8 1.9 collective-permute-start.15
  86.7 13.7 %keys_values.1 = (bf16[768,1536]{1,0:T(8,128)(2,1)}, bf16[1536,1280]{1,0:T(8,128)(2,1)}, bf16[1536,1280]{1,0:T(8,128)(2,1)}) custom-call(s32[2]{0:T(128)} %copy-done.42, bf16[1536,768]{1,0:T(8,128)(2,1)} %bitcast.10, bf16[368,1280]{1,0:T(8,128)(2,1)} %copy-done, bf16[368,1280]{1,0:T(8,128)(2,1)} %collective-permute-done.6.refs_1_.refs_9_.refs_11_.refs_10_.refs_5_, ...), custom_call_target="tpu_custom_call" | custom-call | flops 1 | bytes 1 | tf_op jit(solution)/shard_map/keys_values/pallas_call | solution.py:237
  101.1 1.8 collective-permute-start.20
  103.5 9.6 %attend.2 = (bf16[1280,256]{1,0:T(8,128)(2,1)}, bf16[256,1280]{1,0:T(8,128)(2,1)}, bf16[64,1408]{1,0:T(8,128)(2,1)}, bf16[64,1408]{1,0:T(8,128)(2,1)}, bf16[64,1...) custom-call(s32[2]{0:T(128)} %copy-done.42, bf16[192,1408]{1,0:T(8,128)(2,1)} %copy-done.18, bf16[192,1408]{1,0:T(8,128)(2,1)} %copy-done.52, ...), custom_call_target="tpu_custom_call" | custom-call | flops 1 | bytes 1 | tf_op jit(solution)/shard_map/attend/pallas_call | solution.py:333
  113.2 1.5 assemble.3.refs_20_
  116.3 2.4 collective-permute-start.23
  118.7 2.1 collective-permute-start.22
  120.9 14.2 %attend.3 = (bf16[1280,512]{1,0:T(8,128)(2,1)}, bf16[512,1280]{1,0:T(8,128)(2,1)}, bf16[128,1408]{1,0:T(8,128)(2,1)}, bf16[128,1408]{1,0:T(8,128)(2,1)}, bf16[12...) custom-call(s32[2]{0:T(128)} %copy-done.42, bf16[192,1408]{1,0:T(8,128)(2,1)} %copy-done.18, bf16[192,1408]{1,0:T(8,128)(2,1)} %copy-done.52, ...), custom_call_target="tpu_custom_call" | custom-call | flops 1 | bytes 1 | tf_op jit(solution)/shard_map/attend/pallas_call | solution.py:333
  135.1 8.1 %collective-permute-done.28.refs_24_ = bf16[480,1280]{1,0:T(8,128)(2,1)S(1)} collective-permute-done((bf16[480,1280]{1,0:T(8,128)(2,1)S(1)}, bf16[480,1280]{1,0:T(8,128)(2,1)S(1)}, u32[]{:S(2)}, u32[]{:S(2)}) %collective-permute-start.28) | collective-permute-done | bytes 1228832 | tf_op jit(solution)/shard_map/ppermute | solution.py:772
  143.5 1.6 collective-permute-start.29
  145.7 1.4 collective-permute-start.26
  147.1 2.5 collective-permute-start.25
  150.1 8.9 %collective-permute-done.26.refs_7_ = bf16[128,1408]{1,0:T(8,128)(2,1)S(1)} collective-permute-done((bf16[128,1408]{1,0:T(8,128)(2,1)S(1)}, bf16[128,1408]{1,0:T(8,128)(2,1)S(1)}, u32[]{:S(2)}, u32[]{:S(2)}) %collective-permute-start.26) | collective-permute-done | bytes 360480 | tf_op jit(solution)/shard_map/ppermute | solution.py:772
  159.0 19.4 %collective-permute-done.25.refs_5_ = bf16[128,1408]{1,0:T(8,128)(2,1)S(1)} collective-permute-done((bf16[128,1408]{1,0:T(8,128)(2,1)S(1)}, bf16[128,1408]{1,0:T(8,128)(2,1)S(1)}, u32[]{:S(2)}, u32[]{:S(2)}) %collective-permute-start.25) | collective-permute-done | bytes 360480 | tf_op jit(solution)/shard_map/ppermute | solution.py:772
  180.4 6.2 %collective-permute-done.34.refs_28_ = bf16[240,1280]{1,0:T(8,128)(2,1)S(1)} collective-permute-done((bf16[240,1280]{1,0:T(8,128)(2,1)S(1)}, bf16[240,1280]{1,0:T(8,128)(2,1)S(1)}, u32[]{:S(2)}, u32[]{:S(2)}) %collective-permute-start.34) | collective-permute-done | bytes 614432 | tf_op jit(solution)/shard_map/ppermute | solution.py:772
  189.7 14.2 %feed.1 = (bf16[192,1280]{1,0:T(8,128)(2,1)}, f32[192,1280]{1,0:T(8,128)}, bf16[64,1408]{1,0:T(8,128)(2,1)}, bf16[128,1408]{1,0:T(8,128)(2,1)}, bf16[1280,192]{1...) custom-call(s32[2]{0:T(128)} %copy-done.42, ...), custom_call_target="tpu_custom_call" | custom-call | flops 1 | bytes 1 | tf_op jit(solution)/shard_map/feed/pallas_call | solution.py:450
  203.9 1.4 collective-permute-start.36
  205.4 6.7 %feed_grads.1 = (bf16[480,1280]{1,0:T(8,128)(2,1)}, bf16[480,1280]{1,0:T(8,128)(2,1)}, bf16[480,1280]{1,0:T(8,128)(2,1)}, bf16[480,1280]{1,0:T(8,128)(2,1)}, bf1...) custom-call(s32[2]{0:T(128)} %copy-done.42, ...), custom_call_target="tpu_custom_call" | custom-call | flops 1 | bytes 1 | tf_op jit(solution)/shard_map/feed_grads/pallas_call | solution.py:493
  212.8 2.8 collective-permute-done.36.refs_2_
  218.5 7.5 %collective-permute-done.42.refs_4_ = bf16[64,1408]{1,0:T(8,128)(2,1)S(1)} collective-permute-done((bf16[64,1408]{1,0:T(8,128)(2,1)S(1)}, bf16[64,1408]{1,0:T(8,128)(2,1)S(1)}, u32[]{:S(2)}, u32[]{:S(2)}) %collective-permute-start.42) | collective-permute-done | bytes 180256 | tf_op jit(solution)/shard_map/ppermute | solution.py:908
  228.3 1.3 fusion.14
  229.6 1.3 add_convert_fusion
  231.8 1.5 collective-permute-start.44
  233.3 2.0 collective-permute-start.46
  236.4 8.9 %attend_back.2 = (bf16[512,1280]{1,0:T(8,128)(2,1)}, bf16[512,1280]{1,0:T(8,128)(2,1)}, bf16[256,1280]{1,0:T(8,128)(2,1)}, bf16[64,1280]{1,0:T(8,128)(2,1)}, bf1...) custom-call(s32[2]{0:T(128)} %copy-done.42, ...), custom_call_target="tpu_custom_call" | custom-call | flops 1 | bytes 1 | tf_op jit(solution)/shard_map/attend_back/pallas_call | solution.py:576
  245.4 4.7 %collective-permute-done.47.refs_1_ = bf16[128,1408]{1,0:T(8,128)(2,1)} collective-permute-done((bf16[128,1408]{1,0:T(8,128)(2,1)S(1)}, bf16[128,1408]{1,0:T(8,128)(2,1)}, u32[]{:S(2)}, u32[]{:S(2)}) %collective-permute-start.47) | collective-permute-done | bytes 360480 | tf_op jit(solution)/shard_map/ppermute | solution.py:772
  250.1 2.3 collective-permute-done.46.refs_2_
  255.0 3.1 meet.2
  261.8 9.7 %collective-permute-done.49.refs_4_ = bf16[128,1408]{1,0:T(8,128)(2,1)S(1)} collective-permute-done((bf16[128,1408]{1,0:T(8,128)(2,1)}, bf16[128,1408]{1,0:T(8,128)(2,1)S(1)}, u32[]{:S(2)}, u32[]{:S(2)}) %collective-permute-start.49) | collective-permute-done | bytes 360480 | tf_op jit(solution)/shard_map/ppermute | solution.py:908
  273.2 2.8 collective-permute-start.52
  276.0 15.3 %attend_back.3 = (bf16[1024,1280]{1,0:T(8,128)(2,1)}, bf16[1024,1280]{1,0:T(8,128)(2,1)}, bf16[512,1280]{1,0:T(8,128)(2,1)}, bf16[128,1280]{1,0:T(8,128)(2,1)}, ...) custom-call(s32[2]{0:T(128)} %copy-done.42, ...), custom_call_target="tpu_custom_call" | custom-call | flops 1 | bytes 1 | tf_op jit(solution)/shard_map/attend_back/pallas_call | solution.py:576
  291.4 3.3 cut.2
  296.9 3.9 collective-permute-start.57
  301.7 15.2 %weight_grads.1 = (bf16[352,1280]{1,0:T(8,128)(2,1)}, bf16[352,1280]{1,0:T(8,128)(2,1)}, bf16[352,1280]{1,0:T(8,128)(2,1)}, bf16[352,1280]{1,0:T(8,128)(2,1)}, b...) custom-call(s32[2]{0:T(128)} %copy-done.42, ...), custom_call_target="tpu_custom_call" | custom-call | flops 1 | bytes 1 | tf_op jit(solution)/shard_map/weight_grads/pallas_call | solution.py:646
  322.3 1.5 collective-permute-start.62
  325.6 1.6 collective-permute-start.63
  327.2 9.5 %collective-permute-done.64 = bf16[120,1280]{1,0:T(8,128)(2,1)} collective-permute-done((bf16[120,1280]{1,0:T(8,128)(2,1)S(1)}, bf16[120,1280]{1,0:T(8,128)(2,1)}, u32[]{:S(2)}, u32[]{:S(2)}) %collective-permute-start.64) | collective-permute-done | bytes 307232 | tf_op jit(solution)/shard_map/ppermute | solution.py:772
  336.7 4.1 %collective-permute-done.63 = bf16[120,1280]{1,0:T(8,128)(2,1)} collective-permute-done((bf16[120,1280]{1,0:T(8,128)(2,1)S(1)}, bf16[120,1280]{1,0:T(8,128)(2,1)}, u32[]{:S(2)}, u32[]{:S(2)}) %collective-permute-start.63) | collective-permute-done | bytes 307232 | tf_op jit(solution)/shard_map/ppermute | solution.py:772
  340.8 1.7 meet.3
  344.2 1.7 collective-permute-start.67
  347.2 16.3 %byte_grad.1 = f32[1536,768]{1,0:T(8,128)} custom-call(s32[2]{0:T(128)} %copy-done.42, bf16[1536,768]{1,0:T(8,128)(2,1)} %bitcast.11, bf16[512,1280]{1,0:T(8,128)(2,1)} %get-tuple-element.285.refs_3_.refs_0_, bf16[512,1280]{1,0:T(8,128)(2,1)} %get-tuple-element.254.refs_5_.refs_1_, bf16[1024,1280]{1,0:T(8,128)(2,1)} %get-tuple-element.253.refs_4_.refs_2_, ...), custom_call_target="tpu_custom_call" | custom-call | flops 1 | bytes 1 | tf_op jit(solution)/shard_map/byte_grad/pallas_call | solution.py:706
  363.4 5.1 %collective-permute-done.67 = bf16[120,1280]{1,0:T(8,128)(2,1)} collective-permute-done((bf16[120,1280]{1,0:T(8,128)(2,1)}, bf16[120,1280]{1,0:T(8,128)(2,1)}, u32[]{:S(2)}, u32[]{:S(2)}) %collective-permute-start.67) | collective-permute-done | bytes 307232 | tf_op jit(solution)/shard_map/ppermute | solution.py:772
  368.6 1.4 convert_add_fusion
  370.0 5.5 %collective-permute-done.68.refs_7_ = bf16[128,1280]{1,0:T(8,128)(2,1)} collective-permute-done((bf16[128,1280]{1,0:T(8,128)(2,1)}, bf16[128,1280]{1,0:T(8,128)(2,1)}, u32[]{:S(2)}, u32[]{:S(2)}) %collective-permute-start.68) | collective-permute-done | bytes 327712 | tf_op jit(solution)/shard_map/ppermute | solution.py:772
  375.6 2.5 cut.3
  378.1 2.4 collective-permute-start.72
  380.6 2.0 collective-permute-start.70
  382.6 1.8 multiply_reduce_fusion
  387.9 3.5 latent_grad.1
  391.5 7.3 %collective-permute-done.71 = bf16[88,1280]{1,0:T(8,128)(2,1)S(1)} collective-permute-done((bf16[88,1280]{1,0:T(8,128)(2,1)S(1)}, bf16[88,1280]{1,0:T(8,128)(2,1)S(1)}, u32[]{:S(2)}, u32[]{:S(2)}) %collective-permute-start.71) | collective-permute-done | bytes 225312 | tf_op jit(solution)/shard_map/ppermute | solution.py:772
  (315 shorter events, 57.4 us)
Async XLA Ops:
  2.4 15.4 %collective-permute-start.1 = (bf16[96,1280]{1,0:T(8,128)(2,1)S(1)}, bf16[96,1280]{1,0:T(8,128)(2,1)S(1)}, u32[]{:S(2)}, u32[]{:S(2)}) collective-permute-start(bf16[96,1280]{1,0:T(8,128)(2,1)S(1)} %fusion.8.refs_0_), channel_id=1, source_target_pairs={{0,2},{1,3},{2,0},{3,1},{4,6},{5,7},{6,4},{7,5},{8,10},{9,11},{10,... | collective-permute-start | bytes 737288 | tf_op jit(solution)/shard_map/ppermute | solution.py:772
  6.5 11.5 %collective-permute-start = (bf16[96,1280]{1,0:T(8,128)(2,1)S(1)}, bf16[96,1280]{1,0:T(8,128)(2,1)S(1)}, u32[]{:S(2)}, u32[]{:S(2)}) collective-permute-start(bf16[96,1280]{1,0:T(8,128)(2,1)S(1)} %fusion.8.refs_0_), channel_id=1, source_target_pairs={{0,1},{1,0},{2,3},{3,2},{4,5},{5,4},{6,7},{7,6},{8,9},{9,8},{10,11... | collective-permute-start | bytes 737288 | tf_op jit(solution)/shard_map/ppermute | solution.py:772
  18.7 9.3 %collective-permute-start.3 = (bf16[96,1280]{1,0:T(8,128)(2,1)S(1)}, bf16[96,1280]{1,0:T(8,128)(2,1)S(1)}, u32[]{:S(2)}, u32[]{:S(2)}) collective-permute-start(bf16[96,1280]{1,0:T(8,128)(2,1)S(1)} %collective-permute-done.1.refs_2_), channel_id=1, source_target_pairs={{2,3},{1,0},{6,7},{5,4},{10,11},{9,8},{14,15},{13,12},{18,19},{17,... | collective-permute-start | bytes 737288 | tf_op jit(solution)/shard_map/ppermute | solution.py:908
  29.2 31.5 %collective-permute-start.6 = (bf16[368,1280]{1,0:T(8,128)(2,1)S(1)}, bf16[368,1280]{1,0:T(8,128)(2,1)}, u32[]{:S(2)}, u32[]{:S(2)}) collective-permute-start(bf16[368,1280]{1,0:T(8,128)(2,1)S(1)} %assemble.2.refs_0_.refs_8_.refs_10_.refs_9_.refs_4_), channel_id=1, source_target_pairs={{0,4},{4,0},{8,12},{12,8},{16,20},{20,16},{24,28},{28,24},{1,5},{5... | collective-permute-start | bytes 2826248 | tf_op jit(solution)/shard_map/ppermute | solution.py:772
  29.2 31.4 %collective-permute-start.5 = (bf16[368,1280]{1,0:T(8,128)(2,1)S(1)}, bf16[368,1280]{1,0:T(8,128)(2,1)S(1)}, u32[]{:S(2)}, u32[]{:S(2)}) collective-permute-start(bf16[368,1280]{1,0:T(8,128)(2,1)S(1)} %assemble.2.refs_0_.refs_8_.refs_10_.refs_9_.refs_4_), channel_id=1, source_target_pairs={{0,16},{4,20},{8,24},{12,28},{16,0},{20,4},{24,8},{28,12},{1,17},{... | collective-permute-start | bytes 2826248 | tf_op jit(solution)/shard_map/ppermute | solution.py:772
  30.8 29.8 %collective-permute-start.4 = (bf16[368,1280]{1,0:T(8,128)(2,1)S(1)}, bf16[368,1280]{1,0:T(8,128)(2,1)S(1)}, u32[]{:S(2)}, u32[]{:S(2)}) collective-permute-start(bf16[368,1280]{1,0:T(8,128)(2,1)S(1)} %assemble.2.refs_0_.refs_8_.refs_10_.refs_9_.refs_4_), channel_id=1, source_target_pairs={{0,8},{4,12},{8,0},{12,4},{16,24},{20,28},{24,16},{28,20},{1,9},{5... | collective-permute-start | bytes 2826248 | tf_op jit(solution)/shard_map/ppermute | solution.py:772
  32.6 25.5 %collective-permute-start.8 = (bf16[192,1408]{1,0:T(8,128)(2,1)S(1)}, bf16[192,1408]{1,0:T(8,128)(2,1)S(1)}, u32[]{:S(2)}, u32[]{:S(2)}) collective-permute-start(bf16[192,1408]{1,0:T(8,128)(2,1)S(1)} %fusion.1.refs_0_.refs_8_.x_ref), channel_id=1, source_target_pairs={{0,1},{1,0},{2,3},{3,2},{4,5},{5,4},{6,7},{7,6},{8,9},{9,8},{10,11... | collective-permute-start | bytes 1622024 | tf_op jit(solution)/shard_map/ppermute | solution.py:772
  32.9 27.7 %collective-permute-start.7 = (bf16[192,1408]{1,0:T(8,128)(2,1)S(1)}, bf16[192,1408]{1,0:T(8,128)(2,1)S(1)}, u32[]{:S(2)}, u32[]{:S(2)}) collective-permute-start(bf16[192,1408]{1,0:T(8,128)(2,1)S(1)} %fusion.1.refs_0_.refs_8_.x_ref), channel_id=1, source_target_pairs={{0,2},{1,3},{2,0},{3,1},{4,6},{5,7},{6,4},{7,5},{8,10},{9,11},{10,... | collective-permute-start | bytes 1622024 | tf_op jit(solution)/shard_map/ppermute | solution.py:772
  64.2 17.3 %collective-permute-start.12 = (bf16[368,1280]{1,0:T(8,128)(2,1)S(1)}, bf16[368,1280]{1,0:T(8,128)(2,1)S(1)}, u32[]{:S(2)}, u32[]{:S(2)}) collective-permute-start(bf16[368,1280]{1,0:T(8,128)(2,1)S(1)} %collective-permute-done.5.refs_4_.refs_12_.refs_14_.refs_13_.refs_8_), channel_id=1, source_target_pairs={{0,4},{4,0},{8,12},{12,8},{16,20},{20,16},{24,28},{28,24},{1,5},{5... | collective-permute-start | bytes 2826248 | tf_op jit(solution)/shard_map/ppermute | solution.py:772
  64.3 15.6 %collective-permute-start.13 = (bf16[192,1408]{1,0:T(8,128)(2,1)S(1)}, bf16[192,1408]{1,0:T(8,128)(2,1)S(1)}, u32[]{:S(2)}, u32[]{:S(2)}) collective-permute-start(bf16[192,1408]{1,0:T(8,128)(2,1)S(1)} %fusion.1.refs_0_.refs_8_.x_ref), channel_id=1, source_target_pairs={{1,2},{2,1},{5,6},{6,5},{9,10},{10,9},{13,14},{14,13},{17,18},{18,... | collective-permute-start | bytes 1622024 | tf_op jit(solution)/shard_map/ppermute | solution.py:907
  65.0 16.4 %collective-permute-start.14 = (bf16[192,1408]{1,0:T(8,128)(2,1)S(1)}, bf16[192,1408]{1,0:T(8,128)(2,1)S(1)}, u32[]{:S(2)}, u32[]{:S(2)}) collective-permute-start(bf16[192,1408]{1,0:T(8,128)(2,1)S(1)} %collective-permute-done.7.refs_2_), channel_id=1, source_target_pairs={{2,3},{1,0},{6,7},{5,4},{10,11},{9,8},{14,15},{13,12},{18,19},{17,... | collective-permute-start | bytes 1622024 | tf_op jit(solution)/shard_map/ppermute | solution.py:908
  66.4 13.6 %collective-permute-start.9 = (bf16[192,1280]{1,0:T(8,128)(2,1)S(1)}, bf16[192,1280]{1,0:T(8,128)(2,1)S(1)}, u32[]{:S(2)}, u32[]{:S(2)}) collective-permute-start(bf16[192,1280]{1,0:T(8,128)(2,1)S(1)} %slice.72), channel_id=1, source_target_pairs={{0,16},{4,20},{8,24},{12,28},{16,0},{20,4},{24,8},{28,12},{1,17},{... | collective-permute-start | bytes 1474568 | tf_op jit(solution)/shard_map/ppermute | solution.py:772
  67.0 12.4 %collective-permute-start.10 = (bf16[176,1280]{1,0:T(8,128)(2,1)S(1)}, bf16[176,1280]{1,0:T(8,128)(2,1)S(1)}, u32[]{:S(2)}, u32[]{:S(2)}) collective-permute-start(bf16[176,1280]{1,0:T(8,128)(2,1)S(1)} %slice.73), channel_id=1, source_target_pairs={{0,8},{4,12},{8,0},{12,4},{16,24},{20,28},{24,16},{28,20},{1,9},{5... | collective-permute-start | bytes 1351688 | tf_op jit(solution)/shard_map/ppermute | solution.py:772
  82.7 17.7 %collective-permute-start.16 = (bf16[120,1280]{1,0:T(8,128)(2,1)}, bf16[120,1280]{1,0:T(8,128)(2,1)}, u32[]{:S(2)}, u32[]{:S(2)}) collective-permute-start(bf16[120,1280]{1,0:T(8,128)(2,1)} %constant_dynamic-update-slice_fusion.refs_0_), channel_id=1, source_target_pairs={{0,1},{1,0},{2,3},{3,2},{4,5},{5,4},{6,7},{7,6},{8,9},{9,8},{10,11... | collective-permute-start | bytes 921608 | tf_op jit(solution)/shard_map/ppermute | solution.py:772
  83.8 16.6 %collective-permute-start.15 = (bf16[120,1280]{1,0:T(8,128)(2,1)}, bf16[120,1280]{1,0:T(8,128)(2,1)S(1)}, u32[]{:S(2)}, u32[]{:S(2)}) collective-permute-start(bf16[120,1280]{1,0:T(8,128)(2,1)} %constant_dynamic-update-slice_fusion.refs_0_), channel_id=1, source_target_pairs={{0,2},{1,3},{2,0},{3,1},{4,6},{5,7},{6,4},{7,5},{8,10},{9,11},{10,... | collective-permute-start | bytes 921608 | tf_op jit(solution)/shard_map/ppermute | solution.py:772
  100.4 12.7 %collective-permute-start.19 = (bf16[120,1280]{1,0:T(8,128)(2,1)}, bf16[120,1280]{1,0:T(8,128)(2,1)S(1)}, u32[]{:S(2)}, u32[]{:S(2)}) collective-permute-start(bf16[120,1280]{1,0:T(8,128)(2,1)} %constant_dynamic-update-slice_fusion.refs_0_), channel_id=1, source_target_pairs={{1,2},{2,1},{5,6},{6,5},{9,10},{10,9},{13,14},{14,13},{17,18},{18,... | collective-permute-start | bytes 921608 | tf_op jit(solution)/shard_map/ppermute | solution.py:907
  101.1 12.1 %collective-permute-start.20 = (bf16[120,1280]{1,0:T(8,128)(2,1)S(1)}, bf16[120,1280]{1,0:T(8,128)(2,1)S(1)}, u32[]{:S(2)}, u32[]{:S(2)}) collective-permute-start(bf16[120,1280]{1,0:T(8,128)(2,1)S(1)} %collective-permute-done.15.refs_2_), channel_id=1, source_target_pairs={{2,3},{1,0},{6,7},{5,4},{10,11},{9,8},{14,15},{13,12},{18,19},{17,... | collective-permute-start | bytes 921608 | tf_op jit(solution)/shard_map/ppermute | solution.py:908
  114.8 28.5 %collective-permute-start.28 = (bf16[480,1280]{1,0:T(8,128)(2,1)S(1)}, bf16[480,1280]{1,0:T(8,128)(2,1)S(1)}, u32[]{:S(2)}, u32[]{:S(2)}) collective-permute-start(bf16[480,1280]{1,0:T(8,128)(2,1)S(1)} %assemble.3.refs_20_), channel_id=1, source_target_pairs={{0,16},{4,20},{8,24},{12,28},{16,0},{20,4},{24,8},{28,12},{1,17},{... | collective-permute-start | bytes 3686408 | tf_op jit(solution)/shard_map/ppermute | solution.py:772
  115.7 27.8 %collective-permute-start.27 = (bf16[480,1280]{1,0:T(8,128)(2,1)S(1)}, bf16[480,1280]{1,0:T(8,128)(2,1)S(1)}, u32[]{:S(2)}, u32[]{:S(2)}) collective-permute-start(bf16[480,1280]{1,0:T(8,128)(2,1)S(1)} %assemble.3.refs_20_), channel_id=1, source_target_pairs={{0,8},{4,12},{8,0},{12,4},{16,24},{20,28},{24,16},{28,20},{1,9},{5... | collective-permute-start | bytes 3686408 | tf_op jit(solution)/shard_map/ppermute | solution.py:772
  116.3 27.1 %collective-permute-start.23 = (bf16[64,1408]{1,0:T(8,128)(2,1)}, bf16[64,1408]{1,0:T(8,128)(2,1)S(1)}, u32[]{:S(2)}, u32[]{:S(2)}) collective-permute-start(bf16[64,1408]{1,0:T(8,128)(2,1)} %get-tuple-element.188), channel_id=1, source_target_pairs={{0,3},{1,2},{2,1},{3,0},{4,7},{5,6},{6,5},{7,4},{8,11},{9,10},{10,... | collective-permute-start | bytes 540680 | tf_op jit(solution)/shard_map/ppermute | solution.py:772
  118.7 24.6 %collective-permute-start.22 = (bf16[64,1408]{1,0:T(8,128)(2,1)}, bf16[64,1408]{1,0:T(8,128)(2,1)S(1)}, u32[]{:S(2)}, u32[]{:S(2)}) collective-permute-start(bf16[64,1408]{1,0:T(8,128)(2,1)} %get-tuple-element.186), channel_id=1, source_target_pairs={{0,2},{1,3},{2,0},{3,1},{4,6},{5,7},{6,4},{7,5},{8,10},{9,11},{10,... | collective-permute-start | bytes 540680 | tf_op jit(solution)/shard_map/ppermute | solution.py:772
  120.8 22.6 %collective-permute-start.21 = (bf16[64,1408]{1,0:T(8,128)(2,1)}, bf16[64,1408]{1,0:T(8,128)(2,1)}, u32[]{:S(2)}, u32[]{:S(2)}) collective-permute-start(bf16[64,1408]{1,0:T(8,128)(2,1)} %get-tuple-element.183), channel_id=1, source_target_pairs={{0,1},{1,0},{2,3},{3,2},{4,5},{5,4},{6,7},{7,6},{8,9},{9,8},{10,11... | collective-permute-start | bytes 540680 | tf_op jit(solution)/shard_map/ppermute | solution.py:772
  143.5 34.8 %collective-permute-start.29 = (bf16[240,1280]{1,0:T(8,128)(2,1)S(1)}, bf16[240,1280]{1,0:T(8,128)(2,1)S(1)}, u32[]{:S(2)}, u32[]{:S(2)}) collective-permute-start(bf16[240,1280]{1,0:T(8,128)(2,1)S(1)} %slice.74), channel_id=1, source_target_pairs={{0,16},{4,20},{8,24},{12,28},{16,0},{20,4},{24,8},{28,12},{1,17},{... | collective-permute-start | bytes 1843208 | tf_op jit(solution)/shard_map/ppermute | solution.py:772
  145.1 34.1 %collective-permute-start.30 = (bf16[240,1280]{1,0:T(8,128)(2,1)S(1)}, bf16[240,1280]{1,0:T(8,128)(2,1)S(1)}, u32[]{:S(2)}, u32[]{:S(2)}) collective-permute-start(bf16[240,1280]{1,0:T(8,128)(2,1)S(1)} %slice.75), channel_id=1, source_target_pairs={{0,8},{4,12},{8,0},{12,4},{16,24},{20,28},{24,16},{28,20},{1,9},{5... | collective-permute-start | bytes 1843208 | tf_op jit(solution)/shard_map/ppermute | solution.py:772
  145.7 13.3 %collective-permute-start.26 = (bf16[128,1408]{1,0:T(8,128)(2,1)S(1)}, bf16[128,1408]{1,0:T(8,128)(2,1)S(1)}, u32[]{:S(2)}, u32[]{:S(2)}) collective-permute-start(bf16[128,1408]{1,0:T(8,128)(2,1)S(1)} %copy-done.92), channel_id=1, source_target_pairs={{0,3},{1,2},{2,1},{3,0},{4,7},{5,6},{6,5},{7,4},{8,11},{9,10},{10,... | collective-permute-start | bytes 1081352 | tf_op jit(solution)/shard_map/ppermute | solution.py:772
  147.1 31.2 %collective-permute-start.25 = (bf16[128,1408]{1,0:T(8,128)(2,1)S(1)}, bf16[128,1408]{1,0:T(8,128)(2,1)S(1)}, u32[]{:S(2)}, u32[]{:S(2)}) collective-permute-start(bf16[128,1408]{1,0:T(8,128)(2,1)S(1)} %copy-done.91), channel_id=1, source_target_pairs={{0,2},{1,3},{2,0},{3,1},{4,6},{5,7},{6,4},{7,5},{8,10},{9,11},{10,... | collective-permute-start | bytes 1081352 | tf_op jit(solution)/shard_map/ppermute | solution.py:772
  149.6 28.8 %collective-permute-start.24 = (bf16[128,1408]{1,0:T(8,128)(2,1)S(1)}, bf16[128,1408]{1,0:T(8,128)(2,1)S(1)}, u32[]{:S(2)}, u32[]{:S(2)}) collective-permute-start(bf16[128,1408]{1,0:T(8,128)(2,1)S(1)} %copy-done.90), channel_id=1, source_target_pairs={{0,1},{1,0},{2,3},{3,2},{4,5},{5,4},{6,7},{7,6},{8,9},{9,8},{10,11... | collective-permute-start | bytes 1081352 | tf_op jit(solution)/shard_map/ppermute | solution.py:772
  179.2 8.3 %collective-permute-start.31 = (bf16[480,1280]{1,0:T(8,128)(2,1)S(1)}, bf16[480,1280]{1,0:T(8,128)(2,1)S(1)}, u32[]{:S(2)}, u32[]{:S(2)}) collective-permute-start(bf16[480,1280]{1,0:T(8,128)(2,1)S(1)} %assemble.3.refs_20_), channel_id=1, source_target_pairs={{0,4},{4,0},{8,12},{12,8},{16,20},{20,16},{24,28},{28,24},{1,5},{5... | collective-permute-start | bytes 3686408 | tf_op jit(solution)/shard_map/ppermute | solution.py:772
  179.3 8.2 %collective-permute-start.32 = (bf16[480,1280]{1,0:T(8,128)(2,1)S(1)}, bf16[480,1280]{1,0:T(8,128)(2,1)S(1)}, u32[]{:S(2)}, u32[]{:S(2)}) collective-permute-start(bf16[480,1280]{1,0:T(8,128)(2,1)S(1)} %collective-permute-done.27.refs_22_), channel_id=1, source_target_pairs={{0,4},{4,0},{8,12},{12,8},{16,20},{20,16},{24,28},{28,24},{1,5},{5... | collective-permute-start | bytes 3686408 | tf_op jit(solution)/shard_map/ppermute | solution.py:772
  179.8 7.7 %collective-permute-start.33 = (bf16[480,1280]{1,0:T(8,128)(2,1)S(1)}, bf16[480,1280]{1,0:T(8,128)(2,1)S(1)}, u32[]{:S(2)}, u32[]{:S(2)}) collective-permute-start(bf16[480,1280]{1,0:T(8,128)(2,1)S(1)} %collective-permute-done.28.refs_24_), channel_id=1, source_target_pairs={{0,4},{4,0},{8,12},{12,8},{16,20},{20,16},{24,28},{28,24},{1,5},{5... | collective-permute-start | bytes 3686408 | tf_op jit(solution)/shard_map/ppermute | solution.py:772
  179.9 6.7 %collective-permute-start.34 = (bf16[240,1280]{1,0:T(8,128)(2,1)S(1)}, bf16[240,1280]{1,0:T(8,128)(2,1)S(1)}, u32[]{:S(2)}, u32[]{:S(2)}) collective-permute-start(bf16[240,1280]{1,0:T(8,128)(2,1)S(1)} %collective-permute-done.29.refs_26_), channel_id=1, source_target_pairs={{0,4},{4,0},{8,12},{12,8},{16,20},{20,16},{24,28},{28,24},{1,5},{5... | collective-permute-start | bytes 1843208 | tf_op jit(solution)/shard_map/ppermute | solution.py:772
  180.3 7.2 %collective-permute-start.35 = (bf16[240,1280]{1,0:T(8,128)(2,1)S(1)}, bf16[240,1280]{1,0:T(8,128)(2,1)S(1)}, u32[]{:S(2)}, u32[]{:S(2)}) collective-permute-start(bf16[240,1280]{1,0:T(8,128)(2,1)S(1)} %collective-permute-done.30.refs_27_), channel_id=1, source_target_pairs={{0,4},{4,0},{8,12},{12,8},{16,20},{20,16},{24,28},{28,24},{1,5},{5... | collective-permute-start | bytes 1843208 | tf_op jit(solution)/shard_map/ppermute | solution.py:772
  203.9 8.9 %collective-permute-start.37 = (bf16[64,1408]{1,0:T(8,128)(2,1)}, bf16[64,1408]{1,0:T(8,128)(2,1)S(1)}, u32[]{:S(2)}, u32[]{:S(2)}) collective-permute-start(bf16[64,1408]{1,0:T(8,128)(2,1)} %get-tuple-element.222.refs_0_), channel_id=1, source_target_pairs={{0,1},{1,0},{2,3},{3,2},{4,5},{5,4},{6,7},{7,6},{8,9},{9,8},{10,11... | collective-permute-start | bytes 540680 | tf_op jit(solution)/shard_map/ppermute | solution.py:772
  203.9 11.7 %collective-permute-start.36 = (bf16[64,1408]{1,0:T(8,128)(2,1)}, bf16[64,1408]{1,0:T(8,128)(2,1)S(1)}, u32[]{:S(2)}, u32[]{:S(2)}) collective-permute-start(bf16[64,1408]{1,0:T(8,128)(2,1)} %get-tuple-element.222.refs_0_), channel_id=1, source_target_pairs={{0,2},{1,3},{2,0},{3,1},{4,6},{5,7},{6,4},{7,5},{8,10},{9,11},{10,... | collective-permute-start | bytes 540680 | tf_op jit(solution)/shard_map/ppermute | solution.py:772
  215.6 10.5 %collective-permute-start.40 = (bf16[480,1280]{1,0:T(8,128)(2,1)}, bf16[480,1280]{1,0:T(8,128)(2,1)S(1)}, u32[]{:S(2)}, u32[]{:S(2)}) collective-permute-start(bf16[480,1280]{1,0:T(8,128)(2,1)} %get-tuple-element.219), channel_id=1, source_target_pairs={{0,4},{4,0},{8,12},{12,8},{16,20},{20,16},{24,28},{28,24},{1,5},{5... | collective-permute-start | bytes 3686408 | tf_op jit(solution)/shard_map/ppermute | solution.py:772
  215.6 11.5 %collective-permute-start.39 = (bf16[480,1280]{1,0:T(8,128)(2,1)}, bf16[480,1280]{1,0:T(8,128)(2,1)S(1)}, u32[]{:S(2)}, u32[]{:S(2)}) collective-permute-start(bf16[480,1280]{1,0:T(8,128)(2,1)} %get-tuple-element.217), channel_id=1, source_target_pairs={{0,4},{4,0},{8,12},{12,8},{16,20},{20,16},{24,28},{28,24},{1,5},{5... | collective-permute-start | bytes 3686408 | tf_op jit(solution)/shard_map/ppermute | solution.py:772
  216.1 12.1 %collective-permute-start.38 = (bf16[480,1280]{1,0:T(8,128)(2,1)}, bf16[480,1280]{1,0:T(8,128)(2,1)S(1)}, u32[]{:S(2)}, u32[]{:S(2)}) collective-permute-start(bf16[480,1280]{1,0:T(8,128)(2,1)} %get-tuple-element.215), channel_id=1, source_target_pairs={{0,4},{4,0},{8,12},{12,8},{16,20},{20,16},{24,28},{28,24},{1,5},{5... | collective-permute-start | bytes 3686408 | tf_op jit(solution)/shard_map/ppermute | solution.py:772
  217.2 8.9 %collective-permute-start.42 = (bf16[64,1408]{1,0:T(8,128)(2,1)S(1)}, bf16[64,1408]{1,0:T(8,128)(2,1)S(1)}, u32[]{:S(2)}, u32[]{:S(2)}) collective-permute-start(bf16[64,1408]{1,0:T(8,128)(2,1)S(1)} %collective-permute-done.36.refs_2_), channel_id=1, source_target_pairs={{2,3},{1,0},{6,7},{5,4},{10,11},{9,8},{14,15},{13,12},{18,19},{17,... | collective-permute-start | bytes 540680 | tf_op jit(solution)/shard_map/ppermute | solution.py:908
  228.2 24.1 %collective-permute-start.45 = (bf16[480,1280]{1,0:T(8,128)(2,1)}, bf16[480,1280]{1,0:T(8,128)(2,1)S(1)}, u32[]{:S(2)}, u32[]{:S(2)}) collective-permute-start(bf16[480,1280]{1,0:T(8,128)(2,1)} %get-tuple-element.232), channel_id=1, source_target_pairs={{0,4},{4,0},{8,12},{12,8},{16,20},{20,16},{24,28},{28,24},{1,5},{5... | collective-permute-start | bytes 3686408 | tf_op jit(solution)/shard_map/ppermute | solution.py:772
  230.9 21.4 %collective-permute-start.43 = (bf16[240,1280]{1,0:T(8,128)(2,1)}, bf16[240,1280]{1,0:T(8,128)(2,1)}, u32[]{:S(2)}, u32[]{:S(2)}) collective-permute-start(bf16[240,1280]{1,0:T(8,128)(2,1)} %get-tuple-element.228), channel_id=1, source_target_pairs={{0,16},{4,20},{8,24},{12,28},{16,0},{20,4},{24,8},{28,12},{1,17},{... | collective-permute-start | bytes 1843208 | tf_op jit(solution)/shard_map/ppermute | solution.py:772
  231.8 20.6 %collective-permute-start.44 = (bf16[240,1280]{1,0:T(8,128)(2,1)}, bf16[240,1280]{1,0:T(8,128)(2,1)}, u32[]{:S(2)}, u32[]{:S(2)}) collective-permute-start(bf16[240,1280]{1,0:T(8,128)(2,1)} %get-tuple-element.230), channel_id=1, source_target_pairs={{0,8},{4,12},{8,0},{12,4},{16,24},{20,28},{24,16},{28,20},{1,9},{5... | collective-permute-start | bytes 1843208 | tf_op jit(solution)/shard_map/ppermute | solution.py:772
  233.2 16.8 %collective-permute-start.47 = (bf16[128,1408]{1,0:T(8,128)(2,1)S(1)}, bf16[128,1408]{1,0:T(8,128)(2,1)}, u32[]{:S(2)}, u32[]{:S(2)}) collective-permute-start(bf16[128,1408]{1,0:T(8,128)(2,1)S(1)} %copy-done.67), channel_id=1, source_target_pairs={{0,1},{1,0},{2,3},{3,2},{4,5},{5,4},{6,7},{7,6},{8,9},{9,8},{10,11... | collective-permute-start | bytes 1081352 | tf_op jit(solution)/shard_map/ppermute | solution.py:772
  233.3 19.1 %collective-permute-start.46 = (bf16[128,1408]{1,0:T(8,128)(2,1)S(1)}, bf16[128,1408]{1,0:T(8,128)(2,1)}, u32[]{:S(2)}, u32[]{:S(2)}) collective-permute-start(bf16[128,1408]{1,0:T(8,128)(2,1)S(1)} %copy-done.67), channel_id=1, source_target_pairs={{0,2},{1,3},{2,0},{3,1},{4,6},{5,7},{6,4},{7,5},{8,10},{9,11},{10,... | collective-permute-start | bytes 1081352 | tf_op jit(solution)/shard_map/ppermute | solution.py:772
  258.1 33.2 %collective-permute-start.53 = (bf16[480,1280]{1,0:T(8,128)(2,1)}, bf16[480,1280]{1,0:T(8,128)(2,1)S(1)}, u32[]{:S(2)}, u32[]{:S(2)}) collective-permute-start(bf16[480,1280]{1,0:T(8,128)(2,1)} %get-tuple-element.249), channel_id=1, source_target_pairs={{0,8},{4,12},{8,0},{12,4},{16,24},{20,28},{24,16},{28,20},{1,9},{5... | collective-permute-start | bytes 3686408 | tf_op jit(solution)/shard_map/ppermute | solution.py:772
  258.6 32.7 %collective-permute-start.54 = (bf16[480,1280]{1,0:T(8,128)(2,1)}, bf16[480,1280]{1,0:T(8,128)(2,1)}, u32[]{:S(2)}, u32[]{:S(2)}) collective-permute-start(bf16[480,1280]{1,0:T(8,128)(2,1)} %get-tuple-element.250), channel_id=1, source_target_pairs={{0,16},{4,20},{8,24},{12,28},{16,0},{20,4},{24,8},{28,12},{1,17},{... | collective-permute-start | bytes 3686408 | tf_op jit(solution)/shard_map/ppermute | solution.py:772
  260.5 11.0 %collective-permute-start.49 = (bf16[128,1408]{1,0:T(8,128)(2,1)}, bf16[128,1408]{1,0:T(8,128)(2,1)S(1)}, u32[]{:S(2)}, u32[]{:S(2)}) collective-permute-start(bf16[128,1408]{1,0:T(8,128)(2,1)} %collective-permute-done.46.refs_2_), channel_id=1, source_target_pairs={{2,3},{1,0},{6,7},{5,4},{10,11},{9,8},{14,15},{13,12},{18,19},{17,... | collective-permute-start | bytes 1081352 | tf_op jit(solution)/shard_map/ppermute | solution.py:908
  271.5 19.8 %collective-permute-start.50 = (bf16[64,1280]{1,0:T(8,128)(2,1)}, bf16[64,1280]{1,0:T(8,128)(2,1)S(1)}, u32[]{:S(2)}, u32[]{:S(2)}) collective-permute-start(bf16[64,1280]{1,0:T(8,128)(2,1)} %get-tuple-element.244), channel_id=1, source_target_pairs={{0,1},{1,0},{2,3},{3,2},{4,5},{5,4},{6,7},{7,6},{8,9},{9,8},{10,11... | collective-permute-start | bytes 491528 | tf_op jit(solution)/shard_map/ppermute | solution.py:772
  272.2 19.1 %collective-permute-start.51 = (bf16[64,1280]{1,0:T(8,128)(2,1)}, bf16[64,1280]{1,0:T(8,128)(2,1)S(1)}, u32[]{:S(2)}, u32[]{:S(2)}) collective-permute-start(bf16[64,1280]{1,0:T(8,128)(2,1)} %get-tuple-element.246), channel_id=1, source_target_pairs={{0,2},{1,3},{2,0},{3,1},{4,6},{5,7},{6,4},{7,5},{8,10},{9,11},{10,... | collective-permute-start | bytes 491528 | tf_op jit(solution)/shard_map/ppermute | solution.py:772
  273.2 18.1 %collective-permute-start.52 = (bf16[64,1280]{1,0:T(8,128)(2,1)}, bf16[64,1280]{1,0:T(8,128)(2,1)}, u32[]{:S(2)}, u32[]{:S(2)}) collective-permute-start(bf16[64,1280]{1,0:T(8,128)(2,1)} %get-tuple-element.248), channel_id=1, source_target_pairs={{0,3},{1,2},{2,1},{3,0},{4,7},{5,6},{6,5},{7,4},{8,11},{9,10},{10,... | collective-permute-start | bytes 491528 | tf_op jit(solution)/shard_map/ppermute | solution.py:772
  296.9 20.0 %collective-permute-start.55 = (bf16[128,1280]{1,0:T(8,128)(2,1)}, bf16[128,1280]{1,0:T(8,128)(2,1)S(1)}, u32[]{:S(2)}, u32[]{:S(2)}) collective-permute-start(bf16[128,1280]{1,0:T(8,128)(2,1)} %get-tuple-element.262), channel_id=1, source_target_pairs={{0,1},{1,0},{2,3},{3,2},{4,5},{5,4},{6,7},{7,6},{8,9},{9,8},{10,11... | collective-permute-start | bytes 983048 | tf_op jit(solution)/shard_map/ppermute | solution.py:772
  296.9 20.0 %collective-permute-start.57 = (bf16[128,1280]{1,0:T(8,128)(2,1)}, bf16[128,1280]{1,0:T(8,128)(2,1)S(1)}, u32[]{:S(2)}, u32[]{:S(2)}) collective-permute-start(bf16[128,1280]{1,0:T(8,128)(2,1)} %get-tuple-element.264), channel_id=1, source_target_pairs={{3,2},{0,1},{7,6},{4,5},{11,10},{8,9},{15,14},{12,13},{19,18},{16,... | collective-permute-start | bytes 983048 | tf_op jit(solution)/shard_map/ppermute | solution.py:913
  300.8 16.1 %collective-permute-start.56 = (bf16[128,1280]{1,0:T(8,128)(2,1)}, bf16[128,1280]{1,0:T(8,128)(2,1)S(1)}, u32[]{:S(2)}, u32[]{:S(2)}) collective-permute-start(bf16[128,1280]{1,0:T(8,128)(2,1)} %get-tuple-element.264), channel_id=1, source_target_pairs={{1,2},{2,1},{5,6},{6,5},{9,10},{10,9},{13,14},{14,13},{17,18},{18,... | collective-permute-start | bytes 983048 | tf_op jit(solution)/shard_map/ppermute | solution.py:912
  322.3 18.5 %collective-permute-start.62 = (bf16[192,1280]{1,0:T(8,128)(2,1)S(1)}, bf16[192,1280]{1,0:T(8,128)(2,1)S(1)}, u32[]{:S(2)}, u32[]{:S(2)}) collective-permute-start(bf16[192,1280]{1,0:T(8,128)(2,1)S(1)} %add_convert_fusion.2), channel_id=1, source_target_pairs={{0,8},{4,12},{8,0},{12,4},{16,24},{20,28},{24,16},{28,20},{1,9},{5... | collective-permute-start | bytes 1474568 | tf_op jit(solution)/shard_map/ppermute | solution.py:772
  323.8 17.0 %collective-permute-start.61 = (bf16[160,1280]{1,0:T(8,128)(2,1)S(1)}, bf16[160,1280]{1,0:T(8,128)(2,1)S(1)}, u32[]{:S(2)}, u32[]{:S(2)}) collective-permute-start(bf16[160,1280]{1,0:T(8,128)(2,1)S(1)} %add_convert_fusion.3), channel_id=1, source_target_pairs={{0,16},{4,20},{8,24},{12,28},{16,0},{20,4},{24,8},{28,12},{1,17},{... | collective-permute-start | bytes 1228808 | tf_op jit(solution)/shard_map/ppermute | solution.py:772
  324.6 12.1 %collective-permute-start.64 = (bf16[120,1280]{1,0:T(8,128)(2,1)S(1)}, bf16[120,1280]{1,0:T(8,128)(2,1)}, u32[]{:S(2)}, u32[]{:S(2)}) collective-permute-start(bf16[120,1280]{1,0:T(8,128)(2,1)S(1)} %copy-done.49), channel_id=1, source_target_pairs={{0,3},{1,2},{2,1},{3,0},{4,7},{5,6},{6,5},{7,4},{8,11},{9,10},{10,... | collective-permute-start | bytes 921608 | tf_op jit(solution)/shard_map/ppermute | solution.py:772
  325.6 15.2 %collective-permute-start.63 = (bf16[120,1280]{1,0:T(8,128)(2,1)S(1)}, bf16[120,1280]{1,0:T(8,128)(2,1)}, u32[]{:S(2)}, u32[]{:S(2)}) collective-permute-start(bf16[120,1280]{1,0:T(8,128)(2,1)S(1)} %copy-done.47), channel_id=1, source_target_pairs={{0,1},{1,0},{2,3},{3,2},{4,5},{5,4},{6,7},{7,6},{8,9},{9,8},{10,11... | collective-permute-start | bytes 921608 | tf_op jit(solution)/shard_map/ppermute | solution.py:772
  342.5 33.0 %collective-permute-start.65 = (bf16[352,1280]{1,0:T(8,128)(2,1)}, bf16[352,1280]{1,0:T(8,128)(2,1)S(1)}, u32[]{:S(2)}, u32[]{:S(2)}) collective-permute-start(bf16[352,1280]{1,0:T(8,128)(2,1)} %get-tuple-element.283), channel_id=1, source_target_pairs={{0,8},{4,12},{8,0},{12,4},{16,24},{20,28},{24,16},{28,20},{1,9},{5... | collective-permute-start | bytes 2703368 | tf_op jit(solution)/shard_map/ppermute | solution.py:772
  343.0 32.5 %collective-permute-start.66 = (bf16[352,1280]{1,0:T(8,128)(2,1)}, bf16[352,1280]{1,0:T(8,128)(2,1)}, u32[]{:S(2)}, u32[]{:S(2)}) collective-permute-start(bf16[352,1280]{1,0:T(8,128)(2,1)} %get-tuple-element.284), channel_id=1, source_target_pairs={{0,16},{4,20},{8,24},{12,28},{16,0},{20,4},{24,8},{28,12},{1,17},{... | collective-permute-start | bytes 2703368 | tf_op jit(solution)/shard_map/ppermute | solution.py:772
  344.2 31.3 %collective-permute-start.69 = (bf16[352,1280]{1,0:T(8,128)(2,1)}, bf16[352,1280]{1,0:T(8,128)(2,1)}, u32[]{:S(2)}, u32[]{:S(2)}) collective-permute-start(bf16[352,1280]{1,0:T(8,128)(2,1)} %get-tuple-element.291), channel_id=1, source_target_pairs={{0,4},{4,0},{8,12},{12,8},{16,20},{20,16},{24,28},{28,24},{1,5},{5... | collective-permute-start | bytes 2703368 | tf_op jit(solution)/shard_map/ppermute | solution.py:772
  344.2 24.3 %collective-permute-start.67 = (bf16[120,1280]{1,0:T(8,128)(2,1)}, bf16[120,1280]{1,0:T(8,128)(2,1)}, u32[]{:S(2)}, u32[]{:S(2)}) collective-permute-start(bf16[120,1280]{1,0:T(8,128)(2,1)} %get-tuple-element.287), channel_id=1, source_target_pairs={{0,2},{1,3},{2,0},{3,1},{4,6},{5,7},{6,4},{7,5},{8,10},{9,11},{10,... | collective-permute-start | bytes 921608 | tf_op jit(solution)/shard_map/ppermute | solution.py:772
  345.9 29.6 %collective-permute-start.68 = (bf16[128,1280]{1,0:T(8,128)(2,1)}, bf16[128,1280]{1,0:T(8,128)(2,1)}, u32[]{:S(2)}, u32[]{:S(2)}) collective-permute-start(bf16[128,1280]{1,0:T(8,128)(2,1)} %add_convert_fusion.4), channel_id=1, source_target_pairs={{0,2},{1,3},{2,0},{3,1},{4,6},{5,7},{6,4},{7,5},{8,10},{9,11},{10,... | collective-permute-start | bytes 983048 | tf_op jit(solution)/shard_map/ppermute | solution.py:772
  378.1 13.4 %collective-permute-start.72 = (bf16[88,1280]{1,0:T(8,128)(2,1)S(1)}, bf16[88,1280]{1,0:T(8,128)(2,1)S(1)}, u32[]{:S(2)}, u32[]{:S(2)}) collective-permute-start(bf16[88,1280]{1,0:T(8,128)(2,1)S(1)} %get-tuple-element.301), channel_id=1, source_target_pairs={{0,3},{1,2},{2,1},{3,0},{4,7},{5,6},{6,5},{7,4},{8,11},{9,10},{10,... | collective-permute-start | bytes 675848 | tf_op jit(solution)/shard_map/ppermute | solution.py:772
  380.6 18.3 %collective-permute-start.71 = (bf16[88,1280]{1,0:T(8,128)(2,1)S(1)}, bf16[88,1280]{1,0:T(8,128)(2,1)S(1)}, u32[]{:S(2)}, u32[]{:S(2)}) collective-permute-start(bf16[88,1280]{1,0:T(8,128)(2,1)S(1)} %get-tuple-element.299), channel_id=1, source_target_pairs={{0,2},{1,3},{2,0},{3,1},{4,6},{5,7},{6,4},{7,5},{8,10},{9,11},{10,... | collective-permute-start | bytes 675848 | tf_op jit(solution)/shard_map/ppermute | solution.py:772
  380.6 18.3 %collective-permute-start.70 = (bf16[88,1280]{1,0:T(8,128)(2,1)S(1)}, bf16[88,1280]{1,0:T(8,128)(2,1)S(1)}, u32[]{:S(2)}, u32[]{:S(2)}) collective-permute-start(bf16[88,1280]{1,0:T(8,128)(2,1)S(1)} %get-tuple-element.297), channel_id=1, source_target_pairs={{0,1},{1,0},{2,3},{3,2},{4,5},{5,4},{6,7},{7,6},{8,9},{9,8},{10,11... | collective-permute-start | bytes 675848 | tf_op jit(solution)/shard_map/ppermute | solution.py:772
  (102 other events, 1253.2 us)

commit v3 on v2

--- a/solution.py
+++ b/solution.py
@@ -506,7 +506,7 @@
 ):
     count_parts = len(parts)
     lat = keys.shape[1]
-    block = byte_ids.shape[1]
+    block = byte_ids.shape[2]
     latents = groups * group
     count = len(held.flat)
     score_scale = 1.0 / math.sqrt(HEAD_DIM)
@@ -531,7 +531,8 @@
 
         message = jnp.concatenate(group_values(part_refs, place_ref), axis=0)
         stats = jnp.transpose(message[:, lat:].astype(F32), (1, 0))
-        allowed = bid_ref[0] == stats[6 * HEADS : 6 * HEADS + 1, :]
+        byte_ids = jnp.transpose(jnp.broadcast_to(bid_ref[0], (LANES, block)), (1, 0))[:, :1]
+        allowed = byte_ids == stats[6 * HEADS : 6 * HEADS + 1, :]
         for head in range(HEADS):
             at, _ = head_window(head)
             mask = head_lanes(head)
@@ -583,7 +584,7 @@
                 pl.BlockSpec((latents, lat), own_block),
                 pl.BlockSpec((block, lat), row_block),
                 pl.BlockSpec((block, lat), row_block),
-                pl.BlockSpec((1, block, 1), lambda i, p: (first + i, 0, 0)),
+                pl.BlockSpec((1, 1, block), lambda i, p: (first + i, 0, 0)),
             ]
             + [any_spec()] * count,
             out_specs=[
@@ -776,6 +777,23 @@
     return lax.optimization_barrier((value, *earlier))[0]
 
 
+def passed(value, *earlier, cost):
+    def kernel(in_ref, out_ref):
+        pass
+
+    return pl.pallas_call(
+        kernel,
+        in_specs=[any_spec()],
+        out_specs=any_spec(),
+        out_shape=shape(value.shape, value.dtype),
+        input_output_aliases={0: 0},
+        cost_estimate=pl.CostEstimate(
+            flops=int(cost * 1.1e9), bytes_accessed=1, transcendentals=0
+        ),
+        name="passed",
+    )(tie(value, *earlier))
+
+
 def swap_all(parts, size):
     return [swap(parts[j], "fsdp", size, j) for j in range(1, size)]
 
@@ -957,7 +975,7 @@
     latent_message = jnp.concatenate([latents_flat, ids], axis=1)
     byte_ids = lax.dynamic_slice_in_dim(byte_segments, own * byte_local, byte_local, axis=1)
     byte_ids = byte_ids.astype(F32)
-    byte_row, byte_column = byte_ids[:, None, :], byte_ids[:, :, None]
+    byte_row = byte_ids[:, None, :]
     sizes_one, sizes_two = (kr, kr, qr), (qr, qr, qr)
     half_one, half_two = 2 * key_rows, up_to(3 * query_rows // 2, 16)
     spans_one = {
@@ -991,7 +1009,7 @@
 
     def attend_back(index, one, parts, saved):
         return attend_back_call(
-            place, parts, *saved, byte_column, one, n_f, group, *cuts[index]
+            place, parts, *saved, byte_row, one, n_f, group, *cuts[index]
         )
 
     def weight_grads(lefts, first, last):
@@ -1100,6 +1118,7 @@
     attended_last = [found[0], *[pass_on(found[j], j) for j in range(1, n_f)]]
     plan.gate = [x, y, queries_last, *attended_first[1:]]
     low, high = send(x[:half_two], 4), send(y[half_two:], 2)
+    attended_last[1] = passed(attended_last[1], *attended_last[2:], cost=4)
     plan.gate = [low, high, *attended_last[1:]]
     pairs = [(v, send(v, 1)) for v in (block, x, y, low, high)]
     two = Held(*square_pieces(block, pairs, half_two), spans_two)
@@ -1111,37 +1130,34 @@
     grads = feed_grads((attended_t, normed_t, act_t), (branch, inner, cot_flat))
     plan.gate = near
     first_parts = [first, near[1], near[0], *plan.relay(first, near[0])]
-    arrived = {d: send(grads[d + 1], 1) for d in (6, 4, 2)}
+    near = [pass_on(last, 2), pass_on(last, 1)]
+    arrived = {d: send(grads[d + 1], 1) for d in (6, 4)}
+    low = add(grads[6][:half_two], arrived[6][:half_two])
+    high = add(grads[6][half_two:], arrived[6][half_two:])
     plan.gate = [*arrived.values(), *first_parts[3:]]
-    low = add(tie(grads[6][:half_two], *plan.gate), arrived[6][:half_two])
-    high = add(tie(grads[6][half_two:], *plan.gate), arrived[6][half_two:])
     low, high = send(low, 2), send(high, 4)
-    near = [pass_on(last, 2), pass_on(last, 1)]
+    arrived[2] = send(grads[3], 1)
+    back_first = attend_back(0, one, plan.tied(first_parts), (queries_first, keys, values))
+    plan.gate = [low, high, arrived[2], *near, back_first[0]]
+    last_parts = [last, near[1], near[0], *plan.relay(last, near[0])]
     arrived[0] = send(grads[1], 1)
-    back_first = attend_back(0, one, plan.tied(first_parts), (queries_first, keys, values))
-    plan.gate = [low, high, arrived[0], *near, back_first[0]]
-    last_parts = [last, near[1], near[0], *plan.relay(last, near[0])]
     x, y = meet_call(
         (grads[2], arrived[2]), tie(high, *plan.gate), (grads[4], arrived[4]), low, half_two
     )
-    plan.gate = [x, y]
+    plan.gate = [x, y, arrived[0], *last_parts[3:]]
     terms_two = [grads[0], arrived[0], send(x, 2), send(y, 4)]
-    plan.gate = [x, y, *last_parts[3:]]
     ups_first = back_first[3:]
     ups_first = [ups_first[0], *[pass_on(ups_first[j], j) for j in range(1, n_f)]]
     back_last = attend_back(1, one, plan.tied(last_parts), (queries_last, keys, values))
-    plan.gate = [back_last[0], *ups_first[1:], *terms_two[2:]]
-    cut_two = cut_terms(place, own, plan.tied(terms_two), sizes_two, n_f)
+    plan.gate = [back_last[0], *ups_first[1:]]
     ups = back_last[3:]
-    plan.gate = [cut_two[0]]
     near = [pass_on(ups[1], 1), *plan.spread(ups[3])]
-    arrived_two = [pass_on(cut_two[1], 1), pass_on(cut_two[3], 3)]
     grads = weight_grads(
         ((byte_t,), (latent_t_first, latent_t_last)),
         back_first[:3],
         [tie(back_last[0], *plan.gate), *back_last[1:3]],
     )
-    plan.gate = [*near, grads[0]]
+    plan.gate = [*near, grads[0], *terms_two[2:]]
     arrived = {d: send(grads[d + 1], 1) for d in (6, 4, 2)}
     low = add(grads[6][:half_one], arrived[6][:half_one])
     high = add(grads[6][half_one:], arrived[6][half_one:])
@@ -1149,16 +1165,18 @@
     plan.gate = [low, high, merged, *arrived.values()]
     low, high = send(low, 2), send(high, 4)
     ups_last = [ups[0], *near[:2], pass_on(merged, 2)]
-    plan.gate = [low, high, *arrived_two]
+    cut_two = cut_terms(place, own, plan.tied(terms_two), sizes_two, n_f)
+    plan.gate = [low, high, cut_two[0]]
     x, y = meet_call(
         (grads[2], arrived[2]), tie(high, *plan.gate), (grads[4], arrived[4]), low, half_one
     )
+    arrived_two = [pass_on(cut_two[j], j) for j in range(1, n_f)]
     plan.gate = [x, y]
-    arrived[0] = send(grads[1], 1)
-    terms_one = [grads[0], arrived[0], send(x, 2), send(y, 4)]
-    arrived_two.append(pass_on(cut_two[2], 2))
+    terms_one = [grads[0], None, send(x, 2), send(y, 4)]
     grad_bytes = byte_grad(one, (plan.tied(back_first[:2]), back_last[:2]))
-    plan.gate = [*terms_one[2:], grad_bytes, arrived_two[-1], ups_last[-1]]
+    plan.gate = [x, y, ups_last[-1]]
+    terms_one[1] = send(grads[1], 1)
+    plan.gate = [*terms_one[1:], grad_bytes]
     cut_one = cut_terms(place, own, plan.tied(terms_one), sizes_one, n_f)
     plan.gate = [cut_one[0]]
     grad_one = total(cut_one[0], [pass_on(cut_one[j], j) for j in range(1, n_f)])

time: 407 us -> 385 us (0.946)
  waiting for transfers between devices: 163 us -> 135 us
  starting transfers between devices: 74 us -> 79.1 us
    ppermute x61, waiting for transfers between devices: 136 us -> 112 us  [swap(): return lax.ppermute(value, axis, [(i, i ^ distance) for i in range(size)])]
    ppermute x5, waiting for transfers between devices: 26.6 us -> 22.2 us  [relay(): lax.ppermute(tie(two, *self.gate), 'fsdp', [(2, 3), (1, 0)])]
    unnamed x188 -> x176, local copies, waits for them, and re-layouts: 17 us -> 16.7 us
  transfers between devices with their start and end apart: 73 -> 73, of which waited for: 29 -> 28; matrix products, arithmetic and copies ran while one was open for 3% -> 4% of each run, Pallas kernels for 26% -> 29%
where the time goes in v3:
time: 385 us; the launch traced here: 380 us
  waiting for transfers between devices  135 us (35%)
  Pallas kernels  130 us (34%)
  starting transfers between devices  79.1 us (21%)
  local copies, waits for them, and re-layouts  21 us (5%)
  other arithmetic  13.1 us (3%)
    ppermute x61, waiting for transfers between devices, swap(): return lax.ppermute(value, axis, [(i, i ^ distance) for i in range(size)])  112 us
    ppermute x61, starting transfers between devices, swap(): return lax.ppermute(value, axis, [(i, i ^ distance) for i in range(size)])  62.1 us
    pallas_call x2, Pallas kernels, attend_back_call(): pl.pallas_call(kernel, grid_spec=pltpu.PrefetchScalarGridSpec(num_scalar_...  24 us
    pallas_call x2, Pallas kernels, attend_call(): pl.pallas_call(kernel, grid_spec=pltpu.PrefetchScalarGridSpec(num_scalar_...  23.9 us
    ppermute x5, waiting for transfers between devices, relay(): lax.ppermute(tie(two, *self.gate), 'fsdp', [(2, 3), (1, 0)])  22.2 us
    unnamed x176, local copies, waits for them, and re-layouts  16.7 us
    pallas_call x1, Pallas kernels, byte_grad_call(): pl.pallas_call(kernel, grid_spec=pltpu.PrefetchScalarGridSpec(num_scalar_...  16.4 us
    pallas_call x1, Pallas kernels, weight_grads_call(): pl.pallas_call(kernel, grid_spec=pltpu.PrefetchScalarGridSpec(num_scalar_...  15.1 us
  transfers between devices with their start and end apart: 73, of which 28 were waited for; matrix products, arithmetic and copies ran while one was open for 4% of the time, Pallas kernels for 29%

profile of v3, /device:TPU:0, one launch (start us, length us, event | category | flops | bytes accessed | tf_op | source)
XLA Modules:
  0.0 379.9 jit_solution(15517943238735986751)
XLA Ops:
  2.4 4.1 %collective-permute-start.1 = (bf16[96,1280]{1,0:T(8,128)(2,1)S(1)}, bf16[96,1280]{1,0:T(8,128)(2,1)S(1)}, u32[]{:S(2)}, u32[]{:S(2)}) collective-permute-start(bf16[96,1280]{1,0:T(8,128)(2,1)S(1)} %fusion.8.refs_0_), channel_id=1, source_target_pairs={{0,2},{1,3},{2,0},{3,1},{4,6},{5,7},{6,4},{7,5},{8,10},{9,11},{10,... | collective-permute-start | bytes 737288 | tf_op jit(solution)/shard_map/ppermute | solution.py:773
  6.5 1.6 collective-permute-start
  8.1 9.7 %collective-permute-done.1.refs_2_ = bf16[96,1280]{1,0:T(8,128)(2,1)S(1)} collective-permute-done((bf16[96,1280]{1,0:T(8,128)(2,1)S(1)}, bf16[96,1280]{1,0:T(8,128)(2,1)S(1)}, u32[]{:S(2)}, u32[]{:S(2)}) %collective-permute-start.1) | collective-permute-done | bytes 245792 | tf_op jit(solution)/shard_map/ppermute | solution.py:773
  18.7 1.3 collective-permute-start.3
  20.1 7.9 %collective-permute-done.3.refs_4_ = bf16[96,1280]{1,0:T(8,128)(2,1)S(1)} collective-permute-done((bf16[96,1280]{1,0:T(8,128)(2,1)S(1)}, bf16[96,1280]{1,0:T(8,128)(2,1)S(1)}, u32[]{:S(2)}, u32[]{:S(2)}) %collective-permute-start.3) | collective-permute-done | bytes 245792 | tf_op jit(solution)/shard_map/ppermute | solution.py:926
  29.2 1.6 collective-permute-start.5
  30.8 1.5 collective-permute-start.4
  32.9 4.1 %collective-permute-start.7 = (bf16[192,1408]{1,0:T(8,128)(2,1)S(1)}, bf16[192,1408]{1,0:T(8,128)(2,1)S(1)}, u32[]{:S(2)}, u32[]{:S(2)}) collective-permute-start(bf16[192,1408]{1,0:T(8,128)(2,1)S(1)} %fusion.1.refs_0_.refs_8_.x_ref), channel_id=1, source_target_pairs={{0,2},{1,3},{2,0},{3,1},{4,6},{5,7},{6,4},{7,5},{8,10},{9,11},{10,... | collective-permute-start | bytes 1622024 | tf_op jit(solution)/shard_map/ppermute | solution.py:773
  37.0 21.1 %collective-permute-done.8.refs_1_ = bf16[192,1408]{1,0:T(8,128)(2,1)S(1)} collective-permute-done((bf16[192,1408]{1,0:T(8,128)(2,1)S(1)}, bf16[192,1408]{1,0:T(8,128)(2,1)S(1)}, u32[]{:S(2)}, u32[]{:S(2)}) %collective-permute-start.8) | collective-permute-done | bytes 540704 | tf_op jit(solution)/shard_map/ppermute | solution.py:773
  58.1 2.5 collective-permute-done.7.refs_2_
  60.8 2.5 collective-permute-done.11.refs_3_.refs_11_.refs_13_.refs_12_.refs_7_
  65.0 1.3 collective-permute-start.14
  68.9 10.5 %collective-permute-done.10.refs_7_.refs_15_.refs_17_.refs_16_.refs_11_ = bf16[176,1280]{1,0:T(8,128)(2,1)S(1)} collective-permute-done((bf16[176,1280]{1,0:T(8,128)(2,1)S(1)}, bf16[176,1280]{1,0:T(8,128)(2,1)S(1)}, u32[]{:S(2)}, u32[]{:S(2)}) %collective-permute-start.10) | collective-permute-done | bytes 450592 | tf_op jit(solution)/shard_map/ppermute | solution.py:773
  80.0 1.5 collective-permute-done.14.refs_4_
  83.8 1.9 collective-permute-start.15
  86.7 13.6 %keys_values.1 = (bf16[768,1536]{1,0:T(8,128)(2,1)}, bf16[1536,1280]{1,0:T(8,128)(2,1)}, bf16[1536,1280]{1,0:T(8,128)(2,1)}) custom-call(s32[2]{0:T(128)} %copy-done.44, bf16[1536,768]{1,0:T(8,128)(2,1)} %bitcast.8, bf16[368,1280]{1,0:T(8,128)(2,1)} %copy-done, bf16[368,1280]{1,0:T(8,128)(2,1)} %collective-permute-done.6.refs_1_.refs_9_.refs_11_.refs_10_.refs_5_, ...), custom_call_target="tpu_custom_call" | custom-call | flops 1 | bytes 1 | tf_op jit(solution)/shard_map/keys_values/pallas_call | solution.py:237
  101.0 1.8 collective-permute-start.20
  104.2 9.7 %attend.2 = (bf16[1280,256]{1,0:T(8,128)(2,1)}, bf16[256,1280]{1,0:T(8,128)(2,1)}, bf16[64,1408]{1,0:T(8,128)(2,1)}, bf16[64,1408]{1,0:T(8,128)(2,1)}, bf16[64,1...) custom-call(s32[2]{0:T(128)} %copy-done.44, bf16[192,1408]{1,0:T(8,128)(2,1)} %copy-done.18, bf16[192,1408]{1,0:T(8,128)(2,1)} %copy-done.49, ...), custom_call_target="tpu_custom_call" | custom-call | flops 1 | bytes 1 | tf_op jit(solution)/shard_map/attend/pallas_call | solution.py:333
  113.9 1.6 assemble.3.refs_20_
  117.1 2.4 collective-permute-start.23
  119.5 1.9 collective-permute-start.22
  121.6 14.2 %attend.3 = (bf16[1280,512]{1,0:T(8,128)(2,1)}, bf16[512,1280]{1,0:T(8,128)(2,1)}, bf16[128,1408]{1,0:T(8,128)(2,1)}, bf16[128,1408]{1,0:T(8,128)(2,1)}, bf16[12...) custom-call(s32[2]{0:T(128)} %copy-done.44, bf16[192,1408]{1,0:T(8,128)(2,1)} %copy-done.18, bf16[192,1408]{1,0:T(8,128)(2,1)} %copy-done.49, ...), custom_call_target="tpu_custom_call" | custom-call | flops 1 | bytes 1 | tf_op jit(solution)/shard_map/attend/pallas_call | solution.py:333
  135.9 2.4 collective-permute-start.26
  140.4 3.6 collective-permute-done.28.refs_24_
  144.9 1.9 slice.74
  149.5 19.2 %collective-permute-done.25.refs_5_ = bf16[128,1408]{1,0:T(8,128)(2,1)} collective-permute-done((bf16[128,1408]{1,0:T(8,128)(2,1)}, bf16[128,1408]{1,0:T(8,128)(2,1)}, u32[]{:S(2)}, u32[]{:S(2)}) %collective-permute-start.25) | collective-permute-done | bytes 360480 | tf_op jit(solution)/shard_map/ppermute | solution.py:773
  169.9 7.1 %collective-permute-done.34.refs_28_ = bf16[240,1280]{1,0:T(8,128)(2,1)S(1)} collective-permute-done((bf16[240,1280]{1,0:T(8,128)(2,1)S(1)}, bf16[240,1280]{1,0:T(8,128)(2,1)S(1)}, u32[]{:S(2)}, u32[]{:S(2)}) %collective-permute-start.34) | collective-permute-done | bytes 614432 | tf_op jit(solution)/shard_map/ppermute | solution.py:773
  179.1 14.2 %feed.1 = (bf16[192,1280]{1,0:T(8,128)(2,1)}, f32[192,1280]{1,0:T(8,128)}, bf16[64,1408]{1,0:T(8,128)(2,1)}, bf16[128,1408]{1,0:T(8,128)(2,1)}, bf16[1280,192]{1...) custom-call(s32[2]{0:T(128)} %copy-done.44, ...), custom_call_target="tpu_custom_call" | custom-call | flops 1 | bytes 1 | tf_op jit(solution)/shard_map/feed/pallas_call | solution.py:450
  193.4 3.0 collective-permute-start.36
  196.4 6.7 %feed_grads.1 = (bf16[480,1280]{1,0:T(8,128)(2,1)}, bf16[480,1280]{1,0:T(8,128)(2,1)}, bf16[480,1280]{1,0:T(8,128)(2,1)}, bf16[480,1280]{1,0:T(8,128)(2,1)}, bf1...) custom-call(s32[2]{0:T(128)} %copy-done.44, ...), custom_call_target="tpu_custom_call" | custom-call | flops 1 | bytes 1 | tf_op jit(solution)/shard_map/feed_grads/pallas_call | solution.py:493
  203.9 1.3 collective-permute-done.36.refs_2_
  206.4 1.5 collective-permute-start.41
  207.9 6.8 %collective-permute-done.41.refs_4_ = bf16[64,1408]{1,0:T(8,128)(2,1)S(1)} collective-permute-done((bf16[64,1408]{1,0:T(8,128)(2,1)S(1)}, bf16[64,1408]{1,0:T(8,128)(2,1)S(1)}, u32[]{:S(2)}, u32[]{:S(2)}) %collective-permute-start.41) | collective-permute-done | bytes 180256 | tf_op jit(solution)/shard_map/ppermute | solution.py:926
  215.9 2.6 add_convert_fusion
  219.6 1.5 collective-permute-start.44
  221.1 3.0 collective-permute-start.45
  224.0 8.8 %attend_back.2 = (bf16[512,1280]{1,0:T(8,128)(2,1)}, bf16[512,1280]{1,0:T(8,128)(2,1)}, bf16[256,1280]{1,0:T(8,128)(2,1)}, bf16[64,1280]{1,0:T(8,128)(2,1)}, bf1...) custom-call(s32[2]{0:T(128)} %copy-done.44, ...), custom_call_target="tpu_custom_call" | custom-call | flops 1 | bytes 1 | tf_op jit(solution)/shard_map/attend_back/pallas_call | solution.py:577
  232.8 6.0 %collective-permute-done.46.refs_1_ = bf16[128,1408]{1,0:T(8,128)(2,1)} collective-permute-done((bf16[128,1408]{1,0:T(8,128)(2,1)S(1)}, bf16[128,1408]{1,0:T(8,128)(2,1)}, u32[]{:S(2)}, u32[]{:S(2)}) %collective-permute-start.46) | collective-permute-done | bytes 360480 | tf_op jit(solution)/shard_map/ppermute | solution.py:773
  241.9 1.3 collective-permute-start.49
  244.5 1.3 copy-done.27
  245.8 3.0 meet.2
  248.8 6.0 %collective-permute-done.49.refs_4_ = bf16[128,1408]{1,0:T(8,128)(2,1)S(1)} collective-permute-done((bf16[128,1408]{1,0:T(8,128)(2,1)}, bf16[128,1408]{1,0:T(8,128)(2,1)S(1)}, u32[]{:S(2)}, u32[]{:S(2)}) %collective-permute-start.49) | collective-permute-done | bytes 360480 | tf_op jit(solution)/shard_map/ppermute | solution.py:926
  256.4 3.0 collective-permute-start.51
  259.3 1.4 collective-permute-start.52
  260.7 15.2 %attend_back.3 = (bf16[1024,1280]{1,0:T(8,128)(2,1)}, bf16[1024,1280]{1,0:T(8,128)(2,1)}, bf16[512,1280]{1,0:T(8,128)(2,1)}, bf16[128,1280]{1,0:T(8,128)(2,1)}, ...) custom-call(s32[2]{0:T(128)} %copy-done.44, ...), custom_call_target="tpu_custom_call" | custom-call | flops 1 | bytes 1 | tf_op jit(solution)/shard_map/attend_back/pallas_call | solution.py:577
  277.3 4.6 %collective-permute-start.55 = (bf16[128,1280]{1,0:T(8,128)(2,1)}, bf16[128,1280]{1,0:T(8,128)(2,1)}, u32[]{:S(2)}, u32[]{:S(2)}) collective-permute-start(bf16[128,1280]{1,0:T(8,128)(2,1)} %get-tuple-element.258), channel_id=1, source_target_pairs={{3,2},{0,1},{7,6},{4,5},{11,10},{8,9},{15,14},{12,13},{19,18},{16,... | collective-permute-start | bytes 983048 | tf_op jit(solution)/shard_map/ppermute | solution.py:931
  281.9 1.8 collective-permute-start.54
  283.7 15.1 %weight_grads.1 = (bf16[352,1280]{1,0:T(8,128)(2,1)}, bf16[352,1280]{1,0:T(8,128)(2,1)}, bf16[352,1280]{1,0:T(8,128)(2,1)}, bf16[352,1280]{1,0:T(8,128)(2,1)}, b...) custom-call(s32[2]{0:T(128)} %copy-done.44, ...), custom_call_target="tpu_custom_call" | custom-call | flops 1 | bytes 1 | tf_op jit(solution)/shard_map/weight_grads/pallas_call | solution.py:647
  302.9 1.3 collective-permute-done.60.d
  304.2 1.5 collective-permute-start.62
  307.4 2.6 cut.2
  310.9 6.1 %collective-permute-done.61.h = bf16[160,1280]{1,0:T(8,128)(2,1)S(1)} collective-permute-done((bf16[160,1280]{1,0:T(8,128)(2,1)S(1)}, bf16[160,1280]{1,0:T(8,128)(2,1)S(1)}, u32[]{:S(2)}, u32[]{:S(2)}) %collective-permute-start.61) | collective-permute-done | bytes 409632 | tf_op jit(solution)/shard_map/ppermute | solution.py:773
  318.2 1.7 meet.3
  319.8 4.1 %collective-permute-done.63.refs_7_ = bf16[128,1280]{1,0:T(8,128)(2,1)S(1)} collective-permute-done((bf16[128,1280]{1,0:T(8,128)(2,1)S(1)}, bf16[128,1280]{1,0:T(8,128)(2,1)S(1)}, u32[]{:S(2)}, u32[]{:S(2)}) %collective-permute-start.63) | collective-permute-done | bytes 327712 | tf_op jit(solution)/shard_map/ppermute | solution.py:773
  326.2 4.3 %collective-permute-done.70 = bf16[120,1280]{1,0:T(8,128)(2,1)S(1)} collective-permute-done((bf16[120,1280]{1,0:T(8,128)(2,1)S(1)}, bf16[120,1280]{1,0:T(8,128)(2,1)S(1)}, u32[]{:S(2)}, u32[]{:S(2)}) %collective-permute-start.70) | collective-permute-done | bytes 307232 | tf_op jit(solution)/shard_map/ppermute | solution.py:773
  331.2 1.6 collective-permute-start.72
  332.8 16.4 %byte_grad.1 = f32[1536,768]{1,0:T(8,128)} custom-call(s32[2]{0:T(128)} %copy-done.44, bf16[1536,768]{1,0:T(8,128)(2,1)} %bitcast.9, bf16[512,1280]{1,0:T(8,128)(2,1)} %get-tuple-element.282.refs_3_.refs_0_, bf16[512,1280]{1,0:T(8,128)(2,1)} %get-tuple-element.247.refs_5_.refs_1_, bf16[1024,1280]{1,0:T(8,128)(2,1)} %get-tuple-element.246.refs_4_.refs_2_, ...), custom_call_target="tpu_custom_call" | custom-call | flops 1 | bytes 1 | tf_op jit(solution)/shard_map/byte_grad/pallas_call | solution.py:707
  349.3 1.4 convert_add_fusion
  350.8 2.5 cut.3
  353.3 2.3 collective-permute-start.69
  355.7 5.7 %collective-permute-start.68 = (bf16[88,1280]{1,0:T(8,128)(2,1)S(1)}, bf16[88,1280]{1,0:T(8,128)(2,1)S(1)}, u32[]{:S(2)}, u32[]{:S(2)}) collective-permute-start(bf16[88,1280]{1,0:T(8,128)(2,1)S(1)} %get-tuple-element.291), channel_id=1, source_target_pairs={{0,2},{1,3},{2,0},{3,1},{4,6},{5,7},{6,4},{7,5},{8,10},{9,11},{10,... | collective-permute-start | bytes 675848 | tf_op jit(solution)/shard_map/ppermute | solution.py:773
  361.4 1.8 multiply_reduce_fusion
  366.7 3.5 latent_grad.1
  370.3 6.6 %collective-permute-done.68 = bf16[88,1280]{1,0:T(8,128)(2,1)S(1)} collective-permute-done((bf16[88,1280]{1,0:T(8,128)(2,1)S(1)}, bf16[88,1280]{1,0:T(8,128)(2,1)S(1)}, u32[]{:S(2)}, u32[]{:S(2)}) %collective-permute-start.68) | collective-permute-done | bytes 225312 | tf_op jit(solution)/shard_map/ppermute | solution.py:773
  (301 shorter events, 53.8 us)
Async XLA Ops:
  2.4 15.4 %collective-permute-start.1 = (bf16[96,1280]{1,0:T(8,128)(2,1)S(1)}, bf16[96,1280]{1,0:T(8,128)(2,1)S(1)}, u32[]{:S(2)}, u32[]{:S(2)}) collective-permute-start(bf16[96,1280]{1,0:T(8,128)(2,1)S(1)} %fusion.8.refs_0_), channel_id=1, source_target_pairs={{0,2},{1,3},{2,0},{3,1},{4,6},{5,7},{6,4},{7,5},{8,10},{9,11},{10,... | collective-permute-start | bytes 737288 | tf_op jit(solution)/shard_map/ppermute | solution.py:773
  6.5 11.5 %collective-permute-start = (bf16[96,1280]{1,0:T(8,128)(2,1)S(1)}, bf16[96,1280]{1,0:T(8,128)(2,1)S(1)}, u32[]{:S(2)}, u32[]{:S(2)}) collective-permute-start(bf16[96,1280]{1,0:T(8,128)(2,1)S(1)} %fusion.8.refs_0_), channel_id=1, source_target_pairs={{0,1},{1,0},{2,3},{3,2},{4,5},{5,4},{6,7},{7,6},{8,9},{9,8},{10,11... | collective-permute-start | bytes 737288 | tf_op jit(solution)/shard_map/ppermute | solution.py:773
  18.7 9.3 %collective-permute-start.3 = (bf16[96,1280]{1,0:T(8,128)(2,1)S(1)}, bf16[96,1280]{1,0:T(8,128)(2,1)S(1)}, u32[]{:S(2)}, u32[]{:S(2)}) collective-permute-start(bf16[96,1280]{1,0:T(8,128)(2,1)S(1)} %collective-permute-done.1.refs_2_), channel_id=1, source_target_pairs={{2,3},{1,0},{6,7},{5,4},{10,11},{9,8},{14,15},{13,12},{18,19},{17,... | collective-permute-start | bytes 737288 | tf_op jit(solution)/shard_map/ppermute | solution.py:926
  29.2 31.5 %collective-permute-start.6 = (bf16[368,1280]{1,0:T(8,128)(2,1)S(1)}, bf16[368,1280]{1,0:T(8,128)(2,1)}, u32[]{:S(2)}, u32[]{:S(2)}) collective-permute-start(bf16[368,1280]{1,0:T(8,128)(2,1)S(1)} %assemble.2.refs_0_.refs_8_.refs_10_.refs_9_.refs_4_), channel_id=1, source_target_pairs={{0,4},{4,0},{8,12},{12,8},{16,20},{20,16},{24,28},{28,24},{1,5},{5... | collective-permute-start | bytes 2826248 | tf_op jit(solution)/shard_map/ppermute | solution.py:773
  29.2 31.4 %collective-permute-start.5 = (bf16[368,1280]{1,0:T(8,128)(2,1)S(1)}, bf16[368,1280]{1,0:T(8,128)(2,1)S(1)}, u32[]{:S(2)}, u32[]{:S(2)}) collective-permute-start(bf16[368,1280]{1,0:T(8,128)(2,1)S(1)} %assemble.2.refs_0_.refs_8_.refs_10_.refs_9_.refs_4_), channel_id=1, source_target_pairs={{0,16},{4,20},{8,24},{12,28},{16,0},{20,4},{24,8},{28,12},{1,17},{... | collective-permute-start | bytes 2826248 | tf_op jit(solution)/shard_map/ppermute | solution.py:773
  30.8 29.8 %collective-permute-start.4 = (bf16[368,1280]{1,0:T(8,128)(2,1)S(1)}, bf16[368,1280]{1,0:T(8,128)(2,1)S(1)}, u32[]{:S(2)}, u32[]{:S(2)}) collective-permute-start(bf16[368,1280]{1,0:T(8,128)(2,1)S(1)} %assemble.2.refs_0_.refs_8_.refs_10_.refs_9_.refs_4_), channel_id=1, source_target_pairs={{0,8},{4,12},{8,0},{12,4},{16,24},{20,28},{24,16},{28,20},{1,9},{5... | collective-permute-start | bytes 2826248 | tf_op jit(solution)/shard_map/ppermute | solution.py:773
  32.6 25.5 %collective-permute-start.8 = (bf16[192,1408]{1,0:T(8,128)(2,1)S(1)}, bf16[192,1408]{1,0:T(8,128)(2,1)S(1)}, u32[]{:S(2)}, u32[]{:S(2)}) collective-permute-start(bf16[192,1408]{1,0:T(8,128)(2,1)S(1)} %fusion.1.refs_0_.refs_8_.x_ref), channel_id=1, source_target_pairs={{0,1},{1,0},{2,3},{3,2},{4,5},{5,4},{6,7},{7,6},{8,9},{9,8},{10,11... | collective-permute-start | bytes 1622024 | tf_op jit(solution)/shard_map/ppermute | solution.py:773
  32.9 27.7 %collective-permute-start.7 = (bf16[192,1408]{1,0:T(8,128)(2,1)S(1)}, bf16[192,1408]{1,0:T(8,128)(2,1)S(1)}, u32[]{:S(2)}, u32[]{:S(2)}) collective-permute-start(bf16[192,1408]{1,0:T(8,128)(2,1)S(1)} %fusion.1.refs_0_.refs_8_.x_ref), channel_id=1, source_target_pairs={{0,2},{1,3},{2,0},{3,1},{4,6},{5,7},{6,4},{7,5},{8,10},{9,11},{10,... | collective-permute-start | bytes 1622024 | tf_op jit(solution)/shard_map/ppermute | solution.py:773
  64.2 17.3 %collective-permute-start.12 = (bf16[368,1280]{1,0:T(8,128)(2,1)S(1)}, bf16[368,1280]{1,0:T(8,128)(2,1)S(1)}, u32[]{:S(2)}, u32[]{:S(2)}) collective-permute-start(bf16[368,1280]{1,0:T(8,128)(2,1)S(1)} %collective-permute-done.5.refs_4_.refs_12_.refs_14_.refs_13_.refs_8_), channel_id=1, source_target_pairs={{0,4},{4,0},{8,12},{12,8},{16,20},{20,16},{24,28},{28,24},{1,5},{5... | collective-permute-start | bytes 2826248 | tf_op jit(solution)/shard_map/ppermute | solution.py:773
  64.3 15.6 %collective-permute-start.13 = (bf16[192,1408]{1,0:T(8,128)(2,1)S(1)}, bf16[192,1408]{1,0:T(8,128)(2,1)S(1)}, u32[]{:S(2)}, u32[]{:S(2)}) collective-permute-start(bf16[192,1408]{1,0:T(8,128)(2,1)S(1)} %fusion.1.refs_0_.refs_8_.x_ref), channel_id=1, source_target_pairs={{1,2},{2,1},{5,6},{6,5},{9,10},{10,9},{13,14},{14,13},{17,18},{18,... | collective-permute-start | bytes 1622024 | tf_op jit(solution)/shard_map/ppermute | solution.py:925
  65.0 16.4 %collective-permute-start.14 = (bf16[192,1408]{1,0:T(8,128)(2,1)S(1)}, bf16[192,1408]{1,0:T(8,128)(2,1)S(1)}, u32[]{:S(2)}, u32[]{:S(2)}) collective-permute-start(bf16[192,1408]{1,0:T(8,128)(2,1)S(1)} %collective-permute-done.7.refs_2_), channel_id=1, source_target_pairs={{2,3},{1,0},{6,7},{5,4},{10,11},{9,8},{14,15},{13,12},{18,19},{17,... | collective-permute-start | bytes 1622024 | tf_op jit(solution)/shard_map/ppermute | solution.py:926
  66.4 13.6 %collective-permute-start.9 = (bf16[192,1280]{1,0:T(8,128)(2,1)S(1)}, bf16[192,1280]{1,0:T(8,128)(2,1)S(1)}, u32[]{:S(2)}, u32[]{:S(2)}) collective-permute-start(bf16[192,1280]{1,0:T(8,128)(2,1)S(1)} %slice.72), channel_id=1, source_target_pairs={{0,16},{4,20},{8,24},{12,28},{16,0},{20,4},{24,8},{28,12},{1,17},{... | collective-permute-start | bytes 1474568 | tf_op jit(solution)/shard_map/ppermute | solution.py:773
  67.0 12.4 %collective-permute-start.10 = (bf16[176,1280]{1,0:T(8,128)(2,1)S(1)}, bf16[176,1280]{1,0:T(8,128)(2,1)S(1)}, u32[]{:S(2)}, u32[]{:S(2)}) collective-permute-start(bf16[176,1280]{1,0:T(8,128)(2,1)S(1)} %slice.73), channel_id=1, source_target_pairs={{0,8},{4,12},{8,0},{12,4},{16,24},{20,28},{24,16},{28,20},{1,9},{5... | collective-permute-start | bytes 1351688 | tf_op jit(solution)/shard_map/ppermute | solution.py:773
  82.7 17.6 %collective-permute-start.16 = (bf16[120,1280]{1,0:T(8,128)(2,1)}, bf16[120,1280]{1,0:T(8,128)(2,1)}, u32[]{:S(2)}, u32[]{:S(2)}) collective-permute-start(bf16[120,1280]{1,0:T(8,128)(2,1)} %constant_dynamic-update-slice_fusion.refs_0_), channel_id=1, source_target_pairs={{0,1},{1,0},{2,3},{3,2},{4,5},{5,4},{6,7},{7,6},{8,9},{9,8},{10,11... | collective-permute-start | bytes 921608 | tf_op jit(solution)/shard_map/ppermute | solution.py:773
  83.8 16.5 %collective-permute-start.15 = (bf16[120,1280]{1,0:T(8,128)(2,1)}, bf16[120,1280]{1,0:T(8,128)(2,1)S(1)}, u32[]{:S(2)}, u32[]{:S(2)}) collective-permute-start(bf16[120,1280]{1,0:T(8,128)(2,1)} %constant_dynamic-update-slice_fusion.refs_0_), channel_id=1, source_target_pairs={{0,2},{1,3},{2,0},{3,1},{4,6},{5,7},{6,4},{7,5},{8,10},{9,11},{10,... | collective-permute-start | bytes 921608 | tf_op jit(solution)/shard_map/ppermute | solution.py:773
  100.3 13.5 %collective-permute-start.19 = (bf16[120,1280]{1,0:T(8,128)(2,1)}, bf16[120,1280]{1,0:T(8,128)(2,1)S(1)}, u32[]{:S(2)}, u32[]{:S(2)}) collective-permute-start(bf16[120,1280]{1,0:T(8,128)(2,1)} %constant_dynamic-update-slice_fusion.refs_0_), channel_id=1, source_target_pairs={{1,2},{2,1},{5,6},{6,5},{9,10},{10,9},{13,14},{14,13},{17,18},{18,... | collective-permute-start | bytes 921608 | tf_op jit(solution)/shard_map/ppermute | solution.py:925
  101.0 12.8 %collective-permute-start.20 = (bf16[120,1280]{1,0:T(8,128)(2,1)S(1)}, bf16[120,1280]{1,0:T(8,128)(2,1)S(1)}, u32[]{:S(2)}, u32[]{:S(2)}) collective-permute-start(bf16[120,1280]{1,0:T(8,128)(2,1)S(1)} %collective-permute-done.15.refs_2_), channel_id=1, source_target_pairs={{2,3},{1,0},{6,7},{5,4},{10,11},{9,8},{14,15},{13,12},{18,19},{17,... | collective-permute-start | bytes 921608 | tf_op jit(solution)/shard_map/ppermute | solution.py:926
  115.5 28.5 %collective-permute-start.28 = (bf16[480,1280]{1,0:T(8,128)(2,1)S(1)}, bf16[480,1280]{1,0:T(8,128)(2,1)S(1)}, u32[]{:S(2)}, u32[]{:S(2)}) collective-permute-start(bf16[480,1280]{1,0:T(8,128)(2,1)S(1)} %assemble.3.refs_20_), channel_id=1, source_target_pairs={{0,16},{4,20},{8,24},{12,28},{16,0},{20,4},{24,8},{28,12},{1,17},{... | collective-permute-start | bytes 3686408 | tf_op jit(solution)/shard_map/ppermute | solution.py:773
  116.6 28.3 %collective-permute-start.27 = (bf16[480,1280]{1,0:T(8,128)(2,1)S(1)}, bf16[480,1280]{1,0:T(8,128)(2,1)}, u32[]{:S(2)}, u32[]{:S(2)}) collective-permute-start(bf16[480,1280]{1,0:T(8,128)(2,1)S(1)} %assemble.3.refs_20_), channel_id=1, source_target_pairs={{0,8},{4,12},{8,0},{12,4},{16,24},{20,28},{24,16},{28,20},{1,9},{5... | collective-permute-start | bytes 3686408 | tf_op jit(solution)/shard_map/ppermute | solution.py:773
  117.1 18.8 %collective-permute-start.23 = (bf16[64,1408]{1,0:T(8,128)(2,1)S(1)}, bf16[64,1408]{1,0:T(8,128)(2,1)S(1)}, u32[]{:S(2)}, u32[]{:S(2)}) collective-permute-start(bf16[64,1408]{1,0:T(8,128)(2,1)S(1)} %copy-done.86), channel_id=1, source_target_pairs={{0,3},{1,2},{2,1},{3,0},{4,7},{5,6},{6,5},{7,4},{8,11},{9,10},{10,... | collective-permute-start | bytes 540680 | tf_op jit(solution)/shard_map/ppermute | solution.py:773
  119.5 16.4 %collective-permute-start.22 = (bf16[64,1408]{1,0:T(8,128)(2,1)S(1)}, bf16[64,1408]{1,0:T(8,128)(2,1)S(1)}, u32[]{:S(2)}, u32[]{:S(2)}) collective-permute-start(bf16[64,1408]{1,0:T(8,128)(2,1)S(1)} %copy-done.85), channel_id=1, source_target_pairs={{0,2},{1,3},{2,0},{3,1},{4,6},{5,7},{6,4},{7,5},{8,10},{9,11},{10,... | collective-permute-start | bytes 540680 | tf_op jit(solution)/shard_map/ppermute | solution.py:773
  121.5 14.4 %collective-permute-start.21 = (bf16[64,1408]{1,0:T(8,128)(2,1)S(1)}, bf16[64,1408]{1,0:T(8,128)(2,1)S(1)}, u32[]{:S(2)}, u32[]{:S(2)}) collective-permute-start(bf16[64,1408]{1,0:T(8,128)(2,1)S(1)} %copy-done.84), channel_id=1, source_target_pairs={{0,1},{1,0},{2,3},{3,2},{4,5},{5,4},{6,7},{7,6},{8,9},{9,8},{10,11... | collective-permute-start | bytes 540680 | tf_op jit(solution)/shard_map/ppermute | solution.py:773
  135.9 13.5 %collective-permute-start.26 = (bf16[128,1408]{1,0:T(8,128)(2,1)}, bf16[128,1408]{1,0:T(8,128)(2,1)S(1)}, u32[]{:S(2)}, u32[]{:S(2)}) collective-permute-start(bf16[128,1408]{1,0:T(8,128)(2,1)} %get-tuple-element.192), channel_id=1, source_target_pairs={{0,3},{1,2},{2,1},{3,0},{4,7},{5,6},{6,5},{7,4},{8,11},{9,10},{10,... | collective-permute-start | bytes 1081352 | tf_op jit(solution)/shard_map/ppermute | solution.py:773
  138.3 30.3 %collective-permute-start.25 = (bf16[128,1408]{1,0:T(8,128)(2,1)}, bf16[128,1408]{1,0:T(8,128)(2,1)}, u32[]{:S(2)}, u32[]{:S(2)}) collective-permute-start(bf16[128,1408]{1,0:T(8,128)(2,1)} %get-tuple-element.190), channel_id=1, source_target_pairs={{0,2},{1,3},{2,0},{3,1},{4,6},{5,7},{6,4},{7,5},{8,10},{9,11},{10,... | collective-permute-start | bytes 1081352 | tf_op jit(solution)/shard_map/ppermute | solution.py:773
  139.3 29.3 %collective-permute-start.24 = (bf16[128,1408]{1,0:T(8,128)(2,1)}, bf16[128,1408]{1,0:T(8,128)(2,1)}, u32[]{:S(2)}, u32[]{:S(2)}) collective-permute-start(bf16[128,1408]{1,0:T(8,128)(2,1)} %get-tuple-element.188), channel_id=1, source_target_pairs={{0,1},{1,0},{2,3},{3,2},{4,5},{5,4},{6,7},{7,6},{8,9},{9,8},{10,11... | collective-permute-start | bytes 1081352 | tf_op jit(solution)/shard_map/ppermute | solution.py:773
  146.9 21.8 %collective-permute-start.29 = (bf16[240,1280]{1,0:T(8,128)(2,1)}, bf16[240,1280]{1,0:T(8,128)(2,1)S(1)}, u32[]{:S(2)}, u32[]{:S(2)}) collective-permute-start(bf16[240,1280]{1,0:T(8,128)(2,1)} %slice.74), channel_id=1, source_target_pairs={{0,16},{4,20},{8,24},{12,28},{16,0},{20,4},{24,8},{28,12},{1,17},{... | collective-permute-start | bytes 1843208 | tf_op jit(solution)/shard_map/ppermute | solution.py:773
  147.8 20.8 %collective-permute-start.30 = (bf16[240,1280]{1,0:T(8,128)(2,1)}, bf16[240,1280]{1,0:T(8,128)(2,1)}, u32[]{:S(2)}, u32[]{:S(2)}) collective-permute-start(bf16[240,1280]{1,0:T(8,128)(2,1)} %slice.75), channel_id=1, source_target_pairs={{0,8},{4,12},{8,0},{12,4},{16,24},{20,28},{24,16},{28,20},{1,9},{5... | collective-permute-start | bytes 1843208 | tf_op jit(solution)/shard_map/ppermute | solution.py:773
  168.7 8.3 %collective-permute-start.31 = (bf16[480,1280]{1,0:T(8,128)(2,1)S(1)}, bf16[480,1280]{1,0:T(8,128)(2,1)S(1)}, u32[]{:S(2)}, u32[]{:S(2)}) collective-permute-start(bf16[480,1280]{1,0:T(8,128)(2,1)S(1)} %assemble.3.refs_20_), channel_id=1, source_target_pairs={{0,4},{4,0},{8,12},{12,8},{16,20},{20,16},{24,28},{28,24},{1,5},{5... | collective-permute-start | bytes 3686408 | tf_op jit(solution)/shard_map/ppermute | solution.py:773
  168.8 8.2 %collective-permute-start.32 = (bf16[480,1280]{1,0:T(8,128)(2,1)}, bf16[480,1280]{1,0:T(8,128)(2,1)S(1)}, u32[]{:S(2)}, u32[]{:S(2)}) collective-permute-start(bf16[480,1280]{1,0:T(8,128)(2,1)} %collective-permute-done.27.refs_22_), channel_id=1, source_target_pairs={{0,4},{4,0},{8,12},{12,8},{16,20},{20,16},{24,28},{28,24},{1,5},{5... | collective-permute-start | bytes 3686408 | tf_op jit(solution)/shard_map/ppermute | solution.py:773
  169.3 7.7 %collective-permute-start.33 = (bf16[480,1280]{1,0:T(8,128)(2,1)S(1)}, bf16[480,1280]{1,0:T(8,128)(2,1)S(1)}, u32[]{:S(2)}, u32[]{:S(2)}) collective-permute-start(bf16[480,1280]{1,0:T(8,128)(2,1)S(1)} %collective-permute-done.28.refs_24_), channel_id=1, source_target_pairs={{0,4},{4,0},{8,12},{12,8},{16,20},{20,16},{24,28},{28,24},{1,5},{5... | collective-permute-start | bytes 3686408 | tf_op jit(solution)/shard_map/ppermute | solution.py:773
  169.3 7.6 %collective-permute-start.34 = (bf16[240,1280]{1,0:T(8,128)(2,1)S(1)}, bf16[240,1280]{1,0:T(8,128)(2,1)S(1)}, u32[]{:S(2)}, u32[]{:S(2)}) collective-permute-start(bf16[240,1280]{1,0:T(8,128)(2,1)S(1)} %collective-permute-done.29.refs_26_), channel_id=1, source_target_pairs={{0,4},{4,0},{8,12},{12,8},{16,20},{20,16},{24,28},{28,24},{1,5},{5... | collective-permute-start | bytes 1843208 | tf_op jit(solution)/shard_map/ppermute | solution.py:773
  193.3 10.5 %collective-permute-start.37 = (bf16[64,1408]{1,0:T(8,128)(2,1)}, bf16[64,1408]{1,0:T(8,128)(2,1)S(1)}, u32[]{:S(2)}, u32[]{:S(2)}) collective-permute-start(bf16[64,1408]{1,0:T(8,128)(2,1)} %get-tuple-element.220.refs_0_), channel_id=1, source_target_pairs={{0,1},{1,0},{2,3},{3,2},{4,5},{5,4},{6,7},{7,6},{8,9},{9,8},{10,11... | collective-permute-start | bytes 540680 | tf_op jit(solution)/shard_map/ppermute | solution.py:773
  193.4 11.7 %collective-permute-start.36 = (bf16[64,1408]{1,0:T(8,128)(2,1)}, bf16[64,1408]{1,0:T(8,128)(2,1)S(1)}, u32[]{:S(2)}, u32[]{:S(2)}) collective-permute-start(bf16[64,1408]{1,0:T(8,128)(2,1)} %get-tuple-element.220.refs_0_), channel_id=1, source_target_pairs={{0,2},{1,3},{2,0},{3,1},{4,6},{5,7},{6,4},{7,5},{8,10},{9,11},{10,... | collective-permute-start | bytes 540680 | tf_op jit(solution)/shard_map/ppermute | solution.py:773
  205.2 9.5 %collective-permute-start.39 = (bf16[480,1280]{1,0:T(8,128)(2,1)}, bf16[480,1280]{1,0:T(8,128)(2,1)S(1)}, u32[]{:S(2)}, u32[]{:S(2)}) collective-permute-start(bf16[480,1280]{1,0:T(8,128)(2,1)} %get-tuple-element.217), channel_id=1, source_target_pairs={{0,4},{4,0},{8,12},{12,8},{16,20},{20,16},{24,28},{28,24},{1,5},{5... | collective-permute-start | bytes 3686408 | tf_op jit(solution)/shard_map/ppermute | solution.py:773
  205.2 10.6 %collective-permute-start.38 = (bf16[480,1280]{1,0:T(8,128)(2,1)}, bf16[480,1280]{1,0:T(8,128)(2,1)S(1)}, u32[]{:S(2)}, u32[]{:S(2)}) collective-permute-start(bf16[480,1280]{1,0:T(8,128)(2,1)} %get-tuple-element.215), channel_id=1, source_target_pairs={{0,4},{4,0},{8,12},{12,8},{16,20},{20,16},{24,28},{28,24},{1,5},{5... | collective-permute-start | bytes 3686408 | tf_op jit(solution)/shard_map/ppermute | solution.py:773
  206.4 8.4 %collective-permute-start.41 = (bf16[64,1408]{1,0:T(8,128)(2,1)S(1)}, bf16[64,1408]{1,0:T(8,128)(2,1)S(1)}, u32[]{:S(2)}, u32[]{:S(2)}) collective-permute-start(bf16[64,1408]{1,0:T(8,128)(2,1)S(1)} %collective-permute-done.36.refs_2_), channel_id=1, source_target_pairs={{2,3},{1,0},{6,7},{5,4},{10,11},{9,8},{14,15},{13,12},{18,19},{17,... | collective-permute-start | bytes 540680 | tf_op jit(solution)/shard_map/ppermute | solution.py:926
  215.8 24.4 %collective-permute-start.42 = (bf16[480,1280]{1,0:T(8,128)(2,1)}, bf16[480,1280]{1,0:T(8,128)(2,1)S(1)}, u32[]{:S(2)}, u32[]{:S(2)}) collective-permute-start(bf16[480,1280]{1,0:T(8,128)(2,1)} %get-tuple-element.225), channel_id=1, source_target_pairs={{0,4},{4,0},{8,12},{12,8},{16,20},{20,16},{24,28},{28,24},{1,5},{5... | collective-permute-start | bytes 3686408 | tf_op jit(solution)/shard_map/ppermute | solution.py:773
  218.5 21.6 %collective-permute-start.43 = (bf16[240,1280]{1,0:T(8,128)(2,1)}, bf16[240,1280]{1,0:T(8,128)(2,1)}, u32[]{:S(2)}, u32[]{:S(2)}) collective-permute-start(bf16[240,1280]{1,0:T(8,128)(2,1)} %get-tuple-element.227), channel_id=1, source_target_pairs={{0,16},{4,20},{8,24},{12,28},{16,0},{20,4},{24,8},{28,12},{1,17},{... | collective-permute-start | bytes 1843208 | tf_op jit(solution)/shard_map/ppermute | solution.py:773
  219.6 20.6 %collective-permute-start.44 = (bf16[240,1280]{1,0:T(8,128)(2,1)}, bf16[240,1280]{1,0:T(8,128)(2,1)}, u32[]{:S(2)}, u32[]{:S(2)}) collective-permute-start(bf16[240,1280]{1,0:T(8,128)(2,1)} %get-tuple-element.228), channel_id=1, source_target_pairs={{0,8},{4,12},{8,0},{12,4},{16,24},{20,28},{24,16},{28,20},{1,9},{5... | collective-permute-start | bytes 1843208 | tf_op jit(solution)/shard_map/ppermute | solution.py:773
  221.1 17.8 %collective-permute-start.46 = (bf16[128,1408]{1,0:T(8,128)(2,1)S(1)}, bf16[128,1408]{1,0:T(8,128)(2,1)}, u32[]{:S(2)}, u32[]{:S(2)}) collective-permute-start(bf16[128,1408]{1,0:T(8,128)(2,1)S(1)} %copy-done.63), channel_id=1, source_target_pairs={{0,1},{1,0},{2,3},{3,2},{4,5},{5,4},{6,7},{7,6},{8,9},{9,8},{10,11... | collective-permute-start | bytes 1081352 | tf_op jit(solution)/shard_map/ppermute | solution.py:773
  221.1 19.1 %collective-permute-start.45 = (bf16[128,1408]{1,0:T(8,128)(2,1)S(1)}, bf16[128,1408]{1,0:T(8,128)(2,1)}, u32[]{:S(2)}, u32[]{:S(2)}) collective-permute-start(bf16[128,1408]{1,0:T(8,128)(2,1)S(1)} %copy-done.63), channel_id=1, source_target_pairs={{0,2},{1,3},{2,0},{3,1},{4,6},{5,7},{6,4},{7,5},{8,10},{9,11},{10,... | collective-permute-start | bytes 1081352 | tf_op jit(solution)/shard_map/ppermute | solution.py:773
  241.2 13.6 %collective-permute-start.47 = (bf16[480,1280]{1,0:T(8,128)(2,1)}, bf16[480,1280]{1,0:T(8,128)(2,1)S(1)}, u32[]{:S(2)}, u32[]{:S(2)}) collective-permute-start(bf16[480,1280]{1,0:T(8,128)(2,1)} %get-tuple-element.235), channel_id=1, source_target_pairs={{0,4},{4,0},{8,12},{12,8},{16,20},{20,16},{24,28},{28,24},{1,5},{5... | collective-permute-start | bytes 3686408 | tf_op jit(solution)/shard_map/ppermute | solution.py:773
  241.2 7.6 %collective-permute-start.48 = (bf16[128,1408]{1,0:T(8,128)(2,1)S(1)}, bf16[128,1408]{1,0:T(8,128)(2,1)S(1)}, u32[]{:S(2)}, u32[]{:S(2)}) collective-permute-start(bf16[128,1408]{1,0:T(8,128)(2,1)S(1)} %copy-done.63), channel_id=1, source_target_pairs={{1,2},{2,1},{5,6},{6,5},{9,10},{10,9},{13,14},{14,13},{17,18},{18,... | collective-permute-start | bytes 1081352 | tf_op jit(solution)/shard_map/ppermute | solution.py:925
  241.9 12.9 %collective-permute-start.49 = (bf16[128,1408]{1,0:T(8,128)(2,1)}, bf16[128,1408]{1,0:T(8,128)(2,1)S(1)}, u32[]{:S(2)}, u32[]{:S(2)}) collective-permute-start(bf16[128,1408]{1,0:T(8,128)(2,1)} %collective-permute-done.45.refs_2_), channel_id=1, source_target_pairs={{2,3},{1,0},{6,7},{5,4},{10,11},{9,8},{14,15},{13,12},{18,19},{17,... | collective-permute-start | bytes 1081352 | tf_op jit(solution)/shard_map/ppermute | solution.py:926
  254.8 44.0 %collective-permute-start.56 = (bf16[480,1280]{1,0:T(8,128)(2,1)}, bf16[480,1280]{1,0:T(8,128)(2,1)S(1)}, u32[]{:S(2)}, u32[]{:S(2)}) collective-permute-start(bf16[480,1280]{1,0:T(8,128)(2,1)} %get-tuple-element.259), channel_id=1, source_target_pairs={{0,8},{4,12},{8,0},{12,4},{16,24},{20,28},{24,16},{28,20},{1,9},{5... | collective-permute-start | bytes 3686408 | tf_op jit(solution)/shard_map/ppermute | solution.py:773
  255.4 43.5 %collective-permute-start.57 = (bf16[480,1280]{1,0:T(8,128)(2,1)}, bf16[480,1280]{1,0:T(8,128)(2,1)S(1)}, u32[]{:S(2)}, u32[]{:S(2)}) collective-permute-start(bf16[480,1280]{1,0:T(8,128)(2,1)} %get-tuple-element.260), channel_id=1, source_target_pairs={{0,16},{4,20},{8,24},{12,28},{16,0},{20,4},{24,8},{28,12},{1,17},{... | collective-permute-start | bytes 3686408 | tf_op jit(solution)/shard_map/ppermute | solution.py:773
  256.3 19.6 %collective-permute-start.50 = (bf16[64,1280]{1,0:T(8,128)(2,1)}, bf16[64,1280]{1,0:T(8,128)(2,1)S(1)}, u32[]{:S(2)}, u32[]{:S(2)}) collective-permute-start(bf16[64,1280]{1,0:T(8,128)(2,1)} %get-tuple-element.241), channel_id=1, source_target_pairs={{0,1},{1,0},{2,3},{3,2},{4,5},{5,4},{6,7},{7,6},{8,9},{9,8},{10,11... | collective-permute-start | bytes 491528 | tf_op jit(solution)/shard_map/ppermute | solution.py:773
  256.4 20.3 %collective-permute-start.51 = (bf16[64,1280]{1,0:T(8,128)(2,1)}, bf16[64,1280]{1,0:T(8,128)(2,1)S(1)}, u32[]{:S(2)}, u32[]{:S(2)}) collective-permute-start(bf16[64,1280]{1,0:T(8,128)(2,1)} %get-tuple-element.243), channel_id=1, source_target_pairs={{0,2},{1,3},{2,0},{3,1},{4,6},{5,7},{6,4},{7,5},{8,10},{9,11},{10,... | collective-permute-start | bytes 491528 | tf_op jit(solution)/shard_map/ppermute | solution.py:773
  259.3 18.0 %collective-permute-start.52 = (bf16[64,1280]{1,0:T(8,128)(2,1)}, bf16[64,1280]{1,0:T(8,128)(2,1)}, u32[]{:S(2)}, u32[]{:S(2)}) collective-permute-start(bf16[64,1280]{1,0:T(8,128)(2,1)} %get-tuple-element.245), channel_id=1, source_target_pairs={{0,3},{1,2},{2,1},{3,0},{4,7},{5,6},{6,5},{7,4},{8,11},{9,10},{10,... | collective-permute-start | bytes 491528 | tf_op jit(solution)/shard_map/ppermute | solution.py:773
  277.3 21.5 %collective-permute-start.53 = (bf16[128,1280]{1,0:T(8,128)(2,1)}, bf16[128,1280]{1,0:T(8,128)(2,1)S(1)}, u32[]{:S(2)}, u32[]{:S(2)}) collective-permute-start(bf16[128,1280]{1,0:T(8,128)(2,1)} %get-tuple-element.256), channel_id=1, source_target_pairs={{0,1},{1,0},{2,3},{3,2},{4,5},{5,4},{6,7},{7,6},{8,9},{9,8},{10,11... | collective-permute-start | bytes 983048 | tf_op jit(solution)/shard_map/ppermute | solution.py:773
  277.3 21.5 %collective-permute-start.55 = (bf16[128,1280]{1,0:T(8,128)(2,1)}, bf16[128,1280]{1,0:T(8,128)(2,1)}, u32[]{:S(2)}, u32[]{:S(2)}) collective-permute-start(bf16[128,1280]{1,0:T(8,128)(2,1)} %get-tuple-element.258), channel_id=1, source_target_pairs={{3,2},{0,1},{7,6},{4,5},{11,10},{8,9},{15,14},{12,13},{19,18},{16,... | collective-permute-start | bytes 983048 | tf_op jit(solution)/shard_map/ppermute | solution.py:931
  281.9 16.9 %collective-permute-start.54 = (bf16[128,1280]{1,0:T(8,128)(2,1)}, bf16[128,1280]{1,0:T(8,128)(2,1)}, u32[]{:S(2)}, u32[]{:S(2)}) collective-permute-start(bf16[128,1280]{1,0:T(8,128)(2,1)} %get-tuple-element.258), channel_id=1, source_target_pairs={{1,2},{2,1},{5,6},{6,5},{9,10},{10,9},{13,14},{14,13},{17,18},{18,... | collective-permute-start | bytes 983048 | tf_op jit(solution)/shard_map/ppermute | solution.py:930
  304.2 13.3 %collective-permute-start.62 = (bf16[192,1280]{1,0:T(8,128)(2,1)S(1)}, bf16[192,1280]{1,0:T(8,128)(2,1)S(1)}, u32[]{:S(2)}, u32[]{:S(2)}) collective-permute-start(bf16[192,1280]{1,0:T(8,128)(2,1)S(1)} %add_convert_fusion.2), channel_id=1, source_target_pairs={{0,8},{4,12},{8,0},{12,4},{16,24},{20,28},{24,16},{28,20},{1,9},{5... | collective-permute-start | bytes 1474568 | tf_op jit(solution)/shard_map/ppermute | solution.py:773
  305.7 11.2 %collective-permute-start.61 = (bf16[160,1280]{1,0:T(8,128)(2,1)S(1)}, bf16[160,1280]{1,0:T(8,128)(2,1)S(1)}, u32[]{:S(2)}, u32[]{:S(2)}) collective-permute-start(bf16[160,1280]{1,0:T(8,128)(2,1)S(1)} %add_convert_fusion.3), channel_id=1, source_target_pairs={{0,16},{4,20},{8,24},{12,28},{16,0},{20,4},{24,8},{28,12},{1,17},{... | collective-permute-start | bytes 1228808 | tf_op jit(solution)/shard_map/ppermute | solution.py:773
  306.7 17.2 %collective-permute-start.63 = (bf16[128,1280]{1,0:T(8,128)(2,1)S(1)}, bf16[128,1280]{1,0:T(8,128)(2,1)S(1)}, u32[]{:S(2)}, u32[]{:S(2)}) collective-permute-start(bf16[128,1280]{1,0:T(8,128)(2,1)S(1)} %add_convert_fusion.4), channel_id=1, source_target_pairs={{0,2},{1,3},{2,0},{3,1},{4,6},{5,7},{6,4},{7,5},{8,10},{9,11},{10,... | collective-permute-start | bytes 983048 | tf_op jit(solution)/shard_map/ppermute | solution.py:773
  317.4 13.0 %collective-permute-start.70 = (bf16[120,1280]{1,0:T(8,128)(2,1)S(1)}, bf16[120,1280]{1,0:T(8,128)(2,1)S(1)}, u32[]{:S(2)}, u32[]{:S(2)}) collective-permute-start(bf16[120,1280]{1,0:T(8,128)(2,1)S(1)} %get-tuple-element.295), channel_id=1, source_target_pairs={{0,1},{1,0},{2,3},{3,2},{4,5},{5,4},{6,7},{7,6},{8,9},{9,8},{10,11... | collective-permute-start | bytes 921608 | tf_op jit(solution)/shard_map/ppermute | solution.py:773
  324.6 26.1 %collective-permute-start.64 = (bf16[352,1280]{1,0:T(8,128)(2,1)}, bf16[352,1280]{1,0:T(8,128)(2,1)S(1)}, u32[]{:S(2)}, u32[]{:S(2)}) collective-permute-start(bf16[352,1280]{1,0:T(8,128)(2,1)} %get-tuple-element.279), channel_id=1, source_target_pairs={{0,4},{4,0},{8,12},{12,8},{16,20},{20,16},{24,28},{28,24},{1,5},{5... | collective-permute-start | bytes 2703368 | tf_op jit(solution)/shard_map/ppermute | solution.py:773
  324.6 26.1 %collective-permute-start.65 = (bf16[352,1280]{1,0:T(8,128)(2,1)}, bf16[352,1280]{1,0:T(8,128)(2,1)}, u32[]{:S(2)}, u32[]{:S(2)}) collective-permute-start(bf16[352,1280]{1,0:T(8,128)(2,1)} %get-tuple-element.280), channel_id=1, source_target_pairs={{0,8},{4,12},{8,0},{12,4},{16,24},{20,28},{24,16},{28,20},{1,9},{5... | collective-permute-start | bytes 2703368 | tf_op jit(solution)/shard_map/ppermute | solution.py:773
  325.2 25.6 %collective-permute-start.66 = (bf16[352,1280]{1,0:T(8,128)(2,1)}, bf16[352,1280]{1,0:T(8,128)(2,1)}, u32[]{:S(2)}, u32[]{:S(2)}) collective-permute-start(bf16[352,1280]{1,0:T(8,128)(2,1)} %get-tuple-element.281), channel_id=1, source_target_pairs={{0,16},{4,20},{8,24},{12,28},{16,0},{20,4},{24,8},{28,12},{1,17},{... | collective-permute-start | bytes 2703368 | tf_op jit(solution)/shard_map/ppermute | solution.py:773
  326.2 23.0 %collective-permute-start.71 = (bf16[120,1280]{1,0:T(8,128)(2,1)}, bf16[120,1280]{1,0:T(8,128)(2,1)}, u32[]{:S(2)}, u32[]{:S(2)}) collective-permute-start(bf16[120,1280]{1,0:T(8,128)(2,1)} %get-tuple-element.297), channel_id=1, source_target_pairs={{0,2},{1,3},{2,0},{3,1},{4,6},{5,7},{6,4},{7,5},{8,10},{9,11},{10,... | collective-permute-start | bytes 921608 | tf_op jit(solution)/shard_map/ppermute | solution.py:773
  331.2 18.0 %collective-permute-start.72 = (bf16[120,1280]{1,0:T(8,128)(2,1)}, bf16[120,1280]{1,0:T(8,128)(2,1)}, u32[]{:S(2)}, u32[]{:S(2)}) collective-permute-start(bf16[120,1280]{1,0:T(8,128)(2,1)} %get-tuple-element.299), channel_id=1, source_target_pairs={{0,3},{1,2},{2,1},{3,0},{4,7},{5,6},{6,5},{7,4},{8,11},{9,10},{10,... | collective-permute-start | bytes 921608 | tf_op jit(solution)/shard_map/ppermute | solution.py:773
  353.3 17.0 %collective-permute-start.69 = (bf16[88,1280]{1,0:T(8,128)(2,1)S(1)}, bf16[88,1280]{1,0:T(8,128)(2,1)S(1)}, u32[]{:S(2)}, u32[]{:S(2)}) collective-permute-start(bf16[88,1280]{1,0:T(8,128)(2,1)S(1)} %get-tuple-element.293), channel_id=1, source_target_pairs={{0,3},{1,2},{2,1},{3,0},{4,7},{5,6},{6,5},{7,4},{8,11},{9,10},{10,... | collective-permute-start | bytes 675848 | tf_op jit(solution)/shard_map/ppermute | solution.py:773
  355.7 21.3 %collective-permute-start.68 = (bf16[88,1280]{1,0:T(8,128)(2,1)S(1)}, bf16[88,1280]{1,0:T(8,128)(2,1)S(1)}, u32[]{:S(2)}, u32[]{:S(2)}) collective-permute-start(bf16[88,1280]{1,0:T(8,128)(2,1)S(1)} %get-tuple-element.291), channel_id=1, source_target_pairs={{0,2},{1,3},{2,0},{3,1},{4,6},{5,7},{6,4},{7,5},{8,10},{9,11},{10,... | collective-permute-start | bytes 675848 | tf_op jit(solution)/shard_map/ppermute | solution.py:773
  361.4 15.6 %collective-permute-start.67 = (bf16[88,1280]{1,0:T(8,128)(2,1)S(1)}, bf16[88,1280]{1,0:T(8,128)(2,1)S(1)}, u32[]{:S(2)}, u32[]{:S(2)}) collective-permute-start(bf16[88,1280]{1,0:T(8,128)(2,1)S(1)} %get-tuple-element.289), channel_id=1, source_target_pairs={{0,1},{1,0},{2,3},{3,2},{4,5},{5,4},{6,7},{7,6},{8,9},{9,8},{10,11... | collective-permute-start | bytes 675848 | tf_op jit(solution)/shard_map/ppermute | solution.py:773
  (96 other events, 1077.8 us)

commit v4 on v3

--- a/solution.py
+++ b/solution.py
@@ -1091,19 +1091,20 @@
     plan.gate = [block]
     x, y, other = send(block, 2), send(block, 4), send(block, 1)
     latent_two, latent_one = pass_on(latent_message, 2), pass_on(latent_message, 1)
-    plan.gate = [x, y, other, latent_two, latent_one]
+    plan.gate = [x, y]
     low, high = send(x[:half_one], 4), send(y[half_one:], 2)
+    latent_two = passed(latent_two, latent_one, cost=12)
+    plan.gate = [x, y, latent_two]
     latent_parts = [
         latent_message, latent_one, latent_two, *plan.relay(latent_message, latent_two)
     ]
-    x_other = send(x, 1)
-    y_other = send(tie(y, x_other), 1)
-    plan.gate = [low, high, y_other, *latent_parts[3:]]
-    low_other, high_other = send(low, 1), send(high, 1)
-    pairs = [(block, other), (x, x_other), (y, y_other), (low, low_other), (high, high_other)]
+    plan.gate = [low, high, other]
+    others = [send(v, 1) for v in (x, y, low, high)]
+    pairs = list(zip((block, x, y, low, high), (other, *others)))
     one = held_one(*square_pieces(block, pairs, half_one))
+    plan.gate = [low, high, latent_two]
     two_two, two_one = pass_on(message_two, 2), pass_on(message_two, 1)
-    plan.gate = [low_other, high_other]
+    plan.gate = others
     byte_t, keys, values = key_value(one, tie(bytes_flat, *plan.gate))
     plan.gate = [two_two, two_one, keys]
     parts = [message_two, two_one, two_two, *plan.relay(message_two, two_two)]

time: 385 us -> 377 us (0.979)
  waiting for transfers between devices: 135 us -> 123 us
  starting transfers between devices: 79.1 us -> 86.9 us
    ppermute x61, waiting for transfers between devices: 112 us -> 101 us  [swap(): return lax.ppermute(value, axis, [(i, i ^ distance) for i in range(size)])]
    ppermute x61, starting transfers between devices: 62.1 us -> 69.9 us  [swap(): return lax.ppermute(value, axis, [(i, i ^ distance) for i in range(size)])]
    unnamed x176 -> x156, local copies, waits for them, and re-layouts: 16.7 us -> 14.3 us
  transfers between devices with their start and end apart: 73 -> 73, of which waited for: 28 -> 28; matrix products, arithmetic and copies ran while one was open for 4% -> 3% of each run, Pallas kernels for 29% -> 30%
where the time goes in v4:
time: 377 us; the launch traced here: 371 us
  Pallas kernels  129 us (34%)
  waiting for transfers between devices  123 us (33%)
  starting transfers between devices  86.9 us (23%)
  local copies, waits for them, and re-layouts  17.9 us (5%)
  other arithmetic  12.1 us (3%)
    ppermute x61, waiting for transfers between devices, swap(): return lax.ppermute(value, axis, [(i, i ^ distance) for i in range(size)])  101 us
    ppermute x61, starting transfers between devices, swap(): return lax.ppermute(value, axis, [(i, i ^ distance) for i in range(size)])  69.9 us
    pallas_call x2, Pallas kernels, attend_back_call(): pl.pallas_call(kernel, grid_spec=pltpu.PrefetchScalarGridSpec(num_scalar_...  24 us
    pallas_call x2, Pallas kernels, attend_call(): pl.pallas_call(kernel, grid_spec=pltpu.PrefetchScalarGridSpec(num_scalar_...  23.9 us
    ppermute x5, waiting for transfers between devices, relay(): lax.ppermute(tie(two, *self.gate), 'fsdp', [(2, 3), (1, 0)])  22.5 us
    pallas_call x1, Pallas kernels, byte_grad_call(): pl.pallas_call(kernel, grid_spec=pltpu.PrefetchScalarGridSpec(num_scalar_...  16.4 us
    pallas_call x1, Pallas kernels, weight_grads_call(): pl.pallas_call(kernel, grid_spec=pltpu.PrefetchScalarGridSpec(num_scalar_...  15.1 us
    unnamed x156, local copies, waits for them, and re-layouts  14.3 us
  transfers between devices with their start and end apart: 73, of which 28 were waited for; matrix products, arithmetic and copies ran while one was open for 3% of the time, Pallas kernels for 30%

profile of v4, /device:TPU:0, one launch (start us, length us, event | category | flops | bytes accessed | tf_op | source)
XLA Modules:
  0.0 371.2 jit_solution(7779765000092932072)
XLA Ops:
  2.4 4.1 %collective-permute-start.1 = (bf16[96,1280]{1,0:T(8,128)(2,1)S(1)}, bf16[96,1280]{1,0:T(8,128)(2,1)S(1)}, u32[]{:S(2)}, u32[]{:S(2)}) collective-permute-start(bf16[96,1280]{1,0:T(8,128)(2,1)S(1)} %fusion.8.refs_0_), channel_id=1, source_target_pairs={{0,2},{1,3},{2,0},{3,1},{4,6},{5,7},{6,4},{7,5},{8,10},{9,11},{10,... | collective-permute-start | bytes 737288 | tf_op jit(solution)/shard_map/ppermute | solution.py:773
  6.5 1.6 collective-permute-start
  8.1 9.7 %collective-permute-done.1.refs_2_ = bf16[96,1280]{1,0:T(8,128)(2,1)S(1)} collective-permute-done((bf16[96,1280]{1,0:T(8,128)(2,1)S(1)}, bf16[96,1280]{1,0:T(8,128)(2,1)S(1)}, u32[]{:S(2)}, u32[]{:S(2)}) %collective-permute-start.1) | collective-permute-done | bytes 245792 | tf_op jit(solution)/shard_map/ppermute | solution.py:773
  20.1 7.9 %collective-permute-done.3.refs_4_ = bf16[96,1280]{1,0:T(8,128)(2,1)S(1)} collective-permute-done((bf16[96,1280]{1,0:T(8,128)(2,1)S(1)}, bf16[96,1280]{1,0:T(8,128)(2,1)S(1)}, u32[]{:S(2)}, u32[]{:S(2)}) %collective-permute-start.3) | collective-permute-done | bytes 245792 | tf_op jit(solution)/shard_map/ppermute | solution.py:926
  29.2 1.6 collective-permute-start.4
  30.7 1.5 collective-permute-start.5
  32.8 4.1 %collective-permute-start.8 = (bf16[192,1408]{1,0:T(8,128)(2,1)S(1)}, bf16[192,1408]{1,0:T(8,128)(2,1)}, u32[]{:S(2)}, u32[]{:S(2)}) collective-permute-start(bf16[192,1408]{1,0:T(8,128)(2,1)S(1)} %fusion.1.refs_0_.refs_8_.x_ref), channel_id=1, source_target_pairs={{0,2},{1,3},{2,0},{3,1},{4,6},{5,7},{6,4},{7,5},{8,10},{9,11},{10,... | collective-permute-start | bytes 1622024 | tf_op jit(solution)/shard_map/ppermute | solution.py:773
  36.9 13.2 %collective-permute-done.4.refs_2_.refs_10_.refs_12_.refs_11_.refs_6_ = bf16[368,1280]{1,0:T(8,128)(2,1)S(1)} collective-permute-done((bf16[368,1280]{1,0:T(8,128)(2,1)S(1)}, bf16[368,1280]{1,0:T(8,128)(2,1)S(1)}, u32[]{:S(2)}, u32[]{:S(2)}) %collective-permute-start.4) | collective-permute-done | bytes 942112 | tf_op jit(solution)/shard_map/ppermute | solution.py:773
  50.1 1.5 collective-permute-done.5.refs_4_.refs_12_.refs_14_.refs_13_.refs_8_
  51.7 1.5 collective-permute-start.6
  54.6 4.0 %collective-permute-done.9.refs_1_ = bf16[192,1408]{1,0:T(8,128)(2,1)S(1)} collective-permute-done((bf16[192,1408]{1,0:T(8,128)(2,1)S(1)}, bf16[192,1408]{1,0:T(8,128)(2,1)S(1)}, u32[]{:S(2)}, u32[]{:S(2)}) %collective-permute-start.9) | collective-permute-done | bytes 540704 | tf_op jit(solution)/shard_map/ppermute | solution.py:773
  58.6 2.6 collective-permute-done.8.in_ref
  61.3 1.6 collective-permute-done.7.refs_7_.refs_15_.refs_17_.refs_16_.refs_11_
  65.1 5.4 %collective-permute-start.10 = (bf16[120,1280]{1,0:T(8,128)(2,1)}, bf16[120,1280]{1,0:T(8,128)(2,1)}, u32[]{:S(2)}, u32[]{:S(2)}) collective-permute-start(bf16[120,1280]{1,0:T(8,128)(2,1)} %copy-done.26), channel_id=1, source_target_pairs={{0,2},{1,3},{2,0},{3,1},{4,6},{5,7},{6,4},{7,5},{8,10},{9,11},{10,... | collective-permute-start | bytes 921608 | tf_op jit(solution)/shard_map/ppermute | solution.py:773
  72.5 13.7 %keys_values.1 = (bf16[768,1536]{1,0:T(8,128)(2,1)}, bf16[1536,1280]{1,0:T(8,128)(2,1)}, bf16[1536,1280]{1,0:T(8,128)(2,1)}) custom-call(s32[2]{0:T(128)} %copy-done.38, bf16[1536,768]{1,0:T(8,128)(2,1)} %bitcast.8, bf16[368,1280]{1,0:T(8,128)(2,1)} %copy-done, bf16[368,1280]{1,0:T(8,128)(2,1)} %collective-permute-done.12.refs_1_.refs_9_.refs_11_.refs_10_.refs_5_, ...), custom_call_target="tpu_custom_call" | custom-call | flops 1 | bytes 1 | tf_op jit(solution)/shard_map/keys_values/pallas_call | solution.py:237
  87.6 1.8 collective-permute-start.20
  91.7 9.7 %attend.2 = (bf16[1280,256]{1,0:T(8,128)(2,1)}, bf16[256,1280]{1,0:T(8,128)(2,1)}, bf16[64,1408]{1,0:T(8,128)(2,1)}, bf16[64,1408]{1,0:T(8,128)(2,1)}, bf16[64,1...) custom-call(s32[2]{0:T(128)} %copy-done.38, bf16[192,1408]{1,0:T(8,128)(2,1)} %copy-done.10, bf16[192,1408]{1,0:T(8,128)(2,1)} %copy-done.43, ...), custom_call_target="tpu_custom_call" | custom-call | flops 1 | bytes 1 | tf_op jit(solution)/shard_map/attend/pallas_call | solution.py:333
  102.2 1.5 assemble.3.refs_20_
  105.1 5.8 %collective-permute-start.23 = (bf16[64,1408]{1,0:T(8,128)(2,1)S(1)}, bf16[64,1408]{1,0:T(8,128)(2,1)S(1)}, u32[]{:S(2)}, u32[]{:S(2)}) collective-permute-start(bf16[64,1408]{1,0:T(8,128)(2,1)S(1)} %copy-done.76), channel_id=1, source_target_pairs={{0,3},{1,2},{2,1},{3,0},{4,7},{5,6},{6,5},{7,4},{8,11},{9,10},{10,... | collective-permute-start | bytes 540680 | tf_op jit(solution)/shard_map/ppermute | solution.py:773
  110.9 1.8 collective-permute-start.22
  113.3 14.2 %attend.3 = (bf16[1280,512]{1,0:T(8,128)(2,1)}, bf16[512,1280]{1,0:T(8,128)(2,1)}, bf16[128,1408]{1,0:T(8,128)(2,1)}, bf16[128,1408]{1,0:T(8,128)(2,1)}, bf16[12...) custom-call(s32[2]{0:T(128)} %copy-done.38, bf16[192,1408]{1,0:T(8,128)(2,1)} %copy-done.10, bf16[192,1408]{1,0:T(8,128)(2,1)} %copy-done.43, ...), custom_call_target="tpu_custom_call" | custom-call | flops 1 | bytes 1 | tf_op jit(solution)/shard_map/attend/pallas_call | solution.py:333
  127.6 2.4 collective-permute-start.26
  130.6 1.5 collective-permute-start.24
  133.0 1.9 slice.74
  134.9 1.5 collective-permute-start.29
  136.4 1.3 collective-permute-start.30
  137.7 3.5 collective-permute-done.26.refs_7_
  141.1 19.3 %collective-permute-done.25.refs_5_ = bf16[128,1408]{1,0:T(8,128)(2,1)} collective-permute-done((bf16[128,1408]{1,0:T(8,128)(2,1)}, bf16[128,1408]{1,0:T(8,128)(2,1)}, u32[]{:S(2)}, u32[]{:S(2)}) %collective-permute-start.25) | collective-permute-done | bytes 360480 | tf_op jit(solution)/shard_map/ppermute | solution.py:773
  161.6 7.1 %collective-permute-done.34.refs_28_ = bf16[240,1280]{1,0:T(8,128)(2,1)S(1)} collective-permute-done((bf16[240,1280]{1,0:T(8,128)(2,1)S(1)}, bf16[240,1280]{1,0:T(8,128)(2,1)S(1)}, u32[]{:S(2)}, u32[]{:S(2)}) %collective-permute-start.34) | collective-permute-done | bytes 614432 | tf_op jit(solution)/shard_map/ppermute | solution.py:773
  170.9 14.2 %feed.1 = (bf16[192,1280]{1,0:T(8,128)(2,1)}, f32[192,1280]{1,0:T(8,128)}, bf16[64,1408]{1,0:T(8,128)(2,1)}, bf16[128,1408]{1,0:T(8,128)(2,1)}, bf16[1280,192]{1...) custom-call(s32[2]{0:T(128)} %copy-done.38, ...), custom_call_target="tpu_custom_call" | custom-call | flops 1 | bytes 1 | tf_op jit(solution)/shard_map/feed/pallas_call | solution.py:450
  185.2 3.1 collective-permute-start.36
  188.3 6.6 %feed_grads.1 = (bf16[480,1280]{1,0:T(8,128)(2,1)}, bf16[480,1280]{1,0:T(8,128)(2,1)}, bf16[480,1280]{1,0:T(8,128)(2,1)}, bf16[480,1280]{1,0:T(8,128)(2,1)}, bf1...) custom-call(s32[2]{0:T(128)} %copy-done.38, ...), custom_call_target="tpu_custom_call" | custom-call | flops 1 | bytes 1 | tf_op jit(solution)/shard_map/feed_grads/pallas_call | solution.py:493
  195.7 1.5 collective-permute-done.36.refs_2_
  198.3 1.5 collective-permute-start.41
  199.8 6.8 %collective-permute-done.41.refs_4_ = bf16[64,1408]{1,0:T(8,128)(2,1)S(1)} collective-permute-done((bf16[64,1408]{1,0:T(8,128)(2,1)S(1)}, bf16[64,1408]{1,0:T(8,128)(2,1)S(1)}, u32[]{:S(2)}, u32[]{:S(2)}) %collective-permute-start.41) | collective-permute-done | bytes 180256 | tf_op jit(solution)/shard_map/ppermute | solution.py:926
  207.8 2.6 add_convert_fusion
  210.4 1.4 collective-permute-start.43
  211.8 1.4 collective-permute-start.44
  213.2 3.0 collective-permute-start.45
  216.2 8.8 %attend_back.2 = (bf16[512,1280]{1,0:T(8,128)(2,1)}, bf16[512,1280]{1,0:T(8,128)(2,1)}, bf16[256,1280]{1,0:T(8,128)(2,1)}, bf16[64,1280]{1,0:T(8,128)(2,1)}, bf1...) custom-call(s32[2]{0:T(128)} %copy-done.38, ...), custom_call_target="tpu_custom_call" | custom-call | flops 1 | bytes 1 | tf_op jit(solution)/shard_map/attend_back/pallas_call | solution.py:577
  225.0 6.3 %collective-permute-done.46.refs_1_ = bf16[128,1408]{1,0:T(8,128)(2,1)} collective-permute-done((bf16[128,1408]{1,0:T(8,128)(2,1)}, bf16[128,1408]{1,0:T(8,128)(2,1)}, u32[]{:S(2)}, u32[]{:S(2)}) %collective-permute-start.46) | collective-permute-done | bytes 360480 | tf_op jit(solution)/shard_map/ppermute | solution.py:773
  238.1 3.0 meet.2
  241.2 6.0 %collective-permute-done.49.refs_4_ = bf16[128,1408]{1,0:T(8,128)(2,1)S(1)} collective-permute-done((bf16[128,1408]{1,0:T(8,128)(2,1)}, bf16[128,1408]{1,0:T(8,128)(2,1)S(1)}, u32[]{:S(2)}, u32[]{:S(2)}) %collective-permute-start.49) | collective-permute-done | bytes 360480 | tf_op jit(solution)/shard_map/ppermute | solution.py:926
  248.5 2.9 collective-permute-start.51
  251.4 1.5 collective-permute-start.52
  252.9 15.2 %attend_back.3 = (bf16[1024,1280]{1,0:T(8,128)(2,1)}, bf16[1024,1280]{1,0:T(8,128)(2,1)}, bf16[512,1280]{1,0:T(8,128)(2,1)}, bf16[128,1280]{1,0:T(8,128)(2,1)}, ...) custom-call(s32[2]{0:T(128)} %copy-done.38, ...), custom_call_target="tpu_custom_call" | custom-call | flops 1 | bytes 1 | tf_op jit(solution)/shard_map/attend_back/pallas_call | solution.py:577
  269.5 4.7 %collective-permute-start.55 = (bf16[128,1280]{1,0:T(8,128)(2,1)}, bf16[128,1280]{1,0:T(8,128)(2,1)}, u32[]{:S(2)}, u32[]{:S(2)}) collective-permute-start(bf16[128,1280]{1,0:T(8,128)(2,1)} %get-tuple-element.258), channel_id=1, source_target_pairs={{3,2},{0,1},{7,6},{4,5},{11,10},{8,9},{15,14},{12,13},{19,18},{16,... | collective-permute-start | bytes 983048 | tf_op jit(solution)/shard_map/ppermute | solution.py:931
  274.2 1.8 collective-permute-start.54
  275.9 15.1 %weight_grads.1 = (bf16[352,1280]{1,0:T(8,128)(2,1)}, bf16[352,1280]{1,0:T(8,128)(2,1)}, bf16[352,1280]{1,0:T(8,128)(2,1)}, bf16[352,1280]{1,0:T(8,128)(2,1)}, b...) custom-call(s32[2]{0:T(128)} %copy-done.38, ...), custom_call_target="tpu_custom_call" | custom-call | flops 1 | bytes 1 | tf_op jit(solution)/shard_map/weight_grads/pallas_call | solution.py:647
  296.4 1.3 collective-permute-start.62
  297.7 1.5 collective-permute-start.61
  299.8 2.6 cut.2
  302.4 6.5 %collective-permute-done.61.h = bf16[160,1280]{1,0:T(8,128)(2,1)S(1)} collective-permute-done((bf16[160,1280]{1,0:T(8,128)(2,1)S(1)}, bf16[160,1280]{1,0:T(8,128)(2,1)S(1)}, u32[]{:S(2)}, u32[]{:S(2)}) %collective-permute-start.61) | collective-permute-done | bytes 409632 | tf_op jit(solution)/shard_map/ppermute | solution.py:773
  310.2 1.6 meet.3
  311.9 4.5 %collective-permute-done.63.refs_7_ = bf16[128,1280]{1,0:T(8,128)(2,1)S(1)} collective-permute-done((bf16[128,1280]{1,0:T(8,128)(2,1)S(1)}, bf16[128,1280]{1,0:T(8,128)(2,1)S(1)}, u32[]{:S(2)}, u32[]{:S(2)}) %collective-permute-start.63) | collective-permute-done | bytes 327712 | tf_op jit(solution)/shard_map/ppermute | solution.py:773
  318.4 4.5 %collective-permute-done.70 = bf16[120,1280]{1,0:T(8,128)(2,1)S(1)} collective-permute-done((bf16[120,1280]{1,0:T(8,128)(2,1)S(1)}, bf16[120,1280]{1,0:T(8,128)(2,1)S(1)}, u32[]{:S(2)}, u32[]{:S(2)}) %collective-permute-start.70) | collective-permute-done | bytes 307232 | tf_op jit(solution)/shard_map/ppermute | solution.py:773
  323.7 1.5 collective-permute-start.72
  325.2 16.4 %byte_grad.1 = f32[1536,768]{1,0:T(8,128)} custom-call(s32[2]{0:T(128)} %copy-done.38, bf16[1536,768]{1,0:T(8,128)(2,1)} %bitcast.9, bf16[512,1280]{1,0:T(8,128)(2,1)} %get-tuple-element.282.refs_3_.refs_0_, bf16[512,1280]{1,0:T(8,128)(2,1)} %get-tuple-element.247.refs_5_.refs_1_, bf16[1024,1280]{1,0:T(8,128)(2,1)} %get-tuple-element.246.refs_4_.refs_2_, ...), custom_call_target="tpu_custom_call" | custom-call | flops 1 | bytes 1 | tf_op jit(solution)/shard_map/byte_grad/pallas_call | solution.py:707
  341.7 1.4 convert_add_fusion
  343.2 1.4 cut.3
  344.6 2.4 collective-permute-start.69
  347.0 5.4 %collective-permute-start.68 = (bf16[88,1280]{1,0:T(8,128)(2,1)S(1)}, bf16[88,1280]{1,0:T(8,128)(2,1)S(1)}, u32[]{:S(2)}, u32[]{:S(2)}) collective-permute-start(bf16[88,1280]{1,0:T(8,128)(2,1)S(1)} %get-tuple-element.291), channel_id=1, source_target_pairs={{0,2},{1,3},{2,0},{3,1},{4,6},{5,7},{6,4},{7,5},{8,10},{9,11},{10,... | collective-permute-start | bytes 675848 | tf_op jit(solution)/shard_map/ppermute | solution.py:773
  356.7 3.6 latent_grad.1
  360.4 7.8 %collective-permute-done.68 = bf16[88,1280]{1,0:T(8,128)(2,1)S(1)} collective-permute-done((bf16[88,1280]{1,0:T(8,128)(2,1)S(1)}, bf16[88,1280]{1,0:T(8,128)(2,1)S(1)}, u32[]{:S(2)}, u32[]{:S(2)}) %collective-permute-start.68) | collective-permute-done | bytes 225312 | tf_op jit(solution)/shard_map/ppermute | solution.py:773
  (282 shorter events, 52.3 us)
Async XLA Ops:
  2.4 15.4 %collective-permute-start.1 = (bf16[96,1280]{1,0:T(8,128)(2,1)S(1)}, bf16[96,1280]{1,0:T(8,128)(2,1)S(1)}, u32[]{:S(2)}, u32[]{:S(2)}) collective-permute-start(bf16[96,1280]{1,0:T(8,128)(2,1)S(1)} %fusion.8.refs_0_), channel_id=1, source_target_pairs={{0,2},{1,3},{2,0},{3,1},{4,6},{5,7},{6,4},{7,5},{8,10},{9,11},{10,... | collective-permute-start | bytes 737288 | tf_op jit(solution)/shard_map/ppermute | solution.py:773
  6.5 11.5 %collective-permute-start = (bf16[96,1280]{1,0:T(8,128)(2,1)S(1)}, bf16[96,1280]{1,0:T(8,128)(2,1)S(1)}, u32[]{:S(2)}, u32[]{:S(2)}) collective-permute-start(bf16[96,1280]{1,0:T(8,128)(2,1)S(1)} %fusion.8.refs_0_), channel_id=1, source_target_pairs={{0,1},{1,0},{2,3},{3,2},{4,5},{5,4},{6,7},{7,6},{8,9},{9,8},{10,11... | collective-permute-start | bytes 737288 | tf_op jit(solution)/shard_map/ppermute | solution.py:773
  18.7 9.3 %collective-permute-start.3 = (bf16[96,1280]{1,0:T(8,128)(2,1)S(1)}, bf16[96,1280]{1,0:T(8,128)(2,1)S(1)}, u32[]{:S(2)}, u32[]{:S(2)}) collective-permute-start(bf16[96,1280]{1,0:T(8,128)(2,1)S(1)} %collective-permute-done.1.refs_2_), channel_id=1, source_target_pairs={{2,3},{1,0},{6,7},{5,4},{10,11},{9,8},{14,15},{13,12},{18,19},{17,... | collective-permute-start | bytes 737288 | tf_op jit(solution)/shard_map/ppermute | solution.py:926
  29.2 20.9 %collective-permute-start.4 = (bf16[368,1280]{1,0:T(8,128)(2,1)S(1)}, bf16[368,1280]{1,0:T(8,128)(2,1)S(1)}, u32[]{:S(2)}, u32[]{:S(2)}) collective-permute-start(bf16[368,1280]{1,0:T(8,128)(2,1)S(1)} %assemble.2.refs_0_.refs_8_.refs_10_.refs_9_.refs_4_), channel_id=1, source_target_pairs={{0,8},{4,12},{8,0},{12,4},{16,24},{20,28},{24,16},{28,20},{1,9},{5... | collective-permute-start | bytes 2826248 | tf_op jit(solution)/shard_map/ppermute | solution.py:773
  30.7 20.9 %collective-permute-start.5 = (bf16[368,1280]{1,0:T(8,128)(2,1)S(1)}, bf16[368,1280]{1,0:T(8,128)(2,1)S(1)}, u32[]{:S(2)}, u32[]{:S(2)}) collective-permute-start(bf16[368,1280]{1,0:T(8,128)(2,1)S(1)} %assemble.2.refs_0_.refs_8_.refs_10_.refs_9_.refs_4_), channel_id=1, source_target_pairs={{0,16},{4,20},{8,24},{12,28},{16,0},{20,4},{24,8},{28,12},{1,17},{... | collective-permute-start | bytes 2826248 | tf_op jit(solution)/shard_map/ppermute | solution.py:773
  32.2 29.0 %collective-permute-start.12 = (bf16[368,1280]{1,0:T(8,128)(2,1)S(1)}, bf16[368,1280]{1,0:T(8,128)(2,1)}, u32[]{:S(2)}, u32[]{:S(2)}) collective-permute-start(bf16[368,1280]{1,0:T(8,128)(2,1)S(1)} %assemble.2.refs_0_.refs_8_.refs_10_.refs_9_.refs_4_), channel_id=1, source_target_pairs={{0,4},{4,0},{8,12},{12,8},{16,20},{20,16},{24,28},{28,24},{1,5},{5... | collective-permute-start | bytes 2826248 | tf_op jit(solution)/shard_map/ppermute | solution.py:773
  32.5 26.1 %collective-permute-start.9 = (bf16[192,1408]{1,0:T(8,128)(2,1)S(1)}, bf16[192,1408]{1,0:T(8,128)(2,1)S(1)}, u32[]{:S(2)}, u32[]{:S(2)}) collective-permute-start(bf16[192,1408]{1,0:T(8,128)(2,1)S(1)} %fusion.1.refs_0_.refs_8_.x_ref), channel_id=1, source_target_pairs={{0,1},{1,0},{2,3},{3,2},{4,5},{5,4},{6,7},{7,6},{8,9},{9,8},{10,11... | collective-permute-start | bytes 1622024 | tf_op jit(solution)/shard_map/ppermute | solution.py:773
  32.8 28.5 %collective-permute-start.8 = (bf16[192,1408]{1,0:T(8,128)(2,1)S(1)}, bf16[192,1408]{1,0:T(8,128)(2,1)}, u32[]{:S(2)}, u32[]{:S(2)}) collective-permute-start(bf16[192,1408]{1,0:T(8,128)(2,1)S(1)} %fusion.1.refs_0_.refs_8_.x_ref), channel_id=1, source_target_pairs={{0,2},{1,3},{2,0},{3,1},{4,6},{5,7},{6,4},{7,5},{8,10},{9,11},{10,... | collective-permute-start | bytes 1622024 | tf_op jit(solution)/shard_map/ppermute | solution.py:773
  51.7 11.3 %collective-permute-start.6 = (bf16[192,1280]{1,0:T(8,128)(2,1)S(1)}, bf16[192,1280]{1,0:T(8,128)(2,1)S(1)}, u32[]{:S(2)}, u32[]{:S(2)}) collective-permute-start(bf16[192,1280]{1,0:T(8,128)(2,1)S(1)} %slice.72), channel_id=1, source_target_pairs={{0,16},{4,20},{8,24},{12,28},{16,0},{20,4},{24,8},{28,12},{1,17},{... | collective-permute-start | bytes 1474568 | tf_op jit(solution)/shard_map/ppermute | solution.py:773
  54.1 8.8 %collective-permute-start.7 = (bf16[176,1280]{1,0:T(8,128)(2,1)S(1)}, bf16[176,1280]{1,0:T(8,128)(2,1)}, u32[]{:S(2)}, u32[]{:S(2)}) collective-permute-start(bf16[176,1280]{1,0:T(8,128)(2,1)S(1)} %slice.73), channel_id=1, source_target_pairs={{0,8},{4,12},{8,0},{12,4},{16,24},{20,28},{24,16},{28,20},{1,9},{5... | collective-permute-start | bytes 1351688 | tf_op jit(solution)/shard_map/ppermute | solution.py:773
  63.4 7.7 %collective-permute-start.13 = (bf16[368,1280]{1,0:T(8,128)(2,1)S(1)}, bf16[368,1280]{1,0:T(8,128)(2,1)S(1)}, u32[]{:S(2)}, u32[]{:S(2)}) collective-permute-start(bf16[368,1280]{1,0:T(8,128)(2,1)S(1)} %collective-permute-done.4.refs_2_.refs_10_.refs_12_.refs_11_.refs_6_), channel_id=1, source_target_pairs={{0,4},{4,0},{8,12},{12,8},{16,20},{20,16},{24,28},{28,24},{1,5},{5... | collective-permute-start | bytes 2826248 | tf_op jit(solution)/shard_map/ppermute | solution.py:773
  63.5 8.9 %collective-permute-start.14 = (bf16[368,1280]{1,0:T(8,128)(2,1)S(1)}, bf16[368,1280]{1,0:T(8,128)(2,1)}, u32[]{:S(2)}, u32[]{:S(2)}) collective-permute-start(bf16[368,1280]{1,0:T(8,128)(2,1)S(1)} %collective-permute-done.5.refs_4_.refs_12_.refs_14_.refs_13_.refs_8_), channel_id=1, source_target_pairs={{0,4},{4,0},{8,12},{12,8},{16,20},{20,16},{24,28},{28,24},{1,5},{5... | collective-permute-start | bytes 2826248 | tf_op jit(solution)/shard_map/ppermute | solution.py:773
  64.0 22.2 %collective-permute-start.11 = (bf16[120,1280]{1,0:T(8,128)(2,1)}, bf16[120,1280]{1,0:T(8,128)(2,1)S(1)}, u32[]{:S(2)}, u32[]{:S(2)}) collective-permute-start(bf16[120,1280]{1,0:T(8,128)(2,1)} %copy-done.26), channel_id=1, source_target_pairs={{0,1},{1,0},{2,3},{3,2},{4,5},{5,4},{6,7},{7,6},{8,9},{9,8},{10,11... | collective-permute-start | bytes 921608 | tf_op jit(solution)/shard_map/ppermute | solution.py:773
  65.1 21.9 %collective-permute-start.10 = (bf16[120,1280]{1,0:T(8,128)(2,1)}, bf16[120,1280]{1,0:T(8,128)(2,1)}, u32[]{:S(2)}, u32[]{:S(2)}) collective-permute-start(bf16[120,1280]{1,0:T(8,128)(2,1)} %copy-done.26), channel_id=1, source_target_pairs={{0,2},{1,3},{2,0},{3,1},{4,6},{5,7},{6,4},{7,5},{8,10},{9,11},{10,... | collective-permute-start | bytes 921608 | tf_op jit(solution)/shard_map/ppermute | solution.py:773
  70.4 20.3 %collective-permute-start.17 = (bf16[192,1408]{1,0:T(8,128)(2,1)}, bf16[192,1408]{1,0:T(8,128)(2,1)S(1)}, u32[]{:S(2)}, u32[]{:S(2)}) collective-permute-start(bf16[192,1408]{1,0:T(8,128)(2,1)} %copy-done.10), channel_id=1, source_target_pairs={{1,2},{2,1},{5,6},{6,5},{9,10},{10,9},{13,14},{14,13},{17,18},{18,... | collective-permute-start | bytes 1622024 | tf_op jit(solution)/shard_map/ppermute | solution.py:925
  71.1 20.6 %collective-permute-start.18 = (bf16[192,1408]{1,0:T(8,128)(2,1)}, bf16[192,1408]{1,0:T(8,128)(2,1)}, u32[]{:S(2)}, u32[]{:S(2)}) collective-permute-start(bf16[192,1408]{1,0:T(8,128)(2,1)} %passed.2.refs_2_), channel_id=1, source_target_pairs={{2,3},{1,0},{6,7},{5,4},{10,11},{9,8},{14,15},{13,12},{18,19},{17,... | collective-permute-start | bytes 1622024 | tf_op jit(solution)/shard_map/ppermute | solution.py:926
  86.9 14.4 %collective-permute-start.19 = (bf16[120,1280]{1,0:T(8,128)(2,1)S(1)}, bf16[120,1280]{1,0:T(8,128)(2,1)S(1)}, u32[]{:S(2)}, u32[]{:S(2)}) collective-permute-start(bf16[120,1280]{1,0:T(8,128)(2,1)S(1)} %copy-done.27), channel_id=1, source_target_pairs={{1,2},{2,1},{5,6},{6,5},{9,10},{10,9},{13,14},{14,13},{17,18},{18,... | collective-permute-start | bytes 921608 | tf_op jit(solution)/shard_map/ppermute | solution.py:925
  87.6 14.6 %collective-permute-start.20 = (bf16[120,1280]{1,0:T(8,128)(2,1)}, bf16[120,1280]{1,0:T(8,128)(2,1)S(1)}, u32[]{:S(2)}, u32[]{:S(2)}) collective-permute-start(bf16[120,1280]{1,0:T(8,128)(2,1)} %collective-permute-done.10.refs_2_), channel_id=1, source_target_pairs={{2,3},{1,0},{6,7},{5,4},{10,11},{9,8},{14,15},{13,12},{18,19},{17,... | collective-permute-start | bytes 921608 | tf_op jit(solution)/shard_map/ppermute | solution.py:926
  103.7 28.3 %collective-permute-start.28 = (bf16[480,1280]{1,0:T(8,128)(2,1)S(1)}, bf16[480,1280]{1,0:T(8,128)(2,1)S(1)}, u32[]{:S(2)}, u32[]{:S(2)}) collective-permute-start(bf16[480,1280]{1,0:T(8,128)(2,1)S(1)} %assemble.3.refs_20_), channel_id=1, source_target_pairs={{0,16},{4,20},{8,24},{12,28},{16,0},{20,4},{24,8},{28,12},{1,17},{... | collective-permute-start | bytes 3686408 | tf_op jit(solution)/shard_map/ppermute | solution.py:773
  104.4 28.6 %collective-permute-start.27 = (bf16[480,1280]{1,0:T(8,128)(2,1)S(1)}, bf16[480,1280]{1,0:T(8,128)(2,1)}, u32[]{:S(2)}, u32[]{:S(2)}) collective-permute-start(bf16[480,1280]{1,0:T(8,128)(2,1)S(1)} %assemble.3.refs_20_), channel_id=1, source_target_pairs={{0,8},{4,12},{8,0},{12,4},{16,24},{20,28},{24,16},{28,20},{1,9},{5... | collective-permute-start | bytes 3686408 | tf_op jit(solution)/shard_map/ppermute | solution.py:773
  105.1 22.4 %collective-permute-start.23 = (bf16[64,1408]{1,0:T(8,128)(2,1)S(1)}, bf16[64,1408]{1,0:T(8,128)(2,1)S(1)}, u32[]{:S(2)}, u32[]{:S(2)}) collective-permute-start(bf16[64,1408]{1,0:T(8,128)(2,1)S(1)} %copy-done.76), channel_id=1, source_target_pairs={{0,3},{1,2},{2,1},{3,0},{4,7},{5,6},{6,5},{7,4},{8,11},{9,10},{10,... | collective-permute-start | bytes 540680 | tf_op jit(solution)/shard_map/ppermute | solution.py:773
  110.9 16.6 %collective-permute-start.22 = (bf16[64,1408]{1,0:T(8,128)(2,1)S(1)}, bf16[64,1408]{1,0:T(8,128)(2,1)S(1)}, u32[]{:S(2)}, u32[]{:S(2)}) collective-permute-start(bf16[64,1408]{1,0:T(8,128)(2,1)S(1)} %copy-done.75), channel_id=1, source_target_pairs={{0,2},{1,3},{2,0},{3,1},{4,6},{5,7},{6,4},{7,5},{8,10},{9,11},{10,... | collective-permute-start | bytes 540680 | tf_op jit(solution)/shard_map/ppermute | solution.py:773
  112.7 14.8 %collective-permute-start.21 = (bf16[64,1408]{1,0:T(8,128)(2,1)S(1)}, bf16[64,1408]{1,0:T(8,128)(2,1)S(1)}, u32[]{:S(2)}, u32[]{:S(2)}) collective-permute-start(bf16[64,1408]{1,0:T(8,128)(2,1)S(1)} %copy-done.74), channel_id=1, source_target_pairs={{0,1},{1,0},{2,3},{3,2},{4,5},{5,4},{6,7},{7,6},{8,9},{9,8},{10,11... | collective-permute-start | bytes 540680 | tf_op jit(solution)/shard_map/ppermute | solution.py:773
  127.6 13.5 %collective-permute-start.26 = (bf16[128,1408]{1,0:T(8,128)(2,1)}, bf16[128,1408]{1,0:T(8,128)(2,1)S(1)}, u32[]{:S(2)}, u32[]{:S(2)}) collective-permute-start(bf16[128,1408]{1,0:T(8,128)(2,1)} %get-tuple-element.192), channel_id=1, source_target_pairs={{0,3},{1,2},{2,1},{3,0},{4,7},{5,6},{6,5},{7,4},{8,11},{9,10},{10,... | collective-permute-start | bytes 1081352 | tf_op jit(solution)/shard_map/ppermute | solution.py:773
  129.9 30.5 %collective-permute-start.25 = (bf16[128,1408]{1,0:T(8,128)(2,1)}, bf16[128,1408]{1,0:T(8,128)(2,1)}, u32[]{:S(2)}, u32[]{:S(2)}) collective-permute-start(bf16[128,1408]{1,0:T(8,128)(2,1)} %get-tuple-element.190), channel_id=1, source_target_pairs={{0,2},{1,3},{2,0},{3,1},{4,6},{5,7},{6,4},{7,5},{8,10},{9,11},{10,... | collective-permute-start | bytes 1081352 | tf_op jit(solution)/shard_map/ppermute | solution.py:773
  130.6 29.8 %collective-permute-start.24 = (bf16[128,1408]{1,0:T(8,128)(2,1)}, bf16[128,1408]{1,0:T(8,128)(2,1)}, u32[]{:S(2)}, u32[]{:S(2)}) collective-permute-start(bf16[128,1408]{1,0:T(8,128)(2,1)} %get-tuple-element.188), channel_id=1, source_target_pairs={{0,1},{1,0},{2,3},{3,2},{4,5},{5,4},{6,7},{7,6},{8,9},{9,8},{10,11... | collective-permute-start | bytes 1081352 | tf_op jit(solution)/shard_map/ppermute | solution.py:773
  134.9 25.5 %collective-permute-start.29 = (bf16[240,1280]{1,0:T(8,128)(2,1)}, bf16[240,1280]{1,0:T(8,128)(2,1)S(1)}, u32[]{:S(2)}, u32[]{:S(2)}) collective-permute-start(bf16[240,1280]{1,0:T(8,128)(2,1)} %slice.74), channel_id=1, source_target_pairs={{0,16},{4,20},{8,24},{12,28},{16,0},{20,4},{24,8},{28,12},{1,17},{... | collective-permute-start | bytes 1843208 | tf_op jit(solution)/shard_map/ppermute | solution.py:773
  136.4 24.1 %collective-permute-start.30 = (bf16[240,1280]{1,0:T(8,128)(2,1)}, bf16[240,1280]{1,0:T(8,128)(2,1)}, u32[]{:S(2)}, u32[]{:S(2)}) collective-permute-start(bf16[240,1280]{1,0:T(8,128)(2,1)} %slice.75), channel_id=1, source_target_pairs={{0,8},{4,12},{8,0},{12,4},{16,24},{20,28},{24,16},{28,20},{1,9},{5... | collective-permute-start | bytes 1843208 | tf_op jit(solution)/shard_map/ppermute | solution.py:773
  160.5 8.3 %collective-permute-start.31 = (bf16[480,1280]{1,0:T(8,128)(2,1)S(1)}, bf16[480,1280]{1,0:T(8,128)(2,1)S(1)}, u32[]{:S(2)}, u32[]{:S(2)}) collective-permute-start(bf16[480,1280]{1,0:T(8,128)(2,1)S(1)} %assemble.3.refs_20_), channel_id=1, source_target_pairs={{0,4},{4,0},{8,12},{12,8},{16,20},{20,16},{24,28},{28,24},{1,5},{5... | collective-permute-start | bytes 3686408 | tf_op jit(solution)/shard_map/ppermute | solution.py:773
  160.5 8.2 %collective-permute-start.32 = (bf16[480,1280]{1,0:T(8,128)(2,1)}, bf16[480,1280]{1,0:T(8,128)(2,1)S(1)}, u32[]{:S(2)}, u32[]{:S(2)}) collective-permute-start(bf16[480,1280]{1,0:T(8,128)(2,1)} %collective-permute-done.27.refs_22_), channel_id=1, source_target_pairs={{0,4},{4,0},{8,12},{12,8},{16,20},{20,16},{24,28},{28,24},{1,5},{5... | collective-permute-start | bytes 3686408 | tf_op jit(solution)/shard_map/ppermute | solution.py:773
  161.0 7.7 %collective-permute-start.33 = (bf16[480,1280]{1,0:T(8,128)(2,1)S(1)}, bf16[480,1280]{1,0:T(8,128)(2,1)S(1)}, u32[]{:S(2)}, u32[]{:S(2)}) collective-permute-start(bf16[480,1280]{1,0:T(8,128)(2,1)S(1)} %collective-permute-done.28.refs_24_), channel_id=1, source_target_pairs={{0,4},{4,0},{8,12},{12,8},{16,20},{20,16},{24,28},{28,24},{1,5},{5... | collective-permute-start | bytes 3686408 | tf_op jit(solution)/shard_map/ppermute | solution.py:773
  185.1 10.6 %collective-permute-start.37 = (bf16[64,1408]{1,0:T(8,128)(2,1)}, bf16[64,1408]{1,0:T(8,128)(2,1)S(1)}, u32[]{:S(2)}, u32[]{:S(2)}) collective-permute-start(bf16[64,1408]{1,0:T(8,128)(2,1)} %get-tuple-element.220.refs_0_), channel_id=1, source_target_pairs={{0,1},{1,0},{2,3},{3,2},{4,5},{5,4},{6,7},{7,6},{8,9},{9,8},{10,11... | collective-permute-start | bytes 540680 | tf_op jit(solution)/shard_map/ppermute | solution.py:773
  185.2 12.0 %collective-permute-start.36 = (bf16[64,1408]{1,0:T(8,128)(2,1)}, bf16[64,1408]{1,0:T(8,128)(2,1)S(1)}, u32[]{:S(2)}, u32[]{:S(2)}) collective-permute-start(bf16[64,1408]{1,0:T(8,128)(2,1)} %get-tuple-element.220.refs_0_), channel_id=1, source_target_pairs={{0,2},{1,3},{2,0},{3,1},{4,6},{5,7},{6,4},{7,5},{8,10},{9,11},{10,... | collective-permute-start | bytes 540680 | tf_op jit(solution)/shard_map/ppermute | solution.py:773
  197.1 9.5 %collective-permute-start.39 = (bf16[480,1280]{1,0:T(8,128)(2,1)}, bf16[480,1280]{1,0:T(8,128)(2,1)S(1)}, u32[]{:S(2)}, u32[]{:S(2)}) collective-permute-start(bf16[480,1280]{1,0:T(8,128)(2,1)} %get-tuple-element.217), channel_id=1, source_target_pairs={{0,4},{4,0},{8,12},{12,8},{16,20},{20,16},{24,28},{28,24},{1,5},{5... | collective-permute-start | bytes 3686408 | tf_op jit(solution)/shard_map/ppermute | solution.py:773
  197.1 10.6 %collective-permute-start.38 = (bf16[480,1280]{1,0:T(8,128)(2,1)}, bf16[480,1280]{1,0:T(8,128)(2,1)S(1)}, u32[]{:S(2)}, u32[]{:S(2)}) collective-permute-start(bf16[480,1280]{1,0:T(8,128)(2,1)} %get-tuple-element.215), channel_id=1, source_target_pairs={{0,4},{4,0},{8,12},{12,8},{16,20},{20,16},{24,28},{28,24},{1,5},{5... | collective-permute-start | bytes 3686408 | tf_op jit(solution)/shard_map/ppermute | solution.py:773
  198.3 8.4 %collective-permute-start.41 = (bf16[64,1408]{1,0:T(8,128)(2,1)S(1)}, bf16[64,1408]{1,0:T(8,128)(2,1)S(1)}, u32[]{:S(2)}, u32[]{:S(2)}) collective-permute-start(bf16[64,1408]{1,0:T(8,128)(2,1)S(1)} %collective-permute-done.36.refs_2_), channel_id=1, source_target_pairs={{2,3},{1,0},{6,7},{5,4},{10,11},{9,8},{14,15},{13,12},{18,19},{17,... | collective-permute-start | bytes 540680 | tf_op jit(solution)/shard_map/ppermute | solution.py:926
  207.7 24.8 %collective-permute-start.42 = (bf16[480,1280]{1,0:T(8,128)(2,1)}, bf16[480,1280]{1,0:T(8,128)(2,1)S(1)}, u32[]{:S(2)}, u32[]{:S(2)}) collective-permute-start(bf16[480,1280]{1,0:T(8,128)(2,1)} %get-tuple-element.225), channel_id=1, source_target_pairs={{0,4},{4,0},{8,12},{12,8},{16,20},{20,16},{24,28},{28,24},{1,5},{5... | collective-permute-start | bytes 3686408 | tf_op jit(solution)/shard_map/ppermute | solution.py:773
  210.4 22.1 %collective-permute-start.43 = (bf16[240,1280]{1,0:T(8,128)(2,1)}, bf16[240,1280]{1,0:T(8,128)(2,1)}, u32[]{:S(2)}, u32[]{:S(2)}) collective-permute-start(bf16[240,1280]{1,0:T(8,128)(2,1)} %get-tuple-element.227), channel_id=1, source_target_pairs={{0,16},{4,20},{8,24},{12,28},{16,0},{20,4},{24,8},{28,12},{1,17},{... | collective-permute-start | bytes 1843208 | tf_op jit(solution)/shard_map/ppermute | solution.py:773
  211.8 20.7 %collective-permute-start.44 = (bf16[240,1280]{1,0:T(8,128)(2,1)}, bf16[240,1280]{1,0:T(8,128)(2,1)}, u32[]{:S(2)}, u32[]{:S(2)}) collective-permute-start(bf16[240,1280]{1,0:T(8,128)(2,1)} %get-tuple-element.228), channel_id=1, source_target_pairs={{0,8},{4,12},{8,0},{12,4},{16,24},{20,28},{24,16},{28,20},{1,9},{5... | collective-permute-start | bytes 1843208 | tf_op jit(solution)/shard_map/ppermute | solution.py:773
  213.2 18.0 %collective-permute-start.46 = (bf16[128,1408]{1,0:T(8,128)(2,1)}, bf16[128,1408]{1,0:T(8,128)(2,1)}, u32[]{:S(2)}, u32[]{:S(2)}) collective-permute-start(bf16[128,1408]{1,0:T(8,128)(2,1)} %get-tuple-element.238.refs_0_), channel_id=1, source_target_pairs={{0,1},{1,0},{2,3},{3,2},{4,5},{5,4},{6,7},{7,6},{8,9},{9,8},{10,11... | collective-permute-start | bytes 1081352 | tf_op jit(solution)/shard_map/ppermute | solution.py:773
  213.2 19.3 %collective-permute-start.45 = (bf16[128,1408]{1,0:T(8,128)(2,1)}, bf16[128,1408]{1,0:T(8,128)(2,1)}, u32[]{:S(2)}, u32[]{:S(2)}) collective-permute-start(bf16[128,1408]{1,0:T(8,128)(2,1)} %get-tuple-element.238.refs_0_), channel_id=1, source_target_pairs={{0,2},{1,3},{2,0},{3,1},{4,6},{5,7},{6,4},{7,5},{8,10},{9,11},{10,... | collective-permute-start | bytes 1081352 | tf_op jit(solution)/shard_map/ppermute | solution.py:773
  233.6 13.6 %collective-permute-start.47 = (bf16[480,1280]{1,0:T(8,128)(2,1)}, bf16[480,1280]{1,0:T(8,128)(2,1)S(1)}, u32[]{:S(2)}, u32[]{:S(2)}) collective-permute-start(bf16[480,1280]{1,0:T(8,128)(2,1)} %get-tuple-element.235), channel_id=1, source_target_pairs={{0,4},{4,0},{8,12},{12,8},{16,20},{20,16},{24,28},{28,24},{1,5},{5... | collective-permute-start | bytes 3686408 | tf_op jit(solution)/shard_map/ppermute | solution.py:773
  233.6 7.6 %collective-permute-start.48 = (bf16[128,1408]{1,0:T(8,128)(2,1)}, bf16[128,1408]{1,0:T(8,128)(2,1)S(1)}, u32[]{:S(2)}, u32[]{:S(2)}) collective-permute-start(bf16[128,1408]{1,0:T(8,128)(2,1)} %get-tuple-element.238.refs_0_), channel_id=1, source_target_pairs={{1,2},{2,1},{5,6},{6,5},{9,10},{10,9},{13,14},{14,13},{17,18},{18,... | collective-permute-start | bytes 1081352 | tf_op jit(solution)/shard_map/ppermute | solution.py:925
  234.2 12.9 %collective-permute-start.49 = (bf16[128,1408]{1,0:T(8,128)(2,1)}, bf16[128,1408]{1,0:T(8,128)(2,1)S(1)}, u32[]{:S(2)}, u32[]{:S(2)}) collective-permute-start(bf16[128,1408]{1,0:T(8,128)(2,1)} %collective-permute-done.45.refs_2_), channel_id=1, source_target_pairs={{2,3},{1,0},{6,7},{5,4},{10,11},{9,8},{14,15},{13,12},{18,19},{17,... | collective-permute-start | bytes 1081352 | tf_op jit(solution)/shard_map/ppermute | solution.py:926
  247.2 43.9 %collective-permute-start.56 = (bf16[480,1280]{1,0:T(8,128)(2,1)}, bf16[480,1280]{1,0:T(8,128)(2,1)S(1)}, u32[]{:S(2)}, u32[]{:S(2)}) collective-permute-start(bf16[480,1280]{1,0:T(8,128)(2,1)} %get-tuple-element.259), channel_id=1, source_target_pairs={{0,8},{4,12},{8,0},{12,4},{16,24},{20,28},{24,16},{28,20},{1,9},{5... | collective-permute-start | bytes 3686408 | tf_op jit(solution)/shard_map/ppermute | solution.py:773
  247.8 43.3 %collective-permute-start.57 = (bf16[480,1280]{1,0:T(8,128)(2,1)}, bf16[480,1280]{1,0:T(8,128)(2,1)S(1)}, u32[]{:S(2)}, u32[]{:S(2)}) collective-permute-start(bf16[480,1280]{1,0:T(8,128)(2,1)} %get-tuple-element.260), channel_id=1, source_target_pairs={{0,16},{4,20},{8,24},{12,28},{16,0},{20,4},{24,8},{28,12},{1,17},{... | collective-permute-start | bytes 3686408 | tf_op jit(solution)/shard_map/ppermute | solution.py:773
  248.5 19.6 %collective-permute-start.50 = (bf16[64,1280]{1,0:T(8,128)(2,1)}, bf16[64,1280]{1,0:T(8,128)(2,1)S(1)}, u32[]{:S(2)}, u32[]{:S(2)}) collective-permute-start(bf16[64,1280]{1,0:T(8,128)(2,1)} %get-tuple-element.241), channel_id=1, source_target_pairs={{0,1},{1,0},{2,3},{3,2},{4,5},{5,4},{6,7},{7,6},{8,9},{9,8},{10,11... | collective-permute-start | bytes 491528 | tf_op jit(solution)/shard_map/ppermute | solution.py:773
  248.5 20.3 %collective-permute-start.51 = (bf16[64,1280]{1,0:T(8,128)(2,1)}, bf16[64,1280]{1,0:T(8,128)(2,1)S(1)}, u32[]{:S(2)}, u32[]{:S(2)}) collective-permute-start(bf16[64,1280]{1,0:T(8,128)(2,1)} %get-tuple-element.243), channel_id=1, source_target_pairs={{0,2},{1,3},{2,0},{3,1},{4,6},{5,7},{6,4},{7,5},{8,10},{9,11},{10,... | collective-permute-start | bytes 491528 | tf_op jit(solution)/shard_map/ppermute | solution.py:773
  251.4 18.1 %collective-permute-start.52 = (bf16[64,1280]{1,0:T(8,128)(2,1)}, bf16[64,1280]{1,0:T(8,128)(2,1)}, u32[]{:S(2)}, u32[]{:S(2)}) collective-permute-start(bf16[64,1280]{1,0:T(8,128)(2,1)} %get-tuple-element.245), channel_id=1, source_target_pairs={{0,3},{1,2},{2,1},{3,0},{4,7},{5,6},{6,5},{7,4},{8,11},{9,10},{10,... | collective-permute-start | bytes 491528 | tf_op jit(solution)/shard_map/ppermute | solution.py:773
  269.5 21.6 %collective-permute-start.53 = (bf16[128,1280]{1,0:T(8,128)(2,1)}, bf16[128,1280]{1,0:T(8,128)(2,1)S(1)}, u32[]{:S(2)}, u32[]{:S(2)}) collective-permute-start(bf16[128,1280]{1,0:T(8,128)(2,1)} %get-tuple-element.256), channel_id=1, source_target_pairs={{0,1},{1,0},{2,3},{3,2},{4,5},{5,4},{6,7},{7,6},{8,9},{9,8},{10,11... | collective-permute-start | bytes 983048 | tf_op jit(solution)/shard_map/ppermute | solution.py:773
  269.5 21.6 %collective-permute-start.55 = (bf16[128,1280]{1,0:T(8,128)(2,1)}, bf16[128,1280]{1,0:T(8,128)(2,1)}, u32[]{:S(2)}, u32[]{:S(2)}) collective-permute-start(bf16[128,1280]{1,0:T(8,128)(2,1)} %get-tuple-element.258), channel_id=1, source_target_pairs={{3,2},{0,1},{7,6},{4,5},{11,10},{8,9},{15,14},{12,13},{19,18},{16,... | collective-permute-start | bytes 983048 | tf_op jit(solution)/shard_map/ppermute | solution.py:931
  274.2 16.9 %collective-permute-start.54 = (bf16[128,1280]{1,0:T(8,128)(2,1)}, bf16[128,1280]{1,0:T(8,128)(2,1)}, u32[]{:S(2)}, u32[]{:S(2)}) collective-permute-start(bf16[128,1280]{1,0:T(8,128)(2,1)} %get-tuple-element.258), channel_id=1, source_target_pairs={{1,2},{2,1},{5,6},{6,5},{9,10},{10,9},{13,14},{14,13},{17,18},{18,... | collective-permute-start | bytes 983048 | tf_op jit(solution)/shard_map/ppermute | solution.py:930
  296.4 13.3 %collective-permute-start.62 = (bf16[192,1280]{1,0:T(8,128)(2,1)S(1)}, bf16[192,1280]{1,0:T(8,128)(2,1)S(1)}, u32[]{:S(2)}, u32[]{:S(2)}) collective-permute-start(bf16[192,1280]{1,0:T(8,128)(2,1)S(1)} %add_convert_fusion.2), channel_id=1, source_target_pairs={{0,8},{4,12},{8,0},{12,4},{16,24},{20,28},{24,16},{28,20},{1,9},{5... | collective-permute-start | bytes 1474568 | tf_op jit(solution)/shard_map/ppermute | solution.py:773
  297.7 11.2 %collective-permute-start.61 = (bf16[160,1280]{1,0:T(8,128)(2,1)S(1)}, bf16[160,1280]{1,0:T(8,128)(2,1)S(1)}, u32[]{:S(2)}, u32[]{:S(2)}) collective-permute-start(bf16[160,1280]{1,0:T(8,128)(2,1)S(1)} %add_convert_fusion.3), channel_id=1, source_target_pairs={{0,16},{4,20},{8,24},{12,28},{16,0},{20,4},{24,8},{28,12},{1,17},{... | collective-permute-start | bytes 1228808 | tf_op jit(solution)/shard_map/ppermute | solution.py:773
  299.2 17.2 %collective-permute-start.63 = (bf16[128,1280]{1,0:T(8,128)(2,1)S(1)}, bf16[128,1280]{1,0:T(8,128)(2,1)S(1)}, u32[]{:S(2)}, u32[]{:S(2)}) collective-permute-start(bf16[128,1280]{1,0:T(8,128)(2,1)S(1)} %add_convert_fusion.4), channel_id=1, source_target_pairs={{0,2},{1,3},{2,0},{3,1},{4,6},{5,7},{6,4},{7,5},{8,10},{9,11},{10,... | collective-permute-start | bytes 983048 | tf_op jit(solution)/shard_map/ppermute | solution.py:773
  309.6 13.3 %collective-permute-start.70 = (bf16[120,1280]{1,0:T(8,128)(2,1)S(1)}, bf16[120,1280]{1,0:T(8,128)(2,1)S(1)}, u32[]{:S(2)}, u32[]{:S(2)}) collective-permute-start(bf16[120,1280]{1,0:T(8,128)(2,1)S(1)} %get-tuple-element.295), channel_id=1, source_target_pairs={{0,1},{1,0},{2,3},{3,2},{4,5},{5,4},{6,7},{7,6},{8,9},{9,8},{10,11... | collective-permute-start | bytes 921608 | tf_op jit(solution)/shard_map/ppermute | solution.py:773
  317.1 25.9 %collective-permute-start.64 = (bf16[352,1280]{1,0:T(8,128)(2,1)}, bf16[352,1280]{1,0:T(8,128)(2,1)S(1)}, u32[]{:S(2)}, u32[]{:S(2)}) collective-permute-start(bf16[352,1280]{1,0:T(8,128)(2,1)} %get-tuple-element.279), channel_id=1, source_target_pairs={{0,4},{4,0},{8,12},{12,8},{16,20},{20,16},{24,28},{28,24},{1,5},{5... | collective-permute-start | bytes 2703368 | tf_op jit(solution)/shard_map/ppermute | solution.py:773
  317.1 26.0 %collective-permute-start.65 = (bf16[352,1280]{1,0:T(8,128)(2,1)}, bf16[352,1280]{1,0:T(8,128)(2,1)S(1)}, u32[]{:S(2)}, u32[]{:S(2)}) collective-permute-start(bf16[352,1280]{1,0:T(8,128)(2,1)} %get-tuple-element.280), channel_id=1, source_target_pairs={{0,8},{4,12},{8,0},{12,4},{16,24},{20,28},{24,16},{28,20},{1,9},{5... | collective-permute-start | bytes 2703368 | tf_op jit(solution)/shard_map/ppermute | solution.py:773
  317.8 25.3 %collective-permute-start.66 = (bf16[352,1280]{1,0:T(8,128)(2,1)}, bf16[352,1280]{1,0:T(8,128)(2,1)S(1)}, u32[]{:S(2)}, u32[]{:S(2)}) collective-permute-start(bf16[352,1280]{1,0:T(8,128)(2,1)} %get-tuple-element.281), channel_id=1, source_target_pairs={{0,16},{4,20},{8,24},{12,28},{16,0},{20,4},{24,8},{28,12},{1,17},{... | collective-permute-start | bytes 2703368 | tf_op jit(solution)/shard_map/ppermute | solution.py:773
  318.4 23.2 %collective-permute-start.71 = (bf16[120,1280]{1,0:T(8,128)(2,1)}, bf16[120,1280]{1,0:T(8,128)(2,1)}, u32[]{:S(2)}, u32[]{:S(2)}) collective-permute-start(bf16[120,1280]{1,0:T(8,128)(2,1)} %get-tuple-element.297), channel_id=1, source_target_pairs={{0,2},{1,3},{2,0},{3,1},{4,6},{5,7},{6,4},{7,5},{8,10},{9,11},{10,... | collective-permute-start | bytes 921608 | tf_op jit(solution)/shard_map/ppermute | solution.py:773
  323.7 18.0 %collective-permute-start.72 = (bf16[120,1280]{1,0:T(8,128)(2,1)}, bf16[120,1280]{1,0:T(8,128)(2,1)}, u32[]{:S(2)}, u32[]{:S(2)}) collective-permute-start(bf16[120,1280]{1,0:T(8,128)(2,1)} %get-tuple-element.299), channel_id=1, source_target_pairs={{0,3},{1,2},{2,1},{3,0},{4,7},{5,6},{6,5},{7,4},{8,11},{9,10},{10,... | collective-permute-start | bytes 921608 | tf_op jit(solution)/shard_map/ppermute | solution.py:773
  344.6 15.7 %collective-permute-start.69 = (bf16[88,1280]{1,0:T(8,128)(2,1)S(1)}, bf16[88,1280]{1,0:T(8,128)(2,1)S(1)}, u32[]{:S(2)}, u32[]{:S(2)}) collective-permute-start(bf16[88,1280]{1,0:T(8,128)(2,1)S(1)} %get-tuple-element.293), channel_id=1, source_target_pairs={{0,3},{1,2},{2,1},{3,0},{4,7},{5,6},{6,5},{7,4},{8,11},{9,10},{10,... | collective-permute-start | bytes 675848 | tf_op jit(solution)/shard_map/ppermute | solution.py:773
  347.0 21.1 %collective-permute-start.68 = (bf16[88,1280]{1,0:T(8,128)(2,1)S(1)}, bf16[88,1280]{1,0:T(8,128)(2,1)S(1)}, u32[]{:S(2)}, u32[]{:S(2)}) collective-permute-start(bf16[88,1280]{1,0:T(8,128)(2,1)S(1)} %get-tuple-element.291), channel_id=1, source_target_pairs={{0,2},{1,3},{2,0},{3,1},{4,6},{5,7},{6,4},{7,5},{8,10},{9,11},{10,... | collective-permute-start | bytes 675848 | tf_op jit(solution)/shard_map/ppermute | solution.py:773
  352.4 15.7 %collective-permute-start.67 = (bf16[88,1280]{1,0:T(8,128)(2,1)S(1)}, bf16[88,1280]{1,0:T(8,128)(2,1)S(1)}, u32[]{:S(2)}, u32[]{:S(2)}) collective-permute-start(bf16[88,1280]{1,0:T(8,128)(2,1)S(1)} %get-tuple-element.289), channel_id=1, source_target_pairs={{0,1},{1,0},{2,3},{3,2},{4,5},{5,4},{6,7},{7,6},{8,9},{9,8},{10,11... | collective-permute-start | bytes 675848 | tf_op jit(solution)/shard_map/ppermute | solution.py:773
  (86 other events, 796.6 us)

commit v5 on v4

--- a/solution.py
+++ b/solution.py
@@ -474,27 +474,26 @@
     )(place, *flat_parts, latent_message, cot_flat, *held_gain.flat, *held.flat)
 
 
-def feed_grads_call(place, lefts, rights, n, far):
+def feed_grads_call(place, lefts, rights, n, groups):
     lat, tokens = lefts[0].shape
     width = rights[0].shape[1]
     terms = len(lefts)
 
     def kernel(place_ref, *refs):
         left_refs, right_refs = refs[:terms], refs[terms : 2 * terms]
-        outs = refs[2 * terms :]
-        for distance in range(far):
-            at = pl.multiple_of(jnp.bitwise_xor(place_ref[0], distance) * n, 16)
-            for index in range(terms):
-                chunk = left_refs[index][pl.ds(at, n), :]
-                outs[distance][index * n : (index + 1) * n, :] = dot(
-                    chunk, right_refs[index][...]
-                ).astype(BF)
+        for out, group in zip(refs[2 * terms :], groups):
+            for number, distance in enumerate(group):
+                at = pl.multiple_of(jnp.bitwise_xor(place_ref[0], distance) * n, 16)
+                for index in range(terms):
+                    chunk = left_refs[index][pl.ds(at, n), :]
+                    first = (number * terms + index) * n
+                    out[first : first + n, :] = dot(chunk, right_refs[index][...]).astype(BF)
 
     return pl.pallas_call(
         kernel,
         in_specs=[scalar_spec()] + [whole_spec()] * (2 * terms),
-        out_specs=[whole_spec()] * far,
-        out_shape=[shape((terms * n, width))] * far,
+        out_specs=[whole_spec()] * len(groups),
+        out_shape=[shape((len(group) * terms * n, width)) for group in groups],
         compiler_params=params(0),
         cost_estimate=SMALL,
         name="feed_grads",
@@ -610,7 +609,7 @@
     )(place, *parts, queries, keys, values, byte_ids, *held.flat)
 
 
-def weight_grads_call(place, lefts, rights, some_rows, far):
+def weight_grads_call(place, lefts, rights, some_rows, groups):
     lat = rights[0][0].shape[1]
     chunk = sum(some_rows)
     left_counts, counts = [len(parts) for parts in lefts], [len(parts) for parts in rights]
@@ -620,7 +619,7 @@
         take = lambda n: [refs.pop(0) for _ in range(n)]
         left_refs = [take(n) for n in left_counts]
         right_refs = [take(n) for n in counts]
-        outs = take(far)
+        outs = take(len(groups))
         at = 0
         for index, (left, held) in enumerate(zip((0, 0, 1), refs)):
             factors, column, found = left_refs[left], 0, 0.0
@@ -634,11 +633,13 @@
                 column += some
             held[...] = found.astype(BF)
             some = some_rows[index]
-            for distance in range(far):
-                owner = jnp.bitwise_xor(place_ref[0], distance)
-                outs[distance][at : at + some, :] = held[
-                    pl.ds(pl.multiple_of(owner * some, 16), some), :
-                ]
+            for out, group in zip(outs, groups):
+                for number, distance in enumerate(group):
+                    owner = jnp.bitwise_xor(place_ref[0], distance)
+                    first = number * chunk + at
+                    out[first : first + some, :] = held[
+                        pl.ds(pl.multiple_of(owner * some, 16), some), :
+                    ]
             at += some
 
     tile = lambda i, p: (0, i)
@@ -651,10 +652,10 @@
             grid=(lat // WINDOW,),
             in_specs=[full_block(left.shape) for left in flat_lefts]
             + [pl.BlockSpec((right.shape[0], WINDOW), tile) for right in flat_rights],
-            out_specs=[pl.BlockSpec((chunk, WINDOW), tile)] * far,
+            out_specs=[pl.BlockSpec((len(group) * chunk, WINDOW), tile) for group in groups],
             scratch_shapes=[pltpu.VMEM((lefts[i][0].shape[0], WINDOW), BF) for i in (0, 0, 1)],
         ),
-        out_shape=[shape((chunk, lat))] * far,
+        out_shape=[shape((len(group) * chunk, lat)) for group in groups],
         compiler_params=params(1),
         cost_estimate=SMALL,
         name="weight_grads",
@@ -822,28 +823,29 @@
     return functools.reduce(jnp.add, [v.astype(F32) for v in values]).astype(BF)
 
 
-def meet_call(first, high, second, low, half):
-    rows, lat = first[0].shape
-
-    def kernel(a, b, h, c, d, l, one, two):
-        one[:half, :] = (a[:half, :].astype(F32) + b[:half, :].astype(F32)).astype(BF)
-        one[half:, :] = (
-            a[half:, :].astype(F32) + b[half:, :].astype(F32) + h[...].astype(F32)
-        ).astype(BF)
-        two[:half, :] = (
-            c[:half, :].astype(F32) + d[:half, :].astype(F32) + l[...].astype(F32)
-        ).astype(BF)
-        two[half:, :] = (c[half:, :].astype(F32) + d[half:, :].astype(F32)).astype(BF)
+def meet_call(first, high, second, low, others, half):
+    rows, lat = first.shape
+
+    def kernel(a, h, c, l, o, one, two):
+        def both(ref, start, stop, offset):
+            return ref[start:stop, :].astype(F32) + o[
+                offset + start : offset + stop, :
+            ].astype(F32)
+
+        one[:half, :] = both(a, 0, half, rows).astype(BF)
+        one[half:, :] = (both(a, half, rows, rows) + h[...].astype(F32)).astype(BF)
+        two[:half, :] = (both(c, 0, half, 0) + l[...].astype(F32)).astype(BF)
+        two[half:, :] = both(c, half, rows, 0).astype(BF)
 
     return pl.pallas_call(
         kernel,
-        in_specs=[whole_spec()] * 6,
+        in_specs=[whole_spec()] * 5,
         out_specs=[whole_spec()] * 2,
         out_shape=[shape((rows, lat))] * 2,
         compiler_params=params(0, 24),
         cost_estimate=SMALL,
         name="meet",
-    )(*first, high, *second, low)
+    )(first, high, second, low, others)
 
 
 def cut_call(place, terms, sizes, size):
@@ -852,7 +854,10 @@
 
     def kernel(place_ref, *refs):
         term_refs, outs, acc = refs[: len(terms)], refs[len(terms) : -1], refs[-1]
-        acc[...] = functools.reduce(jnp.add, [ref[...].astype(F32) for ref in term_refs])
+        total_rows = acc.shape[0]
+        acc[...] = functools.reduce(
+            jnp.add, [ref[ref.shape[0] - total_rows :, :].astype(F32) for ref in term_refs]
+        )
         for distance, out in enumerate(outs):
             owner = jnp.bitwise_xor(place_ref[1], distance)
             found, at = [], 0
@@ -1004,18 +1009,17 @@
     def feed(one, two, attended):
         return feed_call(place, attended, latent_message, cot_flat, one, two, cut_rows)
 
-    def feed_grads(lefts, rights):
-        return feed_grads_call(place, lefts, rights, query_rows, n_dp)
+    def feed_grads(lefts, rights, groups):
+        return feed_grads_call(place, lefts, rights, query_rows, groups)
 
     def attend_back(index, one, parts, saved):
         return attend_back_call(
             place, parts, *saved, byte_row, one, n_f, group, *cuts[index]
         )
 
-    def weight_grads(lefts, first, last):
-        return weight_grads_call(
-            place, lefts, list(zip(first, last)), (key_rows, key_rows, query_rows), n_dp
-        )
+    def weight_grads(lefts, first, last, groups):
+        some = (key_rows, key_rows, query_rows)
+        return weight_grads_call(place, lefts, list(zip(first, last)), some, groups)
 
     def byte_grad(one, grads):
         return byte_grad_call(place, bytes_flat, grads, one, rows, cuts)
@@ -1068,11 +1072,15 @@
     new, grad_mixed, *messages, attended_t, branch, normed_t, inner, act_t = feed(
         one, two, attended
     )
-    grad_two = scatter(feed_grads((attended_t, normed_t, act_t), (branch, inner, cot_flat)), sizes_two)
+    each = [(d,) for d in range(n_dp)]
+    grads = feed_grads((attended_t, normed_t, act_t), (branch, inner, cot_flat), each)
+    grad_two = scatter(grads, sizes_two)
     parts = [[m, *swap_all([m] * n_f, n_f)] for m in messages]
     first, last = [attend_back(i, one, parts[i], (queries[i], keys, values)) for i in range(2)]
     grad_bytes = byte_grad(one, (first[:2], last[:2]))
-    grad_one = scatter(weight_grads(((byte_t,), latent_t), first[:3], last[:3]), sizes_one)
+    grad_one = scatter(
+        weight_grads(((byte_t,), latent_t), first[:3], last[:3], each), sizes_one
+    )
     ups = [[ups[0], *swap_all(ups, n_f)] for ups in (first[3:], last[3:])]
     grad_latents = latent_grad_call(place, latent_message, grad_mixed, ups, one)
     return new, grad_latents, grad_bytes, grad_one, grad_two
@@ -1126,27 +1134,25 @@
     new, grad_mixed, first, last, attended_t, branch, normed_t, inner, act_t = feed(
         one, two, list(zip(attended_first, attended_last))
     )
+    groups = [(0,), (2,), (4,), (6,), (7,), (5, 3, 1)]
     plan.gate = []
     near = [pass_on(first, 2), pass_on(first, 1)]
-    grads = feed_grads((attended_t, normed_t, act_t), (branch, inner, cot_flat))
+    grads = feed_grads((attended_t, normed_t, act_t), (branch, inner, cot_flat), groups)
     plan.gate = near
     first_parts = [first, near[1], near[0], *plan.relay(first, near[0])]
     near = [pass_on(last, 2), pass_on(last, 1)]
-    arrived = {d: send(grads[d + 1], 1) for d in (6, 4)}
-    low = add(grads[6][:half_two], arrived[6][:half_two])
-    high = add(grads[6][half_two:], arrived[6][half_two:])
-    plan.gate = [*arrived.values(), *first_parts[3:]]
+    crossing = send(grads[4], 1)
+    low = add(grads[3][:half_two], crossing[:half_two])
+    high = add(grads[3][half_two:], crossing[half_two:])
+    plan.gate = [crossing, *first_parts[3:]]
     low, high = send(low, 2), send(high, 4)
-    arrived[2] = send(grads[3], 1)
+    others = send(grads[5], 1)
     back_first = attend_back(0, one, plan.tied(first_parts), (queries_first, keys, values))
-    plan.gate = [low, high, arrived[2], *near, back_first[0]]
+    plan.gate = [low, high, others, *near, back_first[0]]
     last_parts = [last, near[1], near[0], *plan.relay(last, near[0])]
-    arrived[0] = send(grads[1], 1)
-    x, y = meet_call(
-        (grads[2], arrived[2]), tie(high, *plan.gate), (grads[4], arrived[4]), low, half_two
-    )
-    plan.gate = [x, y, arrived[0], *last_parts[3:]]
-    terms_two = [grads[0], arrived[0], send(x, 2), send(y, 4)]
+    x, y = meet_call(grads[1], tie(high, *plan.gate), grads[2], low, others, half_two)
+    plan.gate = [x, y, *last_parts[3:]]
+    terms_two = [grads[0], others, send(x, 2), send(y, 4)]
     ups_first = back_first[3:]
     ups_first = [ups_first[0], *[pass_on(ups_first[j], j) for j in range(1, n_f)]]
     back_last = attend_back(1, one, plan.tied(last_parts), (queries_last, keys, values))
@@ -1157,27 +1163,26 @@
         ((byte_t,), (latent_t_first, latent_t_last)),
         back_first[:3],
         [tie(back_last[0], *plan.gate), *back_last[1:3]],
+        groups,
     )
     plan.gate = [*near, grads[0], *terms_two[2:]]
-    arrived = {d: send(grads[d + 1], 1) for d in (6, 4, 2)}
-    low = add(grads[6][:half_one], arrived[6][:half_one])
-    high = add(grads[6][half_one:], arrived[6][half_one:])
+    crossing = send(grads[4], 1)
+    others = send(tie(grads[5], crossing), 1)
+    low = add(grads[3][:half_one], crossing[:half_one])
+    high = add(grads[3][half_one:], crossing[half_one:])
     merged = add(tie(ups[2], *plan.gate), near[2])
-    plan.gate = [low, high, merged, *arrived.values()]
+    plan.gate = [low, high, merged]
     low, high = send(low, 2), send(high, 4)
     ups_last = [ups[0], *near[:2], pass_on(merged, 2)]
     cut_two = cut_terms(place, own, plan.tied(terms_two), sizes_two, n_f)
-    plan.gate = [low, high, cut_two[0]]
-    x, y = meet_call(
-        (grads[2], arrived[2]), tie(high, *plan.gate), (grads[4], arrived[4]), low, half_one
-    )
+    plan.gate = [low, high, cut_two[0], others]
+    x, y = meet_call(grads[1], tie(high, *plan.gate), grads[2], low, others, half_one)
+    plan.gate = [x, y, ups_last[-1]]
     arrived_two = [pass_on(cut_two[j], j) for j in range(1, n_f)]
     plan.gate = [x, y]
-    terms_one = [grads[0], None, send(x, 2), send(y, 4)]
+    terms_one = [grads[0], others, send(x, 2), send(y, 4)]
     grad_bytes = byte_grad(one, (plan.tied(back_first[:2]), back_last[:2]))
-    plan.gate = [x, y, ups_last[-1]]
-    terms_one[1] = send(grads[1], 1)
-    plan.gate = [*terms_one[1:], grad_bytes]
+    plan.gate = [*terms_one[2:], grad_bytes]
     cut_one = cut_terms(place, own, plan.tied(terms_one), sizes_one, n_f)
     plan.gate = [cut_one[0]]
     grad_one = total(cut_one[0], [pass_on(cut_one[j], j) for j in range(1, n_f)])

time: 377 us -> 372 us (0.987)
  local copies, waits for them, and re-layouts: 17.9 us -> 13.1 us
  waiting for transfers between devices: 123 us -> 119 us
    unnamed x156 -> x148, local copies, waits for them, and re-layouts: 14.3 us -> 9.41 us
    ppermute x61 -> x57, waiting for transfers between devices: 101 us -> 97.8 us  [swap(): return lax.ppermute(value, axis, [(i, i ^ distance) for i in range(size)])]
    ppermute x61 -> x57, starting transfers between devices: 69.9 us -> 72.3 us  [swap(): return lax.ppermute(value, axis, [(i, i ^ distance) for i in range(size)])]
  transfers between devices with their start and end apart: 73 -> 69, of which waited for: 28 -> 26; matrix products, arithmetic and copies ran while one was open for 3% -> 3% of each run, Pallas kernels for 30% -> 31%
where the time goes in v5:
time: 372 us; the launch traced here: 367 us
  Pallas kernels  131 us (35%)
  waiting for transfers between devices  119 us (32%)
  starting transfers between devices  89.1 us (24%)
  local copies, waits for them, and re-layouts  13.1 us (4%)
  other arithmetic  12.2 us (3%)
    ppermute x57, waiting for transfers between devices, swap(): return lax.ppermute(value, axis, [(i, i ^ distance) for i in range(size)])  97.8 us
    ppermute x57, starting transfers between devices, swap(): return lax.ppermute(value, axis, [(i, i ^ distance) for i in range(size)])  72.3 us
    pallas_call x2, Pallas kernels, attend_back_call(): pl.pallas_call(kernel, grid_spec=pltpu.PrefetchScalarGridSpec(num_scalar_...  24 us
    pallas_call x2, Pallas kernels, attend_call(): pl.pallas_call(kernel, grid_spec=pltpu.PrefetchScalarGridSpec(num_scalar_...  23.9 us
    ppermute x5, waiting for transfers between devices, relay(): lax.ppermute(tie(two, *self.gate), 'fsdp', [(2, 3), (1, 0)])  21.2 us
    pallas_call x1, Pallas kernels, byte_grad_call(): pl.pallas_call(kernel, grid_spec=pltpu.PrefetchScalarGridSpec(num_scalar_...  16.6 us
    pallas_call x1, Pallas kernels, weight_grads_call(): pl.pallas_call(kernel, grid_spec=pltpu.PrefetchScalarGridSpec(num_scalar_...  15 us
    pallas_call x1, Pallas kernels, feed_call(): pl.pallas_call(kernel, in_specs=[scalar_spec()] + [whole_spec()] * (len(f...  14.1 us
  transfers between devices with their start and end apart: 69, of which 26 were waited for; matrix products, arithmetic and copies ran while one was open for 3% of the time, Pallas kernels for 31%

profile of v5, /device:TPU:0, one launch (start us, length us, event | category | flops | bytes accessed | tf_op | source)
XLA Modules:
  0.0 366.8 jit_solution(258864690094487586)
XLA Ops:
  2.4 4.1 %collective-permute-start.1 = (bf16[96,1280]{1,0:T(8,128)(2,1)S(1)}, bf16[96,1280]{1,0:T(8,128)(2,1)S(1)}, u32[]{:S(2)}, u32[]{:S(2)}) collective-permute-start(bf16[96,1280]{1,0:T(8,128)(2,1)S(1)} %fusion.8.refs_0_), channel_id=1, source_target_pairs={{0,2},{1,3},{2,0},{3,1},{4,6},{5,7},{6,4},{7,5},{8,10},{9,11},{10,... | collective-permute-start | bytes 737288 | tf_op jit(solution)/shard_map/ppermute | solution.py:774
  6.5 1.6 collective-permute-start
  8.1 9.7 %collective-permute-done.1.refs_2_ = bf16[96,1280]{1,0:T(8,128)(2,1)S(1)} collective-permute-done((bf16[96,1280]{1,0:T(8,128)(2,1)S(1)}, bf16[96,1280]{1,0:T(8,128)(2,1)S(1)}, u32[]{:S(2)}, u32[]{:S(2)}) %collective-permute-start.1) | collective-permute-done | bytes 245792 | tf_op jit(solution)/shard_map/ppermute | solution.py:774
  20.1 7.9 %collective-permute-done.3.refs_4_ = bf16[96,1280]{1,0:T(8,128)(2,1)S(1)} collective-permute-done((bf16[96,1280]{1,0:T(8,128)(2,1)S(1)}, bf16[96,1280]{1,0:T(8,128)(2,1)S(1)}, u32[]{:S(2)}, u32[]{:S(2)}) %collective-permute-start.3) | collective-permute-done | bytes 245792 | tf_op jit(solution)/shard_map/ppermute | solution.py:931
  29.2 1.6 collective-permute-start.4
  30.7 1.5 collective-permute-start.5
  32.8 4.1 %collective-permute-start.8 = (bf16[192,1408]{1,0:T(8,128)(2,1)S(1)}, bf16[192,1408]{1,0:T(8,128)(2,1)}, u32[]{:S(2)}, u32[]{:S(2)}) collective-permute-start(bf16[192,1408]{1,0:T(8,128)(2,1)S(1)} %fusion.1.refs_0_.refs_8_.x_ref), channel_id=1, source_target_pairs={{0,2},{1,3},{2,0},{3,1},{4,6},{5,7},{6,4},{7,5},{8,10},{9,11},{10,... | collective-permute-start | bytes 1622024 | tf_op jit(solution)/shard_map/ppermute | solution.py:774
  36.9 13.2 %collective-permute-done.4.refs_2_.refs_10_.refs_12_.refs_11_.refs_6_ = bf16[368,1280]{1,0:T(8,128)(2,1)S(1)} collective-permute-done((bf16[368,1280]{1,0:T(8,128)(2,1)S(1)}, bf16[368,1280]{1,0:T(8,128)(2,1)S(1)}, u32[]{:S(2)}, u32[]{:S(2)}) %collective-permute-start.4) | collective-permute-done | bytes 942112 | tf_op jit(solution)/shard_map/ppermute | solution.py:774
  50.1 1.5 collective-permute-done.5.refs_4_.refs_12_.refs_14_.refs_13_.refs_8_
  51.7 1.5 collective-permute-start.6
  54.6 4.0 %collective-permute-done.9.refs_1_ = bf16[192,1408]{1,0:T(8,128)(2,1)S(1)} collective-permute-done((bf16[192,1408]{1,0:T(8,128)(2,1)S(1)}, bf16[192,1408]{1,0:T(8,128)(2,1)S(1)}, u32[]{:S(2)}, u32[]{:S(2)}) %collective-permute-start.9) | collective-permute-done | bytes 540704 | tf_op jit(solution)/shard_map/ppermute | solution.py:774
  58.6 2.6 collective-permute-done.8.in_ref
  61.3 1.6 collective-permute-done.7.refs_7_.refs_15_.refs_17_.refs_16_.refs_11_
  65.1 5.4 %collective-permute-start.10 = (bf16[120,1280]{1,0:T(8,128)(2,1)}, bf16[120,1280]{1,0:T(8,128)(2,1)}, u32[]{:S(2)}, u32[]{:S(2)}) collective-permute-start(bf16[120,1280]{1,0:T(8,128)(2,1)} %copy-done.23), channel_id=1, source_target_pairs={{0,2},{1,3},{2,0},{3,1},{4,6},{5,7},{6,4},{7,5},{8,10},{9,11},{10,... | collective-permute-start | bytes 921608 | tf_op jit(solution)/shard_map/ppermute | solution.py:774
  72.5 13.7 %keys_values.1 = (bf16[768,1536]{1,0:T(8,128)(2,1)}, bf16[1536,1280]{1,0:T(8,128)(2,1)}, bf16[1536,1280]{1,0:T(8,128)(2,1)}) custom-call(s32[2]{0:T(128)} %copy-done.35, bf16[1536,768]{1,0:T(8,128)(2,1)} %bitcast.8, bf16[368,1280]{1,0:T(8,128)(2,1)} %copy-done, bf16[368,1280]{1,0:T(8,128)(2,1)} %collective-permute-done.12.refs_1_.refs_9_.refs_11_.refs_10_.refs_5_, ...), custom_call_target="tpu_custom_call" | custom-call | flops 1 | bytes 1 | tf_op jit(solution)/shard_map/keys_values/pallas_call | solution.py:237
  87.6 1.8 collective-permute-start.20
  91.7 9.7 %attend.2 = (bf16[1280,256]{1,0:T(8,128)(2,1)}, bf16[256,1280]{1,0:T(8,128)(2,1)}, bf16[64,1408]{1,0:T(8,128)(2,1)}, bf16[64,1408]{1,0:T(8,128)(2,1)}, bf16[64,1...) custom-call(s32[2]{0:T(128)} %copy-done.35, bf16[192,1408]{1,0:T(8,128)(2,1)} %copy-done.10, bf16[192,1408]{1,0:T(8,128)(2,1)} %copy-done.40, ...), custom_call_target="tpu_custom_call" | custom-call | flops 1 | bytes 1 | tf_op jit(solution)/shard_map/attend/pallas_call | solution.py:333
  102.2 1.5 assemble.3.refs_20_
  105.1 5.9 %collective-permute-start.23 = (bf16[64,1408]{1,0:T(8,128)(2,1)S(1)}, bf16[64,1408]{1,0:T(8,128)(2,1)S(1)}, u32[]{:S(2)}, u32[]{:S(2)}) collective-permute-start(bf16[64,1408]{1,0:T(8,128)(2,1)S(1)} %copy-done.72), channel_id=1, source_target_pairs={{0,3},{1,2},{2,1},{3,0},{4,7},{5,6},{6,5},{7,4},{8,11},{9,10},{10,... | collective-permute-start | bytes 540680 | tf_op jit(solution)/shard_map/ppermute | solution.py:774
  111.0 1.8 collective-permute-start.22
  113.3 14.2 %attend.3 = (bf16[1280,512]{1,0:T(8,128)(2,1)}, bf16[512,1280]{1,0:T(8,128)(2,1)}, bf16[128,1408]{1,0:T(8,128)(2,1)}, bf16[128,1408]{1,0:T(8,128)(2,1)}, bf16[12...) custom-call(s32[2]{0:T(128)} %copy-done.35, bf16[192,1408]{1,0:T(8,128)(2,1)} %copy-done.10, bf16[192,1408]{1,0:T(8,128)(2,1)} %copy-done.40, ...), custom_call_target="tpu_custom_call" | custom-call | flops 1 | bytes 1 | tf_op jit(solution)/shard_map/attend/pallas_call | solution.py:333
  127.6 2.4 collective-permute-start.26
  130.6 1.5 collective-permute-start.24
  133.0 1.9 slice.74
  134.9 1.4 collective-permute-start.29
  137.7 3.5 collective-permute-done.26.refs_7_
  141.1 19.3 %collective-permute-done.25.refs_5_ = bf16[128,1408]{1,0:T(8,128)(2,1)} collective-permute-done((bf16[128,1408]{1,0:T(8,128)(2,1)}, bf16[128,1408]{1,0:T(8,128)(2,1)}, u32[]{:S(2)}, u32[]{:S(2)}) %collective-permute-start.25) | collective-permute-done | bytes 360480 | tf_op jit(solution)/shard_map/ppermute | solution.py:774
  161.7 7.1 %collective-permute-done.34.refs_28_ = bf16[240,1280]{1,0:T(8,128)(2,1)S(1)} collective-permute-done((bf16[240,1280]{1,0:T(8,128)(2,1)S(1)}, bf16[240,1280]{1,0:T(8,128)(2,1)S(1)}, u32[]{:S(2)}, u32[]{:S(2)}) %collective-permute-start.34) | collective-permute-done | bytes 614432 | tf_op jit(solution)/shard_map/ppermute | solution.py:774
  170.9 14.1 %feed.1 = (bf16[192,1280]{1,0:T(8,128)(2,1)}, f32[192,1280]{1,0:T(8,128)}, bf16[64,1408]{1,0:T(8,128)(2,1)}, bf16[128,1408]{1,0:T(8,128)(2,1)}, bf16[1280,192]{1...) custom-call(s32[2]{0:T(128)} %copy-done.35, ...), custom_call_target="tpu_custom_call" | custom-call | flops 1 | bytes 1 | tf_op jit(solution)/shard_map/feed/pallas_call | solution.py:450
  185.2 3.1 collective-permute-start.36
  188.3 6.5 %feed_grads.1 = (bf16[480,1280]{1,0:T(8,128)(2,1)}, bf16[480,1280]{1,0:T(8,128)(2,1)}, bf16[480,1280]{1,0:T(8,128)(2,1)}, bf16[480,1280]{1,0:T(8,128)(2,1)}, bf1...) custom-call(s32[2]{0:T(128)} %copy-done.35, bf16[1280,192]{1,0:T(8,128)(2,1)} %get-tuple-element.202.refs_0_, ...), custom_call_target="tpu_custom_call" | custom-call | flops 1 | bytes 1 | tf_op jit(solution)/shard_map/feed_grads/pallas_call | solution.py:492
  195.6 1.5 collective-permute-done.36.refs_2_
  197.8 1.5 collective-permute-start.40
  199.3 7.3 %collective-permute-done.40.refs_4_ = bf16[64,1408]{1,0:T(8,128)(2,1)S(1)} collective-permute-done((bf16[64,1408]{1,0:T(8,128)(2,1)S(1)}, bf16[64,1408]{1,0:T(8,128)(2,1)S(1)}, u32[]{:S(2)}, u32[]{:S(2)}) %collective-permute-start.40) | collective-permute-done | bytes 180256 | tf_op jit(solution)/shard_map/ppermute | solution.py:931
  207.3 2.6 add_convert_fusion
  211.3 1.4 collective-permute-start.42
  212.6 3.0 collective-permute-start.44
  215.6 8.8 %attend_back.2 = (bf16[512,1280]{1,0:T(8,128)(2,1)}, bf16[512,1280]{1,0:T(8,128)(2,1)}, bf16[256,1280]{1,0:T(8,128)(2,1)}, bf16[64,1280]{1,0:T(8,128)(2,1)}, bf1...) custom-call(s32[2]{0:T(128)} %copy-done.35, ...), custom_call_target="tpu_custom_call" | custom-call | flops 1 | bytes 1 | tf_op jit(solution)/shard_map/attend_back/pallas_call | solution.py:576
  224.4 6.3 %collective-permute-done.45.refs_1_ = bf16[128,1408]{1,0:T(8,128)(2,1)} collective-permute-done((bf16[128,1408]{1,0:T(8,128)(2,1)}, bf16[128,1408]{1,0:T(8,128)(2,1)}, u32[]{:S(2)}, u32[]{:S(2)}) %collective-permute-start.45) | collective-permute-done | bytes 360480 | tf_op jit(solution)/shard_map/ppermute | solution.py:774
  236.6 3.0 meet.2
  239.6 4.3 %collective-permute-done.47.refs_4_ = bf16[128,1408]{1,0:T(8,128)(2,1)S(1)} collective-permute-done((bf16[128,1408]{1,0:T(8,128)(2,1)}, bf16[128,1408]{1,0:T(8,128)(2,1)S(1)}, u32[]{:S(2)}, u32[]{:S(2)}) %collective-permute-start.47) | collective-permute-done | bytes 360480 | tf_op jit(solution)/shard_map/ppermute | solution.py:931
  245.4 3.0 collective-permute-start.49
  249.5 15.2 %attend_back.3 = (bf16[1024,1280]{1,0:T(8,128)(2,1)}, bf16[1024,1280]{1,0:T(8,128)(2,1)}, bf16[512,1280]{1,0:T(8,128)(2,1)}, bf16[128,1280]{1,0:T(8,128)(2,1)}, ...) custom-call(s32[2]{0:T(128)} %copy-done.35, ...), custom_call_target="tpu_custom_call" | custom-call | flops 1 | bytes 1 | tf_op jit(solution)/shard_map/attend_back/pallas_call | solution.py:576
  266.1 4.7 %collective-permute-start.53 = (bf16[128,1280]{1,0:T(8,128)(2,1)}, bf16[128,1280]{1,0:T(8,128)(2,1)}, u32[]{:S(2)}, u32[]{:S(2)}) collective-permute-start(bf16[128,1280]{1,0:T(8,128)(2,1)} %get-tuple-element.247), channel_id=1, source_target_pairs={{3,2},{0,1},{7,6},{4,5},{11,10},{8,9},{15,14},{12,13},{19,18},{16,... | collective-permute-start | bytes 983048 | tf_op jit(solution)/shard_map/ppermute | solution.py:936
  270.8 1.6 collective-permute-start.52
  272.4 15.0 %weight_grads.1 = (bf16[352,1280]{1,0:T(8,128)(2,1)}, bf16[352,1280]{1,0:T(8,128)(2,1)}, bf16[352,1280]{1,0:T(8,128)(2,1)}, bf16[352,1280]{1,0:T(8,128)(2,1)}, b...) custom-call(s32[2]{0:T(128)} %copy-done.35, bf16[768,1536]{1,0:T(8,128)(2,1)} %get-tuple-element.198.refs_0_, ...), custom_call_target="tpu_custom_call" | custom-call | flops 1 | bytes 1 | tf_op jit(solution)/shard_map/weight_grads/pallas_call | solution.py:648
  287.5 2.6 collective-permute-done.56
  291.7 1.4 collective-permute-start.58
  293.1 1.5 collective-permute-start.57
  295.2 3.9 %cut.2 = (f32[120,1280]{1,0:T(8,128)S(1)}, bf16[120,1280]{1,0:T(8,128)(2,1)}, bf16[120,1280]{1,0:T(8,128)(2,1)}, bf16[120,1280]{1,0:T(8,128)(2,1)}) custom-call(s32[2]{0:T(128)S(1)} %copy-done.37, bf16[480,1280]{1,0:T(8,128)(2,1)S(1)} %copy-done.17, bf16[1440,1280]{1,0:T(8,128)(2,1)S(1)} %collective-permute-done.43.o.refs_1_, ...), custom_call_target="tpu_custom_call" | custom-call | flops 1 | bytes 1 | tf_op jit(solution)/shard_map/cut/pallas_call | solution.py:869
  299.1 5.5 %collective-permute-done.57.h = bf16[160,1280]{1,0:T(8,128)(2,1)S(1)} collective-permute-done((bf16[160,1280]{1,0:T(8,128)(2,1)S(1)}, bf16[160,1280]{1,0:T(8,128)(2,1)S(1)}, u32[]{:S(2)}, u32[]{:S(2)}) %collective-permute-start.57) | collective-permute-done | bytes 409632 | tf_op jit(solution)/shard_map/ppermute | solution.py:774
  305.3 2.0 meet.3
  308.7 1.5 collective-permute-start.61
  310.1 1.8 collective-permute-done.62.refs_7_
  312.6 2.1 collective-permute-start.67
  314.8 2.3 collective-permute-start.68
  317.0 16.6 %byte_grad.1 = f32[1536,768]{1,0:T(8,128)} custom-call(s32[2]{0:T(128)} %copy-done.35, bf16[1536,768]{1,0:T(8,128)(2,1)} %bitcast.9, bf16[512,1280]{1,0:T(8,128)(2,1)} %get-tuple-element.267.refs_3_.refs_0_, bf16[512,1280]{1,0:T(8,128)(2,1)} %get-tuple-element.236.refs_5_.refs_1_, bf16[1024,1280]{1,0:T(8,128)(2,1)} %get-tuple-element.235.refs_4_.refs_2_, ...), custom_call_target="tpu_custom_call" | custom-call | flops 1 | bytes 1 | tf_op jit(solution)/shard_map/byte_grad/pallas_call | solution.py:708
  333.6 3.6 collective-permute-done.67
  337.2 1.5 convert_add_fusion
  338.9 2.2 cut.3
  341.1 1.6 collective-permute-start.65
  342.7 5.6 %collective-permute-start.64 = (bf16[88,1280]{1,0:T(8,128)(2,1)S(1)}, bf16[88,1280]{1,0:T(8,128)(2,1)S(1)}, u32[]{:S(2)}, u32[]{:S(2)}) collective-permute-start(bf16[88,1280]{1,0:T(8,128)(2,1)S(1)} %get-tuple-element.277), channel_id=1, source_target_pairs={{0,2},{1,3},{2,0},{3,1},{4,6},{5,7},{6,4},{7,5},{8,10},{9,11},{10,... | collective-permute-start | bytes 675848 | tf_op jit(solution)/shard_map/ppermute | solution.py:774
  349.9 3.6 latent_grad.1
  353.6 9.9 %collective-permute-done.64 = bf16[88,1280]{1,0:T(8,128)(2,1)S(1)} collective-permute-done((bf16[88,1280]{1,0:T(8,128)(2,1)S(1)}, bf16[88,1280]{1,0:T(8,128)(2,1)S(1)}, u32[]{:S(2)}, u32[]{:S(2)}) %collective-permute-start.64) | collective-permute-done | bytes 225312 | tf_op jit(solution)/shard_map/ppermute | solution.py:774
  (266 shorter events, 46.9 us)
Async XLA Ops:
  2.4 15.4 %collective-permute-start.1 = (bf16[96,1280]{1,0:T(8,128)(2,1)S(1)}, bf16[96,1280]{1,0:T(8,128)(2,1)S(1)}, u32[]{:S(2)}, u32[]{:S(2)}) collective-permute-start(bf16[96,1280]{1,0:T(8,128)(2,1)S(1)} %fusion.8.refs_0_), channel_id=1, source_target_pairs={{0,2},{1,3},{2,0},{3,1},{4,6},{5,7},{6,4},{7,5},{8,10},{9,11},{10,... | collective-permute-start | bytes 737288 | tf_op jit(solution)/shard_map/ppermute | solution.py:774
  6.5 11.5 %collective-permute-start = (bf16[96,1280]{1,0:T(8,128)(2,1)S(1)}, bf16[96,1280]{1,0:T(8,128)(2,1)S(1)}, u32[]{:S(2)}, u32[]{:S(2)}) collective-permute-start(bf16[96,1280]{1,0:T(8,128)(2,1)S(1)} %fusion.8.refs_0_), channel_id=1, source_target_pairs={{0,1},{1,0},{2,3},{3,2},{4,5},{5,4},{6,7},{7,6},{8,9},{9,8},{10,11... | collective-permute-start | bytes 737288 | tf_op jit(solution)/shard_map/ppermute | solution.py:774
  18.7 9.3 %collective-permute-start.3 = (bf16[96,1280]{1,0:T(8,128)(2,1)S(1)}, bf16[96,1280]{1,0:T(8,128)(2,1)S(1)}, u32[]{:S(2)}, u32[]{:S(2)}) collective-permute-start(bf16[96,1280]{1,0:T(8,128)(2,1)S(1)} %collective-permute-done.1.refs_2_), channel_id=1, source_target_pairs={{2,3},{1,0},{6,7},{5,4},{10,11},{9,8},{14,15},{13,12},{18,19},{17,... | collective-permute-start | bytes 737288 | tf_op jit(solution)/shard_map/ppermute | solution.py:931
  29.2 20.9 %collective-permute-start.4 = (bf16[368,1280]{1,0:T(8,128)(2,1)S(1)}, bf16[368,1280]{1,0:T(8,128)(2,1)S(1)}, u32[]{:S(2)}, u32[]{:S(2)}) collective-permute-start(bf16[368,1280]{1,0:T(8,128)(2,1)S(1)} %assemble.2.refs_0_.refs_8_.refs_10_.refs_9_.refs_4_), channel_id=1, source_target_pairs={{0,8},{4,12},{8,0},{12,4},{16,24},{20,28},{24,16},{28,20},{1,9},{5... | collective-permute-start | bytes 2826248 | tf_op jit(solution)/shard_map/ppermute | solution.py:774
  30.7 20.9 %collective-permute-start.5 = (bf16[368,1280]{1,0:T(8,128)(2,1)S(1)}, bf16[368,1280]{1,0:T(8,128)(2,1)S(1)}, u32[]{:S(2)}, u32[]{:S(2)}) collective-permute-start(bf16[368,1280]{1,0:T(8,128)(2,1)S(1)} %assemble.2.refs_0_.refs_8_.refs_10_.refs_9_.refs_4_), channel_id=1, source_target_pairs={{0,16},{4,20},{8,24},{12,28},{16,0},{20,4},{24,8},{28,12},{1,17},{... | collective-permute-start | bytes 2826248 | tf_op jit(solution)/shard_map/ppermute | solution.py:774
  32.2 29.0 %collective-permute-start.12 = (bf16[368,1280]{1,0:T(8,128)(2,1)S(1)}, bf16[368,1280]{1,0:T(8,128)(2,1)}, u32[]{:S(2)}, u32[]{:S(2)}) collective-permute-start(bf16[368,1280]{1,0:T(8,128)(2,1)S(1)} %assemble.2.refs_0_.refs_8_.refs_10_.refs_9_.refs_4_), channel_id=1, source_target_pairs={{0,4},{4,0},{8,12},{12,8},{16,20},{20,16},{24,28},{28,24},{1,5},{5... | collective-permute-start | bytes 2826248 | tf_op jit(solution)/shard_map/ppermute | solution.py:774
  32.5 26.1 %collective-permute-start.9 = (bf16[192,1408]{1,0:T(8,128)(2,1)S(1)}, bf16[192,1408]{1,0:T(8,128)(2,1)S(1)}, u32[]{:S(2)}, u32[]{:S(2)}) collective-permute-start(bf16[192,1408]{1,0:T(8,128)(2,1)S(1)} %fusion.1.refs_0_.refs_8_.x_ref), channel_id=1, source_target_pairs={{0,1},{1,0},{2,3},{3,2},{4,5},{5,4},{6,7},{7,6},{8,9},{9,8},{10,11... | collective-permute-start | bytes 1622024 | tf_op jit(solution)/shard_map/ppermute | solution.py:774
  32.8 28.5 %collective-permute-start.8 = (bf16[192,1408]{1,0:T(8,128)(2,1)S(1)}, bf16[192,1408]{1,0:T(8,128)(2,1)}, u32[]{:S(2)}, u32[]{:S(2)}) collective-permute-start(bf16[192,1408]{1,0:T(8,128)(2,1)S(1)} %fusion.1.refs_0_.refs_8_.x_ref), channel_id=1, source_target_pairs={{0,2},{1,3},{2,0},{3,1},{4,6},{5,7},{6,4},{7,5},{8,10},{9,11},{10,... | collective-permute-start | bytes 1622024 | tf_op jit(solution)/shard_map/ppermute | solution.py:774
  51.7 11.3 %collective-permute-start.6 = (bf16[192,1280]{1,0:T(8,128)(2,1)S(1)}, bf16[192,1280]{1,0:T(8,128)(2,1)S(1)}, u32[]{:S(2)}, u32[]{:S(2)}) collective-permute-start(bf16[192,1280]{1,0:T(8,128)(2,1)S(1)} %slice.72), channel_id=1, source_target_pairs={{0,16},{4,20},{8,24},{12,28},{16,0},{20,4},{24,8},{28,12},{1,17},{... | collective-permute-start | bytes 1474568 | tf_op jit(solution)/shard_map/ppermute | solution.py:774
  54.1 8.8 %collective-permute-start.7 = (bf16[176,1280]{1,0:T(8,128)(2,1)S(1)}, bf16[176,1280]{1,0:T(8,128)(2,1)}, u32[]{:S(2)}, u32[]{:S(2)}) collective-permute-start(bf16[176,1280]{1,0:T(8,128)(2,1)S(1)} %slice.73), channel_id=1, source_target_pairs={{0,8},{4,12},{8,0},{12,4},{16,24},{20,28},{24,16},{28,20},{1,9},{5... | collective-permute-start | bytes 1351688 | tf_op jit(solution)/shard_map/ppermute | solution.py:774
  62.9 7.5 %collective-permute-start.15 = (bf16[192,1280]{1,0:T(8,128)(2,1)S(1)}, bf16[192,1280]{1,0:T(8,128)(2,1)}, u32[]{:S(2)}, u32[]{:S(2)}) collective-permute-start(bf16[192,1280]{1,0:T(8,128)(2,1)S(1)} %collective-permute-done.6.refs_6_.refs_14_.refs_16_.refs_15_.refs_10_), channel_id=1, source_target_pairs={{0,4},{4,0},{8,12},{12,8},{16,20},{20,16},{24,28},{28,24},{1,5},{5... | collective-permute-start | bytes 1474568 | tf_op jit(solution)/shard_map/ppermute | solution.py:774
  63.4 7.7 %collective-permute-start.13 = (bf16[368,1280]{1,0:T(8,128)(2,1)S(1)}, bf16[368,1280]{1,0:T(8,128)(2,1)S(1)}, u32[]{:S(2)}, u32[]{:S(2)}) collective-permute-start(bf16[368,1280]{1,0:T(8,128)(2,1)S(1)} %collective-permute-done.4.refs_2_.refs_10_.refs_12_.refs_11_.refs_6_), channel_id=1, source_target_pairs={{0,4},{4,0},{8,12},{12,8},{16,20},{20,16},{24,28},{28,24},{1,5},{5... | collective-permute-start | bytes 2826248 | tf_op jit(solution)/shard_map/ppermute | solution.py:774
  63.5 8.9 %collective-permute-start.14 = (bf16[368,1280]{1,0:T(8,128)(2,1)S(1)}, bf16[368,1280]{1,0:T(8,128)(2,1)}, u32[]{:S(2)}, u32[]{:S(2)}) collective-permute-start(bf16[368,1280]{1,0:T(8,128)(2,1)S(1)} %collective-permute-done.5.refs_4_.refs_12_.refs_14_.refs_13_.refs_8_), channel_id=1, source_target_pairs={{0,4},{4,0},{8,12},{12,8},{16,20},{20,16},{24,28},{28,24},{1,5},{5... | collective-permute-start | bytes 2826248 | tf_op jit(solution)/shard_map/ppermute | solution.py:774
  64.0 22.2 %collective-permute-start.11 = (bf16[120,1280]{1,0:T(8,128)(2,1)}, bf16[120,1280]{1,0:T(8,128)(2,1)S(1)}, u32[]{:S(2)}, u32[]{:S(2)}) collective-permute-start(bf16[120,1280]{1,0:T(8,128)(2,1)} %copy-done.23), channel_id=1, source_target_pairs={{0,1},{1,0},{2,3},{3,2},{4,5},{5,4},{6,7},{7,6},{8,9},{9,8},{10,11... | collective-permute-start | bytes 921608 | tf_op jit(solution)/shard_map/ppermute | solution.py:774
  65.1 21.9 %collective-permute-start.10 = (bf16[120,1280]{1,0:T(8,128)(2,1)}, bf16[120,1280]{1,0:T(8,128)(2,1)}, u32[]{:S(2)}, u32[]{:S(2)}) collective-permute-start(bf16[120,1280]{1,0:T(8,128)(2,1)} %copy-done.23), channel_id=1, source_target_pairs={{0,2},{1,3},{2,0},{3,1},{4,6},{5,7},{6,4},{7,5},{8,10},{9,11},{10,... | collective-permute-start | bytes 921608 | tf_op jit(solution)/shard_map/ppermute | solution.py:774
  70.4 20.3 %collective-permute-start.17 = (bf16[192,1408]{1,0:T(8,128)(2,1)}, bf16[192,1408]{1,0:T(8,128)(2,1)S(1)}, u32[]{:S(2)}, u32[]{:S(2)}) collective-permute-start(bf16[192,1408]{1,0:T(8,128)(2,1)} %copy-done.10), channel_id=1, source_target_pairs={{1,2},{2,1},{5,6},{6,5},{9,10},{10,9},{13,14},{14,13},{17,18},{18,... | collective-permute-start | bytes 1622024 | tf_op jit(solution)/shard_map/ppermute | solution.py:930
  71.1 20.6 %collective-permute-start.18 = (bf16[192,1408]{1,0:T(8,128)(2,1)}, bf16[192,1408]{1,0:T(8,128)(2,1)}, u32[]{:S(2)}, u32[]{:S(2)}) collective-permute-start(bf16[192,1408]{1,0:T(8,128)(2,1)} %passed.2.refs_2_), channel_id=1, source_target_pairs={{2,3},{1,0},{6,7},{5,4},{10,11},{9,8},{14,15},{13,12},{18,19},{17,... | collective-permute-start | bytes 1622024 | tf_op jit(solution)/shard_map/ppermute | solution.py:931
  86.9 14.5 %collective-permute-start.19 = (bf16[120,1280]{1,0:T(8,128)(2,1)S(1)}, bf16[120,1280]{1,0:T(8,128)(2,1)S(1)}, u32[]{:S(2)}, u32[]{:S(2)}) collective-permute-start(bf16[120,1280]{1,0:T(8,128)(2,1)S(1)} %copy-done.24), channel_id=1, source_target_pairs={{1,2},{2,1},{5,6},{6,5},{9,10},{10,9},{13,14},{14,13},{17,18},{18,... | collective-permute-start | bytes 921608 | tf_op jit(solution)/shard_map/ppermute | solution.py:930
  87.6 14.6 %collective-permute-start.20 = (bf16[120,1280]{1,0:T(8,128)(2,1)}, bf16[120,1280]{1,0:T(8,128)(2,1)S(1)}, u32[]{:S(2)}, u32[]{:S(2)}) collective-permute-start(bf16[120,1280]{1,0:T(8,128)(2,1)} %collective-permute-done.10.refs_2_), channel_id=1, source_target_pairs={{2,3},{1,0},{6,7},{5,4},{10,11},{9,8},{14,15},{13,12},{18,19},{17,... | collective-permute-start | bytes 921608 | tf_op jit(solution)/shard_map/ppermute | solution.py:931
  103.7 28.4 %collective-permute-start.28 = (bf16[480,1280]{1,0:T(8,128)(2,1)S(1)}, bf16[480,1280]{1,0:T(8,128)(2,1)S(1)}, u32[]{:S(2)}, u32[]{:S(2)}) collective-permute-start(bf16[480,1280]{1,0:T(8,128)(2,1)S(1)} %assemble.3.refs_20_), channel_id=1, source_target_pairs={{0,16},{4,20},{8,24},{12,28},{16,0},{20,4},{24,8},{28,12},{1,17},{... | collective-permute-start | bytes 3686408 | tf_op jit(solution)/shard_map/ppermute | solution.py:774
  104.4 28.6 %collective-permute-start.27 = (bf16[480,1280]{1,0:T(8,128)(2,1)S(1)}, bf16[480,1280]{1,0:T(8,128)(2,1)}, u32[]{:S(2)}, u32[]{:S(2)}) collective-permute-start(bf16[480,1280]{1,0:T(8,128)(2,1)S(1)} %assemble.3.refs_20_), channel_id=1, source_target_pairs={{0,8},{4,12},{8,0},{12,4},{16,24},{20,28},{24,16},{28,20},{1,9},{5... | collective-permute-start | bytes 3686408 | tf_op jit(solution)/shard_map/ppermute | solution.py:774
  105.1 22.5 %collective-permute-start.23 = (bf16[64,1408]{1,0:T(8,128)(2,1)S(1)}, bf16[64,1408]{1,0:T(8,128)(2,1)S(1)}, u32[]{:S(2)}, u32[]{:S(2)}) collective-permute-start(bf16[64,1408]{1,0:T(8,128)(2,1)S(1)} %copy-done.72), channel_id=1, source_target_pairs={{0,3},{1,2},{2,1},{3,0},{4,7},{5,6},{6,5},{7,4},{8,11},{9,10},{10,... | collective-permute-start | bytes 540680 | tf_op jit(solution)/shard_map/ppermute | solution.py:774
  111.0 16.6 %collective-permute-start.22 = (bf16[64,1408]{1,0:T(8,128)(2,1)S(1)}, bf16[64,1408]{1,0:T(8,128)(2,1)S(1)}, u32[]{:S(2)}, u32[]{:S(2)}) collective-permute-start(bf16[64,1408]{1,0:T(8,128)(2,1)S(1)} %copy-done.71), channel_id=1, source_target_pairs={{0,2},{1,3},{2,0},{3,1},{4,6},{5,7},{6,4},{7,5},{8,10},{9,11},{10,... | collective-permute-start | bytes 540680 | tf_op jit(solution)/shard_map/ppermute | solution.py:774
  112.7 14.9 %collective-permute-start.21 = (bf16[64,1408]{1,0:T(8,128)(2,1)S(1)}, bf16[64,1408]{1,0:T(8,128)(2,1)S(1)}, u32[]{:S(2)}, u32[]{:S(2)}) collective-permute-start(bf16[64,1408]{1,0:T(8,128)(2,1)S(1)} %copy-done.70), channel_id=1, source_target_pairs={{0,1},{1,0},{2,3},{3,2},{4,5},{5,4},{6,7},{7,6},{8,9},{9,8},{10,11... | collective-permute-start | bytes 540680 | tf_op jit(solution)/shard_map/ppermute | solution.py:774
  127.6 13.5 %collective-permute-start.26 = (bf16[128,1408]{1,0:T(8,128)(2,1)}, bf16[128,1408]{1,0:T(8,128)(2,1)S(1)}, u32[]{:S(2)}, u32[]{:S(2)}) collective-permute-start(bf16[128,1408]{1,0:T(8,128)(2,1)} %get-tuple-element.185), channel_id=1, source_target_pairs={{0,3},{1,2},{2,1},{3,0},{4,7},{5,6},{6,5},{7,4},{8,11},{9,10},{10,... | collective-permute-start | bytes 1081352 | tf_op jit(solution)/shard_map/ppermute | solution.py:774
  130.0 30.5 %collective-permute-start.25 = (bf16[128,1408]{1,0:T(8,128)(2,1)}, bf16[128,1408]{1,0:T(8,128)(2,1)}, u32[]{:S(2)}, u32[]{:S(2)}) collective-permute-start(bf16[128,1408]{1,0:T(8,128)(2,1)} %get-tuple-element.183), channel_id=1, source_target_pairs={{0,2},{1,3},{2,0},{3,1},{4,6},{5,7},{6,4},{7,5},{8,10},{9,11},{10,... | collective-permute-start | bytes 1081352 | tf_op jit(solution)/shard_map/ppermute | solution.py:774
  130.6 29.8 %collective-permute-start.24 = (bf16[128,1408]{1,0:T(8,128)(2,1)}, bf16[128,1408]{1,0:T(8,128)(2,1)}, u32[]{:S(2)}, u32[]{:S(2)}) collective-permute-start(bf16[128,1408]{1,0:T(8,128)(2,1)} %get-tuple-element.181), channel_id=1, source_target_pairs={{0,1},{1,0},{2,3},{3,2},{4,5},{5,4},{6,7},{7,6},{8,9},{9,8},{10,11... | collective-permute-start | bytes 1081352 | tf_op jit(solution)/shard_map/ppermute | solution.py:774
  134.9 25.5 %collective-permute-start.29 = (bf16[240,1280]{1,0:T(8,128)(2,1)}, bf16[240,1280]{1,0:T(8,128)(2,1)S(1)}, u32[]{:S(2)}, u32[]{:S(2)}) collective-permute-start(bf16[240,1280]{1,0:T(8,128)(2,1)} %slice.74), channel_id=1, source_target_pairs={{0,16},{4,20},{8,24},{12,28},{16,0},{20,4},{24,8},{28,12},{1,17},{... | collective-permute-start | bytes 1843208 | tf_op jit(solution)/shard_map/ppermute | solution.py:774
  136.4 24.1 %collective-permute-start.30 = (bf16[240,1280]{1,0:T(8,128)(2,1)}, bf16[240,1280]{1,0:T(8,128)(2,1)}, u32[]{:S(2)}, u32[]{:S(2)}) collective-permute-start(bf16[240,1280]{1,0:T(8,128)(2,1)} %slice.75), channel_id=1, source_target_pairs={{0,8},{4,12},{8,0},{12,4},{16,24},{20,28},{24,16},{28,20},{1,9},{5... | collective-permute-start | bytes 1843208 | tf_op jit(solution)/shard_map/ppermute | solution.py:774
  160.5 8.3 %collective-permute-start.31 = (bf16[480,1280]{1,0:T(8,128)(2,1)S(1)}, bf16[480,1280]{1,0:T(8,128)(2,1)S(1)}, u32[]{:S(2)}, u32[]{:S(2)}) collective-permute-start(bf16[480,1280]{1,0:T(8,128)(2,1)S(1)} %assemble.3.refs_20_), channel_id=1, source_target_pairs={{0,4},{4,0},{8,12},{12,8},{16,20},{20,16},{24,28},{28,24},{1,5},{5... | collective-permute-start | bytes 3686408 | tf_op jit(solution)/shard_map/ppermute | solution.py:774
  160.6 8.2 %collective-permute-start.32 = (bf16[480,1280]{1,0:T(8,128)(2,1)}, bf16[480,1280]{1,0:T(8,128)(2,1)S(1)}, u32[]{:S(2)}, u32[]{:S(2)}) collective-permute-start(bf16[480,1280]{1,0:T(8,128)(2,1)} %collective-permute-done.27.refs_22_), channel_id=1, source_target_pairs={{0,4},{4,0},{8,12},{12,8},{16,20},{20,16},{24,28},{28,24},{1,5},{5... | collective-permute-start | bytes 3686408 | tf_op jit(solution)/shard_map/ppermute | solution.py:774
  161.1 7.7 %collective-permute-start.33 = (bf16[480,1280]{1,0:T(8,128)(2,1)S(1)}, bf16[480,1280]{1,0:T(8,128)(2,1)S(1)}, u32[]{:S(2)}, u32[]{:S(2)}) collective-permute-start(bf16[480,1280]{1,0:T(8,128)(2,1)S(1)} %collective-permute-done.28.refs_24_), channel_id=1, source_target_pairs={{0,4},{4,0},{8,12},{12,8},{16,20},{20,16},{24,28},{28,24},{1,5},{5... | collective-permute-start | bytes 3686408 | tf_op jit(solution)/shard_map/ppermute | solution.py:774
  161.1 7.6 %collective-permute-start.34 = (bf16[240,1280]{1,0:T(8,128)(2,1)S(1)}, bf16[240,1280]{1,0:T(8,128)(2,1)S(1)}, u32[]{:S(2)}, u32[]{:S(2)}) collective-permute-start(bf16[240,1280]{1,0:T(8,128)(2,1)S(1)} %collective-permute-done.29.refs_26_), channel_id=1, source_target_pairs={{0,4},{4,0},{8,12},{12,8},{16,20},{20,16},{24,28},{28,24},{1,5},{5... | collective-permute-start | bytes 1843208 | tf_op jit(solution)/shard_map/ppermute | solution.py:774
  185.1 10.5 %collective-permute-start.37 = (bf16[64,1408]{1,0:T(8,128)(2,1)}, bf16[64,1408]{1,0:T(8,128)(2,1)S(1)}, u32[]{:S(2)}, u32[]{:S(2)}) collective-permute-start(bf16[64,1408]{1,0:T(8,128)(2,1)} %get-tuple-element.211.refs_0_), channel_id=1, source_target_pairs={{0,1},{1,0},{2,3},{3,2},{4,5},{5,4},{6,7},{7,6},{8,9},{9,8},{10,11... | collective-permute-start | bytes 540680 | tf_op jit(solution)/shard_map/ppermute | solution.py:774
  185.2 11.9 %collective-permute-start.36 = (bf16[64,1408]{1,0:T(8,128)(2,1)}, bf16[64,1408]{1,0:T(8,128)(2,1)S(1)}, u32[]{:S(2)}, u32[]{:S(2)}) collective-permute-start(bf16[64,1408]{1,0:T(8,128)(2,1)} %get-tuple-element.211.refs_0_), channel_id=1, source_target_pairs={{0,2},{1,3},{2,0},{3,1},{4,6},{5,7},{6,4},{7,5},{8,10},{9,11},{10,... | collective-permute-start | bytes 540680 | tf_op jit(solution)/shard_map/ppermute | solution.py:774
  197.1 9.5 %collective-permute-start.38 = (bf16[480,1280]{1,0:T(8,128)(2,1)}, bf16[480,1280]{1,0:T(8,128)(2,1)S(1)}, u32[]{:S(2)}, u32[]{:S(2)}) collective-permute-start(bf16[480,1280]{1,0:T(8,128)(2,1)} %get-tuple-element.208), channel_id=1, source_target_pairs={{0,4},{4,0},{8,12},{12,8},{16,20},{20,16},{24,28},{28,24},{1,5},{5... | collective-permute-start | bytes 3686408 | tf_op jit(solution)/shard_map/ppermute | solution.py:774
  197.8 8.8 %collective-permute-start.40 = (bf16[64,1408]{1,0:T(8,128)(2,1)S(1)}, bf16[64,1408]{1,0:T(8,128)(2,1)S(1)}, u32[]{:S(2)}, u32[]{:S(2)}) collective-permute-start(bf16[64,1408]{1,0:T(8,128)(2,1)S(1)} %collective-permute-done.36.refs_2_), channel_id=1, source_target_pairs={{2,3},{1,0},{6,7},{5,4},{10,11},{9,8},{14,15},{13,12},{18,19},{17,... | collective-permute-start | bytes 540680 | tf_op jit(solution)/shard_map/ppermute | solution.py:931
  207.3 24.7 %collective-permute-start.43 = (bf16[1440,1280]{1,0:T(8,128)(2,1)}, bf16[1440,1280]{1,0:T(8,128)(2,1)S(1)}, u32[]{:S(2)}, u32[]{:S(2)}) collective-permute-start(bf16[1440,1280]{1,0:T(8,128)(2,1)} %get-tuple-element.219), channel_id=1, source_target_pairs={{0,4},{4,0},{8,12},{12,8},{16,20},{20,16},{24,28},{28,24},{1,5},{5... | collective-permute-start | bytes 11059208 | tf_op jit(solution)/shard_map/ppermute | solution.py:774
  209.9 22.1 %collective-permute-start.41 = (bf16[240,1280]{1,0:T(8,128)(2,1)}, bf16[240,1280]{1,0:T(8,128)(2,1)}, u32[]{:S(2)}, u32[]{:S(2)}) collective-permute-start(bf16[240,1280]{1,0:T(8,128)(2,1)} %get-tuple-element.216), channel_id=1, source_target_pairs={{0,16},{4,20},{8,24},{12,28},{16,0},{20,4},{24,8},{28,12},{1,17},{... | collective-permute-start | bytes 1843208 | tf_op jit(solution)/shard_map/ppermute | solution.py:774
  211.3 20.7 %collective-permute-start.42 = (bf16[240,1280]{1,0:T(8,128)(2,1)}, bf16[240,1280]{1,0:T(8,128)(2,1)}, u32[]{:S(2)}, u32[]{:S(2)}) collective-permute-start(bf16[240,1280]{1,0:T(8,128)(2,1)} %get-tuple-element.217), channel_id=1, source_target_pairs={{0,8},{4,12},{8,0},{12,4},{16,24},{20,28},{24,16},{28,20},{1,9},{5... | collective-permute-start | bytes 1843208 | tf_op jit(solution)/shard_map/ppermute | solution.py:774
  212.6 18.0 %collective-permute-start.45 = (bf16[128,1408]{1,0:T(8,128)(2,1)}, bf16[128,1408]{1,0:T(8,128)(2,1)}, u32[]{:S(2)}, u32[]{:S(2)}) collective-permute-start(bf16[128,1408]{1,0:T(8,128)(2,1)} %get-tuple-element.227.refs_0_), channel_id=1, source_target_pairs={{0,1},{1,0},{2,3},{3,2},{4,5},{5,4},{6,7},{7,6},{8,9},{9,8},{10,11... | collective-permute-start | bytes 1081352 | tf_op jit(solution)/shard_map/ppermute | solution.py:774
  212.6 19.3 %collective-permute-start.44 = (bf16[128,1408]{1,0:T(8,128)(2,1)}, bf16[128,1408]{1,0:T(8,128)(2,1)}, u32[]{:S(2)}, u32[]{:S(2)}) collective-permute-start(bf16[128,1408]{1,0:T(8,128)(2,1)} %get-tuple-element.227.refs_0_), channel_id=1, source_target_pairs={{0,2},{1,3},{2,0},{3,1},{4,6},{5,7},{6,4},{7,5},{8,10},{9,11},{10,... | collective-permute-start | bytes 1081352 | tf_op jit(solution)/shard_map/ppermute | solution.py:774
  232.0 7.6 %collective-permute-start.46 = (bf16[128,1408]{1,0:T(8,128)(2,1)}, bf16[128,1408]{1,0:T(8,128)(2,1)S(1)}, u32[]{:S(2)}, u32[]{:S(2)}) collective-permute-start(bf16[128,1408]{1,0:T(8,128)(2,1)} %get-tuple-element.227.refs_0_), channel_id=1, source_target_pairs={{1,2},{2,1},{5,6},{6,5},{9,10},{10,9},{13,14},{14,13},{17,18},{18,... | collective-permute-start | bytes 1081352 | tf_op jit(solution)/shard_map/ppermute | solution.py:930
  232.7 11.2 %collective-permute-start.47 = (bf16[128,1408]{1,0:T(8,128)(2,1)}, bf16[128,1408]{1,0:T(8,128)(2,1)S(1)}, u32[]{:S(2)}, u32[]{:S(2)}) collective-permute-start(bf16[128,1408]{1,0:T(8,128)(2,1)} %collective-permute-done.44.refs_2_), channel_id=1, source_target_pairs={{2,3},{1,0},{6,7},{5,4},{10,11},{9,8},{14,15},{13,12},{18,19},{17,... | collective-permute-start | bytes 1081352 | tf_op jit(solution)/shard_map/ppermute | solution.py:931
  243.9 43.5 %collective-permute-start.54 = (bf16[480,1280]{1,0:T(8,128)(2,1)}, bf16[480,1280]{1,0:T(8,128)(2,1)}, u32[]{:S(2)}, u32[]{:S(2)}) collective-permute-start(bf16[480,1280]{1,0:T(8,128)(2,1)} %get-tuple-element.248), channel_id=1, source_target_pairs={{0,8},{4,12},{8,0},{12,4},{16,24},{20,28},{24,16},{28,20},{1,9},{5... | collective-permute-start | bytes 3686408 | tf_op jit(solution)/shard_map/ppermute | solution.py:774
  244.5 42.9 %collective-permute-start.55 = (bf16[480,1280]{1,0:T(8,128)(2,1)}, bf16[480,1280]{1,0:T(8,128)(2,1)}, u32[]{:S(2)}, u32[]{:S(2)}) collective-permute-start(bf16[480,1280]{1,0:T(8,128)(2,1)} %get-tuple-element.249), channel_id=1, source_target_pairs={{0,16},{4,20},{8,24},{12,28},{16,0},{20,4},{24,8},{28,12},{1,17},{... | collective-permute-start | bytes 3686408 | tf_op jit(solution)/shard_map/ppermute | solution.py:774
  245.1 19.6 %collective-permute-start.48 = (bf16[64,1280]{1,0:T(8,128)(2,1)}, bf16[64,1280]{1,0:T(8,128)(2,1)S(1)}, u32[]{:S(2)}, u32[]{:S(2)}) collective-permute-start(bf16[64,1280]{1,0:T(8,128)(2,1)} %get-tuple-element.230), channel_id=1, source_target_pairs={{0,1},{1,0},{2,3},{3,2},{4,5},{5,4},{6,7},{7,6},{8,9},{9,8},{10,11... | collective-permute-start | bytes 491528 | tf_op jit(solution)/shard_map/ppermute | solution.py:774
  245.4 20.0 %collective-permute-start.49 = (bf16[64,1280]{1,0:T(8,128)(2,1)}, bf16[64,1280]{1,0:T(8,128)(2,1)S(1)}, u32[]{:S(2)}, u32[]{:S(2)}) collective-permute-start(bf16[64,1280]{1,0:T(8,128)(2,1)} %get-tuple-element.232), channel_id=1, source_target_pairs={{0,2},{1,3},{2,0},{3,1},{4,6},{5,7},{6,4},{7,5},{8,10},{9,11},{10,... | collective-permute-start | bytes 491528 | tf_op jit(solution)/shard_map/ppermute | solution.py:774
  248.4 17.7 %collective-permute-start.50 = (bf16[64,1280]{1,0:T(8,128)(2,1)}, bf16[64,1280]{1,0:T(8,128)(2,1)}, u32[]{:S(2)}, u32[]{:S(2)}) collective-permute-start(bf16[64,1280]{1,0:T(8,128)(2,1)} %get-tuple-element.234), channel_id=1, source_target_pairs={{0,3},{1,2},{2,1},{3,0},{4,7},{5,6},{6,5},{7,4},{8,11},{9,10},{10,... | collective-permute-start | bytes 491528 | tf_op jit(solution)/shard_map/ppermute | solution.py:774
  266.1 21.3 %collective-permute-start.51 = (bf16[128,1280]{1,0:T(8,128)(2,1)}, bf16[128,1280]{1,0:T(8,128)(2,1)S(1)}, u32[]{:S(2)}, u32[]{:S(2)}) collective-permute-start(bf16[128,1280]{1,0:T(8,128)(2,1)} %get-tuple-element.245), channel_id=1, source_target_pairs={{0,1},{1,0},{2,3},{3,2},{4,5},{5,4},{6,7},{7,6},{8,9},{9,8},{10,11... | collective-permute-start | bytes 983048 | tf_op jit(solution)/shard_map/ppermute | solution.py:774
  266.1 21.3 %collective-permute-start.53 = (bf16[128,1280]{1,0:T(8,128)(2,1)}, bf16[128,1280]{1,0:T(8,128)(2,1)}, u32[]{:S(2)}, u32[]{:S(2)}) collective-permute-start(bf16[128,1280]{1,0:T(8,128)(2,1)} %get-tuple-element.247), channel_id=1, source_target_pairs={{3,2},{0,1},{7,6},{4,5},{11,10},{8,9},{15,14},{12,13},{19,18},{16,... | collective-permute-start | bytes 983048 | tf_op jit(solution)/shard_map/ppermute | solution.py:936
  270.8 16.6 %collective-permute-start.52 = (bf16[128,1280]{1,0:T(8,128)(2,1)}, bf16[128,1280]{1,0:T(8,128)(2,1)}, u32[]{:S(2)}, u32[]{:S(2)}) collective-permute-start(bf16[128,1280]{1,0:T(8,128)(2,1)} %get-tuple-element.247), channel_id=1, source_target_pairs={{1,2},{2,1},{5,6},{6,5},{9,10},{10,9},{13,14},{14,13},{17,18},{18,... | collective-permute-start | bytes 983048 | tf_op jit(solution)/shard_map/ppermute | solution.py:935
  290.1 15.1 %collective-permute-start.59 = (bf16[1056,1280]{1,0:T(8,128)(2,1)}, bf16[1056,1280]{1,0:T(8,128)(2,1)S(1)}, u32[]{:S(2)}, u32[]{:S(2)}) collective-permute-start(bf16[1056,1280]{1,0:T(8,128)(2,1)} %get-tuple-element.260), channel_id=1, source_target_pairs={{0,4},{4,0},{8,12},{12,8},{16,20},{20,16},{24,28},{28,24},{1,5},{5... | collective-permute-start | bytes 8110088 | tf_op jit(solution)/shard_map/ppermute | solution.py:774
  291.7 13.6 %collective-permute-start.58 = (bf16[192,1280]{1,0:T(8,128)(2,1)S(1)}, bf16[192,1280]{1,0:T(8,128)(2,1)S(1)}, u32[]{:S(2)}, u32[]{:S(2)}) collective-permute-start(bf16[192,1280]{1,0:T(8,128)(2,1)S(1)} %add_convert_fusion.2), channel_id=1, source_target_pairs={{0,8},{4,12},{8,0},{12,4},{16,24},{20,28},{24,16},{28,20},{1,9},{5... | collective-permute-start | bytes 1474568 | tf_op jit(solution)/shard_map/ppermute | solution.py:774
  293.1 11.4 %collective-permute-start.57 = (bf16[160,1280]{1,0:T(8,128)(2,1)S(1)}, bf16[160,1280]{1,0:T(8,128)(2,1)S(1)}, u32[]{:S(2)}, u32[]{:S(2)}) collective-permute-start(bf16[160,1280]{1,0:T(8,128)(2,1)S(1)} %add_convert_fusion.3), channel_id=1, source_target_pairs={{0,16},{4,20},{8,24},{12,28},{16,0},{20,4},{24,8},{28,12},{1,17},{... | collective-permute-start | bytes 1228808 | tf_op jit(solution)/shard_map/ppermute | solution.py:774
  294.5 17.3 %collective-permute-start.62 = (bf16[128,1280]{1,0:T(8,128)(2,1)S(1)}, bf16[128,1280]{1,0:T(8,128)(2,1)S(1)}, u32[]{:S(2)}, u32[]{:S(2)}) collective-permute-start(bf16[128,1280]{1,0:T(8,128)(2,1)S(1)} %add_convert_fusion.4), channel_id=1, source_target_pairs={{0,2},{1,3},{2,0},{3,1},{4,6},{5,7},{6,4},{7,5},{8,10},{9,11},{10,... | collective-permute-start | bytes 983048 | tf_op jit(solution)/shard_map/ppermute | solution.py:774
  307.3 31.4 %collective-permute-start.60 = (bf16[352,1280]{1,0:T(8,128)(2,1)}, bf16[352,1280]{1,0:T(8,128)(2,1)S(1)}, u32[]{:S(2)}, u32[]{:S(2)}) collective-permute-start(bf16[352,1280]{1,0:T(8,128)(2,1)} %get-tuple-element.265), channel_id=1, source_target_pairs={{0,8},{4,12},{8,0},{12,4},{16,24},{20,28},{24,16},{28,20},{1,9},{5... | collective-permute-start | bytes 2703368 | tf_op jit(solution)/shard_map/ppermute | solution.py:774
  308.7 30.1 %collective-permute-start.61 = (bf16[352,1280]{1,0:T(8,128)(2,1)}, bf16[352,1280]{1,0:T(8,128)(2,1)}, u32[]{:S(2)}, u32[]{:S(2)}) collective-permute-start(bf16[352,1280]{1,0:T(8,128)(2,1)} %get-tuple-element.266), channel_id=1, source_target_pairs={{0,16},{4,20},{8,24},{12,28},{16,0},{20,4},{24,8},{28,12},{1,17},{... | collective-permute-start | bytes 2703368 | tf_op jit(solution)/shard_map/ppermute | solution.py:774
  312.6 21.0 %collective-permute-start.66 = (bf16[120,1280]{1,0:T(8,128)(2,1)}, bf16[120,1280]{1,0:T(8,128)(2,1)}, u32[]{:S(2)}, u32[]{:S(2)}) collective-permute-start(bf16[120,1280]{1,0:T(8,128)(2,1)} %get-tuple-element.281), channel_id=1, source_target_pairs={{0,1},{1,0},{2,3},{3,2},{4,5},{5,4},{6,7},{7,6},{8,9},{9,8},{10,11... | collective-permute-start | bytes 921608 | tf_op jit(solution)/shard_map/ppermute | solution.py:774
  312.6 24.6 %collective-permute-start.67 = (bf16[120,1280]{1,0:T(8,128)(2,1)}, bf16[120,1280]{1,0:T(8,128)(2,1)}, u32[]{:S(2)}, u32[]{:S(2)}) collective-permute-start(bf16[120,1280]{1,0:T(8,128)(2,1)} %get-tuple-element.283), channel_id=1, source_target_pairs={{0,2},{1,3},{2,0},{3,1},{4,6},{5,7},{6,4},{7,5},{8,10},{9,11},{10,... | collective-permute-start | bytes 921608 | tf_op jit(solution)/shard_map/ppermute | solution.py:774
  314.8 22.5 %collective-permute-start.68 = (bf16[120,1280]{1,0:T(8,128)(2,1)}, bf16[120,1280]{1,0:T(8,128)(2,1)}, u32[]{:S(2)}, u32[]{:S(2)}) collective-permute-start(bf16[120,1280]{1,0:T(8,128)(2,1)} %get-tuple-element.285), channel_id=1, source_target_pairs={{0,3},{1,2},{2,1},{3,0},{4,7},{5,6},{6,5},{7,4},{8,11},{9,10},{10,... | collective-permute-start | bytes 921608 | tf_op jit(solution)/shard_map/ppermute | solution.py:774
  341.1 12.4 %collective-permute-start.65 = (bf16[88,1280]{1,0:T(8,128)(2,1)S(1)}, bf16[88,1280]{1,0:T(8,128)(2,1)S(1)}, u32[]{:S(2)}, u32[]{:S(2)}) collective-permute-start(bf16[88,1280]{1,0:T(8,128)(2,1)S(1)} %get-tuple-element.279), channel_id=1, source_target_pairs={{0,3},{1,2},{2,1},{3,0},{4,7},{5,6},{6,5},{7,4},{8,11},{9,10},{10,... | collective-permute-start | bytes 675848 | tf_op jit(solution)/shard_map/ppermute | solution.py:774
  342.7 20.7 %collective-permute-start.64 = (bf16[88,1280]{1,0:T(8,128)(2,1)S(1)}, bf16[88,1280]{1,0:T(8,128)(2,1)S(1)}, u32[]{:S(2)}, u32[]{:S(2)}) collective-permute-start(bf16[88,1280]{1,0:T(8,128)(2,1)S(1)} %get-tuple-element.277), channel_id=1, source_target_pairs={{0,2},{1,3},{2,0},{3,1},{4,6},{5,7},{6,4},{7,5},{8,10},{9,11},{10,... | collective-permute-start | bytes 675848 | tf_op jit(solution)/shard_map/ppermute | solution.py:774
  348.4 15.1 %collective-permute-start.63 = (bf16[88,1280]{1,0:T(8,128)(2,1)S(1)}, bf16[88,1280]{1,0:T(8,128)(2,1)S(1)}, u32[]{:S(2)}, u32[]{:S(2)}) collective-permute-start(bf16[88,1280]{1,0:T(8,128)(2,1)S(1)} %get-tuple-element.275), channel_id=1, source_target_pairs={{0,1},{1,0},{2,3},{3,2},{4,5},{5,4},{6,7},{7,6},{8,9},{9,8},{10,11... | collective-permute-start | bytes 675848 | tf_op jit(solution)/shard_map/ppermute | solution.py:774
  (78 other events, 745.1 us)

commit v6 on v5

--- a/solution.py
+++ b/solution.py
@@ -1148,6 +1148,7 @@
     low, high = send(low, 2), send(high, 4)
     others = send(grads[5], 1)
     back_first = attend_back(0, one, plan.tied(first_parts), (queries_first, keys, values))
+    near[0] = passed(near[0], near[1], back_first[0], cost=5)
     plan.gate = [low, high, others, *near, back_first[0]]
     last_parts = [last, near[1], near[0], *plan.relay(last, near[0])]
     x, y = meet_call(grads[1], tie(high, *plan.gate), grads[2], low, others, half_two)

time: 372 us -> 369 us (level)
    unnamed x148 -> x168, local copies, waits for them, and re-layouts: 9.41 us -> 8.49 us
  transfers between devices with their start and end apart: 69 -> 69, of which waited for: 26 -> 28; matrix products, arithmetic and copies ran while one was open for 3% -> 3% of each run, Pallas kernels for 31% -> 31%
where the time goes in v6:
time: 369 us; the launch traced here: 364 us
  Pallas kernels  132 us (36%)
  waiting for transfers between devices  117 us (32%)
  starting transfers between devices  88.5 us (24%)
  other arithmetic  12.3 us (3%)
  local copies, waits for them, and re-layouts  12.2 us (3%)
    ppermute x57, waiting for transfers between devices, swap(): return lax.ppermute(value, axis, [(i, i ^ distance) for i in range(size)])  94.5 us
    ppermute x57, starting transfers between devices, swap(): return lax.ppermute(value, axis, [(i, i ^ distance) for i in range(size)])  73 us
    pallas_call x2, Pallas kernels, attend_back_call(): pl.pallas_call(kernel, grid_spec=pltpu.PrefetchScalarGridSpec(num_scalar_...  24 us
    pallas_call x2, Pallas kernels, attend_call(): pl.pallas_call(kernel, grid_spec=pltpu.PrefetchScalarGridSpec(num_scalar_...  23.9 us
    ppermute x5, waiting for transfers between devices, relay(): lax.ppermute(tie(two, *self.gate), 'fsdp', [(2, 3), (1, 0)])  22.6 us
    pallas_call x1, Pallas kernels, byte_grad_call(): pl.pallas_call(kernel, grid_spec=pltpu.PrefetchScalarGridSpec(num_scalar_...  16.4 us
    pallas_call x1, Pallas kernels, weight_grads_call(): pl.pallas_call(kernel, grid_spec=pltpu.PrefetchScalarGridSpec(num_scalar_...  15 us
    pallas_call x1, Pallas kernels, feed_call(): pl.pallas_call(kernel, in_specs=[scalar_spec()] + [whole_spec()] * (len(f...  14.2 us
  transfers between devices with their start and end apart: 69, of which 28 were waited for; matrix products, arithmetic and copies ran while one was open for 3% of the time, Pallas kernels for 31%

profile of v6, /device:TPU:0, one launch (start us, length us, event | category | flops | bytes accessed | tf_op | source)
XLA Modules:
  0.0 364.2 jit_solution(10462970533944853970)
XLA Ops:
  2.4 4.1 %collective-permute-start.1 = (bf16[96,1280]{1,0:T(8,128)(2,1)S(1)}, bf16[96,1280]{1,0:T(8,128)(2,1)S(1)}, u32[]{:S(2)}, u32[]{:S(2)}) collective-permute-start(bf16[96,1280]{1,0:T(8,128)(2,1)S(1)} %fusion.8.refs_0_), channel_id=1, source_target_pairs={{0,2},{1,3},{2,0},{3,1},{4,6},{5,7},{6,4},{7,5},{8,10},{9,11},{10,... | collective-permute-start | bytes 737288 | tf_op jit(solution)/shard_map/ppermute | solution.py:774
  6.5 1.6 collective-permute-start
  8.1 9.7 %collective-permute-done.1.refs_2_ = bf16[96,1280]{1,0:T(8,128)(2,1)S(1)} collective-permute-done((bf16[96,1280]{1,0:T(8,128)(2,1)S(1)}, bf16[96,1280]{1,0:T(8,128)(2,1)S(1)}, u32[]{:S(2)}, u32[]{:S(2)}) %collective-permute-start.1) | collective-permute-done | bytes 245792 | tf_op jit(solution)/shard_map/ppermute | solution.py:774
  20.1 7.9 %collective-permute-done.3.refs_4_ = bf16[96,1280]{1,0:T(8,128)(2,1)S(1)} collective-permute-done((bf16[96,1280]{1,0:T(8,128)(2,1)S(1)}, bf16[96,1280]{1,0:T(8,128)(2,1)S(1)}, u32[]{:S(2)}, u32[]{:S(2)}) %collective-permute-start.3) | collective-permute-done | bytes 245792 | tf_op jit(solution)/shard_map/ppermute | solution.py:931
  29.2 1.6 collective-permute-start.4
  30.7 1.5 collective-permute-start.5
  32.8 4.1 %collective-permute-start.8 = (bf16[192,1408]{1,0:T(8,128)(2,1)S(1)}, bf16[192,1408]{1,0:T(8,128)(2,1)}, u32[]{:S(2)}, u32[]{:S(2)}) collective-permute-start(bf16[192,1408]{1,0:T(8,128)(2,1)S(1)} %fusion.1.refs_0_.refs_8_.x_ref), channel_id=1, source_target_pairs={{0,2},{1,3},{2,0},{3,1},{4,6},{5,7},{6,4},{7,5},{8,10},{9,11},{10,... | collective-permute-start | bytes 1622024 | tf_op jit(solution)/shard_map/ppermute | solution.py:774
  36.9 13.2 %collective-permute-done.4.refs_2_.refs_10_.refs_12_.refs_11_.refs_6_ = bf16[368,1280]{1,0:T(8,128)(2,1)S(1)} collective-permute-done((bf16[368,1280]{1,0:T(8,128)(2,1)S(1)}, bf16[368,1280]{1,0:T(8,128)(2,1)S(1)}, u32[]{:S(2)}, u32[]{:S(2)}) %collective-permute-start.4) | collective-permute-done | bytes 942112 | tf_op jit(solution)/shard_map/ppermute | solution.py:774
  50.1 1.5 collective-permute-done.5.refs_4_.refs_12_.refs_14_.refs_13_.refs_8_
  51.7 1.5 collective-permute-start.6
  53.8 4.9 %collective-permute-done.9.refs_1_ = bf16[192,1408]{1,0:T(8,128)(2,1)S(1)} collective-permute-done((bf16[192,1408]{1,0:T(8,128)(2,1)S(1)}, bf16[192,1408]{1,0:T(8,128)(2,1)S(1)}, u32[]{:S(2)}, u32[]{:S(2)}) %collective-permute-start.9) | collective-permute-done | bytes 540704 | tf_op jit(solution)/shard_map/ppermute | solution.py:774
  58.6 2.6 collective-permute-done.8.in_ref
  64.2 5.4 %collective-permute-start.10 = (bf16[120,1280]{1,0:T(8,128)(2,1)}, bf16[120,1280]{1,0:T(8,128)(2,1)}, u32[]{:S(2)}, u32[]{:S(2)}) collective-permute-start(bf16[120,1280]{1,0:T(8,128)(2,1)} %copy-done.23), channel_id=1, source_target_pairs={{0,2},{1,3},{2,0},{3,1},{4,6},{5,7},{6,4},{7,5},{8,10},{9,11},{10,... | collective-permute-start | bytes 921608 | tf_op jit(solution)/shard_map/ppermute | solution.py:774
  71.6 13.7 %keys_values.1 = (bf16[768,1536]{1,0:T(8,128)(2,1)}, bf16[1536,1280]{1,0:T(8,128)(2,1)}, bf16[1536,1280]{1,0:T(8,128)(2,1)}) custom-call(s32[2]{0:T(128)} %copy-done.39, bf16[1536,768]{1,0:T(8,128)(2,1)} %bitcast.8, bf16[368,1280]{1,0:T(8,128)(2,1)} %copy-done, bf16[368,1280]{1,0:T(8,128)(2,1)} %collective-permute-done.12.refs_1_.refs_9_.refs_11_.refs_10_.refs_5_, ...), custom_call_target="tpu_custom_call" | custom-call | flops 1 | bytes 1 | tf_op jit(solution)/shard_map/keys_values/pallas_call | solution.py:237
  86.7 1.8 collective-permute-start.20
  90.9 9.7 %attend.2 = (bf16[1280,256]{1,0:T(8,128)(2,1)}, bf16[256,1280]{1,0:T(8,128)(2,1)}, bf16[64,1408]{1,0:T(8,128)(2,1)}, bf16[64,1408]{1,0:T(8,128)(2,1)}, bf16[64,1...) custom-call(s32[2]{0:T(128)} %copy-done.39, bf16[192,1408]{1,0:T(8,128)(2,1)} %copy-done.10, bf16[192,1408]{1,0:T(8,128)(2,1)} %copy-done.44, ...), custom_call_target="tpu_custom_call" | custom-call | flops 1 | bytes 1 | tf_op jit(solution)/shard_map/attend/pallas_call | solution.py:333
  101.3 1.5 assemble.3.refs_20_
  102.9 1.6 collective-permute-start.28
  105.1 4.6 %collective-permute-start.23 = (bf16[64,1408]{1,0:T(8,128)(2,1)S(1)}, bf16[64,1408]{1,0:T(8,128)(2,1)S(1)}, u32[]{:S(2)}, u32[]{:S(2)}) collective-permute-start(bf16[64,1408]{1,0:T(8,128)(2,1)S(1)} %copy-done.82), channel_id=1, source_target_pairs={{0,3},{1,2},{2,1},{3,0},{4,7},{5,6},{6,5},{7,4},{8,11},{9,10},{10,... | collective-permute-start | bytes 540680 | tf_op jit(solution)/shard_map/ppermute | solution.py:774
  109.7 2.7 collective-permute-start.22
  113.0 14.2 %attend.3 = (bf16[1280,512]{1,0:T(8,128)(2,1)}, bf16[512,1280]{1,0:T(8,128)(2,1)}, bf16[128,1408]{1,0:T(8,128)(2,1)}, bf16[128,1408]{1,0:T(8,128)(2,1)}, bf16[12...) custom-call(s32[2]{0:T(128)} %copy-done.39, bf16[192,1408]{1,0:T(8,128)(2,1)} %copy-done.10, bf16[192,1408]{1,0:T(8,128)(2,1)} %copy-done.44, ...), custom_call_target="tpu_custom_call" | custom-call | flops 1 | bytes 1 | tf_op jit(solution)/shard_map/attend/pallas_call | solution.py:333
  127.3 2.4 collective-permute-start.26
  130.3 1.5 collective-permute-start.24
  132.7 1.9 slice.74
  136.8 4.1 %collective-permute-done.26.refs_7_ = bf16[128,1408]{1,0:T(8,128)(2,1)S(1)} collective-permute-done((bf16[128,1408]{1,0:T(8,128)(2,1)}, bf16[128,1408]{1,0:T(8,128)(2,1)S(1)}, u32[]{:S(2)}, u32[]{:S(2)}) %collective-permute-start.26) | collective-permute-done | bytes 360480 | tf_op jit(solution)/shard_map/ppermute | solution.py:774
  140.8 19.5 %collective-permute-done.25.refs_5_ = bf16[128,1408]{1,0:T(8,128)(2,1)} collective-permute-done((bf16[128,1408]{1,0:T(8,128)(2,1)}, bf16[128,1408]{1,0:T(8,128)(2,1)}, u32[]{:S(2)}, u32[]{:S(2)}) %collective-permute-start.25) | collective-permute-done | bytes 360480 | tf_op jit(solution)/shard_map/ppermute | solution.py:774
  161.5 7.1 %collective-permute-done.34.refs_28_ = bf16[240,1280]{1,0:T(8,128)(2,1)S(1)} collective-permute-done((bf16[240,1280]{1,0:T(8,128)(2,1)S(1)}, bf16[240,1280]{1,0:T(8,128)(2,1)S(1)}, u32[]{:S(2)}, u32[]{:S(2)}) %collective-permute-start.34) | collective-permute-done | bytes 614432 | tf_op jit(solution)/shard_map/ppermute | solution.py:774
  170.8 14.2 %feed.1 = (bf16[192,1280]{1,0:T(8,128)(2,1)}, f32[192,1280]{1,0:T(8,128)}, bf16[64,1408]{1,0:T(8,128)(2,1)}, bf16[128,1408]{1,0:T(8,128)(2,1)}, bf16[1280,192]{1...) custom-call(s32[2]{0:T(128)} %copy-done.39, ...), custom_call_target="tpu_custom_call" | custom-call | flops 1 | bytes 1 | tf_op jit(solution)/shard_map/feed/pallas_call | solution.py:450
  185.1 3.1 collective-permute-start.36
  188.2 6.7 %feed_grads.1 = (bf16[480,1280]{1,0:T(8,128)(2,1)}, bf16[480,1280]{1,0:T(8,128)(2,1)}, bf16[480,1280]{1,0:T(8,128)(2,1)}, bf16[480,1280]{1,0:T(8,128)(2,1)}, bf1...) custom-call(s32[2]{0:T(128)} %copy-done.39, bf16[1280,192]{1,0:T(8,128)(2,1)} %get-tuple-element.203.refs_0_, ...), custom_call_target="tpu_custom_call" | custom-call | flops 1 | bytes 1 | tf_op jit(solution)/shard_map/feed_grads/pallas_call | solution.py:492
  195.6 1.5 collective-permute-done.36.refs_2_
  197.7 1.5 collective-permute-start.40
  199.3 7.3 %collective-permute-done.40.refs_4_ = bf16[64,1408]{1,0:T(8,128)(2,1)S(1)} collective-permute-done((bf16[64,1408]{1,0:T(8,128)(2,1)S(1)}, bf16[64,1408]{1,0:T(8,128)(2,1)S(1)}, u32[]{:S(2)}, u32[]{:S(2)}) %collective-permute-start.40) | collective-permute-done | bytes 180256 | tf_op jit(solution)/shard_map/ppermute | solution.py:931
  206.7 3.0 collective-permute-start.44
  209.6 2.6 add_convert_fusion
  212.9 1.4 collective-permute-start.42
  214.3 8.8 %attend_back.2 = (bf16[512,1280]{1,0:T(8,128)(2,1)}, bf16[512,1280]{1,0:T(8,128)(2,1)}, bf16[256,1280]{1,0:T(8,128)(2,1)}, bf16[64,1280]{1,0:T(8,128)(2,1)}, bf1...) custom-call(s32[2]{0:T(128)} %copy-done.39, ...), custom_call_target="tpu_custom_call" | custom-call | flops 1 | bytes 1 | tf_op jit(solution)/shard_map/attend_back/pallas_call | solution.py:576
  223.1 1.8 collective-permute-done.45.refs_1_
  230.6 4.2 %meet.2 = (bf16[480,1280]{1,0:T(8,128)(2,1)}, bf16[480,1280]{1,0:T(8,128)(2,1)}) custom-call(bf16[480,1280]{1,0:T(8,128)(2,1)S(1)} %copy-done.13, bf16[240,1280]{1,0:T(8,128)(2,1)S(1)} %collective-permute-done.41.h, bf16[480,1280]{1,0:T(8,128)(2,1)S(1)} %copy-done.14, bf16[240,1280]{1,0:T(8,128)(2,1)} %collective-permute-done.42.l, ...), custom_call_target="tpu_custom_call" | custom-call | flops 1 | bytes 1 | tf_op jit(solution)/shard_map/meet/pallas_call | solution.py:840
  234.7 5.6 %collective-permute-done.47.refs_4_ = bf16[128,1408]{1,0:T(8,128)(2,1)S(1)} collective-permute-done((bf16[128,1408]{1,0:T(8,128)(2,1)}, bf16[128,1408]{1,0:T(8,128)(2,1)S(1)}, u32[]{:S(2)}, u32[]{:S(2)}) %collective-permute-start.47) | collective-permute-done | bytes 360480 | tf_op jit(solution)/shard_map/ppermute | solution.py:931
  240.4 1.4 collective-permute-start.54
  241.8 1.4 collective-permute-start.55
  243.2 2.5 collective-permute-start.49
  245.8 1.8 collective-permute-start.50
  247.6 15.2 %attend_back.3 = (bf16[1024,1280]{1,0:T(8,128)(2,1)}, bf16[1024,1280]{1,0:T(8,128)(2,1)}, bf16[512,1280]{1,0:T(8,128)(2,1)}, bf16[128,1280]{1,0:T(8,128)(2,1)}, ...) custom-call(s32[2]{0:T(128)} %copy-done.39, ...), custom_call_target="tpu_custom_call" | custom-call | flops 1 | bytes 1 | tf_op jit(solution)/shard_map/attend_back/pallas_call | solution.py:576
  264.2 3.9 %collective-permute-start.53 = (bf16[128,1280]{1,0:T(8,128)(2,1)}, bf16[128,1280]{1,0:T(8,128)(2,1)S(1)}, u32[]{:S(2)}, u32[]{:S(2)}) collective-permute-start(bf16[128,1280]{1,0:T(8,128)(2,1)} %get-tuple-element.249), channel_id=1, source_target_pairs={{3,2},{0,1},{7,6},{4,5},{11,10},{8,9},{15,14},{12,13},{19,18},{16,... | collective-permute-start | bytes 983048 | tf_op jit(solution)/shard_map/ppermute | solution.py:936
  269.1 15.0 %weight_grads.1 = (bf16[352,1280]{1,0:T(8,128)(2,1)}, bf16[352,1280]{1,0:T(8,128)(2,1)}, bf16[352,1280]{1,0:T(8,128)(2,1)}, bf16[352,1280]{1,0:T(8,128)(2,1)}, b...) custom-call(s32[2]{0:T(128)} %copy-done.39, bf16[768,1536]{1,0:T(8,128)(2,1)} %get-tuple-element.199.refs_0_, ...), custom_call_target="tpu_custom_call" | custom-call | flops 1 | bytes 1 | tf_op jit(solution)/shard_map/weight_grads/pallas_call | solution.py:648
  286.6 2.7 collective-permute-done.56
  292.1 2.1 collective-permute-start.62
  294.2 4.2 %cut.2 = (f32[120,1280]{1,0:T(8,128)S(1)}, bf16[120,1280]{1,0:T(8,128)(2,1)}, bf16[120,1280]{1,0:T(8,128)(2,1)}, bf16[120,1280]{1,0:T(8,128)(2,1)}) custom-call(s32[2]{0:T(128)S(1)} %copy-done.41, bf16[480,1280]{1,0:T(8,128)(2,1)S(1)} %copy-done.15, bf16[1440,1280]{1,0:T(8,128)(2,1)} %collective-permute-done.43.o.refs_1_, ...), custom_call_target="tpu_custom_call" | custom-call | flops 1 | bytes 1 | tf_op jit(solution)/shard_map/cut/pallas_call | solution.py:869
  298.4 4.5 %collective-permute-done.57.h = bf16[160,1280]{1,0:T(8,128)(2,1)S(1)} collective-permute-done((bf16[160,1280]{1,0:T(8,128)(2,1)S(1)}, bf16[160,1280]{1,0:T(8,128)(2,1)S(1)}, u32[]{:S(2)}, u32[]{:S(2)}) %collective-permute-start.57) | collective-permute-done | bytes 409632 | tf_op jit(solution)/shard_map/ppermute | solution.py:774
  303.0 1.4 collective-permute-done.58.l
  304.4 1.7 meet.3
  307.3 2.2 collective-permute-done.62.refs_7_
  310.2 2.5 collective-permute-start.67
  312.7 1.8 collective-permute-start.68
  314.6 16.4 %byte_grad.1 = f32[1536,768]{1,0:T(8,128)} custom-call(s32[2]{0:T(128)} %copy-done.39, bf16[1536,768]{1,0:T(8,128)(2,1)} %bitcast.9, bf16[512,1280]{1,0:T(8,128)(2,1)} %get-tuple-element.269.refs_3_.refs_0_, bf16[512,1280]{1,0:T(8,128)(2,1)} %get-tuple-element.238.refs_5_.refs_1_, bf16[1024,1280]{1,0:T(8,128)(2,1)} %get-tuple-element.237.refs_4_.refs_2_, ...), custom_call_target="tpu_custom_call" | custom-call | flops 1 | bytes 1 | tf_op jit(solution)/shard_map/byte_grad/pallas_call | solution.py:708
  331.0 3.8 %collective-permute-done.67 = bf16[120,1280]{1,0:T(8,128)(2,1)} collective-permute-done((bf16[120,1280]{1,0:T(8,128)(2,1)}, bf16[120,1280]{1,0:T(8,128)(2,1)}, u32[]{:S(2)}, u32[]{:S(2)}) %collective-permute-start.67) | collective-permute-done | bytes 307232 | tf_op jit(solution)/shard_map/ppermute | solution.py:774
  334.8 1.5 convert_add_fusion
  336.5 2.2 cut.3
  338.8 2.0 collective-permute-start.65
  340.8 7.0 %collective-permute-start.64 = (bf16[88,1280]{1,0:T(8,128)(2,1)S(1)}, bf16[88,1280]{1,0:T(8,128)(2,1)S(1)}, u32[]{:S(2)}, u32[]{:S(2)}) collective-permute-start(bf16[88,1280]{1,0:T(8,128)(2,1)S(1)} %get-tuple-element.279), channel_id=1, source_target_pairs={{0,2},{1,3},{2,0},{3,1},{4,6},{5,7},{6,4},{7,5},{8,10},{9,11},{10,... | collective-permute-start | bytes 675848 | tf_op jit(solution)/shard_map/ppermute | solution.py:774
  349.4 3.0 latent_grad.1
  352.5 8.4 %collective-permute-done.64 = bf16[88,1280]{1,0:T(8,128)(2,1)S(1)} collective-permute-done((bf16[88,1280]{1,0:T(8,128)(2,1)S(1)}, bf16[88,1280]{1,0:T(8,128)(2,1)S(1)}, u32[]{:S(2)}, u32[]{:S(2)}) %collective-permute-start.64) | collective-permute-done | bytes 225312 | tf_op jit(solution)/shard_map/ppermute | solution.py:774
  (287 shorter events, 45.7 us)
Async XLA Ops:
  2.4 15.4 %collective-permute-start.1 = (bf16[96,1280]{1,0:T(8,128)(2,1)S(1)}, bf16[96,1280]{1,0:T(8,128)(2,1)S(1)}, u32[]{:S(2)}, u32[]{:S(2)}) collective-permute-start(bf16[96,1280]{1,0:T(8,128)(2,1)S(1)} %fusion.8.refs_0_), channel_id=1, source_target_pairs={{0,2},{1,3},{2,0},{3,1},{4,6},{5,7},{6,4},{7,5},{8,10},{9,11},{10,... | collective-permute-start | bytes 737288 | tf_op jit(solution)/shard_map/ppermute | solution.py:774
  6.5 11.5 %collective-permute-start = (bf16[96,1280]{1,0:T(8,128)(2,1)S(1)}, bf16[96,1280]{1,0:T(8,128)(2,1)S(1)}, u32[]{:S(2)}, u32[]{:S(2)}) collective-permute-start(bf16[96,1280]{1,0:T(8,128)(2,1)S(1)} %fusion.8.refs_0_), channel_id=1, source_target_pairs={{0,1},{1,0},{2,3},{3,2},{4,5},{5,4},{6,7},{7,6},{8,9},{9,8},{10,11... | collective-permute-start | bytes 737288 | tf_op jit(solution)/shard_map/ppermute | solution.py:774
  18.7 9.3 %collective-permute-start.3 = (bf16[96,1280]{1,0:T(8,128)(2,1)S(1)}, bf16[96,1280]{1,0:T(8,128)(2,1)S(1)}, u32[]{:S(2)}, u32[]{:S(2)}) collective-permute-start(bf16[96,1280]{1,0:T(8,128)(2,1)S(1)} %collective-permute-done.1.refs_2_), channel_id=1, source_target_pairs={{2,3},{1,0},{6,7},{5,4},{10,11},{9,8},{14,15},{13,12},{18,19},{17,... | collective-permute-start | bytes 737288 | tf_op jit(solution)/shard_map/ppermute | solution.py:931
  29.2 20.9 %collective-permute-start.4 = (bf16[368,1280]{1,0:T(8,128)(2,1)S(1)}, bf16[368,1280]{1,0:T(8,128)(2,1)S(1)}, u32[]{:S(2)}, u32[]{:S(2)}) collective-permute-start(bf16[368,1280]{1,0:T(8,128)(2,1)S(1)} %assemble.2.refs_0_.refs_8_.refs_10_.refs_9_.refs_4_), channel_id=1, source_target_pairs={{0,8},{4,12},{8,0},{12,4},{16,24},{20,28},{24,16},{28,20},{1,9},{5... | collective-permute-start | bytes 2826248 | tf_op jit(solution)/shard_map/ppermute | solution.py:774
  30.7 20.9 %collective-permute-start.5 = (bf16[368,1280]{1,0:T(8,128)(2,1)S(1)}, bf16[368,1280]{1,0:T(8,128)(2,1)S(1)}, u32[]{:S(2)}, u32[]{:S(2)}) collective-permute-start(bf16[368,1280]{1,0:T(8,128)(2,1)S(1)} %assemble.2.refs_0_.refs_8_.refs_10_.refs_9_.refs_4_), channel_id=1, source_target_pairs={{0,16},{4,20},{8,24},{12,28},{16,0},{20,4},{24,8},{28,12},{1,17},{... | collective-permute-start | bytes 2826248 | tf_op jit(solution)/shard_map/ppermute | solution.py:774
  32.3 29.0 %collective-permute-start.12 = (bf16[368,1280]{1,0:T(8,128)(2,1)S(1)}, bf16[368,1280]{1,0:T(8,128)(2,1)}, u32[]{:S(2)}, u32[]{:S(2)}) collective-permute-start(bf16[368,1280]{1,0:T(8,128)(2,1)S(1)} %assemble.2.refs_0_.refs_8_.refs_10_.refs_9_.refs_4_), channel_id=1, source_target_pairs={{0,4},{4,0},{8,12},{12,8},{16,20},{20,16},{24,28},{28,24},{1,5},{5... | collective-permute-start | bytes 2826248 | tf_op jit(solution)/shard_map/ppermute | solution.py:774
  32.5 26.1 %collective-permute-start.9 = (bf16[192,1408]{1,0:T(8,128)(2,1)S(1)}, bf16[192,1408]{1,0:T(8,128)(2,1)S(1)}, u32[]{:S(2)}, u32[]{:S(2)}) collective-permute-start(bf16[192,1408]{1,0:T(8,128)(2,1)S(1)} %fusion.1.refs_0_.refs_8_.x_ref), channel_id=1, source_target_pairs={{0,1},{1,0},{2,3},{3,2},{4,5},{5,4},{6,7},{7,6},{8,9},{9,8},{10,11... | collective-permute-start | bytes 1622024 | tf_op jit(solution)/shard_map/ppermute | solution.py:774
  32.8 28.5 %collective-permute-start.8 = (bf16[192,1408]{1,0:T(8,128)(2,1)S(1)}, bf16[192,1408]{1,0:T(8,128)(2,1)}, u32[]{:S(2)}, u32[]{:S(2)}) collective-permute-start(bf16[192,1408]{1,0:T(8,128)(2,1)S(1)} %fusion.1.refs_0_.refs_8_.x_ref), channel_id=1, source_target_pairs={{0,2},{1,3},{2,0},{3,1},{4,6},{5,7},{6,4},{7,5},{8,10},{9,11},{10,... | collective-permute-start | bytes 1622024 | tf_op jit(solution)/shard_map/ppermute | solution.py:774
  51.7 10.4 %collective-permute-start.6 = (bf16[192,1280]{1,0:T(8,128)(2,1)S(1)}, bf16[192,1280]{1,0:T(8,128)(2,1)S(1)}, u32[]{:S(2)}, u32[]{:S(2)}) collective-permute-start(bf16[192,1280]{1,0:T(8,128)(2,1)S(1)} %slice.72), channel_id=1, source_target_pairs={{0,16},{4,20},{8,24},{12,28},{16,0},{20,4},{24,8},{28,12},{1,17},{... | collective-permute-start | bytes 1474568 | tf_op jit(solution)/shard_map/ppermute | solution.py:774
  53.3 8.8 %collective-permute-start.7 = (bf16[176,1280]{1,0:T(8,128)(2,1)S(1)}, bf16[176,1280]{1,0:T(8,128)(2,1)}, u32[]{:S(2)}, u32[]{:S(2)}) collective-permute-start(bf16[176,1280]{1,0:T(8,128)(2,1)S(1)} %slice.73), channel_id=1, source_target_pairs={{0,8},{4,12},{8,0},{12,4},{16,24},{20,28},{24,16},{28,20},{1,9},{5... | collective-permute-start | bytes 1351688 | tf_op jit(solution)/shard_map/ppermute | solution.py:774
  62.0 7.5 %collective-permute-start.15 = (bf16[192,1280]{1,0:T(8,128)(2,1)S(1)}, bf16[192,1280]{1,0:T(8,128)(2,1)}, u32[]{:S(2)}, u32[]{:S(2)}) collective-permute-start(bf16[192,1280]{1,0:T(8,128)(2,1)S(1)} %collective-permute-done.6.refs_6_.refs_14_.refs_16_.refs_15_.refs_10_), channel_id=1, source_target_pairs={{0,4},{4,0},{8,12},{12,8},{16,20},{20,16},{24,28},{28,24},{1,5},{5... | collective-permute-start | bytes 1474568 | tf_op jit(solution)/shard_map/ppermute | solution.py:774
  62.6 7.7 %collective-permute-start.13 = (bf16[368,1280]{1,0:T(8,128)(2,1)S(1)}, bf16[368,1280]{1,0:T(8,128)(2,1)S(1)}, u32[]{:S(2)}, u32[]{:S(2)}) collective-permute-start(bf16[368,1280]{1,0:T(8,128)(2,1)S(1)} %collective-permute-done.4.refs_2_.refs_10_.refs_12_.refs_11_.refs_6_), channel_id=1, source_target_pairs={{0,4},{4,0},{8,12},{12,8},{16,20},{20,16},{24,28},{28,24},{1,5},{5... | collective-permute-start | bytes 2826248 | tf_op jit(solution)/shard_map/ppermute | solution.py:774
  62.6 8.9 %collective-permute-start.14 = (bf16[368,1280]{1,0:T(8,128)(2,1)S(1)}, bf16[368,1280]{1,0:T(8,128)(2,1)}, u32[]{:S(2)}, u32[]{:S(2)}) collective-permute-start(bf16[368,1280]{1,0:T(8,128)(2,1)S(1)} %collective-permute-done.5.refs_4_.refs_12_.refs_14_.refs_13_.refs_8_), channel_id=1, source_target_pairs={{0,4},{4,0},{8,12},{12,8},{16,20},{20,16},{24,28},{28,24},{1,5},{5... | collective-permute-start | bytes 2826248 | tf_op jit(solution)/shard_map/ppermute | solution.py:774
  63.1 22.2 %collective-permute-start.11 = (bf16[120,1280]{1,0:T(8,128)(2,1)}, bf16[120,1280]{1,0:T(8,128)(2,1)S(1)}, u32[]{:S(2)}, u32[]{:S(2)}) collective-permute-start(bf16[120,1280]{1,0:T(8,128)(2,1)} %copy-done.23), channel_id=1, source_target_pairs={{0,1},{1,0},{2,3},{3,2},{4,5},{5,4},{6,7},{7,6},{8,9},{9,8},{10,11... | collective-permute-start | bytes 921608 | tf_op jit(solution)/shard_map/ppermute | solution.py:774
  64.2 21.9 %collective-permute-start.10 = (bf16[120,1280]{1,0:T(8,128)(2,1)}, bf16[120,1280]{1,0:T(8,128)(2,1)}, u32[]{:S(2)}, u32[]{:S(2)}) collective-permute-start(bf16[120,1280]{1,0:T(8,128)(2,1)} %copy-done.23), channel_id=1, source_target_pairs={{0,2},{1,3},{2,0},{3,1},{4,6},{5,7},{6,4},{7,5},{8,10},{9,11},{10,... | collective-permute-start | bytes 921608 | tf_op jit(solution)/shard_map/ppermute | solution.py:774
  69.5 20.3 %collective-permute-start.17 = (bf16[192,1408]{1,0:T(8,128)(2,1)}, bf16[192,1408]{1,0:T(8,128)(2,1)S(1)}, u32[]{:S(2)}, u32[]{:S(2)}) collective-permute-start(bf16[192,1408]{1,0:T(8,128)(2,1)} %copy-done.10), channel_id=1, source_target_pairs={{1,2},{2,1},{5,6},{6,5},{9,10},{10,9},{13,14},{14,13},{17,18},{18,... | collective-permute-start | bytes 1622024 | tf_op jit(solution)/shard_map/ppermute | solution.py:930
  70.3 20.6 %collective-permute-start.18 = (bf16[192,1408]{1,0:T(8,128)(2,1)}, bf16[192,1408]{1,0:T(8,128)(2,1)}, u32[]{:S(2)}, u32[]{:S(2)}) collective-permute-start(bf16[192,1408]{1,0:T(8,128)(2,1)} %passed.3.refs_2_), channel_id=1, source_target_pairs={{2,3},{1,0},{6,7},{5,4},{10,11},{9,8},{14,15},{13,12},{18,19},{17,... | collective-permute-start | bytes 1622024 | tf_op jit(solution)/shard_map/ppermute | solution.py:931
  86.1 14.5 %collective-permute-start.19 = (bf16[120,1280]{1,0:T(8,128)(2,1)S(1)}, bf16[120,1280]{1,0:T(8,128)(2,1)S(1)}, u32[]{:S(2)}, u32[]{:S(2)}) collective-permute-start(bf16[120,1280]{1,0:T(8,128)(2,1)S(1)} %copy-done.24), channel_id=1, source_target_pairs={{1,2},{2,1},{5,6},{6,5},{9,10},{10,9},{13,14},{14,13},{17,18},{18,... | collective-permute-start | bytes 921608 | tf_op jit(solution)/shard_map/ppermute | solution.py:930
  86.7 14.6 %collective-permute-start.20 = (bf16[120,1280]{1,0:T(8,128)(2,1)}, bf16[120,1280]{1,0:T(8,128)(2,1)S(1)}, u32[]{:S(2)}, u32[]{:S(2)}) collective-permute-start(bf16[120,1280]{1,0:T(8,128)(2,1)} %collective-permute-done.10.refs_2_), channel_id=1, source_target_pairs={{2,3},{1,0},{6,7},{5,4},{10,11},{9,8},{14,15},{13,12},{18,19},{17,... | collective-permute-start | bytes 921608 | tf_op jit(solution)/shard_map/ppermute | solution.py:931
  102.9 28.9 %collective-permute-start.28 = (bf16[480,1280]{1,0:T(8,128)(2,1)S(1)}, bf16[480,1280]{1,0:T(8,128)(2,1)S(1)}, u32[]{:S(2)}, u32[]{:S(2)}) collective-permute-start(bf16[480,1280]{1,0:T(8,128)(2,1)S(1)} %assemble.3.refs_20_), channel_id=1, source_target_pairs={{0,16},{4,20},{8,24},{12,28},{16,0},{20,4},{24,8},{28,12},{1,17},{... | collective-permute-start | bytes 3686408 | tf_op jit(solution)/shard_map/ppermute | solution.py:774
  104.4 28.2 %collective-permute-start.27 = (bf16[480,1280]{1,0:T(8,128)(2,1)S(1)}, bf16[480,1280]{1,0:T(8,128)(2,1)}, u32[]{:S(2)}, u32[]{:S(2)}) collective-permute-start(bf16[480,1280]{1,0:T(8,128)(2,1)S(1)} %assemble.3.refs_20_), channel_id=1, source_target_pairs={{0,8},{4,12},{8,0},{12,4},{16,24},{20,28},{24,16},{28,20},{1,9},{5... | collective-permute-start | bytes 3686408 | tf_op jit(solution)/shard_map/ppermute | solution.py:774
  105.1 22.1 %collective-permute-start.23 = (bf16[64,1408]{1,0:T(8,128)(2,1)S(1)}, bf16[64,1408]{1,0:T(8,128)(2,1)S(1)}, u32[]{:S(2)}, u32[]{:S(2)}) collective-permute-start(bf16[64,1408]{1,0:T(8,128)(2,1)S(1)} %copy-done.82), channel_id=1, source_target_pairs={{0,3},{1,2},{2,1},{3,0},{4,7},{5,6},{6,5},{7,4},{8,11},{9,10},{10,... | collective-permute-start | bytes 540680 | tf_op jit(solution)/shard_map/ppermute | solution.py:774
  109.7 17.5 %collective-permute-start.22 = (bf16[64,1408]{1,0:T(8,128)(2,1)S(1)}, bf16[64,1408]{1,0:T(8,128)(2,1)S(1)}, u32[]{:S(2)}, u32[]{:S(2)}) collective-permute-start(bf16[64,1408]{1,0:T(8,128)(2,1)S(1)} %copy-done.81), channel_id=1, source_target_pairs={{0,2},{1,3},{2,0},{3,1},{4,6},{5,7},{6,4},{7,5},{8,10},{9,11},{10,... | collective-permute-start | bytes 540680 | tf_op jit(solution)/shard_map/ppermute | solution.py:774
  112.4 14.8 %collective-permute-start.21 = (bf16[64,1408]{1,0:T(8,128)(2,1)S(1)}, bf16[64,1408]{1,0:T(8,128)(2,1)S(1)}, u32[]{:S(2)}, u32[]{:S(2)}) collective-permute-start(bf16[64,1408]{1,0:T(8,128)(2,1)S(1)} %copy-done.80), channel_id=1, source_target_pairs={{0,1},{1,0},{2,3},{3,2},{4,5},{5,4},{6,7},{7,6},{8,9},{9,8},{10,11... | collective-permute-start | bytes 540680 | tf_op jit(solution)/shard_map/ppermute | solution.py:774
  127.3 13.5 %collective-permute-start.26 = (bf16[128,1408]{1,0:T(8,128)(2,1)}, bf16[128,1408]{1,0:T(8,128)(2,1)S(1)}, u32[]{:S(2)}, u32[]{:S(2)}) collective-permute-start(bf16[128,1408]{1,0:T(8,128)(2,1)} %get-tuple-element.186), channel_id=1, source_target_pairs={{0,3},{1,2},{2,1},{3,0},{4,7},{5,6},{6,5},{7,4},{8,11},{9,10},{10,... | collective-permute-start | bytes 1081352 | tf_op jit(solution)/shard_map/ppermute | solution.py:774
  129.7 30.6 %collective-permute-start.25 = (bf16[128,1408]{1,0:T(8,128)(2,1)}, bf16[128,1408]{1,0:T(8,128)(2,1)}, u32[]{:S(2)}, u32[]{:S(2)}) collective-permute-start(bf16[128,1408]{1,0:T(8,128)(2,1)} %get-tuple-element.184), channel_id=1, source_target_pairs={{0,2},{1,3},{2,0},{3,1},{4,6},{5,7},{6,4},{7,5},{8,10},{9,11},{10,... | collective-permute-start | bytes 1081352 | tf_op jit(solution)/shard_map/ppermute | solution.py:774
  130.3 30.0 %collective-permute-start.24 = (bf16[128,1408]{1,0:T(8,128)(2,1)}, bf16[128,1408]{1,0:T(8,128)(2,1)}, u32[]{:S(2)}, u32[]{:S(2)}) collective-permute-start(bf16[128,1408]{1,0:T(8,128)(2,1)} %get-tuple-element.182), channel_id=1, source_target_pairs={{0,1},{1,0},{2,3},{3,2},{4,5},{5,4},{6,7},{7,6},{8,9},{9,8},{10,11... | collective-permute-start | bytes 1081352 | tf_op jit(solution)/shard_map/ppermute | solution.py:774
  134.6 25.7 %collective-permute-start.29 = (bf16[240,1280]{1,0:T(8,128)(2,1)}, bf16[240,1280]{1,0:T(8,128)(2,1)S(1)}, u32[]{:S(2)}, u32[]{:S(2)}) collective-permute-start(bf16[240,1280]{1,0:T(8,128)(2,1)} %slice.74), channel_id=1, source_target_pairs={{0,16},{4,20},{8,24},{12,28},{16,0},{20,4},{24,8},{28,12},{1,17},{... | collective-permute-start | bytes 1843208 | tf_op jit(solution)/shard_map/ppermute | solution.py:774
  135.5 24.9 %collective-permute-start.30 = (bf16[240,1280]{1,0:T(8,128)(2,1)}, bf16[240,1280]{1,0:T(8,128)(2,1)}, u32[]{:S(2)}, u32[]{:S(2)}) collective-permute-start(bf16[240,1280]{1,0:T(8,128)(2,1)} %slice.75), channel_id=1, source_target_pairs={{0,8},{4,12},{8,0},{12,4},{16,24},{20,28},{24,16},{28,20},{1,9},{5... | collective-permute-start | bytes 1843208 | tf_op jit(solution)/shard_map/ppermute | solution.py:774
  160.3 8.3 %collective-permute-start.31 = (bf16[480,1280]{1,0:T(8,128)(2,1)S(1)}, bf16[480,1280]{1,0:T(8,128)(2,1)S(1)}, u32[]{:S(2)}, u32[]{:S(2)}) collective-permute-start(bf16[480,1280]{1,0:T(8,128)(2,1)S(1)} %assemble.3.refs_20_), channel_id=1, source_target_pairs={{0,4},{4,0},{8,12},{12,8},{16,20},{20,16},{24,28},{28,24},{1,5},{5... | collective-permute-start | bytes 3686408 | tf_op jit(solution)/shard_map/ppermute | solution.py:774
  160.4 8.2 %collective-permute-start.32 = (bf16[480,1280]{1,0:T(8,128)(2,1)}, bf16[480,1280]{1,0:T(8,128)(2,1)S(1)}, u32[]{:S(2)}, u32[]{:S(2)}) collective-permute-start(bf16[480,1280]{1,0:T(8,128)(2,1)} %collective-permute-done.27.refs_22_), channel_id=1, source_target_pairs={{0,4},{4,0},{8,12},{12,8},{16,20},{20,16},{24,28},{28,24},{1,5},{5... | collective-permute-start | bytes 3686408 | tf_op jit(solution)/shard_map/ppermute | solution.py:774
  160.9 7.7 %collective-permute-start.33 = (bf16[480,1280]{1,0:T(8,128)(2,1)S(1)}, bf16[480,1280]{1,0:T(8,128)(2,1)S(1)}, u32[]{:S(2)}, u32[]{:S(2)}) collective-permute-start(bf16[480,1280]{1,0:T(8,128)(2,1)S(1)} %collective-permute-done.28.refs_24_), channel_id=1, source_target_pairs={{0,4},{4,0},{8,12},{12,8},{16,20},{20,16},{24,28},{28,24},{1,5},{5... | collective-permute-start | bytes 3686408 | tf_op jit(solution)/shard_map/ppermute | solution.py:774
  161.0 7.6 %collective-permute-start.34 = (bf16[240,1280]{1,0:T(8,128)(2,1)S(1)}, bf16[240,1280]{1,0:T(8,128)(2,1)S(1)}, u32[]{:S(2)}, u32[]{:S(2)}) collective-permute-start(bf16[240,1280]{1,0:T(8,128)(2,1)S(1)} %collective-permute-done.29.refs_26_), channel_id=1, source_target_pairs={{0,4},{4,0},{8,12},{12,8},{16,20},{20,16},{24,28},{28,24},{1,5},{5... | collective-permute-start | bytes 1843208 | tf_op jit(solution)/shard_map/ppermute | solution.py:774
  161.4 7.2 %collective-permute-start.35 = (bf16[240,1280]{1,0:T(8,128)(2,1)}, bf16[240,1280]{1,0:T(8,128)(2,1)S(1)}, u32[]{:S(2)}, u32[]{:S(2)}) collective-permute-start(bf16[240,1280]{1,0:T(8,128)(2,1)} %collective-permute-done.30.refs_27_), channel_id=1, source_target_pairs={{0,4},{4,0},{8,12},{12,8},{16,20},{20,16},{24,28},{28,24},{1,5},{5... | collective-permute-start | bytes 1843208 | tf_op jit(solution)/shard_map/ppermute | solution.py:774
  185.0 10.6 %collective-permute-start.37 = (bf16[64,1408]{1,0:T(8,128)(2,1)}, bf16[64,1408]{1,0:T(8,128)(2,1)S(1)}, u32[]{:S(2)}, u32[]{:S(2)}) collective-permute-start(bf16[64,1408]{1,0:T(8,128)(2,1)} %get-tuple-element.212.refs_0_), channel_id=1, source_target_pairs={{0,1},{1,0},{2,3},{3,2},{4,5},{5,4},{6,7},{7,6},{8,9},{9,8},{10,11... | collective-permute-start | bytes 540680 | tf_op jit(solution)/shard_map/ppermute | solution.py:774
  185.1 11.9 %collective-permute-start.36 = (bf16[64,1408]{1,0:T(8,128)(2,1)}, bf16[64,1408]{1,0:T(8,128)(2,1)S(1)}, u32[]{:S(2)}, u32[]{:S(2)}) collective-permute-start(bf16[64,1408]{1,0:T(8,128)(2,1)} %get-tuple-element.212.refs_0_), channel_id=1, source_target_pairs={{0,2},{1,3},{2,0},{3,1},{4,6},{5,7},{6,4},{7,5},{8,10},{9,11},{10,... | collective-permute-start | bytes 540680 | tf_op jit(solution)/shard_map/ppermute | solution.py:774
  197.0 9.5 %collective-permute-start.38 = (bf16[480,1280]{1,0:T(8,128)(2,1)}, bf16[480,1280]{1,0:T(8,128)(2,1)S(1)}, u32[]{:S(2)}, u32[]{:S(2)}) collective-permute-start(bf16[480,1280]{1,0:T(8,128)(2,1)} %get-tuple-element.209), channel_id=1, source_target_pairs={{0,4},{4,0},{8,12},{12,8},{16,20},{20,16},{24,28},{28,24},{1,5},{5... | collective-permute-start | bytes 3686408 | tf_op jit(solution)/shard_map/ppermute | solution.py:774
  197.7 8.8 %collective-permute-start.40 = (bf16[64,1408]{1,0:T(8,128)(2,1)S(1)}, bf16[64,1408]{1,0:T(8,128)(2,1)S(1)}, u32[]{:S(2)}, u32[]{:S(2)}) collective-permute-start(bf16[64,1408]{1,0:T(8,128)(2,1)S(1)} %collective-permute-done.36.refs_2_), channel_id=1, source_target_pairs={{2,3},{1,0},{6,7},{5,4},{10,11},{9,8},{14,15},{13,12},{18,19},{17,... | collective-permute-start | bytes 540680 | tf_op jit(solution)/shard_map/ppermute | solution.py:931
  206.6 22.0 %collective-permute-start.43 = (bf16[1440,1280]{1,0:T(8,128)(2,1)}, bf16[1440,1280]{1,0:T(8,128)(2,1)}, u32[]{:S(2)}, u32[]{:S(2)}) collective-permute-start(bf16[1440,1280]{1,0:T(8,128)(2,1)} %get-tuple-element.220), channel_id=1, source_target_pairs={{0,4},{4,0},{8,12},{12,8},{16,20},{20,16},{24,28},{28,24},{1,5},{5... | collective-permute-start | bytes 11059208 | tf_op jit(solution)/shard_map/ppermute | solution.py:774
  206.6 18.3 %collective-permute-start.45 = (bf16[128,1408]{1,0:T(8,128)(2,1)S(1)}, bf16[128,1408]{1,0:T(8,128)(2,1)S(1)}, u32[]{:S(2)}, u32[]{:S(2)}) collective-permute-start(bf16[128,1408]{1,0:T(8,128)(2,1)S(1)} %copy-done.57), channel_id=1, source_target_pairs={{0,1},{1,0},{2,3},{3,2},{4,5},{5,4},{6,7},{7,6},{8,9},{9,8},{10,11... | collective-permute-start | bytes 1081352 | tf_op jit(solution)/shard_map/ppermute | solution.py:774
  206.7 19.5 %collective-permute-start.44 = (bf16[128,1408]{1,0:T(8,128)(2,1)S(1)}, bf16[128,1408]{1,0:T(8,128)(2,1)S(1)}, u32[]{:S(2)}, u32[]{:S(2)}) collective-permute-start(bf16[128,1408]{1,0:T(8,128)(2,1)S(1)} %copy-done.57), channel_id=1, source_target_pairs={{0,2},{1,3},{2,0},{3,1},{4,6},{5,7},{6,4},{7,5},{8,10},{9,11},{10,... | collective-permute-start | bytes 1081352 | tf_op jit(solution)/shard_map/ppermute | solution.py:774
  212.2 15.9 %collective-permute-start.41 = (bf16[240,1280]{1,0:T(8,128)(2,1)}, bf16[240,1280]{1,0:T(8,128)(2,1)S(1)}, u32[]{:S(2)}, u32[]{:S(2)}) collective-permute-start(bf16[240,1280]{1,0:T(8,128)(2,1)} %get-tuple-element.217), channel_id=1, source_target_pairs={{0,16},{4,20},{8,24},{12,28},{16,0},{20,4},{24,8},{28,12},{1,17},{... | collective-permute-start | bytes 1843208 | tf_op jit(solution)/shard_map/ppermute | solution.py:774
  212.9 15.7 %collective-permute-start.42 = (bf16[240,1280]{1,0:T(8,128)(2,1)}, bf16[240,1280]{1,0:T(8,128)(2,1)}, u32[]{:S(2)}, u32[]{:S(2)}) collective-permute-start(bf16[240,1280]{1,0:T(8,128)(2,1)} %get-tuple-element.218), channel_id=1, source_target_pairs={{0,8},{4,12},{8,0},{12,4},{16,24},{20,28},{24,16},{28,20},{1,9},{5... | collective-permute-start | bytes 1843208 | tf_op jit(solution)/shard_map/ppermute | solution.py:774
  229.2 11.1 %collective-permute-start.47 = (bf16[128,1408]{1,0:T(8,128)(2,1)}, bf16[128,1408]{1,0:T(8,128)(2,1)S(1)}, u32[]{:S(2)}, u32[]{:S(2)}) collective-permute-start(bf16[128,1408]{1,0:T(8,128)(2,1)} %passed.5.refs_2_), channel_id=1, source_target_pairs={{2,3},{1,0},{6,7},{5,4},{10,11},{9,8},{14,15},{13,12},{18,19},{17,... | collective-permute-start | bytes 1081352 | tf_op jit(solution)/shard_map/ppermute | solution.py:931
  240.4 45.2 %collective-permute-start.54 = (bf16[480,1280]{1,0:T(8,128)(2,1)}, bf16[480,1280]{1,0:T(8,128)(2,1)S(1)}, u32[]{:S(2)}, u32[]{:S(2)}) collective-permute-start(bf16[480,1280]{1,0:T(8,128)(2,1)} %get-tuple-element.250), channel_id=1, source_target_pairs={{0,8},{4,12},{8,0},{12,4},{16,24},{20,28},{24,16},{28,20},{1,9},{5... | collective-permute-start | bytes 3686408 | tf_op jit(solution)/shard_map/ppermute | solution.py:774
  241.8 43.8 %collective-permute-start.55 = (bf16[480,1280]{1,0:T(8,128)(2,1)}, bf16[480,1280]{1,0:T(8,128)(2,1)S(1)}, u32[]{:S(2)}, u32[]{:S(2)}) collective-permute-start(bf16[480,1280]{1,0:T(8,128)(2,1)} %get-tuple-element.251), channel_id=1, source_target_pairs={{0,16},{4,20},{8,24},{12,28},{16,0},{20,4},{24,8},{28,12},{1,17},{... | collective-permute-start | bytes 3686408 | tf_op jit(solution)/shard_map/ppermute | solution.py:774
  243.2 19.6 %collective-permute-start.48 = (bf16[64,1280]{1,0:T(8,128)(2,1)}, bf16[64,1280]{1,0:T(8,128)(2,1)S(1)}, u32[]{:S(2)}, u32[]{:S(2)}) collective-permute-start(bf16[64,1280]{1,0:T(8,128)(2,1)} %get-tuple-element.232), channel_id=1, source_target_pairs={{0,1},{1,0},{2,3},{3,2},{4,5},{5,4},{6,7},{7,6},{8,9},{9,8},{10,11... | collective-permute-start | bytes 491528 | tf_op jit(solution)/shard_map/ppermute | solution.py:774
  243.2 19.6 %collective-permute-start.49 = (bf16[64,1280]{1,0:T(8,128)(2,1)}, bf16[64,1280]{1,0:T(8,128)(2,1)S(1)}, u32[]{:S(2)}, u32[]{:S(2)}) collective-permute-start(bf16[64,1280]{1,0:T(8,128)(2,1)} %get-tuple-element.234), channel_id=1, source_target_pairs={{0,2},{1,3},{2,0},{3,1},{4,6},{5,7},{6,4},{7,5},{8,10},{9,11},{10,... | collective-permute-start | bytes 491528 | tf_op jit(solution)/shard_map/ppermute | solution.py:774
  245.8 17.8 %collective-permute-start.50 = (bf16[64,1280]{1,0:T(8,128)(2,1)}, bf16[64,1280]{1,0:T(8,128)(2,1)S(1)}, u32[]{:S(2)}, u32[]{:S(2)}) collective-permute-start(bf16[64,1280]{1,0:T(8,128)(2,1)} %get-tuple-element.236), channel_id=1, source_target_pairs={{0,3},{1,2},{2,1},{3,0},{4,7},{5,6},{6,5},{7,4},{8,11},{9,10},{10,... | collective-permute-start | bytes 491528 | tf_op jit(solution)/shard_map/ppermute | solution.py:774
  264.2 19.9 %collective-permute-start.51 = (bf16[128,1280]{1,0:T(8,128)(2,1)}, bf16[128,1280]{1,0:T(8,128)(2,1)S(1)}, u32[]{:S(2)}, u32[]{:S(2)}) collective-permute-start(bf16[128,1280]{1,0:T(8,128)(2,1)} %get-tuple-element.247), channel_id=1, source_target_pairs={{0,1},{1,0},{2,3},{3,2},{4,5},{5,4},{6,7},{7,6},{8,9},{9,8},{10,11... | collective-permute-start | bytes 983048 | tf_op jit(solution)/shard_map/ppermute | solution.py:774
  264.2 20.6 %collective-permute-start.53 = (bf16[128,1280]{1,0:T(8,128)(2,1)}, bf16[128,1280]{1,0:T(8,128)(2,1)S(1)}, u32[]{:S(2)}, u32[]{:S(2)}) collective-permute-start(bf16[128,1280]{1,0:T(8,128)(2,1)} %get-tuple-element.249), channel_id=1, source_target_pairs={{3,2},{0,1},{7,6},{4,5},{11,10},{8,9},{15,14},{12,13},{19,18},{16,... | collective-permute-start | bytes 983048 | tf_op jit(solution)/shard_map/ppermute | solution.py:936
  268.1 16.7 %collective-permute-start.52 = (bf16[128,1280]{1,0:T(8,128)(2,1)}, bf16[128,1280]{1,0:T(8,128)(2,1)S(1)}, u32[]{:S(2)}, u32[]{:S(2)}) collective-permute-start(bf16[128,1280]{1,0:T(8,128)(2,1)} %get-tuple-element.249), channel_id=1, source_target_pairs={{1,2},{2,1},{5,6},{6,5},{9,10},{10,9},{13,14},{14,13},{17,18},{18,... | collective-permute-start | bytes 983048 | tf_op jit(solution)/shard_map/ppermute | solution.py:935
  289.3 15.1 %collective-permute-start.59 = (bf16[1056,1280]{1,0:T(8,128)(2,1)}, bf16[1056,1280]{1,0:T(8,128)(2,1)S(1)}, u32[]{:S(2)}, u32[]{:S(2)}) collective-permute-start(bf16[1056,1280]{1,0:T(8,128)(2,1)} %get-tuple-element.262), channel_id=1, source_target_pairs={{0,4},{4,0},{8,12},{12,8},{16,20},{20,16},{24,28},{28,24},{1,5},{5... | collective-permute-start | bytes 8110088 | tf_op jit(solution)/shard_map/ppermute | solution.py:774
  290.8 13.6 %collective-permute-start.58 = (bf16[192,1280]{1,0:T(8,128)(2,1)S(1)}, bf16[192,1280]{1,0:T(8,128)(2,1)S(1)}, u32[]{:S(2)}, u32[]{:S(2)}) collective-permute-start(bf16[192,1280]{1,0:T(8,128)(2,1)S(1)} %add_convert_fusion.2), channel_id=1, source_target_pairs={{0,8},{4,12},{8,0},{12,4},{16,24},{20,28},{24,16},{28,20},{1,9},{5... | collective-permute-start | bytes 1474568 | tf_op jit(solution)/shard_map/ppermute | solution.py:774
  291.5 11.5 %collective-permute-start.57 = (bf16[160,1280]{1,0:T(8,128)(2,1)S(1)}, bf16[160,1280]{1,0:T(8,128)(2,1)S(1)}, u32[]{:S(2)}, u32[]{:S(2)}) collective-permute-start(bf16[160,1280]{1,0:T(8,128)(2,1)S(1)} %add_convert_fusion.3), channel_id=1, source_target_pairs={{0,16},{4,20},{8,24},{12,28},{16,0},{20,4},{24,8},{28,12},{1,17},{... | collective-permute-start | bytes 1228808 | tf_op jit(solution)/shard_map/ppermute | solution.py:774
  292.1 17.3 %collective-permute-start.62 = (bf16[128,1280]{1,0:T(8,128)(2,1)S(1)}, bf16[128,1280]{1,0:T(8,128)(2,1)S(1)}, u32[]{:S(2)}, u32[]{:S(2)}) collective-permute-start(bf16[128,1280]{1,0:T(8,128)(2,1)S(1)} %add_convert_fusion.4), channel_id=1, source_target_pairs={{0,2},{1,3},{2,0},{3,1},{4,6},{5,7},{6,4},{7,5},{8,10},{9,11},{10,... | collective-permute-start | bytes 983048 | tf_op jit(solution)/shard_map/ppermute | solution.py:774
  306.1 30.3 %collective-permute-start.60 = (bf16[352,1280]{1,0:T(8,128)(2,1)}, bf16[352,1280]{1,0:T(8,128)(2,1)S(1)}, u32[]{:S(2)}, u32[]{:S(2)}) collective-permute-start(bf16[352,1280]{1,0:T(8,128)(2,1)} %get-tuple-element.267), channel_id=1, source_target_pairs={{0,8},{4,12},{8,0},{12,4},{16,24},{20,28},{24,16},{28,20},{1,9},{5... | collective-permute-start | bytes 2703368 | tf_op jit(solution)/shard_map/ppermute | solution.py:774
  306.7 29.7 %collective-permute-start.61 = (bf16[352,1280]{1,0:T(8,128)(2,1)}, bf16[352,1280]{1,0:T(8,128)(2,1)}, u32[]{:S(2)}, u32[]{:S(2)}) collective-permute-start(bf16[352,1280]{1,0:T(8,128)(2,1)} %get-tuple-element.268), channel_id=1, source_target_pairs={{0,16},{4,20},{8,24},{12,28},{16,0},{20,4},{24,8},{28,12},{1,17},{... | collective-permute-start | bytes 2703368 | tf_op jit(solution)/shard_map/ppermute | solution.py:774
  310.2 20.8 %collective-permute-start.66 = (bf16[120,1280]{1,0:T(8,128)(2,1)}, bf16[120,1280]{1,0:T(8,128)(2,1)}, u32[]{:S(2)}, u32[]{:S(2)}) collective-permute-start(bf16[120,1280]{1,0:T(8,128)(2,1)} %get-tuple-element.283), channel_id=1, source_target_pairs={{0,1},{1,0},{2,3},{3,2},{4,5},{5,4},{6,7},{7,6},{8,9},{9,8},{10,11... | collective-permute-start | bytes 921608 | tf_op jit(solution)/shard_map/ppermute | solution.py:774
  310.2 24.6 %collective-permute-start.67 = (bf16[120,1280]{1,0:T(8,128)(2,1)}, bf16[120,1280]{1,0:T(8,128)(2,1)}, u32[]{:S(2)}, u32[]{:S(2)}) collective-permute-start(bf16[120,1280]{1,0:T(8,128)(2,1)} %get-tuple-element.285), channel_id=1, source_target_pairs={{0,2},{1,3},{2,0},{3,1},{4,6},{5,7},{6,4},{7,5},{8,10},{9,11},{10,... | collective-permute-start | bytes 921608 | tf_op jit(solution)/shard_map/ppermute | solution.py:774
  312.7 22.1 %collective-permute-start.68 = (bf16[120,1280]{1,0:T(8,128)(2,1)}, bf16[120,1280]{1,0:T(8,128)(2,1)}, u32[]{:S(2)}, u32[]{:S(2)}) collective-permute-start(bf16[120,1280]{1,0:T(8,128)(2,1)} %get-tuple-element.287), channel_id=1, source_target_pairs={{0,3},{1,2},{2,1},{3,0},{4,7},{5,6},{6,5},{7,4},{8,11},{9,10},{10,... | collective-permute-start | bytes 921608 | tf_op jit(solution)/shard_map/ppermute | solution.py:774
  338.8 13.7 %collective-permute-start.65 = (bf16[88,1280]{1,0:T(8,128)(2,1)S(1)}, bf16[88,1280]{1,0:T(8,128)(2,1)S(1)}, u32[]{:S(2)}, u32[]{:S(2)}) collective-permute-start(bf16[88,1280]{1,0:T(8,128)(2,1)S(1)} %get-tuple-element.281), channel_id=1, source_target_pairs={{0,3},{1,2},{2,1},{3,0},{4,7},{5,6},{6,5},{7,4},{8,11},{9,10},{10,... | collective-permute-start | bytes 675848 | tf_op jit(solution)/shard_map/ppermute | solution.py:774
  340.8 20.1 %collective-permute-start.64 = (bf16[88,1280]{1,0:T(8,128)(2,1)S(1)}, bf16[88,1280]{1,0:T(8,128)(2,1)S(1)}, u32[]{:S(2)}, u32[]{:S(2)}) collective-permute-start(bf16[88,1280]{1,0:T(8,128)(2,1)S(1)} %get-tuple-element.279), channel_id=1, source_target_pairs={{0,2},{1,3},{2,0},{3,1},{4,6},{5,7},{6,4},{7,5},{8,10},{9,11},{10,... | collective-permute-start | bytes 675848 | tf_op jit(solution)/shard_map/ppermute | solution.py:774
  347.8 13.1 %collective-permute-start.63 = (bf16[88,1280]{1,0:T(8,128)(2,1)S(1)}, bf16[88,1280]{1,0:T(8,128)(2,1)S(1)}, u32[]{:S(2)}, u32[]{:S(2)}) collective-permute-start(bf16[88,1280]{1,0:T(8,128)(2,1)S(1)} %get-tuple-element.277), channel_id=1, source_target_pairs={{0,1},{1,0},{2,3},{3,2},{4,5},{5,4},{6,7},{7,6},{8,9},{9,8},{10,11... | collective-permute-start | bytes 675848 | tf_op jit(solution)/shard_map/ppermute | solution.py:774
  (88 other events, 863.4 us)

commit v7 on v6

--- a/solution.py
+++ b/solution.py
@@ -315,7 +315,7 @@
             top = jnp.max(scores, axis=-1, keepdims=True)
             exponent = jnp.exp(scores - top)
             total = jnp.sum(exponent, axis=-1, keepdims=True)
-            found = dot(exponent.astype(BF), value_ref[:, window]) / total
+            found = dot(exponent.astype(BF), value_ref[:, window]) * (1.0 / total)
             if head == 0:
                 acc[:, window] = found
             else:
@@ -400,7 +400,7 @@
         summed = functools.reduce(
             jnp.add, [s * value[:, :lat].astype(F32) for s, value in zip(shares, found)]
         )
-        attended = (summed / total).astype(BF)
+        attended = (summed * (1.0 / total)).astype(BF)
         log_total = top + jnp.log(total)
         attended_t[...] = jnp.transpose(attended, (1, 0))
 

time: 369 us -> 369 us (level)
  no operation moved by 1% of the time
where the time goes in v7:
time: 369 us; the launch traced here: 364 us
  Pallas kernels  132 us (36%)
  waiting for transfers between devices  117 us (32%)
  starting transfers between devices  88.5 us (24%)
  other arithmetic  12.3 us (3%)
  local copies, waits for them, and re-layouts  12.2 us (3%)
    ppermute x57, waiting for transfers between devices, swap(): return lax.ppermute(value, axis, [(i, i ^ distance) for i in range(size)])  94.5 us
    ppermute x57, starting transfers between devices, swap(): return lax.ppermute(value, axis, [(i, i ^ distance) for i in range(size)])  73 us
    pallas_call x2, Pallas kernels, attend_back_call(): pl.pallas_call(kernel, grid_spec=pltpu.PrefetchScalarGridSpec(num_scalar_...  24 us
    pallas_call x2, Pallas kernels, attend_call(): pl.pallas_call(kernel, grid_spec=pltpu.PrefetchScalarGridSpec(num_scalar_...  23.9 us
    ppermute x5, waiting for transfers between devices, relay(): lax.ppermute(tie(two, *self.gate), 'fsdp', [(2, 3), (1, 0)])  22.6 us
    pallas_call x1, Pallas kernels, byte_grad_call(): pl.pallas_call(kernel, grid_spec=pltpu.PrefetchScalarGridSpec(num_scalar_...  16.4 us
    pallas_call x1, Pallas kernels, weight_grads_call(): pl.pallas_call(kernel, grid_spec=pltpu.PrefetchScalarGridSpec(num_scalar_...  15 us
    pallas_call x1, Pallas kernels, feed_call(): pl.pallas_call(kernel, in_specs=[scalar_spec()] + [whole_spec()] * (len(f...  14.2 us
  transfers between devices with their start and end apart: 69, of which 28 were waited for; matrix products, arithmetic and copies ran while one was open for 3% of the time, Pallas kernels for 31%

profile of v7, /device:TPU:0, one launch (start us, length us, event | category | flops | bytes accessed | tf_op | source)
XLA Modules:
  0.0 364.2 jit_solution(10462970533944853970)
XLA Ops:
  2.4 4.1 %collective-permute-start.1 = (bf16[96,1280]{1,0:T(8,128)(2,1)S(1)}, bf16[96,1280]{1,0:T(8,128)(2,1)S(1)}, u32[]{:S(2)}, u32[]{:S(2)}) collective-permute-start(bf16[96,1280]{1,0:T(8,128)(2,1)S(1)} %fusion.8.refs_0_), channel_id=1, source_target_pairs={{0,2},{1,3},{2,0},{3,1},{4,6},{5,7},{6,4},{7,5},{8,10},{9,11},{10,... | collective-permute-start | bytes 737288 | tf_op jit(solution)/shard_map/ppermute | solution.py:774
  6.5 1.6 collective-permute-start
  8.1 9.7 %collective-permute-done.1.refs_2_ = bf16[96,1280]{1,0:T(8,128)(2,1)S(1)} collective-permute-done((bf16[96,1280]{1,0:T(8,128)(2,1)S(1)}, bf16[96,1280]{1,0:T(8,128)(2,1)S(1)}, u32[]{:S(2)}, u32[]{:S(2)}) %collective-permute-start.1) | collective-permute-done | bytes 245792 | tf_op jit(solution)/shard_map/ppermute | solution.py:774
  20.1 7.9 %collective-permute-done.3.refs_4_ = bf16[96,1280]{1,0:T(8,128)(2,1)S(1)} collective-permute-done((bf16[96,1280]{1,0:T(8,128)(2,1)S(1)}, bf16[96,1280]{1,0:T(8,128)(2,1)S(1)}, u32[]{:S(2)}, u32[]{:S(2)}) %collective-permute-start.3) | collective-permute-done | bytes 245792 | tf_op jit(solution)/shard_map/ppermute | solution.py:931
  29.2 1.6 collective-permute-start.4
  30.7 1.5 collective-permute-start.5
  32.8 4.1 %collective-permute-start.8 = (bf16[192,1408]{1,0:T(8,128)(2,1)S(1)}, bf16[192,1408]{1,0:T(8,128)(2,1)}, u32[]{:S(2)}, u32[]{:S(2)}) collective-permute-start(bf16[192,1408]{1,0:T(8,128)(2,1)S(1)} %fusion.1.refs_0_.refs_8_.x_ref), channel_id=1, source_target_pairs={{0,2},{1,3},{2,0},{3,1},{4,6},{5,7},{6,4},{7,5},{8,10},{9,11},{10,... | collective-permute-start | bytes 1622024 | tf_op jit(solution)/shard_map/ppermute | solution.py:774
  36.9 13.2 %collective-permute-done.4.refs_2_.refs_10_.refs_12_.refs_11_.refs_6_ = bf16[368,1280]{1,0:T(8,128)(2,1)S(1)} collective-permute-done((bf16[368,1280]{1,0:T(8,128)(2,1)S(1)}, bf16[368,1280]{1,0:T(8,128)(2,1)S(1)}, u32[]{:S(2)}, u32[]{:S(2)}) %collective-permute-start.4) | collective-permute-done | bytes 942112 | tf_op jit(solution)/shard_map/ppermute | solution.py:774
  50.1 1.5 collective-permute-done.5.refs_4_.refs_12_.refs_14_.refs_13_.refs_8_
  51.7 1.5 collective-permute-start.6
  53.8 4.9 %collective-permute-done.9.refs_1_ = bf16[192,1408]{1,0:T(8,128)(2,1)S(1)} collective-permute-done((bf16[192,1408]{1,0:T(8,128)(2,1)S(1)}, bf16[192,1408]{1,0:T(8,128)(2,1)S(1)}, u32[]{:S(2)}, u32[]{:S(2)}) %collective-permute-start.9) | collective-permute-done | bytes 540704 | tf_op jit(solution)/shard_map/ppermute | solution.py:774
  58.6 2.6 collective-permute-done.8.in_ref
  64.2 5.4 %collective-permute-start.10 = (bf16[120,1280]{1,0:T(8,128)(2,1)}, bf16[120,1280]{1,0:T(8,128)(2,1)}, u32[]{:S(2)}, u32[]{:S(2)}) collective-permute-start(bf16[120,1280]{1,0:T(8,128)(2,1)} %copy-done.23), channel_id=1, source_target_pairs={{0,2},{1,3},{2,0},{3,1},{4,6},{5,7},{6,4},{7,5},{8,10},{9,11},{10,... | collective-permute-start | bytes 921608 | tf_op jit(solution)/shard_map/ppermute | solution.py:774
  71.6 13.7 %keys_values.1 = (bf16[768,1536]{1,0:T(8,128)(2,1)}, bf16[1536,1280]{1,0:T(8,128)(2,1)}, bf16[1536,1280]{1,0:T(8,128)(2,1)}) custom-call(s32[2]{0:T(128)} %copy-done.39, bf16[1536,768]{1,0:T(8,128)(2,1)} %bitcast.8, bf16[368,1280]{1,0:T(8,128)(2,1)} %copy-done, bf16[368,1280]{1,0:T(8,128)(2,1)} %collective-permute-done.12.refs_1_.refs_9_.refs_11_.refs_10_.refs_5_, ...), custom_call_target="tpu_custom_call" | custom-call | flops 1 | bytes 1 | tf_op jit(solution)/shard_map/keys_values/pallas_call | solution.py:237
  86.7 1.8 collective-permute-start.20
  90.9 9.7 %attend.2 = (bf16[1280,256]{1,0:T(8,128)(2,1)}, bf16[256,1280]{1,0:T(8,128)(2,1)}, bf16[64,1408]{1,0:T(8,128)(2,1)}, bf16[64,1408]{1,0:T(8,128)(2,1)}, bf16[64,1...) custom-call(s32[2]{0:T(128)} %copy-done.39, bf16[192,1408]{1,0:T(8,128)(2,1)} %copy-done.10, bf16[192,1408]{1,0:T(8,128)(2,1)} %copy-done.44, ...), custom_call_target="tpu_custom_call" | custom-call | flops 1 | bytes 1 | tf_op jit(solution)/shard_map/attend/pallas_call | solution.py:333
  101.3 1.5 assemble.3.refs_20_
  102.9 1.6 collective-permute-start.28
  105.1 4.6 %collective-permute-start.23 = (bf16[64,1408]{1,0:T(8,128)(2,1)S(1)}, bf16[64,1408]{1,0:T(8,128)(2,1)S(1)}, u32[]{:S(2)}, u32[]{:S(2)}) collective-permute-start(bf16[64,1408]{1,0:T(8,128)(2,1)S(1)} %copy-done.82), channel_id=1, source_target_pairs={{0,3},{1,2},{2,1},{3,0},{4,7},{5,6},{6,5},{7,4},{8,11},{9,10},{10,... | collective-permute-start | bytes 540680 | tf_op jit(solution)/shard_map/ppermute | solution.py:774
  109.7 2.7 collective-permute-start.22
  113.0 14.2 %attend.3 = (bf16[1280,512]{1,0:T(8,128)(2,1)}, bf16[512,1280]{1,0:T(8,128)(2,1)}, bf16[128,1408]{1,0:T(8,128)(2,1)}, bf16[128,1408]{1,0:T(8,128)(2,1)}, bf16[12...) custom-call(s32[2]{0:T(128)} %copy-done.39, bf16[192,1408]{1,0:T(8,128)(2,1)} %copy-done.10, bf16[192,1408]{1,0:T(8,128)(2,1)} %copy-done.44, ...), custom_call_target="tpu_custom_call" | custom-call | flops 1 | bytes 1 | tf_op jit(solution)/shard_map/attend/pallas_call | solution.py:333
  127.3 2.4 collective-permute-start.26
  130.3 1.5 collective-permute-start.24
  132.7 1.9 slice.74
  136.8 4.1 %collective-permute-done.26.refs_7_ = bf16[128,1408]{1,0:T(8,128)(2,1)S(1)} collective-permute-done((bf16[128,1408]{1,0:T(8,128)(2,1)}, bf16[128,1408]{1,0:T(8,128)(2,1)S(1)}, u32[]{:S(2)}, u32[]{:S(2)}) %collective-permute-start.26) | collective-permute-done | bytes 360480 | tf_op jit(solution)/shard_map/ppermute | solution.py:774
  140.8 19.5 %collective-permute-done.25.refs_5_ = bf16[128,1408]{1,0:T(8,128)(2,1)} collective-permute-done((bf16[128,1408]{1,0:T(8,128)(2,1)}, bf16[128,1408]{1,0:T(8,128)(2,1)}, u32[]{:S(2)}, u32[]{:S(2)}) %collective-permute-start.25) | collective-permute-done | bytes 360480 | tf_op jit(solution)/shard_map/ppermute | solution.py:774
  161.5 7.1 %collective-permute-done.34.refs_28_ = bf16[240,1280]{1,0:T(8,128)(2,1)S(1)} collective-permute-done((bf16[240,1280]{1,0:T(8,128)(2,1)S(1)}, bf16[240,1280]{1,0:T(8,128)(2,1)S(1)}, u32[]{:S(2)}, u32[]{:S(2)}) %collective-permute-start.34) | collective-permute-done | bytes 614432 | tf_op jit(solution)/shard_map/ppermute | solution.py:774
  170.8 14.2 %feed.1 = (bf16[192,1280]{1,0:T(8,128)(2,1)}, f32[192,1280]{1,0:T(8,128)}, bf16[64,1408]{1,0:T(8,128)(2,1)}, bf16[128,1408]{1,0:T(8,128)(2,1)}, bf16[1280,192]{1...) custom-call(s32[2]{0:T(128)} %copy-done.39, ...), custom_call_target="tpu_custom_call" | custom-call | flops 1 | bytes 1 | tf_op jit(solution)/shard_map/feed/pallas_call | solution.py:450
  185.1 3.1 collective-permute-start.36
  188.2 6.7 %feed_grads.1 = (bf16[480,1280]{1,0:T(8,128)(2,1)}, bf16[480,1280]{1,0:T(8,128)(2,1)}, bf16[480,1280]{1,0:T(8,128)(2,1)}, bf16[480,1280]{1,0:T(8,128)(2,1)}, bf1...) custom-call(s32[2]{0:T(128)} %copy-done.39, bf16[1280,192]{1,0:T(8,128)(2,1)} %get-tuple-element.203.refs_0_, ...), custom_call_target="tpu_custom_call" | custom-call | flops 1 | bytes 1 | tf_op jit(solution)/shard_map/feed_grads/pallas_call | solution.py:492
  195.6 1.5 collective-permute-done.36.refs_2_
  197.7 1.5 collective-permute-start.40
  199.3 7.3 %collective-permute-done.40.refs_4_ = bf16[64,1408]{1,0:T(8,128)(2,1)S(1)} collective-permute-done((bf16[64,1408]{1,0:T(8,128)(2,1)S(1)}, bf16[64,1408]{1,0:T(8,128)(2,1)S(1)}, u32[]{:S(2)}, u32[]{:S(2)}) %collective-permute-start.40) | collective-permute-done | bytes 180256 | tf_op jit(solution)/shard_map/ppermute | solution.py:931
  206.7 3.0 collective-permute-start.44
  209.6 2.6 add_convert_fusion
  212.9 1.4 collective-permute-start.42
  214.3 8.8 %attend_back.2 = (bf16[512,1280]{1,0:T(8,128)(2,1)}, bf16[512,1280]{1,0:T(8,128)(2,1)}, bf16[256,1280]{1,0:T(8,128)(2,1)}, bf16[64,1280]{1,0:T(8,128)(2,1)}, bf1...) custom-call(s32[2]{0:T(128)} %copy-done.39, ...), custom_call_target="tpu_custom_call" | custom-call | flops 1 | bytes 1 | tf_op jit(solution)/shard_map/attend_back/pallas_call | solution.py:576
  223.1 1.8 collective-permute-done.45.refs_1_
  230.6 4.2 %meet.2 = (bf16[480,1280]{1,0:T(8,128)(2,1)}, bf16[480,1280]{1,0:T(8,128)(2,1)}) custom-call(bf16[480,1280]{1,0:T(8,128)(2,1)S(1)} %copy-done.13, bf16[240,1280]{1,0:T(8,128)(2,1)S(1)} %collective-permute-done.41.h, bf16[480,1280]{1,0:T(8,128)(2,1)S(1)} %copy-done.14, bf16[240,1280]{1,0:T(8,128)(2,1)} %collective-permute-done.42.l, ...), custom_call_target="tpu_custom_call" | custom-call | flops 1 | bytes 1 | tf_op jit(solution)/shard_map/meet/pallas_call | solution.py:840
  234.7 5.6 %collective-permute-done.47.refs_4_ = bf16[128,1408]{1,0:T(8,128)(2,1)S(1)} collective-permute-done((bf16[128,1408]{1,0:T(8,128)(2,1)}, bf16[128,1408]{1,0:T(8,128)(2,1)S(1)}, u32[]{:S(2)}, u32[]{:S(2)}) %collective-permute-start.47) | collective-permute-done | bytes 360480 | tf_op jit(solution)/shard_map/ppermute | solution.py:931
  240.4 1.4 collective-permute-start.54
  241.8 1.4 collective-permute-start.55
  243.2 2.5 collective-permute-start.49
  245.8 1.8 collective-permute-start.50
  247.6 15.2 %attend_back.3 = (bf16[1024,1280]{1,0:T(8,128)(2,1)}, bf16[1024,1280]{1,0:T(8,128)(2,1)}, bf16[512,1280]{1,0:T(8,128)(2,1)}, bf16[128,1280]{1,0:T(8,128)(2,1)}, ...) custom-call(s32[2]{0:T(128)} %copy-done.39, ...), custom_call_target="tpu_custom_call" | custom-call | flops 1 | bytes 1 | tf_op jit(solution)/shard_map/attend_back/pallas_call | solution.py:576
  264.2 3.9 %collective-permute-start.53 = (bf16[128,1280]{1,0:T(8,128)(2,1)}, bf16[128,1280]{1,0:T(8,128)(2,1)S(1)}, u32[]{:S(2)}, u32[]{:S(2)}) collective-permute-start(bf16[128,1280]{1,0:T(8,128)(2,1)} %get-tuple-element.249), channel_id=1, source_target_pairs={{3,2},{0,1},{7,6},{4,5},{11,10},{8,9},{15,14},{12,13},{19,18},{16,... | collective-permute-start | bytes 983048 | tf_op jit(solution)/shard_map/ppermute | solution.py:936
  269.1 15.0 %weight_grads.1 = (bf16[352,1280]{1,0:T(8,128)(2,1)}, bf16[352,1280]{1,0:T(8,128)(2,1)}, bf16[352,1280]{1,0:T(8,128)(2,1)}, bf16[352,1280]{1,0:T(8,128)(2,1)}, b...) custom-call(s32[2]{0:T(128)} %copy-done.39, bf16[768,1536]{1,0:T(8,128)(2,1)} %get-tuple-element.199.refs_0_, ...), custom_call_target="tpu_custom_call" | custom-call | flops 1 | bytes 1 | tf_op jit(solution)/shard_map/weight_grads/pallas_call | solution.py:648
  286.6 2.7 collective-permute-done.56
  292.1 2.1 collective-permute-start.62
  294.2 4.2 %cut.2 = (f32[120,1280]{1,0:T(8,128)S(1)}, bf16[120,1280]{1,0:T(8,128)(2,1)}, bf16[120,1280]{1,0:T(8,128)(2,1)}, bf16[120,1280]{1,0:T(8,128)(2,1)}) custom-call(s32[2]{0:T(128)S(1)} %copy-done.41, bf16[480,1280]{1,0:T(8,128)(2,1)S(1)} %copy-done.15, bf16[1440,1280]{1,0:T(8,128)(2,1)} %collective-permute-done.43.o.refs_1_, ...), custom_call_target="tpu_custom_call" | custom-call | flops 1 | bytes 1 | tf_op jit(solution)/shard_map/cut/pallas_call | solution.py:869
  298.4 4.5 %collective-permute-done.57.h = bf16[160,1280]{1,0:T(8,128)(2,1)S(1)} collective-permute-done((bf16[160,1280]{1,0:T(8,128)(2,1)S(1)}, bf16[160,1280]{1,0:T(8,128)(2,1)S(1)}, u32[]{:S(2)}, u32[]{:S(2)}) %collective-permute-start.57) | collective-permute-done | bytes 409632 | tf_op jit(solution)/shard_map/ppermute | solution.py:774
  303.0 1.4 collective-permute-done.58.l
  304.4 1.7 meet.3
  307.3 2.2 collective-permute-done.62.refs_7_
  310.2 2.5 collective-permute-start.67
  312.7 1.8 collective-permute-start.68
  314.6 16.4 %byte_grad.1 = f32[1536,768]{1,0:T(8,128)} custom-call(s32[2]{0:T(128)} %copy-done.39, bf16[1536,768]{1,0:T(8,128)(2,1)} %bitcast.9, bf16[512,1280]{1,0:T(8,128)(2,1)} %get-tuple-element.269.refs_3_.refs_0_, bf16[512,1280]{1,0:T(8,128)(2,1)} %get-tuple-element.238.refs_5_.refs_1_, bf16[1024,1280]{1,0:T(8,128)(2,1)} %get-tuple-element.237.refs_4_.refs_2_, ...), custom_call_target="tpu_custom_call" | custom-call | flops 1 | bytes 1 | tf_op jit(solution)/shard_map/byte_grad/pallas_call | solution.py:708
  331.0 3.8 %collective-permute-done.67 = bf16[120,1280]{1,0:T(8,128)(2,1)} collective-permute-done((bf16[120,1280]{1,0:T(8,128)(2,1)}, bf16[120,1280]{1,0:T(8,128)(2,1)}, u32[]{:S(2)}, u32[]{:S(2)}) %collective-permute-start.67) | collective-permute-done | bytes 307232 | tf_op jit(solution)/shard_map/ppermute | solution.py:774
  334.8 1.5 convert_add_fusion
  336.5 2.2 cut.3
  338.8 2.0 collective-permute-start.65
  340.8 7.0 %collective-permute-start.64 = (bf16[88,1280]{1,0:T(8,128)(2,1)S(1)}, bf16[88,1280]{1,0:T(8,128)(2,1)S(1)}, u32[]{:S(2)}, u32[]{:S(2)}) collective-permute-start(bf16[88,1280]{1,0:T(8,128)(2,1)S(1)} %get-tuple-element.279), channel_id=1, source_target_pairs={{0,2},{1,3},{2,0},{3,1},{4,6},{5,7},{6,4},{7,5},{8,10},{9,11},{10,... | collective-permute-start | bytes 675848 | tf_op jit(solution)/shard_map/ppermute | solution.py:774
  349.4 3.0 latent_grad.1
  352.5 8.4 %collective-permute-done.64 = bf16[88,1280]{1,0:T(8,128)(2,1)S(1)} collective-permute-done((bf16[88,1280]{1,0:T(8,128)(2,1)S(1)}, bf16[88,1280]{1,0:T(8,128)(2,1)S(1)}, u32[]{:S(2)}, u32[]{:S(2)}) %collective-permute-start.64) | collective-permute-done | bytes 225312 | tf_op jit(solution)/shard_map/ppermute | solution.py:774
  (287 shorter events, 45.7 us)
Async XLA Ops:
  2.4 15.4 %collective-permute-start.1 = (bf16[96,1280]{1,0:T(8,128)(2,1)S(1)}, bf16[96,1280]{1,0:T(8,128)(2,1)S(1)}, u32[]{:S(2)}, u32[]{:S(2)}) collective-permute-start(bf16[96,1280]{1,0:T(8,128)(2,1)S(1)} %fusion.8.refs_0_), channel_id=1, source_target_pairs={{0,2},{1,3},{2,0},{3,1},{4,6},{5,7},{6,4},{7,5},{8,10},{9,11},{10,... | collective-permute-start | bytes 737288 | tf_op jit(solution)/shard_map/ppermute | solution.py:774
  6.5 11.5 %collective-permute-start = (bf16[96,1280]{1,0:T(8,128)(2,1)S(1)}, bf16[96,1280]{1,0:T(8,128)(2,1)S(1)}, u32[]{:S(2)}, u32[]{:S(2)}) collective-permute-start(bf16[96,1280]{1,0:T(8,128)(2,1)S(1)} %fusion.8.refs_0_), channel_id=1, source_target_pairs={{0,1},{1,0},{2,3},{3,2},{4,5},{5,4},{6,7},{7,6},{8,9},{9,8},{10,11... | collective-permute-start | bytes 737288 | tf_op jit(solution)/shard_map/ppermute | solution.py:774
  18.7 9.3 %collective-permute-start.3 = (bf16[96,1280]{1,0:T(8,128)(2,1)S(1)}, bf16[96,1280]{1,0:T(8,128)(2,1)S(1)}, u32[]{:S(2)}, u32[]{:S(2)}) collective-permute-start(bf16[96,1280]{1,0:T(8,128)(2,1)S(1)} %collective-permute-done.1.refs_2_), channel_id=1, source_target_pairs={{2,3},{1,0},{6,7},{5,4},{10,11},{9,8},{14,15},{13,12},{18,19},{17,... | collective-permute-start | bytes 737288 | tf_op jit(solution)/shard_map/ppermute | solution.py:931
  29.2 20.9 %collective-permute-start.4 = (bf16[368,1280]{1,0:T(8,128)(2,1)S(1)}, bf16[368,1280]{1,0:T(8,128)(2,1)S(1)}, u32[]{:S(2)}, u32[]{:S(2)}) collective-permute-start(bf16[368,1280]{1,0:T(8,128)(2,1)S(1)} %assemble.2.refs_0_.refs_8_.refs_10_.refs_9_.refs_4_), channel_id=1, source_target_pairs={{0,8},{4,12},{8,0},{12,4},{16,24},{20,28},{24,16},{28,20},{1,9},{5... | collective-permute-start | bytes 2826248 | tf_op jit(solution)/shard_map/ppermute | solution.py:774
  30.7 20.9 %collective-permute-start.5 = (bf16[368,1280]{1,0:T(8,128)(2,1)S(1)}, bf16[368,1280]{1,0:T(8,128)(2,1)S(1)}, u32[]{:S(2)}, u32[]{:S(2)}) collective-permute-start(bf16[368,1280]{1,0:T(8,128)(2,1)S(1)} %assemble.2.refs_0_.refs_8_.refs_10_.refs_9_.refs_4_), channel_id=1, source_target_pairs={{0,16},{4,20},{8,24},{12,28},{16,0},{20,4},{24,8},{28,12},{1,17},{... | collective-permute-start | bytes 2826248 | tf_op jit(solution)/shard_map/ppermute | solution.py:774
  32.3 29.0 %collective-permute-start.12 = (bf16[368,1280]{1,0:T(8,128)(2,1)S(1)}, bf16[368,1280]{1,0:T(8,128)(2,1)}, u32[]{:S(2)}, u32[]{:S(2)}) collective-permute-start(bf16[368,1280]{1,0:T(8,128)(2,1)S(1)} %assemble.2.refs_0_.refs_8_.refs_10_.refs_9_.refs_4_), channel_id=1, source_target_pairs={{0,4},{4,0},{8,12},{12,8},{16,20},{20,16},{24,28},{28,24},{1,5},{5... | collective-permute-start | bytes 2826248 | tf_op jit(solution)/shard_map/ppermute | solution.py:774
  32.5 26.1 %collective-permute-start.9 = (bf16[192,1408]{1,0:T(8,128)(2,1)S(1)}, bf16[192,1408]{1,0:T(8,128)(2,1)S(1)}, u32[]{:S(2)}, u32[]{:S(2)}) collective-permute-start(bf16[192,1408]{1,0:T(8,128)(2,1)S(1)} %fusion.1.refs_0_.refs_8_.x_ref), channel_id=1, source_target_pairs={{0,1},{1,0},{2,3},{3,2},{4,5},{5,4},{6,7},{7,6},{8,9},{9,8},{10,11... | collective-permute-start | bytes 1622024 | tf_op jit(solution)/shard_map/ppermute | solution.py:774
  32.8 28.5 %collective-permute-start.8 = (bf16[192,1408]{1,0:T(8,128)(2,1)S(1)}, bf16[192,1408]{1,0:T(8,128)(2,1)}, u32[]{:S(2)}, u32[]{:S(2)}) collective-permute-start(bf16[192,1408]{1,0:T(8,128)(2,1)S(1)} %fusion.1.refs_0_.refs_8_.x_ref), channel_id=1, source_target_pairs={{0,2},{1,3},{2,0},{3,1},{4,6},{5,7},{6,4},{7,5},{8,10},{9,11},{10,... | collective-permute-start | bytes 1622024 | tf_op jit(solution)/shard_map/ppermute | solution.py:774
  51.7 10.4 %collective-permute-start.6 = (bf16[192,1280]{1,0:T(8,128)(2,1)S(1)}, bf16[192,1280]{1,0:T(8,128)(2,1)S(1)}, u32[]{:S(2)}, u32[]{:S(2)}) collective-permute-start(bf16[192,1280]{1,0:T(8,128)(2,1)S(1)} %slice.72), channel_id=1, source_target_pairs={{0,16},{4,20},{8,24},{12,28},{16,0},{20,4},{24,8},{28,12},{1,17},{... | collective-permute-start | bytes 1474568 | tf_op jit(solution)/shard_map/ppermute | solution.py:774
  53.3 8.8 %collective-permute-start.7 = (bf16[176,1280]{1,0:T(8,128)(2,1)S(1)}, bf16[176,1280]{1,0:T(8,128)(2,1)}, u32[]{:S(2)}, u32[]{:S(2)}) collective-permute-start(bf16[176,1280]{1,0:T(8,128)(2,1)S(1)} %slice.73), channel_id=1, source_target_pairs={{0,8},{4,12},{8,0},{12,4},{16,24},{20,28},{24,16},{28,20},{1,9},{5... | collective-permute-start | bytes 1351688 | tf_op jit(solution)/shard_map/ppermute | solution.py:774
  62.0 7.5 %collective-permute-start.15 = (bf16[192,1280]{1,0:T(8,128)(2,1)S(1)}, bf16[192,1280]{1,0:T(8,128)(2,1)}, u32[]{:S(2)}, u32[]{:S(2)}) collective-permute-start(bf16[192,1280]{1,0:T(8,128)(2,1)S(1)} %collective-permute-done.6.refs_6_.refs_14_.refs_16_.refs_15_.refs_10_), channel_id=1, source_target_pairs={{0,4},{4,0},{8,12},{12,8},{16,20},{20,16},{24,28},{28,24},{1,5},{5... | collective-permute-start | bytes 1474568 | tf_op jit(solution)/shard_map/ppermute | solution.py:774
  62.6 7.7 %collective-permute-start.13 = (bf16[368,1280]{1,0:T(8,128)(2,1)S(1)}, bf16[368,1280]{1,0:T(8,128)(2,1)S(1)}, u32[]{:S(2)}, u32[]{:S(2)}) collective-permute-start(bf16[368,1280]{1,0:T(8,128)(2,1)S(1)} %collective-permute-done.4.refs_2_.refs_10_.refs_12_.refs_11_.refs_6_), channel_id=1, source_target_pairs={{0,4},{4,0},{8,12},{12,8},{16,20},{20,16},{24,28},{28,24},{1,5},{5... | collective-permute-start | bytes 2826248 | tf_op jit(solution)/shard_map/ppermute | solution.py:774
  62.6 8.9 %collective-permute-start.14 = (bf16[368,1280]{1,0:T(8,128)(2,1)S(1)}, bf16[368,1280]{1,0:T(8,128)(2,1)}, u32[]{:S(2)}, u32[]{:S(2)}) collective-permute-start(bf16[368,1280]{1,0:T(8,128)(2,1)S(1)} %collective-permute-done.5.refs_4_.refs_12_.refs_14_.refs_13_.refs_8_), channel_id=1, source_target_pairs={{0,4},{4,0},{8,12},{12,8},{16,20},{20,16},{24,28},{28,24},{1,5},{5... | collective-permute-start | bytes 2826248 | tf_op jit(solution)/shard_map/ppermute | solution.py:774
  63.1 22.2 %collective-permute-start.11 = (bf16[120,1280]{1,0:T(8,128)(2,1)}, bf16[120,1280]{1,0:T(8,128)(2,1)S(1)}, u32[]{:S(2)}, u32[]{:S(2)}) collective-permute-start(bf16[120,1280]{1,0:T(8,128)(2,1)} %copy-done.23), channel_id=1, source_target_pairs={{0,1},{1,0},{2,3},{3,2},{4,5},{5,4},{6,7},{7,6},{8,9},{9,8},{10,11... | collective-permute-start | bytes 921608 | tf_op jit(solution)/shard_map/ppermute | solution.py:774
  64.2 21.9 %collective-permute-start.10 = (bf16[120,1280]{1,0:T(8,128)(2,1)}, bf16[120,1280]{1,0:T(8,128)(2,1)}, u32[]{:S(2)}, u32[]{:S(2)}) collective-permute-start(bf16[120,1280]{1,0:T(8,128)(2,1)} %copy-done.23), channel_id=1, source_target_pairs={{0,2},{1,3},{2,0},{3,1},{4,6},{5,7},{6,4},{7,5},{8,10},{9,11},{10,... | collective-permute-start | bytes 921608 | tf_op jit(solution)/shard_map/ppermute | solution.py:774
  69.5 20.3 %collective-permute-start.17 = (bf16[192,1408]{1,0:T(8,128)(2,1)}, bf16[192,1408]{1,0:T(8,128)(2,1)S(1)}, u32[]{:S(2)}, u32[]{:S(2)}) collective-permute-start(bf16[192,1408]{1,0:T(8,128)(2,1)} %copy-done.10), channel_id=1, source_target_pairs={{1,2},{2,1},{5,6},{6,5},{9,10},{10,9},{13,14},{14,13},{17,18},{18,... | collective-permute-start | bytes 1622024 | tf_op jit(solution)/shard_map/ppermute | solution.py:930
  70.3 20.6 %collective-permute-start.18 = (bf16[192,1408]{1,0:T(8,128)(2,1)}, bf16[192,1408]{1,0:T(8,128)(2,1)}, u32[]{:S(2)}, u32[]{:S(2)}) collective-permute-start(bf16[192,1408]{1,0:T(8,128)(2,1)} %passed.3.refs_2_), channel_id=1, source_target_pairs={{2,3},{1,0},{6,7},{5,4},{10,11},{9,8},{14,15},{13,12},{18,19},{17,... | collective-permute-start | bytes 1622024 | tf_op jit(solution)/shard_map/ppermute | solution.py:931
  86.1 14.5 %collective-permute-start.19 = (bf16[120,1280]{1,0:T(8,128)(2,1)S(1)}, bf16[120,1280]{1,0:T(8,128)(2,1)S(1)}, u32[]{:S(2)}, u32[]{:S(2)}) collective-permute-start(bf16[120,1280]{1,0:T(8,128)(2,1)S(1)} %copy-done.24), channel_id=1, source_target_pairs={{1,2},{2,1},{5,6},{6,5},{9,10},{10,9},{13,14},{14,13},{17,18},{18,... | collective-permute-start | bytes 921608 | tf_op jit(solution)/shard_map/ppermute | solution.py:930
  86.7 14.6 %collective-permute-start.20 = (bf16[120,1280]{1,0:T(8,128)(2,1)}, bf16[120,1280]{1,0:T(8,128)(2,1)S(1)}, u32[]{:S(2)}, u32[]{:S(2)}) collective-permute-start(bf16[120,1280]{1,0:T(8,128)(2,1)} %collective-permute-done.10.refs_2_), channel_id=1, source_target_pairs={{2,3},{1,0},{6,7},{5,4},{10,11},{9,8},{14,15},{13,12},{18,19},{17,... | collective-permute-start | bytes 921608 | tf_op jit(solution)/shard_map/ppermute | solution.py:931
  102.9 28.9 %collective-permute-start.28 = (bf16[480,1280]{1,0:T(8,128)(2,1)S(1)}, bf16[480,1280]{1,0:T(8,128)(2,1)S(1)}, u32[]{:S(2)}, u32[]{:S(2)}) collective-permute-start(bf16[480,1280]{1,0:T(8,128)(2,1)S(1)} %assemble.3.refs_20_), channel_id=1, source_target_pairs={{0,16},{4,20},{8,24},{12,28},{16,0},{20,4},{24,8},{28,12},{1,17},{... | collective-permute-start | bytes 3686408 | tf_op jit(solution)/shard_map/ppermute | solution.py:774
  104.4 28.2 %collective-permute-start.27 = (bf16[480,1280]{1,0:T(8,128)(2,1)S(1)}, bf16[480,1280]{1,0:T(8,128)(2,1)}, u32[]{:S(2)}, u32[]{:S(2)}) collective-permute-start(bf16[480,1280]{1,0:T(8,128)(2,1)S(1)} %assemble.3.refs_20_), channel_id=1, source_target_pairs={{0,8},{4,12},{8,0},{12,4},{16,24},{20,28},{24,16},{28,20},{1,9},{5... | collective-permute-start | bytes 3686408 | tf_op jit(solution)/shard_map/ppermute | solution.py:774
  105.1 22.1 %collective-permute-start.23 = (bf16[64,1408]{1,0:T(8,128)(2,1)S(1)}, bf16[64,1408]{1,0:T(8,128)(2,1)S(1)}, u32[]{:S(2)}, u32[]{:S(2)}) collective-permute-start(bf16[64,1408]{1,0:T(8,128)(2,1)S(1)} %copy-done.82), channel_id=1, source_target_pairs={{0,3},{1,2},{2,1},{3,0},{4,7},{5,6},{6,5},{7,4},{8,11},{9,10},{10,... | collective-permute-start | bytes 540680 | tf_op jit(solution)/shard_map/ppermute | solution.py:774
  109.7 17.5 %collective-permute-start.22 = (bf16[64,1408]{1,0:T(8,128)(2,1)S(1)}, bf16[64,1408]{1,0:T(8,128)(2,1)S(1)}, u32[]{:S(2)}, u32[]{:S(2)}) collective-permute-start(bf16[64,1408]{1,0:T(8,128)(2,1)S(1)} %copy-done.81), channel_id=1, source_target_pairs={{0,2},{1,3},{2,0},{3,1},{4,6},{5,7},{6,4},{7,5},{8,10},{9,11},{10,... | collective-permute-start | bytes 540680 | tf_op jit(solution)/shard_map/ppermute | solution.py:774
  112.4 14.8 %collective-permute-start.21 = (bf16[64,1408]{1,0:T(8,128)(2,1)S(1)}, bf16[64,1408]{1,0:T(8,128)(2,1)S(1)}, u32[]{:S(2)}, u32[]{:S(2)}) collective-permute-start(bf16[64,1408]{1,0:T(8,128)(2,1)S(1)} %copy-done.80), channel_id=1, source_target_pairs={{0,1},{1,0},{2,3},{3,2},{4,5},{5,4},{6,7},{7,6},{8,9},{9,8},{10,11... | collective-permute-start | bytes 540680 | tf_op jit(solution)/shard_map/ppermute | solution.py:774
  127.3 13.5 %collective-permute-start.26 = (bf16[128,1408]{1,0:T(8,128)(2,1)}, bf16[128,1408]{1,0:T(8,128)(2,1)S(1)}, u32[]{:S(2)}, u32[]{:S(2)}) collective-permute-start(bf16[128,1408]{1,0:T(8,128)(2,1)} %get-tuple-element.186), channel_id=1, source_target_pairs={{0,3},{1,2},{2,1},{3,0},{4,7},{5,6},{6,5},{7,4},{8,11},{9,10},{10,... | collective-permute-start | bytes 1081352 | tf_op jit(solution)/shard_map/ppermute | solution.py:774
  129.7 30.6 %collective-permute-start.25 = (bf16[128,1408]{1,0:T(8,128)(2,1)}, bf16[128,1408]{1,0:T(8,128)(2,1)}, u32[]{:S(2)}, u32[]{:S(2)}) collective-permute-start(bf16[128,1408]{1,0:T(8,128)(2,1)} %get-tuple-element.184), channel_id=1, source_target_pairs={{0,2},{1,3},{2,0},{3,1},{4,6},{5,7},{6,4},{7,5},{8,10},{9,11},{10,... | collective-permute-start | bytes 1081352 | tf_op jit(solution)/shard_map/ppermute | solution.py:774
  130.3 30.0 %collective-permute-start.24 = (bf16[128,1408]{1,0:T(8,128)(2,1)}, bf16[128,1408]{1,0:T(8,128)(2,1)}, u32[]{:S(2)}, u32[]{:S(2)}) collective-permute-start(bf16[128,1408]{1,0:T(8,128)(2,1)} %get-tuple-element.182), channel_id=1, source_target_pairs={{0,1},{1,0},{2,3},{3,2},{4,5},{5,4},{6,7},{7,6},{8,9},{9,8},{10,11... | collective-permute-start | bytes 1081352 | tf_op jit(solution)/shard_map/ppermute | solution.py:774
  134.6 25.7 %collective-permute-start.29 = (bf16[240,1280]{1,0:T(8,128)(2,1)}, bf16[240,1280]{1,0:T(8,128)(2,1)S(1)}, u32[]{:S(2)}, u32[]{:S(2)}) collective-permute-start(bf16[240,1280]{1,0:T(8,128)(2,1)} %slice.74), channel_id=1, source_target_pairs={{0,16},{4,20},{8,24},{12,28},{16,0},{20,4},{24,8},{28,12},{1,17},{... | collective-permute-start | bytes 1843208 | tf_op jit(solution)/shard_map/ppermute | solution.py:774
  135.5 24.9 %collective-permute-start.30 = (bf16[240,1280]{1,0:T(8,128)(2,1)}, bf16[240,1280]{1,0:T(8,128)(2,1)}, u32[]{:S(2)}, u32[]{:S(2)}) collective-permute-start(bf16[240,1280]{1,0:T(8,128)(2,1)} %slice.75), channel_id=1, source_target_pairs={{0,8},{4,12},{8,0},{12,4},{16,24},{20,28},{24,16},{28,20},{1,9},{5... | collective-permute-start | bytes 1843208 | tf_op jit(solution)/shard_map/ppermute | solution.py:774
  160.3 8.3 %collective-permute-start.31 = (bf16[480,1280]{1,0:T(8,128)(2,1)S(1)}, bf16[480,1280]{1,0:T(8,128)(2,1)S(1)}, u32[]{:S(2)}, u32[]{:S(2)}) collective-permute-start(bf16[480,1280]{1,0:T(8,128)(2,1)S(1)} %assemble.3.refs_20_), channel_id=1, source_target_pairs={{0,4},{4,0},{8,12},{12,8},{16,20},{20,16},{24,28},{28,24},{1,5},{5... | collective-permute-start | bytes 3686408 | tf_op jit(solution)/shard_map/ppermute | solution.py:774
  160.4 8.2 %collective-permute-start.32 = (bf16[480,1280]{1,0:T(8,128)(2,1)}, bf16[480,1280]{1,0:T(8,128)(2,1)S(1)}, u32[]{:S(2)}, u32[]{:S(2)}) collective-permute-start(bf16[480,1280]{1,0:T(8,128)(2,1)} %collective-permute-done.27.refs_22_), channel_id=1, source_target_pairs={{0,4},{4,0},{8,12},{12,8},{16,20},{20,16},{24,28},{28,24},{1,5},{5... | collective-permute-start | bytes 3686408 | tf_op jit(solution)/shard_map/ppermute | solution.py:774
  160.9 7.7 %collective-permute-start.33 = (bf16[480,1280]{1,0:T(8,128)(2,1)S(1)}, bf16[480,1280]{1,0:T(8,128)(2,1)S(1)}, u32[]{:S(2)}, u32[]{:S(2)}) collective-permute-start(bf16[480,1280]{1,0:T(8,128)(2,1)S(1)} %collective-permute-done.28.refs_24_), channel_id=1, source_target_pairs={{0,4},{4,0},{8,12},{12,8},{16,20},{20,16},{24,28},{28,24},{1,5},{5... | collective-permute-start | bytes 3686408 | tf_op jit(solution)/shard_map/ppermute | solution.py:774
  161.0 7.6 %collective-permute-start.34 = (bf16[240,1280]{1,0:T(8,128)(2,1)S(1)}, bf16[240,1280]{1,0:T(8,128)(2,1)S(1)}, u32[]{:S(2)}, u32[]{:S(2)}) collective-permute-start(bf16[240,1280]{1,0:T(8,128)(2,1)S(1)} %collective-permute-done.29.refs_26_), channel_id=1, source_target_pairs={{0,4},{4,0},{8,12},{12,8},{16,20},{20,16},{24,28},{28,24},{1,5},{5... | collective-permute-start | bytes 1843208 | tf_op jit(solution)/shard_map/ppermute | solution.py:774
  161.4 7.2 %collective-permute-start.35 = (bf16[240,1280]{1,0:T(8,128)(2,1)}, bf16[240,1280]{1,0:T(8,128)(2,1)S(1)}, u32[]{:S(2)}, u32[]{:S(2)}) collective-permute-start(bf16[240,1280]{1,0:T(8,128)(2,1)} %collective-permute-done.30.refs_27_), channel_id=1, source_target_pairs={{0,4},{4,0},{8,12},{12,8},{16,20},{20,16},{24,28},{28,24},{1,5},{5... | collective-permute-start | bytes 1843208 | tf_op jit(solution)/shard_map/ppermute | solution.py:774
  185.0 10.6 %collective-permute-start.37 = (bf16[64,1408]{1,0:T(8,128)(2,1)}, bf16[64,1408]{1,0:T(8,128)(2,1)S(1)}, u32[]{:S(2)}, u32[]{:S(2)}) collective-permute-start(bf16[64,1408]{1,0:T(8,128)(2,1)} %get-tuple-element.212.refs_0_), channel_id=1, source_target_pairs={{0,1},{1,0},{2,3},{3,2},{4,5},{5,4},{6,7},{7,6},{8,9},{9,8},{10,11... | collective-permute-start | bytes 540680 | tf_op jit(solution)/shard_map/ppermute | solution.py:774
  185.1 11.9 %collective-permute-start.36 = (bf16[64,1408]{1,0:T(8,128)(2,1)}, bf16[64,1408]{1,0:T(8,128)(2,1)S(1)}, u32[]{:S(2)}, u32[]{:S(2)}) collective-permute-start(bf16[64,1408]{1,0:T(8,128)(2,1)} %get-tuple-element.212.refs_0_), channel_id=1, source_target_pairs={{0,2},{1,3},{2,0},{3,1},{4,6},{5,7},{6,4},{7,5},{8,10},{9,11},{10,... | collective-permute-start | bytes 540680 | tf_op jit(solution)/shard_map/ppermute | solution.py:774
  197.0 9.5 %collective-permute-start.38 = (bf16[480,1280]{1,0:T(8,128)(2,1)}, bf16[480,1280]{1,0:T(8,128)(2,1)S(1)}, u32[]{:S(2)}, u32[]{:S(2)}) collective-permute-start(bf16[480,1280]{1,0:T(8,128)(2,1)} %get-tuple-element.209), channel_id=1, source_target_pairs={{0,4},{4,0},{8,12},{12,8},{16,20},{20,16},{24,28},{28,24},{1,5},{5... | collective-permute-start | bytes 3686408 | tf_op jit(solution)/shard_map/ppermute | solution.py:774
  197.7 8.8 %collective-permute-start.40 = (bf16[64,1408]{1,0:T(8,128)(2,1)S(1)}, bf16[64,1408]{1,0:T(8,128)(2,1)S(1)}, u32[]{:S(2)}, u32[]{:S(2)}) collective-permute-start(bf16[64,1408]{1,0:T(8,128)(2,1)S(1)} %collective-permute-done.36.refs_2_), channel_id=1, source_target_pairs={{2,3},{1,0},{6,7},{5,4},{10,11},{9,8},{14,15},{13,12},{18,19},{17,... | collective-permute-start | bytes 540680 | tf_op jit(solution)/shard_map/ppermute | solution.py:931
  206.6 22.0 %collective-permute-start.43 = (bf16[1440,1280]{1,0:T(8,128)(2,1)}, bf16[1440,1280]{1,0:T(8,128)(2,1)}, u32[]{:S(2)}, u32[]{:S(2)}) collective-permute-start(bf16[1440,1280]{1,0:T(8,128)(2,1)} %get-tuple-element.220), channel_id=1, source_target_pairs={{0,4},{4,0},{8,12},{12,8},{16,20},{20,16},{24,28},{28,24},{1,5},{5... | collective-permute-start | bytes 11059208 | tf_op jit(solution)/shard_map/ppermute | solution.py:774
  206.6 18.3 %collective-permute-start.45 = (bf16[128,1408]{1,0:T(8,128)(2,1)S(1)}, bf16[128,1408]{1,0:T(8,128)(2,1)S(1)}, u32[]{:S(2)}, u32[]{:S(2)}) collective-permute-start(bf16[128,1408]{1,0:T(8,128)(2,1)S(1)} %copy-done.57), channel_id=1, source_target_pairs={{0,1},{1,0},{2,3},{3,2},{4,5},{5,4},{6,7},{7,6},{8,9},{9,8},{10,11... | collective-permute-start | bytes 1081352 | tf_op jit(solution)/shard_map/ppermute | solution.py:774
  206.7 19.5 %collective-permute-start.44 = (bf16[128,1408]{1,0:T(8,128)(2,1)S(1)}, bf16[128,1408]{1,0:T(8,128)(2,1)S(1)}, u32[]{:S(2)}, u32[]{:S(2)}) collective-permute-start(bf16[128,1408]{1,0:T(8,128)(2,1)S(1)} %copy-done.57), channel_id=1, source_target_pairs={{0,2},{1,3},{2,0},{3,1},{4,6},{5,7},{6,4},{7,5},{8,10},{9,11},{10,... | collective-permute-start | bytes 1081352 | tf_op jit(solution)/shard_map/ppermute | solution.py:774
  212.2 15.9 %collective-permute-start.41 = (bf16[240,1280]{1,0:T(8,128)(2,1)}, bf16[240,1280]{1,0:T(8,128)(2,1)S(1)}, u32[]{:S(2)}, u32[]{:S(2)}) collective-permute-start(bf16[240,1280]{1,0:T(8,128)(2,1)} %get-tuple-element.217), channel_id=1, source_target_pairs={{0,16},{4,20},{8,24},{12,28},{16,0},{20,4},{24,8},{28,12},{1,17},{... | collective-permute-start | bytes 1843208 | tf_op jit(solution)/shard_map/ppermute | solution.py:774
  212.9 15.7 %collective-permute-start.42 = (bf16[240,1280]{1,0:T(8,128)(2,1)}, bf16[240,1280]{1,0:T(8,128)(2,1)}, u32[]{:S(2)}, u32[]{:S(2)}) collective-permute-start(bf16[240,1280]{1,0:T(8,128)(2,1)} %get-tuple-element.218), channel_id=1, source_target_pairs={{0,8},{4,12},{8,0},{12,4},{16,24},{20,28},{24,16},{28,20},{1,9},{5... | collective-permute-start | bytes 1843208 | tf_op jit(solution)/shard_map/ppermute | solution.py:774
  229.2 11.1 %collective-permute-start.47 = (bf16[128,1408]{1,0:T(8,128)(2,1)}, bf16[128,1408]{1,0:T(8,128)(2,1)S(1)}, u32[]{:S(2)}, u32[]{:S(2)}) collective-permute-start(bf16[128,1408]{1,0:T(8,128)(2,1)} %passed.5.refs_2_), channel_id=1, source_target_pairs={{2,3},{1,0},{6,7},{5,4},{10,11},{9,8},{14,15},{13,12},{18,19},{17,... | collective-permute-start | bytes 1081352 | tf_op jit(solution)/shard_map/ppermute | solution.py:931
  240.4 45.2 %collective-permute-start.54 = (bf16[480,1280]{1,0:T(8,128)(2,1)}, bf16[480,1280]{1,0:T(8,128)(2,1)S(1)}, u32[]{:S(2)}, u32[]{:S(2)}) collective-permute-start(bf16[480,1280]{1,0:T(8,128)(2,1)} %get-tuple-element.250), channel_id=1, source_target_pairs={{0,8},{4,12},{8,0},{12,4},{16,24},{20,28},{24,16},{28,20},{1,9},{5... | collective-permute-start | bytes 3686408 | tf_op jit(solution)/shard_map/ppermute | solution.py:774
  241.8 43.8 %collective-permute-start.55 = (bf16[480,1280]{1,0:T(8,128)(2,1)}, bf16[480,1280]{1,0:T(8,128)(2,1)S(1)}, u32[]{:S(2)}, u32[]{:S(2)}) collective-permute-start(bf16[480,1280]{1,0:T(8,128)(2,1)} %get-tuple-element.251), channel_id=1, source_target_pairs={{0,16},{4,20},{8,24},{12,28},{16,0},{20,4},{24,8},{28,12},{1,17},{... | collective-permute-start | bytes 3686408 | tf_op jit(solution)/shard_map/ppermute | solution.py:774
  243.2 19.6 %collective-permute-start.48 = (bf16[64,1280]{1,0:T(8,128)(2,1)}, bf16[64,1280]{1,0:T(8,128)(2,1)S(1)}, u32[]{:S(2)}, u32[]{:S(2)}) collective-permute-start(bf16[64,1280]{1,0:T(8,128)(2,1)} %get-tuple-element.232), channel_id=1, source_target_pairs={{0,1},{1,0},{2,3},{3,2},{4,5},{5,4},{6,7},{7,6},{8,9},{9,8},{10,11... | collective-permute-start | bytes 491528 | tf_op jit(solution)/shard_map/ppermute | solution.py:774
  243.2 19.6 %collective-permute-start.49 = (bf16[64,1280]{1,0:T(8,128)(2,1)}, bf16[64,1280]{1,0:T(8,128)(2,1)S(1)}, u32[]{:S(2)}, u32[]{:S(2)}) collective-permute-start(bf16[64,1280]{1,0:T(8,128)(2,1)} %get-tuple-element.234), channel_id=1, source_target_pairs={{0,2},{1,3},{2,0},{3,1},{4,6},{5,7},{6,4},{7,5},{8,10},{9,11},{10,... | collective-permute-start | bytes 491528 | tf_op jit(solution)/shard_map/ppermute | solution.py:774
  245.8 17.8 %collective-permute-start.50 = (bf16[64,1280]{1,0:T(8,128)(2,1)}, bf16[64,1280]{1,0:T(8,128)(2,1)S(1)}, u32[]{:S(2)}, u32[]{:S(2)}) collective-permute-start(bf16[64,1280]{1,0:T(8,128)(2,1)} %get-tuple-element.236), channel_id=1, source_target_pairs={{0,3},{1,2},{2,1},{3,0},{4,7},{5,6},{6,5},{7,4},{8,11},{9,10},{10,... | collective-permute-start | bytes 491528 | tf_op jit(solution)/shard_map/ppermute | solution.py:774
  264.2 19.9 %collective-permute-start.51 = (bf16[128,1280]{1,0:T(8,128)(2,1)}, bf16[128,1280]{1,0:T(8,128)(2,1)S(1)}, u32[]{:S(2)}, u32[]{:S(2)}) collective-permute-start(bf16[128,1280]{1,0:T(8,128)(2,1)} %get-tuple-element.247), channel_id=1, source_target_pairs={{0,1},{1,0},{2,3},{3,2},{4,5},{5,4},{6,7},{7,6},{8,9},{9,8},{10,11... | collective-permute-start | bytes 983048 | tf_op jit(solution)/shard_map/ppermute | solution.py:774
  264.2 20.6 %collective-permute-start.53 = (bf16[128,1280]{1,0:T(8,128)(2,1)}, bf16[128,1280]{1,0:T(8,128)(2,1)S(1)}, u32[]{:S(2)}, u32[]{:S(2)}) collective-permute-start(bf16[128,1280]{1,0:T(8,128)(2,1)} %get-tuple-element.249), channel_id=1, source_target_pairs={{3,2},{0,1},{7,6},{4,5},{11,10},{8,9},{15,14},{12,13},{19,18},{16,... | collective-permute-start | bytes 983048 | tf_op jit(solution)/shard_map/ppermute | solution.py:936
  268.1 16.7 %collective-permute-start.52 = (bf16[128,1280]{1,0:T(8,128)(2,1)}, bf16[128,1280]{1,0:T(8,128)(2,1)S(1)}, u32[]{:S(2)}, u32[]{:S(2)}) collective-permute-start(bf16[128,1280]{1,0:T(8,128)(2,1)} %get-tuple-element.249), channel_id=1, source_target_pairs={{1,2},{2,1},{5,6},{6,5},{9,10},{10,9},{13,14},{14,13},{17,18},{18,... | collective-permute-start | bytes 983048 | tf_op jit(solution)/shard_map/ppermute | solution.py:935
  289.3 15.1 %collective-permute-start.59 = (bf16[1056,1280]{1,0:T(8,128)(2,1)}, bf16[1056,1280]{1,0:T(8,128)(2,1)S(1)}, u32[]{:S(2)}, u32[]{:S(2)}) collective-permute-start(bf16[1056,1280]{1,0:T(8,128)(2,1)} %get-tuple-element.262), channel_id=1, source_target_pairs={{0,4},{4,0},{8,12},{12,8},{16,20},{20,16},{24,28},{28,24},{1,5},{5... | collective-permute-start | bytes 8110088 | tf_op jit(solution)/shard_map/ppermute | solution.py:774
  290.8 13.6 %collective-permute-start.58 = (bf16[192,1280]{1,0:T(8,128)(2,1)S(1)}, bf16[192,1280]{1,0:T(8,128)(2,1)S(1)}, u32[]{:S(2)}, u32[]{:S(2)}) collective-permute-start(bf16[192,1280]{1,0:T(8,128)(2,1)S(1)} %add_convert_fusion.2), channel_id=1, source_target_pairs={{0,8},{4,12},{8,0},{12,4},{16,24},{20,28},{24,16},{28,20},{1,9},{5... | collective-permute-start | bytes 1474568 | tf_op jit(solution)/shard_map/ppermute | solution.py:774
  291.5 11.5 %collective-permute-start.57 = (bf16[160,1280]{1,0:T(8,128)(2,1)S(1)}, bf16[160,1280]{1,0:T(8,128)(2,1)S(1)}, u32[]{:S(2)}, u32[]{:S(2)}) collective-permute-start(bf16[160,1280]{1,0:T(8,128)(2,1)S(1)} %add_convert_fusion.3), channel_id=1, source_target_pairs={{0,16},{4,20},{8,24},{12,28},{16,0},{20,4},{24,8},{28,12},{1,17},{... | collective-permute-start | bytes 1228808 | tf_op jit(solution)/shard_map/ppermute | solution.py:774
  292.1 17.3 %collective-permute-start.62 = (bf16[128,1280]{1,0:T(8,128)(2,1)S(1)}, bf16[128,1280]{1,0:T(8,128)(2,1)S(1)}, u32[]{:S(2)}, u32[]{:S(2)}) collective-permute-start(bf16[128,1280]{1,0:T(8,128)(2,1)S(1)} %add_convert_fusion.4), channel_id=1, source_target_pairs={{0,2},{1,3},{2,0},{3,1},{4,6},{5,7},{6,4},{7,5},{8,10},{9,11},{10,... | collective-permute-start | bytes 983048 | tf_op jit(solution)/shard_map/ppermute | solution.py:774
  306.1 30.3 %collective-permute-start.60 = (bf16[352,1280]{1,0:T(8,128)(2,1)}, bf16[352,1280]{1,0:T(8,128)(2,1)S(1)}, u32[]{:S(2)}, u32[]{:S(2)}) collective-permute-start(bf16[352,1280]{1,0:T(8,128)(2,1)} %get-tuple-element.267), channel_id=1, source_target_pairs={{0,8},{4,12},{8,0},{12,4},{16,24},{20,28},{24,16},{28,20},{1,9},{5... | collective-permute-start | bytes 2703368 | tf_op jit(solution)/shard_map/ppermute | solution.py:774
  306.7 29.7 %collective-permute-start.61 = (bf16[352,1280]{1,0:T(8,128)(2,1)}, bf16[352,1280]{1,0:T(8,128)(2,1)}, u32[]{:S(2)}, u32[]{:S(2)}) collective-permute-start(bf16[352,1280]{1,0:T(8,128)(2,1)} %get-tuple-element.268), channel_id=1, source_target_pairs={{0,16},{4,20},{8,24},{12,28},{16,0},{20,4},{24,8},{28,12},{1,17},{... | collective-permute-start | bytes 2703368 | tf_op jit(solution)/shard_map/ppermute | solution.py:774
  310.2 20.8 %collective-permute-start.66 = (bf16[120,1280]{1,0:T(8,128)(2,1)}, bf16[120,1280]{1,0:T(8,128)(2,1)}, u32[]{:S(2)}, u32[]{:S(2)}) collective-permute-start(bf16[120,1280]{1,0:T(8,128)(2,1)} %get-tuple-element.283), channel_id=1, source_target_pairs={{0,1},{1,0},{2,3},{3,2},{4,5},{5,4},{6,7},{7,6},{8,9},{9,8},{10,11... | collective-permute-start | bytes 921608 | tf_op jit(solution)/shard_map/ppermute | solution.py:774
  310.2 24.6 %collective-permute-start.67 = (bf16[120,1280]{1,0:T(8,128)(2,1)}, bf16[120,1280]{1,0:T(8,128)(2,1)}, u32[]{:S(2)}, u32[]{:S(2)}) collective-permute-start(bf16[120,1280]{1,0:T(8,128)(2,1)} %get-tuple-element.285), channel_id=1, source_target_pairs={{0,2},{1,3},{2,0},{3,1},{4,6},{5,7},{6,4},{7,5},{8,10},{9,11},{10,... | collective-permute-start | bytes 921608 | tf_op jit(solution)/shard_map/ppermute | solution.py:774
  312.7 22.1 %collective-permute-start.68 = (bf16[120,1280]{1,0:T(8,128)(2,1)}, bf16[120,1280]{1,0:T(8,128)(2,1)}, u32[]{:S(2)}, u32[]{:S(2)}) collective-permute-start(bf16[120,1280]{1,0:T(8,128)(2,1)} %get-tuple-element.287), channel_id=1, source_target_pairs={{0,3},{1,2},{2,1},{3,0},{4,7},{5,6},{6,5},{7,4},{8,11},{9,10},{10,... | collective-permute-start | bytes 921608 | tf_op jit(solution)/shard_map/ppermute | solution.py:774
  338.8 13.7 %collective-permute-start.65 = (bf16[88,1280]{1,0:T(8,128)(2,1)S(1)}, bf16[88,1280]{1,0:T(8,128)(2,1)S(1)}, u32[]{:S(2)}, u32[]{:S(2)}) collective-permute-start(bf16[88,1280]{1,0:T(8,128)(2,1)S(1)} %get-tuple-element.281), channel_id=1, source_target_pairs={{0,3},{1,2},{2,1},{3,0},{4,7},{5,6},{6,5},{7,4},{8,11},{9,10},{10,... | collective-permute-start | bytes 675848 | tf_op jit(solution)/shard_map/ppermute | solution.py:774
  340.8 20.1 %collective-permute-start.64 = (bf16[88,1280]{1,0:T(8,128)(2,1)S(1)}, bf16[88,1280]{1,0:T(8,128)(2,1)S(1)}, u32[]{:S(2)}, u32[]{:S(2)}) collective-permute-start(bf16[88,1280]{1,0:T(8,128)(2,1)S(1)} %get-tuple-element.279), channel_id=1, source_target_pairs={{0,2},{1,3},{2,0},{3,1},{4,6},{5,7},{6,4},{7,5},{8,10},{9,11},{10,... | collective-permute-start | bytes 675848 | tf_op jit(solution)/shard_map/ppermute | solution.py:774
  347.8 13.1 %collective-permute-start.63 = (bf16[88,1280]{1,0:T(8,128)(2,1)S(1)}, bf16[88,1280]{1,0:T(8,128)(2,1)S(1)}, u32[]{:S(2)}, u32[]{:S(2)}) collective-permute-start(bf16[88,1280]{1,0:T(8,128)(2,1)S(1)} %get-tuple-element.277), channel_id=1, source_target_pairs={{0,1},{1,0},{2,3},{3,2},{4,5},{5,4},{6,7},{7,6},{8,9},{9,8},{10,11... | collective-permute-start | bytes 675848 | tf_op jit(solution)/shard_map/ppermute | solution.py:774
  (88 other events, 863.4 us)
